TPU v7x, 32 devices: a whole 2x2x4 slice. The times are simulated.
32 devices in a mesh: samp: 8 (over z, y), cell: 4 (over x, core).
Axes of the slice: x: 2, y: 2, z: 4, core: 2. Of those that a mesh axis runs over, the one named last changes fastest.
Arguments:
- points: float32 [24, 16384], P(None, 'samp'), may hold values from -1 to 1
- yields: bfloat16 [16384, 1024], P('samp', 'cell'), may hold values from -6 to 6
- term_index: int32 [512, 2], replicated, may hold values from 0 to 95, as said below
- block_group: int32 [8], replicated, may hold values from 0 to 7
Outputs:
- coefficients: float32 [512, 1024], P('cell')
- sobol: float32 [8, 1024], P(None, 'cell')
Inputs may be any that keep to these rules, and one draw needn't show every extreme that they name: `term_index`: row 0 is 0, 0 (the constant term); every other row names one parameter with degree 1 to 3 and column 0, or two different parameters with degrees 1 to 3 each, the lower column first; no two rows are the same.
All inputs are finite; a program needn't handle non-finite values.
Results may differ from a plain program's by a relative error of at most 0.0037.
Values sent between devices are 32-bit elements; how exact they have to be, the bound alone decides.
No kernel may reach another device: no remote copies, remote signals or barrier semaphores. Data moves between devices by JAX's collectives and lax.ppermute only.
A program may use at most 64 MiB of HBM per device.

v0:
```python
import functools

import jax
import jax.numpy as jnp
from jax import lax
from jax.experimental import pallas as pl
from jax.experimental.pallas import tpu as pltpu
from jax.sharding import PartitionSpec as P

BLOCK = 64
GROUPS = 8
TILE = 128
HIGH = lax.Precision.HIGHEST


def split3(values):
    top = values.astype(jnp.bfloat16).astype(jnp.float32)
    rest = values - top
    middle = rest.astype(jnp.bfloat16).astype(jnp.float32)
    return top, middle, rest - middle


def picks(column, params, width):
    span = 3 * params
    degree = column % 4
    place = (degree - 1) * params + column // 4
    lanes = lax.broadcasted_iota(jnp.int32, (column.shape[0], width), 1)
    hit = (lanes == place) | (lanes == place + span) | (lanes == place + 2 * span)
    hit = (hit & (degree > 0)) | ((lanes == 3 * span) & (degree == 0))
    return hit.astype(jnp.float32).astype(jnp.bfloat16)


def design_kernel(chunk, cell_ref, index_ref, points_ref, psi_ref, fold_ref, table_ref):
    params, samples = points_ref.shape
    terms = index_ref.shape[0]
    width = table_ref.shape[0]
    span = 3 * params
    xs = points_ref[...]
    first = 1.7320508075688772 * xs
    second = 2.23606797749979 * (1.5 * xs * xs - 0.5)
    third = 2.6457513110645907 * (2.5 * xs * xs * xs - 1.5 * xs)
    for at, rows in enumerate((first, second, third)):
        for part, values in enumerate(split3(rows)):
            table_ref[pl.ds(part * span + at * params, params), :] = values
    table_ref[pl.ds(3 * span, width - 3 * span), :] = jnp.ones((width - 3 * span, samples), jnp.float32)
    pick_a = picks(index_ref[:, 0:1], params, width)
    pick_b = picks(index_ref[:, 1:2], params, width)
    for start in range(0, samples, chunk):
        table = table_ref[:, start:start + chunk].astype(jnp.bfloat16)
        left = jnp.dot(pick_a, table, preferred_element_type=jnp.float32)
        right = jnp.dot(pick_b, table, preferred_element_type=jnp.float32)
        psi_ref[:, start:start + chunk] = (left * right).astype(jnp.bfloat16)
    blocks = terms // TILE
    part_rows = fold_ref.shape[0] // 2
    cell = cell_ref[0]
    for block in range(blocks):
        rows = psi_ref[pl.ds(pl.multiple_of(block * TILE + cell * part_rows, part_rows), part_rows), :]
        reach = (block + 1) * TILE
        value = lax.dot_general(
            rows, psi_ref[0:reach, :], (((1,), (1,)), ((), ())), preferred_element_type=jnp.float32
        )
        half, at = fold_place(block, blocks)
        fold_ref[half * part_rows:(half + 1) * part_rows, at:at + reach] = value


def fold_place(block, blocks):
    low = min(block, blocks - 1 - block)
    return low, 0 if block == low else (low + 1) * TILE


def design(points, term_index, cell, n_cell):
    params, samples = points.shape
    terms = term_index.shape[0]
    blocks = terms // TILE
    rows = 2 * TILE // n_cell
    return pl.pallas_call(
        functools.partial(design_kernel, 512),
        out_shape=(
            jax.ShapeDtypeStruct((terms, samples), jnp.bfloat16),
            jax.ShapeDtypeStruct((rows, (blocks + 1) * TILE), jnp.float32),
        ),
        in_specs=[
            pl.BlockSpec(memory_space=pltpu.SMEM),
            pl.BlockSpec(memory_space=pltpu.VMEM),
            pl.BlockSpec(memory_space=pltpu.VMEM),
        ],
        out_specs=(pl.BlockSpec(memory_space=pltpu.VMEM),) * 2,
        scratch_shapes=[pltpu.VMEM((256, samples), jnp.float32)],
        compiler_params=pltpu.CompilerParams(vmem_limit_bytes=32 * 2**20),
        name="design",
    )(cell.reshape(1), term_index, points)


def lane_of(values, at):
    return jnp.broadcast_to(values[:, at:at + 1], values.shape)


def row_of(values, at):
    return jnp.broadcast_to(values[at:at + 1, :], values.shape)


def sweep_tile(bands):
    bands = list(bands)
    shape = bands[0].shape
    subs = lax.broadcasted_iota(jnp.int32, shape, 0)
    lanes = lax.broadcasted_iota(jnp.int32, shape, 1)
    for at in range(len(bands)):
        base = 8 * at
        own = bands[at]
        inside = (lanes >= base) & (lanes < base + 8)
        columns = [lane_of(own, base + k) for k in range(8)]
        pivot = [[row_of(columns[k], i) if k <= i else None for k in range(8)] for i in range(8)]
        edged = jnp.where(inside, jnp.where(lanes == subs + base, -1.0, 0.0), own)
        rows = [row_of(edged, i) for i in range(8)]
        factor = [[None] * 8 for _ in range(8)]
        pairs = []
        for p in range(0, 8, 2):
            q = p + 1
            a, b, d = pivot[p][p], pivot[q][p], pivot[q][q]
            inverse = 1.0 / (a * d - b * b)
            pairs.append((a, b, d, inverse))
            mixed = [None] * 8
            for i in range(q + 1, 8):
                e, f = pivot[i][p], pivot[i][q]
                mixed[i] = (d * e - b * f, a * f - b * e)
                factor[i][p], factor[i][q] = mixed[i][0] * inverse, mixed[i][1] * inverse
            for i in range(q + 1, 8):
                for k in range(q + 1, i + 1):
                    less = mixed[i][0] * pivot[k][p] + mixed[i][1] * pivot[k][q]
                    pivot[i][k] = pivot[i][k] - less * inverse
                rows[i] = rows[i] - (factor[i][p] * rows[p] + factor[i][q] * rows[q])
        for p in range(0, 8, 2):
            a, b, d, inverse = pairs[p // 2]
            top, low = rows[p], rows[p + 1]
            rows[p], rows[p + 1] = (d * top - b * low) * inverse, (a * low - b * top) * inverse
        for p in range(6, 0, -2):
            for i in range(p):
                rows[i] = rows[i] - (factor[p][i] * rows[p] + factor[p + 1][i] * rows[p + 1])
        for step in range(1, len(bands)):
            other = (at + step) % len(bands)
            value = jnp.where(inside, 0.0, bands[other])
            for k in range(7, -1, -1):
                value = value - lane_of(bands[other], base + k) * rows[k]
            bands[other] = value
        fresh = rows[0]
        for i in range(1, 8):
            fresh = jnp.where(subs == i, rows[i], fresh)
        bands[at] = fresh
    return bands


def stacked_dot(left, right):
    a = [part.astype(jnp.bfloat16) for part in split3(left)]
    b = [part.astype(jnp.bfloat16) for part in split3(right)]
    left = jnp.concatenate([a[0], a[0], a[1], a[1], a[0], a[2]], axis=1)
    right = jnp.concatenate([b[0], b[1], b[0], b[1], b[2], b[0]], axis=0)
    return jnp.dot(left, right, preferred_element_type=jnp.float32)


def sweep_block(gram_ref, block):
    band = slice(block * TILE, (block + 1) * TILE)
    bands = sweep_tile(gram_ref[block * TILE + at:block * TILE + at + 8, band] for at in range(0, TILE, 8))
    minus = jnp.concatenate(bands, axis=0)
    old = gram_ref[band, :]
    columns = gram_ref[:, band]
    fresh = -stacked_dot(minus, old)
    gram_ref[...] -= stacked_dot(columns, fresh)
    gram_ref[band, :] = fresh
    gram_ref[:, band] = fresh.T
    gram_ref[band, band] = minus


def first_kernel(where_ref, *refs):
    out_ref, scale_ref = refs[-2:]
    terms = out_ref.shape[0]
    blocks = terms // TILE
    for step, ref in enumerate(refs[:-2]):
        piece = ref.shape[0] // 2
        start = pl.multiple_of((where_ref[0] ^ step) * piece, piece)
        for block in range(blocks):
            half, lane = fold_place(block, blocks)
            reach = (block + 1) * TILE
            out_ref[pl.ds(start + block * TILE, piece), 0:reach] = (
                ref[half * piece:(half + 1) * piece, lane:lane + reach]
            )
    for block in range(blocks):
        for other in range(block):
            tile = out_ref[block * TILE:(block + 1) * TILE, other * TILE:(other + 1) * TILE]
            out_ref[other * TILE:(other + 1) * TILE, block * TILE:(block + 1) * TILE] = tile.T
    diagonal = lax.broadcasted_iota(jnp.int32, (TILE, TILE), 0) == lax.broadcasted_iota(jnp.int32, (TILE, TILE), 1)
    across = []
    for block in range(blocks):
        band = slice(block * TILE, (block + 1) * TILE)
        only = jnp.where(diagonal, out_ref[band, band], 0.0)
        scale_ref[band, :] = lax.rsqrt(jnp.sum(only, axis=1, keepdims=True))
        across.append(lax.rsqrt(jnp.sum(only, axis=0, keepdims=True)))
    out_ref[...] = out_ref[...] * scale_ref[...] * jnp.concatenate(across, axis=1)
    sweep_block(out_ref, 0)


def next_kernel(block, in_ref, out_ref):
    out_ref[...] = in_ref[...]
    sweep_block(out_ref, block)


STEP_COST = pl.CostEstimate(flops=5 * 10**9, bytes_accessed=2 * 2**20, transcendentals=512)
VMEM = pl.BlockSpec(memory_space=pltpu.VMEM)
SMEM = pl.BlockSpec(memory_space=pltpu.SMEM)
BIG = pltpu.CompilerParams(vmem_limit_bytes=32 * 2**20)


def first_block(where, pieces, terms):
    return pl.pallas_call(
        first_kernel,
        out_shape=(
            jax.ShapeDtypeStruct((terms, terms), jnp.float32),
            jax.ShapeDtypeStruct((terms, 1), jnp.float32),
        ),
        in_specs=[SMEM] + [VMEM] * len(pieces),
        out_specs=(VMEM, VMEM),
        compiler_params=BIG,
        cost_estimate=STEP_COST,
        name="block_0",
    )(where, *pieces)


def next_block(gram, block):
    return pl.pallas_call(
        functools.partial(next_kernel, block),
        out_shape=jax.ShapeDtypeStruct(gram.shape, jnp.float32),
        in_specs=[VMEM],
        out_specs=VMEM,
        input_output_aliases={0: 0},
        compiler_params=BIG,
        cost_estimate=STEP_COST,
        name="block_%d" % block,
    )(gram)


def finish_kernel(samples, n_cell, rows, where_ref, group_ref, inverse_ref, scale_ref, *refs):
    pieces = refs[:-(n_cell + 3)]
    coef_refs = refs[-(n_cell + 3):-3]
    sobol_ref, cross_ref, hold_ref = refs[-3:]
    step = 0
    for ref in pieces:
        for at in range(0, ref.shape[0], rows):
            cross_ref[pl.ds(pl.multiple_of((where_ref[0] ^ step) * rows, rows), rows), :] = ref[at:at + rows, :]
            step += 1
    terms, cells = cross_ref.shape
    scaled = scale_ref[...] * cross_ref[...]
    scaled = jnp.dot(inverse_ref[...], scaled, precision=HIGH, preferred_element_type=jnp.float32)
    coef = -scale_ref[...] * scaled
    hold_ref[...] = coef * jnp.sqrt(jnp.float32(samples))
    share = terms // n_cell
    for step, ref in enumerate(coef_refs):
        ref[...] = hold_ref[pl.ds(pl.multiple_of((where_ref[1] ^ step) * share, share), share), :]
    squares = coef * coef
    keep = lax.broadcasted_iota(jnp.int32, squares.shape, 0) >= 1
    squares = jnp.where(keep, squares, 0.0)
    sums = [
        jnp.sum(squares[at:at + BLOCK], axis=0, keepdims=True) for at in range(0, terms, BLOCK)
    ]
    total = functools.reduce(jnp.add, sums)
    for group in range(GROUPS):
        part = jnp.zeros_like(total)
        for at, value in enumerate(sums):
            part = part + jnp.where(group_ref[at] == group, value, 0.0)
        sobol_ref[group:group + 1, :] = part / total


def finish(where, inverse, scale, pieces, rows, block_group, samples, n_cell):
    terms = inverse.shape[0]
    cells = pieces[0].shape[1]
    share = jax.ShapeDtypeStruct((terms // n_cell, cells), jnp.float32)
    *shares, sobol = pl.pallas_call(
        functools.partial(finish_kernel, samples, n_cell, rows),
        out_shape=(share,) * n_cell + (jax.ShapeDtypeStruct((GROUPS, cells), jnp.float32),),
        in_specs=[SMEM, SMEM] + [VMEM] * (2 + len(pieces)),
        out_specs=(VMEM,) * (n_cell + 1),
        scratch_shapes=[pltpu.VMEM((terms, cells), jnp.float32)] * 2,
        compiler_params=BIG,
        name="finish",
    )(where, block_group, inverse, scale, *pieces)
    return shares, sobol


def join_kernel(where_ref, *refs):
    out_ref = refs[-1]
    for step, ref in enumerate(refs[:-1]):
        wide = ref.shape[1]
        out_ref[:, pl.ds(pl.multiple_of((where_ref[0] ^ step) * wide, wide), wide)] = ref[...]


def join_columns(where, shares):
    rows, wide = shares[0].shape
    return pl.pallas_call(
        join_kernel,
        out_shape=jax.ShapeDtypeStruct((rows, wide * len(shares)), jnp.float32),
        in_specs=[SMEM] + [VMEM] * len(shares),
        out_specs=VMEM,
        name="join_columns",
    )(where, *shares)


def swap(values, axis, step):
    size = lax.axis_size(axis)
    return lax.ppermute(values, axis, [(at, at ^ step) for at in range(size)])


def exchange(pieces):
    return lax.all_to_all(pieces, "samp", split_axis=0, concat_axis=0)


def spread(piece):
    return jnp.broadcast_to(piece[None], (lax.axis_size("samp"),) + piece.shape)


def halve(values, me, bit):
    rows, lanes = values.shape
    halves = values.reshape(2, rows // 2, lanes)
    mine = (me >> bit) & 1
    kept = lax.dynamic_index_in_dim(halves, mine, axis=0, keepdims=False)
    sent = lax.dynamic_index_in_dim(halves, mine ^ 1, axis=0, keepdims=False)
    return kept + swap(sent, "samp", 1 << bit)


def on_device(points, yields, term_index, block_group):
    n_samp = lax.axis_size("samp")
    n_cell = lax.axis_size("cell")
    me, cell = lax.axis_index("samp"), lax.axis_index("cell")
    blocks = term_index.shape[0] // TILE
    psi, fold = design(points, term_index, cell, n_cell)
    pieces = fold.reshape((n_samp, 8, -1) if fold.shape[0] % (8 * n_samp) else (n_samp, -1, fold.shape[1]))
    came = exchange(pieces)
    cross = jnp.dot(psi, yields, preferred_element_type=jnp.float32)
    came, cross = lax.optimization_barrier((came, cross))
    part = halve(cross, me, 0)
    fold = exchange(spread(jnp.sum(came, axis=0))).reshape(fold.shape)
    part = halve(part, me, 1)
    fold, part = lax.optimization_barrier((fold, part))
    part = halve(part, me, 2)
    bit = 8
    while bit < n_samp:
        part = part + swap(part, "samp", bit)
        bit *= 2
    held, order = [fold], [0]
    step = n_cell // 2
    while step:
        held = held + [swap(value, "cell", step) for value in held]
        order = order + [value ^ step for value in order]
        step //= 2
    held, part = lax.optimization_barrier((held, part))
    gram, scale = first_block(cell.reshape(1), [held[order.index(at)] for at in range(n_cell)], term_index.shape[0])
    rows = part.shape[0]
    for block in range(1, blocks):
        if block <= 2:
            part = jnp.concatenate([part, swap(part, "samp", 8 >> block)], axis=0)
            gram, part = lax.optimization_barrier((gram, part))
        gram = next_block(gram, block)
    pieces = [part, swap(part, "samp", 1)]
    spot = ((me & 1) << 2) | (me & 2) | ((me >> 2) & 1)
    where = jnp.stack([spot, cell])
    shares, sobol = finish(where, gram, scale, pieces, rows, block_group, points.shape[1] * n_samp, n_cell)
    shares = [shares[0]] + [swap(shares[step], "cell", step) for step in range(1, n_cell)]
    return (join_columns(cell.reshape(1), shares), sobol)


def solution(mesh):
    placed = (P(None, "samp"), P("samp", "cell"), P(), P())
    return jax.shard_map(
        on_device,
        mesh=mesh,
        in_specs=placed,
        out_specs=(P("cell", None), P(None, "cell")),
        check_vma=False,
    )
```

profile of v0, /device:TPU:0, one launch (start us, length us, event | category | flops | bytes accessed | tf_op | source)
XLA Modules:
  0.0 89.5 jit_solution(17248492238631275941)
XLA Ops:
  1.6 0.9 %copy-done.1 = f32[24,2048]{1,0:T(8,128)S(1)} copy-done((f32[24,2048]{1,0:T(8,128)S(1)}, f32[24,2048]{1,0:T(8,128)}, u32[]{:S(2)}) %copy-start.1) | copy-done | bytes 196632
  2.5 4.0 %design.1 = (bf16[512,2048]{1,0:T(8,128)(2,1)S(1)}, f32[64,640]{1,0:T(8,128)}) custom-call(s32[1]{0:T(128)} %bitcast.cell_ref.where_ref, s32[512,2]{1,0:T(8,128)S(1)} %copy.9.index_ref, f32[24,2048]{1,0:T(8,128)S(1)} %copy-done.1), custom_call_target="tpu_custom_call" | custom-call | tf_op jit(solution)/shard_map/design/pallas_call | solution.py:76
  6.5 7.3 %all-to-all-start = ((f32[8,8,640]{2,1,0:T(8,128)}), f32[8,8,640]{2,1,0:T(8,128)S(1)}, u32[]{:S(2)}, u32[]{:S(2)}) async-start(f32[8,8,640]{2,1,0:T(8,128)} %bitcast.2), calls=%async_computation | async-start | bytes 327680 | tf_op jit(solution)/shard_map/all_to_all | solution.py:311
  13.8 1.5 %fusion = f32[512,256]{1,0:T(8,128)} fusion(bf16[512,2048]{1,0:T(8,128)(2,1)S(1)} %get-tuple-element.25, bf16[2048,256]{1,0:T(8,128)(2,1)S(1)} %copy-done), kind=kOutput, calls=%fused_computation.9 | convolution fusion | flops 536870912 | bytes 3670016 | tf_op jit(solution)/shard_map/dot_general | solution.py:335
  15.3 6.1 %all-to-all-done = f32[8,8,640]{2,1,0:T(8,128)S(1)} async-done(((f32[8,8,640]{2,1,0:T(8,128)}), f32[8,8,640]{2,1,0:T(8,128)S(1)}, u32[]{:S(2)}, u32[]{:S(2)}) %all-to-all-start) | async-done | bytes 163872 | tf_op jit(solution)/shard_map/all_to_all | solution.py:311
  21.3 1.0 %dynamic-slice_bitcast_fusion = f32[256,256]{1,0:T(8,128)S(1)} fusion(f32[2,256,256]{2,1,0:T(8,128)} %bitcast.28, s32[]{:T(128)S(6)} %select_n.22), kind=kLoop, calls=%fused_computation.2 | loop fusion | bytes 524292 | tf_op jit(solution)/shard_map/jit(dynamic_index_in_dim)/squeeze | solution.py:323
  22.3 1.0 %collective-permute-start = (f32[256,256]{1,0:T(8,128)S(1)}, f32[256,256]{1,0:T(8,128)S(1)}, u32[]{:S(2)}, u32[]{:S(2)}) collective-permute-start(f32[256,256]{1,0:T(8,128)S(1)} %dynamic-slice_bitcast_fusion), channel_id=1, source_target_pairs={{0,4},{4,0},{8,12},{12,8},{16,20},{20,16},{24,28},{28,24},{1,5},{5... | collective-permute-start | bytes 786440 | tf_op jit(solution)/shard_map/ppermute | solution.py:307
  23.3 5.7 %collective-permute-done = f32[256,256]{1,0:T(8,128)S(1)} collective-permute-done((f32[256,256]{1,0:T(8,128)S(1)}, f32[256,256]{1,0:T(8,128)S(1)}, u32[]{:S(2)}, u32[]{:S(2)}) %collective-permute-start) | collective-permute-done | bytes 262176 | tf_op jit(solution)/shard_map/ppermute | solution.py:307
  29.0 1.0 %bitcast_add_fusion = f32[256,256]{1,0:T(8,128)S(1)} fusion(f32[256,256]{1,0:T(8,128)S(1)} %collective-permute-done, f32[2,256,256]{2,1,0:T(8,128)} %bitcast.29, s32[]{:T(128)S(6)} %select_n.21), kind=kLoop, calls=%fused_computation.1 | loop fusion | flops 65536 | bytes 786436 | tf_op jit(solution)/shard_map/add | solution.py:324
  30.8 4.5 %all-to-all-start.1 = ((f32[8,8,640]{2,1,0:T(8,128)}), f32[8,8,640]{2,1,0:T(8,128)S(1)}, u32[]{:S(2)}, u32[]{:S(2)}) async-start(f32[8,8,640]{2,1,0:T(8,128)} %broadcast_in_dim.2), calls=%async_computation.1 | async-start | bytes 327680 | tf_op jit(solution)/shard_map/all_to_all | solution.py:311
  35.3 7.5 %all-to-all-done.1 = f32[8,8,640]{2,1,0:T(8,128)S(1)} async-done(((f32[8,8,640]{2,1,0:T(8,128)}), f32[8,8,640]{2,1,0:T(8,128)S(1)}, u32[]{:S(2)}, u32[]{:S(2)}) %all-to-all-start.1) | async-done | bytes 163872 | tf_op jit(solution)/shard_map/all_to_all | solution.py:311
  42.9 1.5 %collective-permute-start.2 = (f32[64,640]{1,0:T(8,128)S(1)}, f32[64,640]{1,0:T(8,128)S(1)}, u32[]{:S(2)}, u32[]{:S(2)}) collective-permute-start(f32[64,640]{1,0:T(8,128)S(1)} %bitcast.21), channel_id=1, source_target_pairs={{0,2},{1,3},{2,0},{3,1},{4,6},{5,7},{6,4},{7,5},{8,10},{9,11},{10,... | collective-permute-start | bytes 491528 | tf_op jit(solution)/shard_map/ppermute | solution.py:307
  44.8 3.4 %collective-permute-done.2.refs_2_ = f32[64,640]{1,0:T(8,128)S(1)} collective-permute-done((f32[64,640]{1,0:T(8,128)S(1)}, f32[64,640]{1,0:T(8,128)S(1)}, u32[]{:S(2)}, u32[]{:S(2)}) %collective-permute-start.2) | collective-permute-done | bytes 163872 | tf_op jit(solution)/shard_map/ppermute | solution.py:307
  48.2 1.4 %collective-permute-done.5 = f32[64,256]{1,0:T(8,128)S(1)} collective-permute-done((f32[64,256]{1,0:T(8,128)S(1)}, f32[64,256]{1,0:T(8,128)S(1)}, u32[]{:S(2)}, u32[]{:S(2)}) %collective-permute-start.5) | collective-permute-done | bytes 65568 | tf_op jit(solution)/shard_map/ppermute | solution.py:307
  50.0 5.7 %block_0.1 = (f32[512,512]{1,0:T(8,128)S(1)}, f32[512,1]{1,0:T(8,128)S(1)}) custom-call(s32[1]{0:T(128)} %bitcast.cell_ref.where_ref, f32[64,640]{1,0:T(8,128)S(1)} %bitcast.23, f32[64,640]{1,0:T(8,128)S(1)} %collective-permute-done.3.refs_1_, f32[64,640]{1,0:T(8,128)S(1)} %collective-permute-done.2.refs_2_, f32[64,640]{1,0:T(8,128)S(1)} %collective-permute-done.4.refs_3_), custom_call_target="tpu_custom_call" | custom-call | flops 5000000000 | bytes 2097152 | tf_op jit(solution)/shard_map/block_0/pallas_call | solution.py:213
  56.5 5.5 %block_1.1.in_ref = f32[512,512]{1,0:T(8,128)S(1)} custom-call(f32[512,512]{1,0:T(8,128)S(1)} %get-tuple-element.36.in_ref), custom_call_target="tpu_custom_call", output_to_operand_aliasing={{}: (0, {})} | custom-call | flops 5000000000 | bytes 2097152 | tf_op jit(solution)/shard_map/block_1/pallas_call | solution.py:228
  62.0 5.7 %block_2.1.in_ref = f32[512,512]{1,0:T(8,128)S(1)} custom-call(f32[512,512]{1,0:T(8,128)S(1)} %block_1.1.in_ref), custom_call_target="tpu_custom_call", output_to_operand_aliasing={{}: (0, {})} | custom-call | flops 5000000000 | bytes 2097152 | tf_op jit(solution)/shard_map/block_2/pallas_call | solution.py:228
  67.7 1.6 %collective-permute-start.8 = (f32[256,256]{1,0:T(8,128)S(1)}, f32[256,256]{1,0:T(8,128)S(1)}, u32[]{:S(2)}, u32[]{:S(2)}) collective-permute-start(f32[256,256]{1,0:T(8,128)S(1)} %pad_maximum_fusion.refs_0_), channel_id=1, source_target_pairs={{0,4},{4,0},{8,12},{12,8},{16,20},{20,16},{24,28},{28,24},{1,5},{5... | collective-permute-start | bytes 786440 | tf_op jit(solution)/shard_map/ppermute | solution.py:307
  69.3 5.4 %block_3.1.inverse_ref = f32[512,512]{1,0:T(8,128)S(1)} custom-call(f32[512,512]{1,0:T(8,128)S(1)} %block_2.1.in_ref), custom_call_target="tpu_custom_call", output_to_operand_aliasing={{}: (0, {})} | custom-call | flops 5000000000 | bytes 2097152 | tf_op jit(solution)/shard_map/block_3/pallas_call | solution.py:228
  75.5 2.4 %finish.1 = (f32[128,256]{1,0:T(8,128)S(1)}, f32[128,256]{1,0:T(8,128)S(1)}, f32[128,256]{1,0:T(8,128)S(1)}, f32[128,256]{1,0:T(8,128)S(1)}, f32[8,256]{1,0:T(8,128)}) custom-call(s32[2]{0:T(128)S(1)} %pad_add_fusion.where_ref, s32[8]{0:T(128)S(1)} %copy-done.3, f32[512,512]{1,0:T(8,128)S(1)} %block_3.1.inverse_ref, ...), custom_call_target="tpu_custom_call" | custom-call | tf_op jit(solution)/shard_map/finish/pallas_call | solution.py:275
  78.6 1.5 %collective-permute-start.10 = (f32[128,256]{1,0:T(8,128)S(1)}, f32[128,256]{1,0:T(8,128)S(1)}, u32[]{:S(2)}, u32[]{:S(2)}) collective-permute-start(f32[128,256]{1,0:T(8,128)S(1)} %get-tuple-element.43), channel_id=1, source_target_pairs={{0,2},{1,3},{2,0},{3,1},{4,6},{5,7},{6,4},{7,5},{8,10},{9,11},{10,... | collective-permute-start | bytes 393224 | tf_op jit(solution)/shard_map/ppermute | solution.py:307
  80.4 4.4 %collective-permute-done.10.refs_2_ = f32[128,256]{1,0:T(8,128)S(1)} collective-permute-done((f32[128,256]{1,0:T(8,128)S(1)}, f32[128,256]{1,0:T(8,128)S(1)}, u32[]{:S(2)}, u32[]{:S(2)}) %collective-permute-start.10) | collective-permute-done | bytes 131104 | tf_op jit(solution)/shard_map/ppermute | solution.py:307
  84.9 2.0 %collective-permute-done.11.refs_3_ = f32[128,256]{1,0:T(8,128)S(1)} collective-permute-done((f32[128,256]{1,0:T(8,128)S(1)}, f32[128,256]{1,0:T(8,128)S(1)}, u32[]{:S(2)}, u32[]{:S(2)}) %collective-permute-start.11) | collective-permute-done | bytes 131104 | tf_op jit(solution)/shard_map/ppermute | solution.py:307
  87.5 1.9 %join_columns.1 = f32[128,1024]{1,0:T(8,128)} custom-call(s32[1]{0:T(128)} %bitcast.cell_ref.where_ref, f32[128,256]{1,0:T(8,128)} %copy-done.2, f32[128,256]{1,0:T(8,128)} %copy-done.4, f32[128,256]{1,0:T(8,128)} %copy-done.5, f32[128,256]{1,0:T(8,128)} %copy-done.6), custom_call_target="tpu_custom_call" | custom-call | tf_op jit(solution)/shard_map/join_columns/pallas_call | solution.py:296
  (38 shorter events, 6.0 us)
Async XLA Ops:
  0.6 13.2 %copy-start = (bf16[2048,256]{1,0:T(8,128)(2,1)S(1)}, bf16[2048,256]{1,0:T(8,128)(2,1)}, u32[]{:S(2)}) copy-start(bf16[2048,256]{1,0:T(8,128)(2,1)} %param.5) | copy-start | bytes 3145732
  1.6 0.9 %copy-start.1 = (f32[24,2048]{1,0:T(8,128)S(1)}, f32[24,2048]{1,0:T(8,128)}, u32[]{:S(2)}) copy-start(f32[24,2048]{1,0:T(8,128)} %points_ref.1) | copy-start | bytes 589828
  6.5 14.8 %all-to-all-start = ((f32[8,8,640]{2,1,0:T(8,128)}), f32[8,8,640]{2,1,0:T(8,128)S(1)}, u32[]{:S(2)}, u32[]{:S(2)}) async-start(f32[8,8,640]{2,1,0:T(8,128)} %bitcast.2), calls=%async_computation | async-start | bytes 327680 | tf_op jit(solution)/shard_map/all_to_all | solution.py:311
  22.3 6.7 %collective-permute-start = (f32[256,256]{1,0:T(8,128)S(1)}, f32[256,256]{1,0:T(8,128)S(1)}, u32[]{:S(2)}, u32[]{:S(2)}) collective-permute-start(f32[256,256]{1,0:T(8,128)S(1)} %dynamic-slice_bitcast_fusion), channel_id=1, source_target_pairs={{0,4},{4,0},{8,12},{12,8},{16,20},{20,16},{24,28},{28,24},{1,5},{5... | collective-permute-start | bytes 786440 | tf_op jit(solution)/shard_map/ppermute | solution.py:307
  30.0 5.3 %collective-permute-start.1 = (f32[128,256]{1,0:T(8,128)S(1)}, f32[128,256]{1,0:T(8,128)S(1)}, u32[]{:S(2)}, u32[]{:S(2)}) collective-permute-start(f32[128,256]{1,0:T(8,128)S(1)} %dynamic-slice_bitcast_fusion.1), channel_id=1, source_target_pairs={{0,8},{4,12},{8,0},{12,4},{16,24},{20,28},{24,16},{28,20},{1,9},{5... | collective-permute-start | bytes 393224 | tf_op jit(solution)/shard_map/ppermute | solution.py:307
  30.8 12.0 %all-to-all-start.1 = ((f32[8,8,640]{2,1,0:T(8,128)}), f32[8,8,640]{2,1,0:T(8,128)S(1)}, u32[]{:S(2)}, u32[]{:S(2)}) async-start(f32[8,8,640]{2,1,0:T(8,128)} %broadcast_in_dim.2), calls=%async_computation.1 | async-start | bytes 327680 | tf_op jit(solution)/shard_map/all_to_all | solution.py:311
  42.9 5.3 %collective-permute-start.2 = (f32[64,640]{1,0:T(8,128)S(1)}, f32[64,640]{1,0:T(8,128)S(1)}, u32[]{:S(2)}, u32[]{:S(2)}) collective-permute-start(f32[64,640]{1,0:T(8,128)S(1)} %bitcast.21), channel_id=1, source_target_pairs={{0,2},{1,3},{2,0},{3,1},{4,6},{5,7},{6,4},{7,5},{8,10},{9,11},{10,... | collective-permute-start | bytes 491528 | tf_op jit(solution)/shard_map/ppermute | solution.py:307
  44.3 5.2 %collective-permute-start.5 = (f32[64,256]{1,0:T(8,128)S(1)}, f32[64,256]{1,0:T(8,128)S(1)}, u32[]{:S(2)}, u32[]{:S(2)}) collective-permute-start(f32[64,256]{1,0:T(8,128)S(1)} %dynamic-slice_bitcast_fusion.2), channel_id=1, source_target_pairs={{0,16},{4,20},{8,24},{12,28},{16,0},{20,4},{24,8},{28,12},{1,17},{... | collective-permute-start | bytes 196616 | tf_op jit(solution)/shard_map/ppermute | solution.py:307
  44.8 4.8 %collective-permute-start.3 = (f32[64,640]{1,0:T(8,128)S(1)}, f32[64,640]{1,0:T(8,128)S(1)}, u32[]{:S(2)}, u32[]{:S(2)}) collective-permute-start(f32[64,640]{1,0:T(8,128)S(1)} %bitcast.22), channel_id=1, source_target_pairs={{0,1},{1,0},{2,3},{3,2},{4,5},{5,4},{6,7},{7,6},{8,9},{9,8},{10,11... | collective-permute-start | bytes 491528 | tf_op jit(solution)/shard_map/ppermute | solution.py:307
  48.2 1.4 %collective-permute-start.4 = (f32[64,640]{1,0:T(8,128)S(1)}, f32[64,640]{1,0:T(8,128)S(1)}, u32[]{:S(2)}, u32[]{:S(2)}) collective-permute-start(f32[64,640]{1,0:T(8,128)S(1)} %collective-permute-done.2.refs_2_), channel_id=1, source_target_pairs={{0,1},{1,0},{2,3},{3,2},{4,5},{5,4},{6,7},{7,6},{8,9},{9,8},{10,11... | collective-permute-start | bytes 491528 | tf_op jit(solution)/shard_map/ppermute | solution.py:307
  49.6 6.1 %collective-permute-start.6 = (f32[64,256]{1,0:T(8,128)S(1)}, f32[64,256]{1,0:T(8,128)S(1)}, u32[]{:S(2)}, u32[]{:S(2)}) collective-permute-start(f32[64,256]{1,0:T(8,128)S(1)} %bitcast_add_fusion.2), channel_id=1, source_target_pairs={{0,16},{4,20},{8,24},{12,28},{16,0},{20,4},{24,8},{28,12},{1,17},{... | collective-permute-start | bytes 196616 | tf_op jit(solution)/shard_map/ppermute | solution.py:307
  55.7 6.3 %collective-permute-start.7 = (f32[128,256]{1,0:T(8,128)S(1)}, f32[128,256]{1,0:T(8,128)S(1)}, u32[]{:S(2)}, u32[]{:S(2)}) collective-permute-start(f32[128,256]{1,0:T(8,128)S(1)} %pad_maximum_fusion.1), channel_id=1, source_target_pairs={{0,8},{4,12},{8,0},{12,4},{16,24},{20,28},{24,16},{28,20},{1,9},{5... | collective-permute-start | bytes 393224 | tf_op jit(solution)/shard_map/ppermute | solution.py:307
  67.7 7.8 %copy-start.3 = (s32[8]{0:T(128)S(1)}, s32[8]{0:T(128)}, u32[]{:S(2)}) copy-start(s32[8]{0:T(128)} %group_ref.1) | copy-start | bytes 100
  67.7 7.8 %collective-permute-start.8 = (f32[256,256]{1,0:T(8,128)S(1)}, f32[256,256]{1,0:T(8,128)S(1)}, u32[]{:S(2)}, u32[]{:S(2)}) collective-permute-start(f32[256,256]{1,0:T(8,128)S(1)} %pad_maximum_fusion.refs_0_), channel_id=1, source_target_pairs={{0,4},{4,0},{8,12},{12,8},{16,20},{20,16},{24,28},{28,24},{1,5},{5... | collective-permute-start | bytes 786440 | tf_op jit(solution)/shard_map/ppermute | solution.py:307
  77.9 0.7 copy-start.2
  78.6 1.9 %collective-permute-start.9 = (f32[128,256]{1,0:T(8,128)S(1)}, f32[128,256]{1,0:T(8,128)S(1)}, u32[]{:S(2)}, u32[]{:S(2)}) collective-permute-start(f32[128,256]{1,0:T(8,128)S(1)} %get-tuple-element.42), channel_id=1, source_target_pairs={{0,1},{1,0},{2,3},{3,2},{4,5},{5,4},{6,7},{7,6},{8,9},{9,8},{10,11... | collective-permute-start | bytes 393224 | tf_op jit(solution)/shard_map/ppermute | solution.py:307
  78.6 6.3 %collective-permute-start.10 = (f32[128,256]{1,0:T(8,128)S(1)}, f32[128,256]{1,0:T(8,128)S(1)}, u32[]{:S(2)}, u32[]{:S(2)}) collective-permute-start(f32[128,256]{1,0:T(8,128)S(1)} %get-tuple-element.43), channel_id=1, source_target_pairs={{0,2},{1,3},{2,0},{3,1},{4,6},{5,7},{6,4},{7,5},{8,10},{9,11},{10,... | collective-permute-start | bytes 393224 | tf_op jit(solution)/shard_map/ppermute | solution.py:307
  80.0 6.8 %collective-permute-start.11 = (f32[128,256]{1,0:T(8,128)S(1)}, f32[128,256]{1,0:T(8,128)S(1)}, u32[]{:S(2)}, u32[]{:S(2)}) collective-permute-start(f32[128,256]{1,0:T(8,128)S(1)} %get-tuple-element.44), channel_id=1, source_target_pairs={{0,3},{1,2},{2,1},{3,0},{4,7},{5,6},{6,5},{7,4},{8,11},{9,10},{10,... | collective-permute-start | bytes 393224 | tf_op jit(solution)/shard_map/ppermute | solution.py:307
  80.4 6.5 %copy-start.4 = (f32[128,256]{1,0:T(8,128)}, f32[128,256]{1,0:T(8,128)S(1)}, u32[]{:S(2)}) copy-start(f32[128,256]{1,0:T(8,128)S(1)} %collective-permute-done.9.refs_1_) | copy-start | bytes 393220
  84.9 2.0 %copy-start.5 = (f32[128,256]{1,0:T(8,128)}, f32[128,256]{1,0:T(8,128)S(1)}, u32[]{:S(2)}) copy-start(f32[128,256]{1,0:T(8,128)S(1)} %collective-permute-done.10.refs_2_) | copy-start | bytes 393220
  86.9 0.6 copy-start.6
where the time goes:
time: 89.9 us; the launch traced here: 89.5 us
  waiting for transfers between devices  31.4 us (35%)
  Pallas kernels  30.5 us (34%)
  starting transfers between devices  19.3 us (21%)
  local copies, waits for them, and re-layouts  4.82 us (5%)
  matrix products  1.51 us (2%)
  other arithmetic  1.13 us (1%)
    ppermute x12, waiting for transfers between devices, swap(): return lax.ppermute(values, axis, [(at, at ^ step) for at in range(size)])  17.8 us
    pallas_call x3, Pallas kernels, next_block(): pl.pallas_call(functools.partial(next_kernel, block), out_shape=jax.Shape...  16.5 us
    all_to_all x2, waiting for transfers between devices, exchange(): return lax.all_to_all(pieces, 'samp', split_axis=0, concat_axis=0)  13.6 us
    all_to_all x2, starting transfers between devices, exchange(): return lax.all_to_all(pieces, 'samp', split_axis=0, concat_axis=0)  11.8 us
    ppermute x12, starting transfers between devices, swap(): return lax.ppermute(values, axis, [(at, at ^ step) for at in range(size)])  7.56 us
    pallas_call x1, Pallas kernels, first_block(): pl.pallas_call(first_kernel, out_shape=(jax.ShapeDtypeStruct((terms, term...  5.67 us
    pallas_call x1, Pallas kernels, design(): pl.pallas_call(functools.partial(design_kernel, 512), out_shape=(jax.Shap...  4 us
    unnamed x15, local copies, waits for them, and re-layouts  3.15 us
  transfers between devices with their start and end apart: 14, of which 8 were waited for; matrix products, arithmetic and copies ran while one was open for 3% of the time, Pallas kernels for 18%

commit v1 on v0

--- a/solution.py
+++ b/solution.py
@@ -11,6 +11,10 @@
 GROUPS = 8
 TILE = 128
 HIGH = lax.Precision.HIGHEST
+VMEM = pl.BlockSpec(memory_space=pltpu.VMEM)
+SMEM = pl.BlockSpec(memory_space=pltpu.SMEM)
+BIG = pltpu.CompilerParams(vmem_limit_bytes=16 * 2**20)
+SMALL = pltpu.CompilerParams(vmem_limit_bytes=8 * 2**20)
 
 
 def split3(values):
@@ -24,15 +28,15 @@
     span = 3 * params
     degree = column % 4
     place = (degree - 1) * params + column // 4
-    lanes = lax.broadcasted_iota(jnp.int32, (column.shape[0], width), 1)
-    hit = (lanes == place) | (lanes == place + span) | (lanes == place + 2 * span)
-    hit = (hit & (degree > 0)) | ((lanes == 3 * span) & (degree == 0))
-    return hit.astype(jnp.float32).astype(jnp.bfloat16)
+    at = lax.broadcasted_iota(jnp.int32, (width, column.shape[1]), 0)
+    hit = (at == place) | (at == place + span) | (at == place + 2 * span)
+    hit = (hit & (degree > 0)) | ((at == 3 * span) & (degree == 0))
+    return hit.astype(jnp.float32).T.astype(jnp.bfloat16)
 
 
 def design_kernel(chunk, cell_ref, index_ref, points_ref, psi_ref, fold_ref, table_ref):
     params, samples = points_ref.shape
-    terms = index_ref.shape[0]
+    terms = index_ref.shape[1]
     width = table_ref.shape[0]
     span = 3 * params
     xs = points_ref[...]
@@ -43,8 +47,8 @@
         for part, values in enumerate(split3(rows)):
             table_ref[pl.ds(part * span + at * params, params), :] = values
     table_ref[pl.ds(3 * span, width - 3 * span), :] = jnp.ones((width - 3 * span, samples), jnp.float32)
-    pick_a = picks(index_ref[:, 0:1], params, width)
-    pick_b = picks(index_ref[:, 1:2], params, width)
+    pick_a = picks(index_ref[0:1, :], params, width)
+    pick_b = picks(index_ref[1:2, :], params, width)
     for start in range(0, samples, chunk):
         table = table_ref[:, start:start + chunk].astype(jnp.bfloat16)
         left = jnp.dot(pick_a, table, preferred_element_type=jnp.float32)
@@ -79,20 +83,38 @@
             jax.ShapeDtypeStruct((terms, samples), jnp.bfloat16),
             jax.ShapeDtypeStruct((rows, (blocks + 1) * TILE), jnp.float32),
         ),
-        in_specs=[
-            pl.BlockSpec(memory_space=pltpu.SMEM),
-            pl.BlockSpec(memory_space=pltpu.VMEM),
-            pl.BlockSpec(memory_space=pltpu.VMEM),
+        in_specs=[SMEM, VMEM, VMEM],
+        out_specs=(VMEM, VMEM),
+        scratch_shapes=[
+            pltpu.VMEM((256, samples), jnp.float32),
         ],
-        out_specs=(pl.BlockSpec(memory_space=pltpu.VMEM),) * 2,
-        scratch_shapes=[pltpu.VMEM((256, samples), jnp.float32)],
-        compiler_params=pltpu.CompilerParams(vmem_limit_bytes=32 * 2**20),
+        compiler_params=BIG,
         name="design",
-    )(cell.reshape(1), term_index, points)
+    )(cell.reshape(1), term_index.T, points)
+
+
+def cross_kernel(low_ref, psi_ref, yields_ref, kept_ref, sent_ref):
+    rows = kept_ref.shape[0]
+    for ref, which in ((sent_ref, low_ref[0] ^ 1), (kept_ref, low_ref[0])):
+        part = psi_ref[pl.ds(pl.multiple_of(which * rows, rows), rows), :]
+        ref[...] = jnp.dot(part, yields_ref[...], preferred_element_type=jnp.float32)
+
+
+def cross_halves(psi, yields, low):
+    half = jax.ShapeDtypeStruct((psi.shape[0] // 2, yields.shape[1]), jnp.float32)
+    return pl.pallas_call(
+        cross_kernel,
+        out_shape=(half, half),
+        in_specs=[SMEM, VMEM, VMEM],
+        out_specs=(VMEM, VMEM),
+        compiler_params=SMALL,
+        name="cross_halves",
+    )(low.reshape(1), psi, yields)
 
 
 def lane_of(values, at):
-    return jnp.broadcast_to(values[:, at:at + 1], values.shape)
+    lanes = jnp.full(values.shape, at, jnp.int32)
+    return jnp.take_along_axis(values, lanes, axis=1, mode="promise_in_bounds")
 
 
 def row_of(values, at):
@@ -204,9 +226,6 @@
 
 
 STEP_COST = pl.CostEstimate(flops=5 * 10**9, bytes_accessed=2 * 2**20, transcendentals=512)
-VMEM = pl.BlockSpec(memory_space=pltpu.VMEM)
-SMEM = pl.BlockSpec(memory_space=pltpu.SMEM)
-BIG = pltpu.CompilerParams(vmem_limit_bytes=32 * 2**20)
 
 
 def first_block(where, pieces, terms):
@@ -237,10 +256,12 @@
     )(gram)
 
 
-def finish_kernel(samples, n_cell, rows, where_ref, group_ref, inverse_ref, scale_ref, *refs):
-    pieces = refs[:-(n_cell + 3)]
-    coef_refs = refs[-(n_cell + 3):-3]
-    sobol_ref, cross_ref, hold_ref = refs[-3:]
+def solve_kernel(samples, steps, rows, finish, where_ref, group_ref, inverse_ref, scale_ref, *refs):
+    count = len(steps)
+    pieces = refs[:2]
+    others = refs[2:-(count + finish + 1)]
+    cross_ref = refs[-1]
+    shares = refs[-(count + finish + 1):-(finish + 1)]
     step = 0
     for ref in pieces:
         for at in range(0, ref.shape[0], rows):
@@ -248,40 +269,49 @@
             step += 1
     terms, cells = cross_ref.shape
     scaled = scale_ref[...] * cross_ref[...]
-    scaled = jnp.dot(inverse_ref[...], scaled, precision=HIGH, preferred_element_type=jnp.float32)
-    coef = -scale_ref[...] * scaled
-    hold_ref[...] = coef * jnp.sqrt(jnp.float32(samples))
-    share = terms // n_cell
-    for step, ref in enumerate(coef_refs):
-        ref[...] = hold_ref[pl.ds(pl.multiple_of((where_ref[1] ^ step) * share, share), share), :]
-    squares = coef * coef
-    keep = lax.broadcasted_iota(jnp.int32, squares.shape, 0) >= 1
-    squares = jnp.where(keep, squares, 0.0)
-    sums = [
-        jnp.sum(squares[at:at + BLOCK], axis=0, keepdims=True) for at in range(0, terms, BLOCK)
-    ]
-    total = functools.reduce(jnp.add, sums)
+    size = jnp.sqrt(jnp.float32(samples))
+    share = shares[0].shape[0]
+    for step, ref in zip(steps, shares):
+        band = pl.ds(pl.multiple_of((where_ref[1] ^ step) * share, share), share)
+        value = jnp.dot(inverse_ref[band, :], scaled, precision=HIGH, preferred_element_type=jnp.float32)
+        ref[...] = -scale_ref[band, :] * value * size
+    if not finish:
+        return
+    sobol_ref = refs[-2]
+    totals, labels = [], []
+    for step, ref in enumerate(shares + others):
+        owner = where_ref[1] ^ step
+        value = ref[...] / size
+        squares = value * value
+        row = lax.broadcasted_iota(jnp.int32, squares.shape, 0) + owner * share
+        squares = jnp.where(row >= 1, squares, 0.0)
+        for at in range(0, share, BLOCK):
+            totals.append(jnp.sum(squares[at:at + BLOCK], axis=0, keepdims=True))
+            labels.append(group_ref[owner * (share // BLOCK) + at // BLOCK])
+    total = functools.reduce(jnp.add, totals)
     for group in range(GROUPS):
         part = jnp.zeros_like(total)
-        for at, value in enumerate(sums):
-            part = part + jnp.where(group_ref[at] == group, value, 0.0)
+        for label, value in zip(labels, totals):
+            part = part + jnp.where(label == group, value, 0.0)
         sobol_ref[group:group + 1, :] = part / total
 
 
-def finish(where, inverse, scale, pieces, rows, block_group, samples, n_cell):
+def solve(where, inverse, scale, pieces, rows, block_group, samples, n_cell, steps, others=()):
     terms = inverse.shape[0]
     cells = pieces[0].shape[1]
-    share = jax.ShapeDtypeStruct((terms // n_cell, cells), jnp.float32)
-    *shares, sobol = pl.pallas_call(
-        functools.partial(finish_kernel, samples, n_cell, rows),
-        out_shape=(share,) * n_cell + (jax.ShapeDtypeStruct((GROUPS, cells), jnp.float32),),
-        in_specs=[SMEM, SMEM] + [VMEM] * (2 + len(pieces)),
-        out_specs=(VMEM,) * (n_cell + 1),
-        scratch_shapes=[pltpu.VMEM((terms, cells), jnp.float32)] * 2,
+    finish = len(others) > 0
+    out = (jax.ShapeDtypeStruct((terms // n_cell, cells), jnp.float32),) * len(steps)
+    if finish:
+        out += (jax.ShapeDtypeStruct((GROUPS, cells), jnp.float32),)
+    return pl.pallas_call(
+        functools.partial(solve_kernel, samples, steps, rows, finish),
+        out_shape=out,
+        in_specs=[SMEM, SMEM] + [VMEM] * (2 + len(pieces) + len(others)),
+        out_specs=(VMEM,) * len(out),
+        scratch_shapes=[pltpu.VMEM((terms, cells), jnp.float32)],
         compiler_params=BIG,
-        name="finish",
-    )(where, block_group, inverse, scale, *pieces)
-    return shares, sobol
+        name="solve_near" if finish else "solve_far",
+    )(where, block_group, inverse, scale, *pieces, *others)
 
 
 def join_kernel(where_ref, *refs):
@@ -298,6 +328,7 @@
         out_shape=jax.ShapeDtypeStruct((rows, wide * len(shares)), jnp.float32),
         in_specs=[SMEM] + [VMEM] * len(shares),
         out_specs=VMEM,
+        compiler_params=SMALL,
         name="join_columns",
     )(where, *shares)
 
@@ -332,9 +363,9 @@
     psi, fold = design(points, term_index, cell, n_cell)
     pieces = fold.reshape((n_samp, 8, -1) if fold.shape[0] % (8 * n_samp) else (n_samp, -1, fold.shape[1]))
     came = exchange(pieces)
-    cross = jnp.dot(psi, yields, preferred_element_type=jnp.float32)
-    came, cross = lax.optimization_barrier((came, cross))
-    part = halve(cross, me, 0)
+    kept, sent = cross_halves(psi, yields, me & 1)
+    part = kept + swap(sent, "samp", 1)
+    came, part = lax.optimization_barrier((came, part))
     fold = exchange(spread(jnp.sum(came, axis=0))).reshape(fold.shape)
     part = halve(part, me, 1)
     fold, part = lax.optimization_barrier((fold, part))
@@ -360,8 +391,11 @@
     pieces = [part, swap(part, "samp", 1)]
     spot = ((me & 1) << 2) | (me & 2) | ((me >> 2) & 1)
     where = jnp.stack([spot, cell])
-    shares, sobol = finish(where, gram, scale, pieces, rows, block_group, points.shape[1] * n_samp, n_cell)
-    shares = [shares[0]] + [swap(shares[step], "cell", step) for step in range(1, n_cell)]
+    given = (where, gram, scale, pieces, rows, block_group, points.shape[1] * n_samp, n_cell)
+    far = list(solve(*given, tuple(range(n_cell // 2, n_cell))))
+    came = [swap(value, "cell", n_cell // 2 + at) for at, value in enumerate(far)]
+    *near, sobol = solve(*given, tuple(range(n_cell // 2)), far)
+    shares = [near[0]] + [swap(near[step], "cell", step) for step in range(1, n_cell // 2)] + came
     return (join_columns(cell.reshape(1), shares), sobol)
 
 

time: 89.9 us -> 81.5 us (0.907)
  waiting for transfers between devices: 31.4 us -> 27.3 us
  Pallas kernels: 30.5 us -> 28.3 us
  starting transfers between devices: 19.3 us -> 21 us
  matrix products: 1.51 us -> 0 us
  local copies, waits for them, and re-layouts: 4.82 us -> 3.54 us
  other arithmetic: 1.13 us -> 0.18 us
    all_to_all x2, waiting for transfers between devices: 13.6 us -> 7.53 us  [exchange(): return lax.all_to_all(pieces, 'samp', split_axis=0, concat_axis=0)]
    ppermute x12, starting transfers between devices: 7.56 us -> 9.76 us  [swap(): return lax.ppermute(values, axis, [(at, at ^ step) for at in range(size)])]
    ppermute x12, waiting for transfers between devices: 17.8 us -> 19.7 us  [swap(): return lax.ppermute(values, axis, [(at, at ^ step) for at in range(size)])]
    pallas_call x3, Pallas kernels: 16.5 us -> 14.7 us  [next_block(): pl.pallas_call(functools.partial(next_kernel, block), out_shape=jax.Shape...]
    pallas_call x1 -> x3, Pallas kernels: 2.38 us -> 3.92 us  [the longest x2 3.21 us: solve(): pl.pallas_call(functools.partial(solve_kernel, samples, steps, rows, fini...]
    dot_general x1 -> x0, matrix products: 1.51 us -> none  [on_device(): cross = jnp.dot(psi, yields, preferred_element_type=jnp.float32)]
    pallas_call x1, Pallas kernels: 1.92 us -> 0.83 us  [join_columns(): pl.pallas_call(join_kernel, out_shape=jax.ShapeDtypeStruct((rows, wide *...]
    add x3 -> x2, other arithmetic: 1.01 us -> 0.03 us  [halve(): return kept + swap(sent, 'samp', 1 << bit)]
  transfers between devices with their start and end apart: 14 -> 14, of which waited for: 8 -> 8; matrix products, arithmetic and copies ran while one was open for 3% -> 1% of each run, Pallas kernels for 18% -> 19%
where the time goes in v1:
time: 81.5 us; the launch traced here: 81.1 us
  Pallas kernels  28.3 us (35%)
  waiting for transfers between devices  27.3 us (33%)
  starting transfers between devices  21 us (26%)
  local copies, waits for them, and re-layouts  3.54 us (4%)
    ppermute x12, waiting for transfers between devices, swap(): return lax.ppermute(values, axis, [(at, at ^ step) for at in range(size)])  19.7 us
    pallas_call x3, Pallas kernels, next_block(): pl.pallas_call(functools.partial(next_kernel, block), out_shape=jax.Shape...  14.7 us
    all_to_all x2, starting transfers between devices, exchange(): return lax.all_to_all(pieces, 'samp', split_axis=0, concat_axis=0)  11.3 us
    ppermute x12, starting transfers between devices, swap(): return lax.ppermute(values, axis, [(at, at ^ step) for at in range(size)])  9.76 us
    all_to_all x2, waiting for transfers between devices, exchange(): return lax.all_to_all(pieces, 'samp', split_axis=0, concat_axis=0)  7.53 us
    pallas_call x1, Pallas kernels, first_block(): pl.pallas_call(first_kernel, out_shape=(jax.ShapeDtypeStruct((terms, term...  5.13 us
    pallas_call x1, Pallas kernels, design(): pl.pallas_call(functools.partial(design_kernel, 512), out_shape=(jax.Shap...  3.68 us
    pallas_call x2, Pallas kernels, solve(): pl.pallas_call(functools.partial(solve_kernel, samples, steps, rows, fini...  3.21 us
  transfers between devices with their start and end apart: 14, of which 8 were waited for; matrix products, arithmetic and copies ran while one was open for 1% of the time, Pallas kernels for 19%

profile of v1, /device:TPU:0, one launch (start us, length us, event | category | flops | bytes accessed | tf_op | source)
XLA Modules:
  0.0 81.1 jit_solution(7745378248512955750)
XLA Ops:
  0.6 0.9 %copy-done.1 = f32[24,2048]{1,0:T(8,128)S(1)} copy-done((f32[24,2048]{1,0:T(8,128)S(1)}, f32[24,2048]{1,0:T(8,128)}, u32[]{:S(2)}) %copy-start.1) | copy-done | bytes 196632
  2.2 3.7 %design.1 = (bf16[512,2048]{1,0:T(8,128)(2,1)S(1)}, f32[64,640]{1,0:T(8,128)}) custom-call(s32[1]{0:T(128)} %bitcast.cell_ref.where_ref, s32[2,512]{1,0:T(2,128)S(1)} %bitcast.19, f32[24,2048]{1,0:T(8,128)S(1)} %copy-done.1), custom_call_target="tpu_custom_call" | custom-call | tf_op jit(solution)/shard_map/design/pallas_call | solution.py:80
  5.9 7.3 %all-to-all-start = ((f32[8,8,640]{2,1,0:T(8,128)}), f32[8,8,640]{2,1,0:T(8,128)S(1)}, u32[]{:S(2)}, u32[]{:S(2)}) async-start(f32[8,8,640]{2,1,0:T(8,128)} %bitcast.3), calls=%async_computation | async-start | bytes 327680 | tf_op jit(solution)/shard_map/all_to_all | solution.py:342
  13.2 1.2 %copy-done = bf16[2048,256]{1,0:T(8,128)(2,1)S(1)} copy-done((bf16[2048,256]{1,0:T(8,128)(2,1)S(1)}, bf16[2048,256]{1,0:T(8,128)(2,1)}, u32[]{:S(2)}) %copy-start) | copy-done | bytes 1048600
  15.2 2.1 %collective-permute-start = (f32[256,256]{1,0:T(8,128)S(1)}, f32[256,256]{1,0:T(8,128)S(1)}, u32[]{:S(2)}, u32[]{:S(2)}) collective-permute-start(f32[256,256]{1,0:T(8,128)S(1)} %get-tuple-element.29), channel_id=1, source_target_pairs={{0,4},{4,0},{8,12},{12,8},{16,20},{20,16},{24,28},{28,24},{1,5},{5... | collective-permute-start | bytes 786440 | tf_op jit(solution)/shard_map/ppermute | solution.py:338
  17.2 6.8 %collective-permute-done = f32[256,256]{1,0:T(8,128)S(1)} collective-permute-done((f32[256,256]{1,0:T(8,128)S(1)}, f32[256,256]{1,0:T(8,128)S(1)}, u32[]{:S(2)}, u32[]{:S(2)}) %collective-permute-start) | collective-permute-done | bytes 262176 | tf_op jit(solution)/shard_map/ppermute | solution.py:338
  24.2 1.4 %collective-permute-start.1 = (f32[128,256]{1,0:T(8,128)S(1)}, f32[128,256]{1,0:T(8,128)S(1)}, u32[]{:S(2)}, u32[]{:S(2)}) collective-permute-start(f32[128,256]{1,0:T(8,128)S(1)} %dynamic-slice_bitcast_fusion), channel_id=1, source_target_pairs={{0,8},{4,12},{8,0},{12,4},{16,24},{20,28},{24,16},{28,20},{1,9},{5... | collective-permute-start | bytes 393224 | tf_op jit(solution)/shard_map/ppermute | solution.py:338
  26.2 4.0 %all-to-all-start.1 = ((f32[8,8,640]{2,1,0:T(8,128)}), f32[8,8,640]{2,1,0:T(8,128)S(1)}, u32[]{:S(2)}, u32[]{:S(2)}) async-start(f32[8,8,640]{2,1,0:T(8,128)} %broadcast_in_dim.2), calls=%async_computation.1 | async-start | bytes 327680 | tf_op jit(solution)/shard_map/all_to_all | solution.py:342
  30.2 7.5 %all-to-all-done.1 = f32[8,8,640]{2,1,0:T(8,128)S(1)} async-done(((f32[8,8,640]{2,1,0:T(8,128)}), f32[8,8,640]{2,1,0:T(8,128)S(1)}, u32[]{:S(2)}, u32[]{:S(2)}) %all-to-all-start.1) | async-done | bytes 163872 | tf_op jit(solution)/shard_map/all_to_all | solution.py:342
  37.8 1.5 %collective-permute-start.2 = (f32[64,640]{1,0:T(8,128)S(1)}, f32[64,640]{1,0:T(8,128)S(1)}, u32[]{:S(2)}, u32[]{:S(2)}) collective-permute-start(f32[64,640]{1,0:T(8,128)S(1)} %bitcast.16), channel_id=1, source_target_pairs={{0,2},{1,3},{2,0},{3,1},{4,6},{5,7},{6,4},{7,5},{8,10},{9,11},{10,... | collective-permute-start | bytes 491528 | tf_op jit(solution)/shard_map/ppermute | solution.py:338
  39.7 3.4 %collective-permute-done.2.refs_2_ = f32[64,640]{1,0:T(8,128)S(1)} collective-permute-done((f32[64,640]{1,0:T(8,128)S(1)}, f32[64,640]{1,0:T(8,128)S(1)}, u32[]{:S(2)}, u32[]{:S(2)}) %collective-permute-start.2) | collective-permute-done | bytes 163872 | tf_op jit(solution)/shard_map/ppermute | solution.py:338
  43.1 1.4 %collective-permute-done.5 = f32[64,256]{1,0:T(8,128)S(1)} collective-permute-done((f32[64,256]{1,0:T(8,128)S(1)}, f32[64,256]{1,0:T(8,128)S(1)}, u32[]{:S(2)}, u32[]{:S(2)}) %collective-permute-start.5) | collective-permute-done | bytes 65568 | tf_op jit(solution)/shard_map/ppermute | solution.py:338
  44.9 5.1 %block_0.1 = (f32[512,512]{1,0:T(8,128)S(1)}, f32[512,1]{1,0:T(8,128)S(1)}) custom-call(s32[1]{0:T(128)} %bitcast.cell_ref.where_ref, f32[64,640]{1,0:T(8,128)S(1)} %bitcast.18, f32[64,640]{1,0:T(8,128)S(1)} %collective-permute-done.3.refs_1_, f32[64,640]{1,0:T(8,128)S(1)} %collective-permute-done.2.refs_2_, f32[64,640]{1,0:T(8,128)S(1)} %collective-permute-done.4.refs_3_), custom_call_target="tpu_custom_call" | custom-call | flops 5000000000 | bytes 2097152 | tf_op jit(solution)/shard_map/block_0/pallas_call | solution.py:232
  50.9 4.9 %block_1.1.in_ref = f32[512,512]{1,0:T(8,128)S(1)} custom-call(f32[512,512]{1,0:T(8,128)S(1)} %get-tuple-element.40.in_ref), custom_call_target="tpu_custom_call", output_to_operand_aliasing={{}: (0, {})} | custom-call | flops 5000000000 | bytes 2097152 | tf_op jit(solution)/shard_map/block_1/pallas_call | solution.py:247
  55.8 5.1 %block_2.1.in_ref = f32[512,512]{1,0:T(8,128)S(1)} custom-call(f32[512,512]{1,0:T(8,128)S(1)} %block_1.1.in_ref), custom_call_target="tpu_custom_call", output_to_operand_aliasing={{}: (0, {})} | custom-call | flops 5000000000 | bytes 2097152 | tf_op jit(solution)/shard_map/block_2/pallas_call | solution.py:247
  60.9 1.6 %collective-permute-start.8 = (f32[256,256]{1,0:T(8,128)S(1)}, f32[256,256]{1,0:T(8,128)S(1)}, u32[]{:S(2)}, u32[]{:S(2)}) collective-permute-start(f32[256,256]{1,0:T(8,128)S(1)} %pad_maximum_fusion.refs_0_), channel_id=1, source_target_pairs={{0,4},{4,0},{8,12},{12,8},{16,20},{20,16},{24,28},{28,24},{1,5},{5... | collective-permute-start | bytes 786440 | tf_op jit(solution)/shard_map/ppermute | solution.py:338
  62.4 4.8 %block_3.1.inverse_ref = f32[512,512]{1,0:T(8,128)S(1)} custom-call(f32[512,512]{1,0:T(8,128)S(1)} %block_2.1.in_ref), custom_call_target="tpu_custom_call", output_to_operand_aliasing={{}: (0, {})} | custom-call | flops 5000000000 | bytes 2097152 | tf_op jit(solution)/shard_map/block_3/pallas_call | solution.py:247
  67.3 1.4 %collective-permute-done.8.refs_1_ = f32[256,256]{1,0:T(8,128)S(1)} collective-permute-done((f32[256,256]{1,0:T(8,128)S(1)}, f32[256,256]{1,0:T(8,128)S(1)}, u32[]{:S(2)}, u32[]{:S(2)}) %collective-permute-start.8) | collective-permute-done | bytes 262176 | tf_op jit(solution)/shard_map/ppermute | solution.py:338
  68.7 1.3 %solve_far.1 = (f32[128,256]{1,0:T(8,128)S(1)}, f32[128,256]{1,0:T(8,128)S(1)}) custom-call(s32[2]{0:T(128)S(1)} %pad_add_fusion.where_ref, s32[8]{0:T(128)S(1)} %copy-done.3, f32[512,512]{1,0:T(8,128)S(1)} %block_3.1.inverse_ref, f32[512,1]{1,0:T(8,128)S(1)} %get-tuple-element.43.scale_ref, f32[256,256]{1,0:T(8,128)S(1)} %pad_maximum_fusion.refs_0_, ...), custom_call_target="tpu_custom_call" | custom-call | tf_op jit(solution)/shard_map/solve_far/pallas_call | solution.py:306
  70.0 2.0 %solve_near.1 = (f32[128,256]{1,0:T(8,128)S(1)}, f32[128,256]{1,0:T(8,128)S(1)}, f32[8,256]{1,0:T(8,128)}) custom-call(s32[2]{0:T(128)S(1)} %pad_add_fusion.where_ref, s32[8]{0:T(128)S(1)} %copy-done.3, f32[512,512]{1,0:T(8,128)S(1)} %block_3.1.inverse_ref, f32[512,1]{1,0:T(8,128)S(1)} %get-tuple-element.43.scale_ref, ...), custom_call_target="tpu_custom_call" | custom-call | tf_op jit(solution)/shard_map/solve_near/pallas_call | solution.py:306
  71.9 1.5 %collective-permute-start.10 = (f32[128,256]{1,0:T(8,128)S(1)}, f32[128,256]{1,0:T(8,128)S(1)}, u32[]{:S(2)}, u32[]{:S(2)}) collective-permute-start(f32[128,256]{1,0:T(8,128)S(1)} %get-tuple-element.45.refs_2_), channel_id=1, source_target_pairs={{0,2},{1,3},{2,0},{3,1},{4,6},{5,7},{6,4},{7,5},{8,10},{9,11},{10,... | collective-permute-start | bytes 393224 | tf_op jit(solution)/shard_map/ppermute | solution.py:338
  73.8 4.4 %collective-permute-done.10.refs_2_ = f32[128,256]{1,0:T(8,128)S(1)} collective-permute-done((f32[128,256]{1,0:T(8,128)S(1)}, f32[128,256]{1,0:T(8,128)S(1)}, u32[]{:S(2)}, u32[]{:S(2)}) %collective-permute-start.10) | collective-permute-done | bytes 131104 | tf_op jit(solution)/shard_map/ppermute | solution.py:338
  78.2 2.0 %collective-permute-done.11.refs_3_ = f32[128,256]{1,0:T(8,128)S(1)} collective-permute-done((f32[128,256]{1,0:T(8,128)S(1)}, f32[128,256]{1,0:T(8,128)S(1)}, u32[]{:S(2)}, u32[]{:S(2)}) %collective-permute-start.11) | collective-permute-done | bytes 131104 | tf_op jit(solution)/shard_map/ppermute | solution.py:338
  80.2 0.8 %join_columns.1 = f32[128,1024]{1,0:T(8,128)} custom-call(s32[1]{0:T(128)} %bitcast.cell_ref.where_ref, f32[128,256]{1,0:T(8,128)S(1)} %get-tuple-element.47.refs_0_, f32[128,256]{1,0:T(8,128)S(1)} %collective-permute-done.9.refs_1_, f32[128,256]{1,0:T(8,128)S(1)} %collective-permute-done.10.refs_2_, f32[128,256]{1,0:T(8,128)S(1)} %collective-permute-done.11.refs_3_), custom_call_target="tpu_custom_call" | custom-call | tf_op jit(solution)/shard_map/join_columns/pallas_call | solution.py:326
  (31 shorter events, 4.3 us)
Async XLA Ops:
  0.6 0.9 %copy-start.1 = (f32[24,2048]{1,0:T(8,128)S(1)}, f32[24,2048]{1,0:T(8,128)}, u32[]{:S(2)}) copy-start(f32[24,2048]{1,0:T(8,128)} %points_ref.1) | copy-start | bytes 589828
  1.6 0.7 copy-start.2
  5.9 18.2 %all-to-all-start = ((f32[8,8,640]{2,1,0:T(8,128)}), f32[8,8,640]{2,1,0:T(8,128)S(1)}, u32[]{:S(2)}, u32[]{:S(2)}) async-start(f32[8,8,640]{2,1,0:T(8,128)} %bitcast.3), calls=%async_computation | async-start | bytes 327680 | tf_op jit(solution)/shard_map/all_to_all | solution.py:342
  13.2 1.2 %copy-start = (bf16[2048,256]{1,0:T(8,128)(2,1)S(1)}, bf16[2048,256]{1,0:T(8,128)(2,1)}, u32[]{:S(2)}) copy-start(bf16[2048,256]{1,0:T(8,128)(2,1)} %yields_ref.1) | copy-start | bytes 3145732
  15.2 8.9 %collective-permute-start = (f32[256,256]{1,0:T(8,128)S(1)}, f32[256,256]{1,0:T(8,128)S(1)}, u32[]{:S(2)}, u32[]{:S(2)}) collective-permute-start(f32[256,256]{1,0:T(8,128)S(1)} %get-tuple-element.29), channel_id=1, source_target_pairs={{0,4},{4,0},{8,12},{12,8},{16,20},{20,16},{24,28},{28,24},{1,5},{5... | collective-permute-start | bytes 786440 | tf_op jit(solution)/shard_map/ppermute | solution.py:338
  24.2 6.0 %collective-permute-start.1 = (f32[128,256]{1,0:T(8,128)S(1)}, f32[128,256]{1,0:T(8,128)S(1)}, u32[]{:S(2)}, u32[]{:S(2)}) collective-permute-start(f32[128,256]{1,0:T(8,128)S(1)} %dynamic-slice_bitcast_fusion), channel_id=1, source_target_pairs={{0,8},{4,12},{8,0},{12,4},{16,24},{20,28},{24,16},{28,20},{1,9},{5... | collective-permute-start | bytes 393224 | tf_op jit(solution)/shard_map/ppermute | solution.py:338
  26.2 11.5 %all-to-all-start.1 = ((f32[8,8,640]{2,1,0:T(8,128)}), f32[8,8,640]{2,1,0:T(8,128)S(1)}, u32[]{:S(2)}, u32[]{:S(2)}) async-start(f32[8,8,640]{2,1,0:T(8,128)} %broadcast_in_dim.2), calls=%async_computation.1 | async-start | bytes 327680 | tf_op jit(solution)/shard_map/all_to_all | solution.py:342
  37.8 5.3 %collective-permute-start.2 = (f32[64,640]{1,0:T(8,128)S(1)}, f32[64,640]{1,0:T(8,128)S(1)}, u32[]{:S(2)}, u32[]{:S(2)}) collective-permute-start(f32[64,640]{1,0:T(8,128)S(1)} %bitcast.16), channel_id=1, source_target_pairs={{0,2},{1,3},{2,0},{3,1},{4,6},{5,7},{6,4},{7,5},{8,10},{9,11},{10,... | collective-permute-start | bytes 491528 | tf_op jit(solution)/shard_map/ppermute | solution.py:338
  39.2 5.2 %collective-permute-start.5 = (f32[64,256]{1,0:T(8,128)S(1)}, f32[64,256]{1,0:T(8,128)S(1)}, u32[]{:S(2)}, u32[]{:S(2)}) collective-permute-start(f32[64,256]{1,0:T(8,128)S(1)} %dynamic-slice_bitcast_fusion.1), channel_id=1, source_target_pairs={{0,16},{4,20},{8,24},{12,28},{16,0},{20,4},{24,8},{28,12},{1,17},{... | collective-permute-start | bytes 196616 | tf_op jit(solution)/shard_map/ppermute | solution.py:338
  39.7 4.8 %collective-permute-start.3 = (f32[64,640]{1,0:T(8,128)S(1)}, f32[64,640]{1,0:T(8,128)S(1)}, u32[]{:S(2)}, u32[]{:S(2)}) collective-permute-start(f32[64,640]{1,0:T(8,128)S(1)} %bitcast.17), channel_id=1, source_target_pairs={{0,1},{1,0},{2,3},{3,2},{4,5},{5,4},{6,7},{7,6},{8,9},{9,8},{10,11... | collective-permute-start | bytes 491528 | tf_op jit(solution)/shard_map/ppermute | solution.py:338
  43.1 1.4 %collective-permute-start.4 = (f32[64,640]{1,0:T(8,128)S(1)}, f32[64,640]{1,0:T(8,128)S(1)}, u32[]{:S(2)}, u32[]{:S(2)}) collective-permute-start(f32[64,640]{1,0:T(8,128)S(1)} %collective-permute-done.2.refs_2_), channel_id=1, source_target_pairs={{0,1},{1,0},{2,3},{3,2},{4,5},{5,4},{6,7},{7,6},{8,9},{9,8},{10,11... | collective-permute-start | bytes 491528 | tf_op jit(solution)/shard_map/ppermute | solution.py:338
  44.5 5.8 %collective-permute-start.6 = (f32[64,256]{1,0:T(8,128)S(1)}, f32[64,256]{1,0:T(8,128)S(1)}, u32[]{:S(2)}, u32[]{:S(2)}) collective-permute-start(f32[64,256]{1,0:T(8,128)S(1)} %bitcast_add_fusion.1), channel_id=1, source_target_pairs={{0,16},{4,20},{8,24},{12,28},{16,0},{20,4},{24,8},{28,12},{1,17},{... | collective-permute-start | bytes 196616 | tf_op jit(solution)/shard_map/ppermute | solution.py:338
  50.2 5.5 %collective-permute-start.7 = (f32[128,256]{1,0:T(8,128)S(1)}, f32[128,256]{1,0:T(8,128)S(1)}, u32[]{:S(2)}, u32[]{:S(2)}) collective-permute-start(f32[128,256]{1,0:T(8,128)S(1)} %pad_maximum_fusion.1), channel_id=1, source_target_pairs={{0,8},{4,12},{8,0},{12,4},{16,24},{20,28},{24,16},{28,20},{1,9},{5... | collective-permute-start | bytes 393224 | tf_op jit(solution)/shard_map/ppermute | solution.py:338
  60.9 7.8 %copy-start.3 = (s32[8]{0:T(128)S(1)}, s32[8]{0:T(128)}, u32[]{:S(2)}) copy-start(s32[8]{0:T(128)} %group_ref.3) | copy-start | bytes 100
  60.9 7.8 %collective-permute-start.8 = (f32[256,256]{1,0:T(8,128)S(1)}, f32[256,256]{1,0:T(8,128)S(1)}, u32[]{:S(2)}, u32[]{:S(2)}) collective-permute-start(f32[256,256]{1,0:T(8,128)S(1)} %pad_maximum_fusion.refs_0_), channel_id=1, source_target_pairs={{0,4},{4,0},{8,12},{12,8},{16,20},{20,16},{24,28},{28,24},{1,5},{5... | collective-permute-start | bytes 786440 | tf_op jit(solution)/shard_map/ppermute | solution.py:338
  71.9 1.9 %collective-permute-start.9 = (f32[128,256]{1,0:T(8,128)S(1)}, f32[128,256]{1,0:T(8,128)S(1)}, u32[]{:S(2)}, u32[]{:S(2)}) collective-permute-start(f32[128,256]{1,0:T(8,128)S(1)} %get-tuple-element.48), channel_id=1, source_target_pairs={{0,1},{1,0},{2,3},{3,2},{4,5},{5,4},{6,7},{7,6},{8,9},{9,8},{10,11... | collective-permute-start | bytes 393224 | tf_op jit(solution)/shard_map/ppermute | solution.py:338
  71.9 6.3 %collective-permute-start.10 = (f32[128,256]{1,0:T(8,128)S(1)}, f32[128,256]{1,0:T(8,128)S(1)}, u32[]{:S(2)}, u32[]{:S(2)}) collective-permute-start(f32[128,256]{1,0:T(8,128)S(1)} %get-tuple-element.45.refs_2_), channel_id=1, source_target_pairs={{0,2},{1,3},{2,0},{3,1},{4,6},{5,7},{6,4},{7,5},{8,10},{9,11},{10,... | collective-permute-start | bytes 393224 | tf_op jit(solution)/shard_map/ppermute | solution.py:338
  73.4 6.8 %collective-permute-start.11 = (f32[128,256]{1,0:T(8,128)S(1)}, f32[128,256]{1,0:T(8,128)S(1)}, u32[]{:S(2)}, u32[]{:S(2)}) collective-permute-start(f32[128,256]{1,0:T(8,128)S(1)} %get-tuple-element.46.refs_3_), channel_id=1, source_target_pairs={{0,3},{1,2},{2,1},{3,0},{4,7},{5,6},{6,5},{7,4},{8,11},{9,10},{10,... | collective-permute-start | bytes 393224 | tf_op jit(solution)/shard_map/ppermute | solution.py:338

commit v2 on v1

--- a/solution.py
+++ b/solution.py
@@ -225,7 +225,7 @@
     sweep_block(out_ref, block)
 
 
-STEP_COST = pl.CostEstimate(flops=5 * 10**9, bytes_accessed=2 * 2**20, transcendentals=512)
+STEP_COST = pl.CostEstimate(flops=10**9, bytes_accessed=2**20, transcendentals=512)
 
 
 def first_block(where, pieces, terms):
@@ -310,6 +310,7 @@
         out_specs=(VMEM,) * len(out),
         scratch_shapes=[pltpu.VMEM((terms, cells), jnp.float32)],
         compiler_params=BIG,
+        cost_estimate=pl.CostEstimate(flops=(5 if finish else 1) * 10**9, bytes_accessed=2**20, transcendentals=0),
         name="solve_near" if finish else "solve_far",
     )(where, block_group, inverse, scale, *pieces, *others)
 
@@ -338,21 +339,16 @@
     return lax.ppermute(values, axis, [(at, at ^ step) for at in range(size)])
 
 
+def pick(values, at):
+    return lax.dynamic_index_in_dim(values, at, axis=0, keepdims=False)
+
+
 def exchange(pieces):
     return lax.all_to_all(pieces, "samp", split_axis=0, concat_axis=0)
 
 
 def spread(piece):
     return jnp.broadcast_to(piece[None], (lax.axis_size("samp"),) + piece.shape)
-
-
-def halve(values, me, bit):
-    rows, lanes = values.shape
-    halves = values.reshape(2, rows // 2, lanes)
-    mine = (me >> bit) & 1
-    kept = lax.dynamic_index_in_dim(halves, mine, axis=0, keepdims=False)
-    sent = lax.dynamic_index_in_dim(halves, mine ^ 1, axis=0, keepdims=False)
-    return kept + swap(sent, "samp", 1 << bit)
 
 
 def on_device(points, yields, term_index, block_group):
@@ -364,12 +360,15 @@
     pieces = fold.reshape((n_samp, 8, -1) if fold.shape[0] % (8 * n_samp) else (n_samp, -1, fold.shape[1]))
     came = exchange(pieces)
     kept, sent = cross_halves(psi, yields, me & 1)
-    part = kept + swap(sent, "samp", 1)
-    came, part = lax.optimization_barrier((came, part))
+    came, kept, sent = lax.optimization_barrier((came, kept, sent))
+    half = kept + swap(sent, "samp", 1)
     fold = exchange(spread(jnp.sum(came, axis=0))).reshape(fold.shape)
-    part = halve(part, me, 1)
-    fold, part = lax.optimization_barrier((fold, part))
-    part = halve(part, me, 2)
+    fold, half = lax.optimization_barrier((fold, half))
+    quarters = half.reshape(4, half.shape[0] // 4, half.shape[1])
+    mine = (me & 2) | ((me >> 2) & 1)
+    part = pick(quarters, mine)
+    for flip, step in ((1, 4), (2, 2), (3, 6)):
+        part = part + swap(pick(quarters, mine ^ flip), "samp", step)
     bit = 8
     while bit < n_samp:
         part = part + swap(part, "samp", bit)
@@ -389,7 +388,7 @@
             gram, part = lax.optimization_barrier((gram, part))
         gram = next_block(gram, block)
     pieces = [part, swap(part, "samp", 1)]
-    spot = ((me & 1) << 2) | (me & 2) | ((me >> 2) & 1)
+    spot = ((me & 1) << 2) | mine
     where = jnp.stack([spot, cell])
     given = (where, gram, scale, pieces, rows, block_group, points.shape[1] * n_samp, n_cell)
     far = list(solve(*given, tuple(range(n_cell // 2, n_cell))))

time: 81.5 us -> 80.7 us (level)
  waiting for transfers between devices: 27.3 us -> 24.1 us
  starting transfers between devices: 21 us -> 23.5 us
    ppermute x12 -> x13, starting transfers between devices: 9.76 us -> 12.7 us  [swap(): return lax.ppermute(values, axis, [(at, at ^ step) for at in range(size)])]
    all_to_all x2, waiting for transfers between devices: 7.53 us -> 5.63 us  [exchange(): return lax.all_to_all(pieces, 'samp', split_axis=0, concat_axis=0)]
    ppermute x12 -> x13, waiting for transfers between devices: 19.7 us -> 18.4 us  [swap(): return lax.ppermute(values, axis, [(at, at ^ step) for at in range(size)])]
  transfers between devices with their start and end apart: 14 -> 15, of which waited for: 8 -> 7; matrix products, arithmetic and copies ran while one was open for 1% -> 0% of each run, Pallas kernels for 19% -> 26%
where the time goes in v2:
time: 80.7 us; the launch traced here: 80.3 us
  Pallas kernels  28.3 us (35%)
  waiting for transfers between devices  24.1 us (30%)
  starting transfers between devices  23.5 us (29%)
  local copies, waits for them, and re-layouts  3.53 us (4%)
    ppermute x13, waiting for transfers between devices, swap(): return lax.ppermute(values, axis, [(at, at ^ step) for at in range(size)])  18.4 us
    pallas_call x3, Pallas kernels, next_block(): pl.pallas_call(functools.partial(next_kernel, block), out_shape=jax.Shape...  14.7 us
    ppermute x13, starting transfers between devices, swap(): return lax.ppermute(values, axis, [(at, at ^ step) for at in range(size)])  12.7 us
    all_to_all x2, starting transfers between devices, exchange(): return lax.all_to_all(pieces, 'samp', split_axis=0, concat_axis=0)  10.8 us
    all_to_all x2, waiting for transfers between devices, exchange(): return lax.all_to_all(pieces, 'samp', split_axis=0, concat_axis=0)  5.63 us
    pallas_call x1, Pallas kernels, first_block(): pl.pallas_call(first_kernel, out_shape=(jax.ShapeDtypeStruct((terms, term...  5.12 us
    pallas_call x1, Pallas kernels, design(): pl.pallas_call(functools.partial(design_kernel, 512), out_shape=(jax.Shap...  3.68 us
    pallas_call x2, Pallas kernels, solve(): pl.pallas_call(functools.partial(solve_kernel, samples, steps, rows, fini...  3.2 us
  transfers between devices with their start and end apart: 15, of which 7 were waited for; matrix products, arithmetic and copies ran while one was open for 0% of the time, Pallas kernels for 26%

profile of v2, /device:TPU:0, one launch (start us, length us, event | category | flops | bytes accessed | tf_op | source)
XLA Modules:
  0.0 80.3 jit_solution(13024681824734665002)
XLA Ops:
  0.6 0.9 %copy-done.1 = f32[24,2048]{1,0:T(8,128)S(1)} copy-done((f32[24,2048]{1,0:T(8,128)S(1)}, f32[24,2048]{1,0:T(8,128)}, u32[]{:S(2)}) %copy-start.1) | copy-done | bytes 196632
  2.2 3.7 %design.1 = (bf16[512,2048]{1,0:T(8,128)(2,1)S(1)}, f32[64,640]{1,0:T(8,128)}) custom-call(s32[1]{0:T(128)} %bitcast.cell_ref.where_ref, s32[2,512]{1,0:T(2,128)S(1)} %bitcast.22, f32[24,2048]{1,0:T(8,128)S(1)} %copy-done.1), custom_call_target="tpu_custom_call" | custom-call | tf_op jit(solution)/shard_map/design/pallas_call | solution.py:80
  5.9 7.3 %all-to-all-start = ((f32[8,8,640]{2,1,0:T(8,128)}), f32[8,8,640]{2,1,0:T(8,128)S(1)}, u32[]{:S(2)}, u32[]{:S(2)}) async-start(f32[8,8,640]{2,1,0:T(8,128)} %bitcast.3), calls=%async_computation | async-start | bytes 327680 | tf_op jit(solution)/shard_map/all_to_all | solution.py:347
  13.2 1.2 %copy-done = bf16[2048,256]{1,0:T(8,128)(2,1)S(1)} copy-done((bf16[2048,256]{1,0:T(8,128)(2,1)S(1)}, bf16[2048,256]{1,0:T(8,128)(2,1)}, u32[]{:S(2)}) %copy-start) | copy-done | bytes 1048600
  15.2 5.6 %all-to-all-done = f32[8,8,640]{2,1,0:T(8,128)S(1)} async-done(((f32[8,8,640]{2,1,0:T(8,128)}), f32[8,8,640]{2,1,0:T(8,128)S(1)}, u32[]{:S(2)}, u32[]{:S(2)}) %all-to-all-start) | async-done | bytes 163872 | tf_op jit(solution)/shard_map/all_to_all | solution.py:347
  21.5 3.6 %all-to-all-start.1 = ((f32[8,8,640]{2,1,0:T(8,128)}), f32[8,8,640]{2,1,0:T(8,128)S(1)}, u32[]{:S(2)}, u32[]{:S(2)}) async-start(f32[8,8,640]{2,1,0:T(8,128)} %broadcast_in_dim.2), calls=%async_computation.1 | async-start | bytes 327680 | tf_op jit(solution)/shard_map/all_to_all | solution.py:347
  25.0 1.7 %collective-permute-start = (f32[256,256]{1,0:T(8,128)S(1)}, f32[256,256]{1,0:T(8,128)S(1)}, u32[]{:S(2)}, u32[]{:S(2)}) collective-permute-start(f32[256,256]{1,0:T(8,128)S(1)} %get-tuple-element.33), channel_id=1, source_target_pairs={{0,4},{4,0},{8,12},{12,8},{16,20},{20,16},{24,28},{28,24},{1,5},{5... | collective-permute-start | bytes 786440 | tf_op jit(solution)/shard_map/ppermute | solution.py:339
  26.8 6.9 %collective-permute-done = f32[256,256]{1,0:T(8,128)S(1)} collective-permute-done((f32[256,256]{1,0:T(8,128)S(1)}, f32[256,256]{1,0:T(8,128)S(1)}, u32[]{:S(2)}, u32[]{:S(2)}) %collective-permute-start) | collective-permute-done | bytes 262176 | tf_op jit(solution)/shard_map/ppermute | solution.py:339
  33.8 1.5 %collective-permute-start.1 = (f32[64,640]{1,0:T(8,128)S(1)}, f32[64,640]{1,0:T(8,128)S(1)}, u32[]{:S(2)}, u32[]{:S(2)}) collective-permute-start(f32[64,640]{1,0:T(8,128)S(1)} %bitcast.19), channel_id=1, source_target_pairs={{0,2},{1,3},{2,0},{3,1},{4,6},{5,7},{6,4},{7,5},{8,10},{9,11},{10,... | collective-permute-start | bytes 491528 | tf_op jit(solution)/shard_map/ppermute | solution.py:339
  35.3 2.4 %collective-permute-start.4 = (f32[64,256]{1,0:T(8,128)S(1)}, f32[64,256]{1,0:T(8,128)S(1)}, u32[]{:S(2)}, u32[]{:S(2)}) collective-permute-start(f32[64,256]{1,0:T(8,128)S(1)} %get-tuple-element.52), channel_id=1, source_target_pairs={{0,16},{4,20},{8,24},{12,28},{16,0},{20,4},{24,8},{28,12},{1,17},{... | collective-permute-start | bytes 196616 | tf_op jit(solution)/shard_map/ppermute | solution.py:339
  37.8 1.5 %collective-permute-start.5 = (f32[64,256]{1,0:T(8,128)S(1)}, f32[64,256]{1,0:T(8,128)S(1)}, u32[]{:S(2)}, u32[]{:S(2)}) collective-permute-start(f32[64,256]{1,0:T(8,128)S(1)} %get-tuple-element.54), channel_id=1, source_target_pairs={{0,8},{4,12},{8,0},{12,4},{16,24},{20,28},{24,16},{28,20},{1,9},{5... | collective-permute-start | bytes 196616 | tf_op jit(solution)/shard_map/ppermute | solution.py:339
  40.3 1.7 %collective-permute-done.4 = f32[64,256]{1,0:T(8,128)S(1)} collective-permute-done((f32[64,256]{1,0:T(8,128)S(1)}, f32[64,256]{1,0:T(8,128)S(1)}, u32[]{:S(2)}, u32[]{:S(2)}) %collective-permute-start.4) | collective-permute-done | bytes 65568 | tf_op jit(solution)/shard_map/ppermute | solution.py:339
  42.8 2.5 %collective-permute-done.6 = f32[64,256]{1,0:T(8,128)S(1)} collective-permute-done((f32[64,256]{1,0:T(8,128)S(1)}, f32[64,256]{1,0:T(8,128)S(1)}, u32[]{:S(2)}, u32[]{:S(2)}) %collective-permute-start.6) | collective-permute-done | bytes 65568 | tf_op jit(solution)/shard_map/ppermute | solution.py:339
  45.4 5.1 %block_0.1 = (f32[512,512]{1,0:T(8,128)S(1)}, f32[512,1]{1,0:T(8,128)S(1)}) custom-call(s32[1]{0:T(128)} %bitcast.cell_ref.where_ref, f32[64,640]{1,0:T(8,128)S(1)} %bitcast.21, f32[64,640]{1,0:T(8,128)S(1)} %collective-permute-done.2.refs_1_, f32[64,640]{1,0:T(8,128)S(1)} %collective-permute-done.1.refs_2_, f32[64,640]{1,0:T(8,128)S(1)} %collective-permute-done.3.refs_3_), custom_call_target="tpu_custom_call" | custom-call | flops 1000000000 | bytes 1048576 | tf_op jit(solution)/shard_map/block_0/pallas_call | solution.py:232
  50.6 1.3 %collective-permute-start.8 = (f32[128,256]{1,0:T(8,128)S(1)}, f32[128,256]{1,0:T(8,128)S(1)}, u32[]{:S(2)}, u32[]{:S(2)}) collective-permute-start(f32[128,256]{1,0:T(8,128)S(1)} %pad_maximum_fusion.1), channel_id=1, source_target_pairs={{0,8},{4,12},{8,0},{12,4},{16,24},{20,28},{24,16},{28,20},{1,9},{5... | collective-permute-start | bytes 393224 | tf_op jit(solution)/shard_map/ppermute | solution.py:339
  51.9 4.8 %block_1.1.in_ref = f32[512,512]{1,0:T(8,128)S(1)} custom-call(f32[512,512]{1,0:T(8,128)S(1)} %get-tuple-element.42.in_ref), custom_call_target="tpu_custom_call", output_to_operand_aliasing={{}: (0, {})} | custom-call | flops 1000000000 | bytes 1048576 | tf_op jit(solution)/shard_map/block_1/pallas_call | solution.py:247
  56.8 1.2 %collective-permute-start.9 = (f32[256,256]{1,0:T(8,128)S(1)}, f32[256,256]{1,0:T(8,128)S(1)}, u32[]{:S(2)}, u32[]{:S(2)}) collective-permute-start(f32[256,256]{1,0:T(8,128)S(1)} %pad_maximum_fusion.refs_0_), channel_id=1, source_target_pairs={{0,4},{4,0},{8,12},{12,8},{16,20},{20,16},{24,28},{28,24},{1,5},{5... | collective-permute-start | bytes 786440 | tf_op jit(solution)/shard_map/ppermute | solution.py:339
  58.0 5.1 %block_2.1.in_ref = f32[512,512]{1,0:T(8,128)S(1)} custom-call(f32[512,512]{1,0:T(8,128)S(1)} %block_1.1.in_ref), custom_call_target="tpu_custom_call", output_to_operand_aliasing={{}: (0, {})} | custom-call | flops 1000000000 | bytes 1048576 | tf_op jit(solution)/shard_map/block_2/pallas_call | solution.py:247
  63.1 4.8 %block_3.1.inverse_ref = f32[512,512]{1,0:T(8,128)S(1)} custom-call(f32[512,512]{1,0:T(8,128)S(1)} %block_2.1.in_ref), custom_call_target="tpu_custom_call", output_to_operand_aliasing={{}: (0, {})} | custom-call | flops 1000000000 | bytes 1048576 | tf_op jit(solution)/shard_map/block_3/pallas_call | solution.py:247
  67.9 1.3 %solve_far.1 = (f32[128,256]{1,0:T(8,128)S(1)}, f32[128,256]{1,0:T(8,128)S(1)}) custom-call(s32[2]{0:T(128)S(1)} %pad_add_fusion.where_ref, s32[8]{0:T(128)S(1)} %copy-done.3, f32[512,512]{1,0:T(8,128)S(1)} %block_3.1.inverse_ref, f32[512,1]{1,0:T(8,128)S(1)} %get-tuple-element.45.scale_ref, f32[256,256]{1,0:T(8,128)S(1)} %pad_maximum_fusion.refs_0_, ...), custom_call_target="tpu_custom_call" | custom-call | flops 1000000000 | bytes 1048576 | tf_op jit(solution)/shard_map/solve_far/pallas_call | solution.py:306
  69.2 1.9 %solve_near.1 = (f32[128,256]{1,0:T(8,128)S(1)}, f32[128,256]{1,0:T(8,128)S(1)}, f32[8,256]{1,0:T(8,128)}) custom-call(s32[2]{0:T(128)S(1)} %pad_add_fusion.where_ref, s32[8]{0:T(128)S(1)} %copy-done.3, f32[512,512]{1,0:T(8,128)S(1)} %block_3.1.inverse_ref, f32[512,1]{1,0:T(8,128)S(1)} %get-tuple-element.45.scale_ref, ...), custom_call_target="tpu_custom_call" | custom-call | flops 5000000000 | bytes 1048576 | tf_op jit(solution)/shard_map/solve_near/pallas_call | solution.py:306
  71.7 1.3 %collective-permute-start.12 = (f32[128,256]{1,0:T(8,128)S(1)}, f32[128,256]{1,0:T(8,128)S(1)}, u32[]{:S(2)}, u32[]{:S(2)}) collective-permute-start(f32[128,256]{1,0:T(8,128)S(1)} %get-tuple-element.48.refs_3_), channel_id=1, source_target_pairs={{0,3},{1,2},{2,1},{3,0},{4,7},{5,6},{6,5},{7,4},{8,11},{9,10},{10,... | collective-permute-start | bytes 393224 | tf_op jit(solution)/shard_map/ppermute | solution.py:339
  73.0 4.4 %collective-permute-done.11.refs_2_ = f32[128,256]{1,0:T(8,128)S(1)} collective-permute-done((f32[128,256]{1,0:T(8,128)S(1)}, f32[128,256]{1,0:T(8,128)S(1)}, u32[]{:S(2)}, u32[]{:S(2)}) %collective-permute-start.11) | collective-permute-done | bytes 131104 | tf_op jit(solution)/shard_map/ppermute | solution.py:339
  77.5 2.0 %collective-permute-done.12.refs_3_ = f32[128,256]{1,0:T(8,128)S(1)} collective-permute-done((f32[128,256]{1,0:T(8,128)S(1)}, f32[128,256]{1,0:T(8,128)S(1)}, u32[]{:S(2)}, u32[]{:S(2)}) %collective-permute-start.12) | collective-permute-done | bytes 131104 | tf_op jit(solution)/shard_map/ppermute | solution.py:339
  (31 shorter events, 5.6 us)
Async XLA Ops:
  0.6 0.9 %copy-start.1 = (f32[24,2048]{1,0:T(8,128)S(1)}, f32[24,2048]{1,0:T(8,128)}, u32[]{:S(2)}) copy-start(f32[24,2048]{1,0:T(8,128)} %points_ref.1) | copy-start | bytes 589828
  1.6 0.7 copy-start.2
  5.9 14.8 %all-to-all-start = ((f32[8,8,640]{2,1,0:T(8,128)}), f32[8,8,640]{2,1,0:T(8,128)S(1)}, u32[]{:S(2)}, u32[]{:S(2)}) async-start(f32[8,8,640]{2,1,0:T(8,128)} %bitcast.3), calls=%async_computation | async-start | bytes 327680 | tf_op jit(solution)/shard_map/all_to_all | solution.py:347
  13.2 1.2 %copy-start = (bf16[2048,256]{1,0:T(8,128)(2,1)S(1)}, bf16[2048,256]{1,0:T(8,128)(2,1)}, u32[]{:S(2)}) copy-start(bf16[2048,256]{1,0:T(8,128)(2,1)} %yields_ref.1) | copy-start | bytes 3145732
  21.5 12.3 %all-to-all-start.1 = ((f32[8,8,640]{2,1,0:T(8,128)}), f32[8,8,640]{2,1,0:T(8,128)S(1)}, u32[]{:S(2)}, u32[]{:S(2)}) async-start(f32[8,8,640]{2,1,0:T(8,128)} %broadcast_in_dim.2), calls=%async_computation.1 | async-start | bytes 327680 | tf_op jit(solution)/shard_map/all_to_all | solution.py:347
  25.0 8.7 %collective-permute-start = (f32[256,256]{1,0:T(8,128)S(1)}, f32[256,256]{1,0:T(8,128)S(1)}, u32[]{:S(2)}, u32[]{:S(2)}) collective-permute-start(f32[256,256]{1,0:T(8,128)S(1)} %get-tuple-element.33), channel_id=1, source_target_pairs={{0,4},{4,0},{8,12},{12,8},{16,20},{20,16},{24,28},{28,24},{1,5},{5... | collective-permute-start | bytes 786440 | tf_op jit(solution)/shard_map/ppermute | solution.py:339
  33.8 6.0 %collective-permute-start.1 = (f32[64,640]{1,0:T(8,128)S(1)}, f32[64,640]{1,0:T(8,128)S(1)}, u32[]{:S(2)}, u32[]{:S(2)}) collective-permute-start(f32[64,640]{1,0:T(8,128)S(1)} %bitcast.19), channel_id=1, source_target_pairs={{0,2},{1,3},{2,0},{3,1},{4,6},{5,7},{6,4},{7,5},{8,10},{9,11},{10,... | collective-permute-start | bytes 491528 | tf_op jit(solution)/shard_map/ppermute | solution.py:339
  35.3 6.6 %collective-permute-start.4 = (f32[64,256]{1,0:T(8,128)S(1)}, f32[64,256]{1,0:T(8,128)S(1)}, u32[]{:S(2)}, u32[]{:S(2)}) collective-permute-start(f32[64,256]{1,0:T(8,128)S(1)} %get-tuple-element.52), channel_id=1, source_target_pairs={{0,16},{4,20},{8,24},{12,28},{16,0},{20,4},{24,8},{28,12},{1,17},{... | collective-permute-start | bytes 196616 | tf_op jit(solution)/shard_map/ppermute | solution.py:339
  37.8 5.0 %collective-permute-start.5 = (f32[64,256]{1,0:T(8,128)S(1)}, f32[64,256]{1,0:T(8,128)S(1)}, u32[]{:S(2)}, u32[]{:S(2)}) collective-permute-start(f32[64,256]{1,0:T(8,128)S(1)} %get-tuple-element.54), channel_id=1, source_target_pairs={{0,8},{4,12},{8,0},{12,4},{16,24},{20,28},{24,16},{28,20},{1,9},{5... | collective-permute-start | bytes 196616 | tf_op jit(solution)/shard_map/ppermute | solution.py:339
  39.2 6.1 %collective-permute-start.6 = (f32[64,256]{1,0:T(8,128)S(1)}, f32[64,256]{1,0:T(8,128)S(1)}, u32[]{:S(2)}, u32[]{:S(2)}) collective-permute-start(f32[64,256]{1,0:T(8,128)S(1)} %get-tuple-element.53), channel_id=1, source_target_pairs={{0,24},{4,28},{8,16},{12,20},{16,8},{20,12},{24,0},{28,4},{1,25},{... | collective-permute-start | bytes 196616 | tf_op jit(solution)/shard_map/ppermute | solution.py:339
  39.8 5.5 %collective-permute-start.2 = (f32[64,640]{1,0:T(8,128)S(1)}, f32[64,640]{1,0:T(8,128)S(1)}, u32[]{:S(2)}, u32[]{:S(2)}) collective-permute-start(f32[64,640]{1,0:T(8,128)S(1)} %bitcast.20), channel_id=1, source_target_pairs={{0,1},{1,0},{2,3},{3,2},{4,5},{5,4},{6,7},{7,6},{8,9},{9,8},{10,11... | collective-permute-start | bytes 491528 | tf_op jit(solution)/shard_map/ppermute | solution.py:339
  39.8 5.5 %collective-permute-start.3 = (f32[64,640]{1,0:T(8,128)S(1)}, f32[64,640]{1,0:T(8,128)S(1)}, u32[]{:S(2)}, u32[]{:S(2)}) collective-permute-start(f32[64,640]{1,0:T(8,128)S(1)} %collective-permute-done.1.refs_2_), channel_id=1, source_target_pairs={{0,1},{1,0},{2,3},{3,2},{4,5},{5,4},{6,7},{7,6},{8,9},{9,8},{10,11... | collective-permute-start | bytes 491528 | tf_op jit(solution)/shard_map/ppermute | solution.py:339
  45.3 5.2 %collective-permute-start.7 = (f32[64,256]{1,0:T(8,128)S(1)}, f32[64,256]{1,0:T(8,128)S(1)}, u32[]{:S(2)}, u32[]{:S(2)}) collective-permute-start(f32[64,256]{1,0:T(8,128)S(1)} %fusion.1), channel_id=1, source_target_pairs={{0,16},{4,20},{8,24},{12,28},{16,0},{20,4},{24,8},{28,12},{1,17},{... | collective-permute-start | bytes 196616 | tf_op jit(solution)/shard_map/ppermute | solution.py:339
  50.6 6.2 %collective-permute-start.8 = (f32[128,256]{1,0:T(8,128)S(1)}, f32[128,256]{1,0:T(8,128)S(1)}, u32[]{:S(2)}, u32[]{:S(2)}) collective-permute-start(f32[128,256]{1,0:T(8,128)S(1)} %pad_maximum_fusion.1), channel_id=1, source_target_pairs={{0,8},{4,12},{8,0},{12,4},{16,24},{20,28},{24,16},{28,20},{1,9},{5... | collective-permute-start | bytes 393224 | tf_op jit(solution)/shard_map/ppermute | solution.py:339
  56.8 11.2 %collective-permute-start.9 = (f32[256,256]{1,0:T(8,128)S(1)}, f32[256,256]{1,0:T(8,128)S(1)}, u32[]{:S(2)}, u32[]{:S(2)}) collective-permute-start(f32[256,256]{1,0:T(8,128)S(1)} %pad_maximum_fusion.refs_0_), channel_id=1, source_target_pairs={{0,4},{4,0},{8,12},{12,8},{16,20},{20,16},{24,28},{28,24},{1,5},{5... | collective-permute-start | bytes 786440 | tf_op jit(solution)/shard_map/ppermute | solution.py:339
  63.1 4.8 %copy-start.3 = (s32[8]{0:T(128)S(1)}, s32[8]{0:T(128)}, u32[]{:S(2)}) copy-start(s32[8]{0:T(128)} %group_ref.3) | copy-start | bytes 100
  71.2 1.9 %collective-permute-start.10 = (f32[128,256]{1,0:T(8,128)S(1)}, f32[128,256]{1,0:T(8,128)S(1)}, u32[]{:S(2)}, u32[]{:S(2)}) collective-permute-start(f32[128,256]{1,0:T(8,128)S(1)} %get-tuple-element.50), channel_id=1, source_target_pairs={{0,1},{1,0},{2,3},{3,2},{4,5},{5,4},{6,7},{7,6},{8,9},{9,8},{10,11... | collective-permute-start | bytes 393224 | tf_op jit(solution)/shard_map/ppermute | solution.py:339
  71.2 6.3 %collective-permute-start.11 = (f32[128,256]{1,0:T(8,128)S(1)}, f32[128,256]{1,0:T(8,128)S(1)}, u32[]{:S(2)}, u32[]{:S(2)}) collective-permute-start(f32[128,256]{1,0:T(8,128)S(1)} %get-tuple-element.47.refs_2_), channel_id=1, source_target_pairs={{0,2},{1,3},{2,0},{3,1},{4,6},{5,7},{6,4},{7,5},{8,10},{9,11},{10,... | collective-permute-start | bytes 393224 | tf_op jit(solution)/shard_map/ppermute | solution.py:339
  71.7 7.8 %collective-permute-start.12 = (f32[128,256]{1,0:T(8,128)S(1)}, f32[128,256]{1,0:T(8,128)S(1)}, u32[]{:S(2)}, u32[]{:S(2)}) collective-permute-start(f32[128,256]{1,0:T(8,128)S(1)} %get-tuple-element.48.refs_3_), channel_id=1, source_target_pairs={{0,3},{1,2},{2,1},{3,0},{4,7},{5,6},{6,5},{7,4},{8,11},{9,10},{10,... | collective-permute-start | bytes 393224 | tf_op jit(solution)/shard_map/ppermute | solution.py:339

commit v3 on v2

--- a/solution.py
+++ b/solution.py
@@ -131,42 +131,20 @@
         own = bands[at]
         inside = (lanes >= base) & (lanes < base + 8)
         columns = [lane_of(own, base + k) for k in range(8)]
-        pivot = [[row_of(columns[k], i) if k <= i else None for k in range(8)] for i in range(8)]
-        edged = jnp.where(inside, jnp.where(lanes == subs + base, -1.0, 0.0), own)
-        rows = [row_of(edged, i) for i in range(8)]
-        factor = [[None] * 8 for _ in range(8)]
-        pairs = []
-        for p in range(0, 8, 2):
-            q = p + 1
-            a, b, d = pivot[p][p], pivot[q][p], pivot[q][q]
-            inverse = 1.0 / (a * d - b * b)
-            pairs.append((a, b, d, inverse))
-            mixed = [None] * 8
-            for i in range(q + 1, 8):
-                e, f = pivot[i][p], pivot[i][q]
-                mixed[i] = (d * e - b * f, a * f - b * e)
-                factor[i][p], factor[i][q] = mixed[i][0] * inverse, mixed[i][1] * inverse
-            for i in range(q + 1, 8):
-                for k in range(q + 1, i + 1):
-                    less = mixed[i][0] * pivot[k][p] + mixed[i][1] * pivot[k][q]
-                    pivot[i][k] = pivot[i][k] - less * inverse
-                rows[i] = rows[i] - (factor[i][p] * rows[p] + factor[i][q] * rows[q])
-        for p in range(0, 8, 2):
-            a, b, d, inverse = pairs[p // 2]
-            top, low = rows[p], rows[p + 1]
-            rows[p], rows[p + 1] = (d * top - b * low) * inverse, (a * low - b * top) * inverse
-        for p in range(6, 0, -2):
-            for i in range(p):
-                rows[i] = rows[i] - (factor[p][i] * rows[p] + factor[p + 1][i] * rows[p + 1])
+        fresh = jnp.where(inside, jnp.where(lanes == subs + base, -1.0, 0.0), own)
+        for p in range(8):
+            inverse = 1.0 / row_of(columns[p], p)
+            factor = jnp.where(subs == p, 1.0 - inverse, columns[p] * inverse)
+            for k in range(p + 1, 8):
+                columns[k] = columns[k] - factor * row_of(columns[k], p)
+            fresh = fresh - factor * row_of(fresh, p)
+        rows = [row_of(fresh, k) for k in range(8)]
         for step in range(1, len(bands)):
             other = (at + step) % len(bands)
             value = jnp.where(inside, 0.0, bands[other])
-            for k in range(7, -1, -1):
+            for k in range(8):
                 value = value - lane_of(bands[other], base + k) * rows[k]
             bands[other] = value
-        fresh = rows[0]
-        for i in range(1, 8):
-            fresh = jnp.where(subs == i, rows[i], fresh)
         bands[at] = fresh
     return bands
 
@@ -258,8 +236,8 @@
 
 def solve_kernel(samples, steps, rows, finish, where_ref, group_ref, inverse_ref, scale_ref, *refs):
     count = len(steps)
-    pieces = refs[:2]
-    others = refs[2:-(count + finish + 1)]
+    pieces = refs[:4]
+    others = refs[4:-(count + finish + 1)]
     cross_ref = refs[-1]
     shares = refs[-(count + finish + 1):-(finish + 1)]
     step = 0
@@ -343,6 +321,12 @@
     return lax.dynamic_index_in_dim(values, at, axis=0, keepdims=False)
 
 
+def halve(values, me, bit):
+    halves = values.reshape(2, values.shape[0] // 2, values.shape[1])
+    mine = (me >> bit) & 1
+    return pick(halves, mine) + swap(pick(halves, mine ^ 1), "samp", 1 << bit)
+
+
 def exchange(pieces):
     return lax.all_to_all(pieces, "samp", split_axis=0, concat_axis=0)
 
@@ -364,15 +348,7 @@
     half = kept + swap(sent, "samp", 1)
     fold = exchange(spread(jnp.sum(came, axis=0))).reshape(fold.shape)
     fold, half = lax.optimization_barrier((fold, half))
-    quarters = half.reshape(4, half.shape[0] // 4, half.shape[1])
-    mine = (me & 2) | ((me >> 2) & 1)
-    part = pick(quarters, mine)
-    for flip, step in ((1, 4), (2, 2), (3, 6)):
-        part = part + swap(pick(quarters, mine ^ flip), "samp", step)
-    bit = 8
-    while bit < n_samp:
-        part = part + swap(part, "samp", bit)
-        bit *= 2
+    part = halve(half, me, 1)
     held, order = [fold], [0]
     step = n_cell // 2
     while step:
@@ -381,20 +357,30 @@
         step //= 2
     held, part = lax.optimization_barrier((held, part))
     gram, scale = first_block(cell.reshape(1), [held[order.index(at)] for at in range(n_cell)], term_index.shape[0])
+    part = halve(part, me, 2)
+    bit = 8
+    while bit < n_samp:
+        part = part + swap(part, "samp", bit)
+        bit *= 2
     rows = part.shape[0]
     for block in range(1, blocks):
-        if block <= 2:
-            part = jnp.concatenate([part, swap(part, "samp", 8 >> block)], axis=0)
+        if block == 1:
             gram, part = lax.optimization_barrier((gram, part))
+            pair = jnp.concatenate([part, swap(part, "samp", 4)], axis=0)
+        elif block == 2:
+            gram, pair = lax.optimization_barrier((gram, pair))
+            pieces = [pair, swap(pair, "samp", 2), swap(pair, "samp", 1)]
+        elif block == 3:
+            gram, pieces = lax.optimization_barrier((gram, pieces))
+            pieces = pieces + [swap(pieces[1], "samp", 1)]
         gram = next_block(gram, block)
-    pieces = [part, swap(part, "samp", 1)]
-    spot = ((me & 1) << 2) | mine
+    spot = ((me & 1) << 2) | (me & 2) | ((me >> 2) & 1)
     where = jnp.stack([spot, cell])
     given = (where, gram, scale, pieces, rows, block_group, points.shape[1] * n_samp, n_cell)
-    far = list(solve(*given, tuple(range(n_cell // 2, n_cell))))
-    came = [swap(value, "cell", n_cell // 2 + at) for at, value in enumerate(far)]
-    *near, sobol = solve(*given, tuple(range(n_cell // 2)), far)
-    shares = [near[0]] + [swap(near[step], "cell", step) for step in range(1, n_cell // 2)] + came
+    far = list(solve(*given, tuple(range(1, n_cell))))
+    came = [swap(value, "cell", 1 + at) for at, value in enumerate(far)]
+    near, sobol = solve(*given, (0,), far)
+    shares = [near] + came
     return (join_columns(cell.reshape(1), shares), sobol)
 
 

time: 80.7 us -> 78.9 us (0.978)
  waiting for transfers between devices: 24.1 us -> 21.8 us
    ppermute x13, waiting for transfers between devices: 18.4 us -> 16.2 us  [swap(): return lax.ppermute(values, axis, [(at, at ^ step) for at in range(size)])]
  transfers between devices with their start and end apart: 15 -> 15, of which waited for: 7 -> 8; matrix products, arithmetic and copies ran while one was open for 0% -> 0% of each run, Pallas kernels for 26% -> 28%
where the time goes in v3:
time: 78.9 us; the launch traced here: 78.5 us
  Pallas kernels  28.1 us (36%)
  starting transfers between devices  24 us (30%)
  waiting for transfers between devices  21.8 us (28%)
  local copies, waits for them, and re-layouts  3.53 us (4%)
  between operations  0.81 us (1%)
    ppermute x13, waiting for transfers between devices, swap(): return lax.ppermute(values, axis, [(at, at ^ step) for at in range(size)])  16.2 us
    pallas_call x3, Pallas kernels, next_block(): pl.pallas_call(functools.partial(next_kernel, block), out_shape=jax.Shape...  14.6 us
    ppermute x13, starting transfers between devices, swap(): return lax.ppermute(values, axis, [(at, at ^ step) for at in range(size)])  13.2 us
    all_to_all x2, starting transfers between devices, exchange(): return lax.all_to_all(pieces, 'samp', split_axis=0, concat_axis=0)  10.8 us
    all_to_all x2, waiting for transfers between devices, exchange(): return lax.all_to_all(pieces, 'samp', split_axis=0, concat_axis=0)  5.63 us
    pallas_call x1, Pallas kernels, first_block(): pl.pallas_call(first_kernel, out_shape=(jax.ShapeDtypeStruct((terms, term...  5.04 us
    pallas_call x1, Pallas kernels, design(): pl.pallas_call(functools.partial(design_kernel, 512), out_shape=(jax.Shap...  3.68 us
    pallas_call x2, Pallas kernels, solve(): pl.pallas_call(functools.partial(solve_kernel, samples, steps, rows, fini...  3.3 us
  transfers between devices with their start and end apart: 15, of which 8 were waited for; matrix products, arithmetic and copies ran while one was open for 0% of the time, Pallas kernels for 28%

profile of v3, /device:TPU:0, one launch (start us, length us, event | category | flops | bytes accessed | tf_op | source)
XLA Modules:
  0.0 78.5 jit_solution(8125246700924772790)
XLA Ops:
  2.2 3.7 %design.1 = (bf16[512,2048]{1,0:T(8,128)(2,1)S(1)}, f32[64,640]{1,0:T(8,128)}) custom-call(s32[1]{0:T(128)} %bitcast.cell_ref.where_ref, s32[2,512]{1,0:T(2,128)S(1)} %bitcast.19, f32[24,2048]{1,0:T(8,128)S(1)} %copy-done.1), custom_call_target="tpu_custom_call" | custom-call | tf_op jit(solution)/shard_map/design/pallas_call | solution.py:80
  5.9 7.3 %all-to-all-start = ((f32[8,8,640]{2,1,0:T(8,128)}), f32[8,8,640]{2,1,0:T(8,128)S(1)}, u32[]{:S(2)}, u32[]{:S(2)}) async-start(f32[8,8,640]{2,1,0:T(8,128)} %bitcast.3), calls=%async_computation | async-start | bytes 327680 | tf_op jit(solution)/shard_map/all_to_all | solution.py:331
  13.2 1.2 %copy-done = bf16[2048,256]{1,0:T(8,128)(2,1)S(1)} copy-done((bf16[2048,256]{1,0:T(8,128)(2,1)S(1)}, bf16[2048,256]{1,0:T(8,128)(2,1)}, u32[]{:S(2)}) %copy-start) | copy-done | bytes 1048600
  15.2 5.6 %all-to-all-done = f32[8,8,640]{2,1,0:T(8,128)S(1)} async-done(((f32[8,8,640]{2,1,0:T(8,128)}), f32[8,8,640]{2,1,0:T(8,128)S(1)}, u32[]{:S(2)}, u32[]{:S(2)}) %all-to-all-start) | async-done | bytes 163872 | tf_op jit(solution)/shard_map/all_to_all | solution.py:331
  21.5 3.6 %all-to-all-start.1 = ((f32[8,8,640]{2,1,0:T(8,128)}), f32[8,8,640]{2,1,0:T(8,128)S(1)}, u32[]{:S(2)}, u32[]{:S(2)}) async-start(f32[8,8,640]{2,1,0:T(8,128)} %broadcast_in_dim.2), calls=%async_computation.1 | async-start | bytes 327680 | tf_op jit(solution)/shard_map/all_to_all | solution.py:331
  25.0 1.7 %collective-permute-start = (f32[256,256]{1,0:T(8,128)S(1)}, f32[256,256]{1,0:T(8,128)S(1)}, u32[]{:S(2)}, u32[]{:S(2)}) collective-permute-start(f32[256,256]{1,0:T(8,128)S(1)} %get-tuple-element.37), channel_id=1, source_target_pairs={{0,4},{4,0},{8,12},{12,8},{16,20},{20,16},{24,28},{28,24},{1,5},{5... | collective-permute-start | bytes 786440 | tf_op jit(solution)/shard_map/ppermute | solution.py:317
  26.8 6.9 %collective-permute-done = f32[256,256]{1,0:T(8,128)S(1)} collective-permute-done((f32[256,256]{1,0:T(8,128)S(1)}, f32[256,256]{1,0:T(8,128)S(1)}, u32[]{:S(2)}, u32[]{:S(2)}) %collective-permute-start) | collective-permute-done | bytes 262176 | tf_op jit(solution)/shard_map/ppermute | solution.py:317
  33.8 1.5 %collective-permute-start.1 = (f32[64,640]{1,0:T(8,128)S(1)}, f32[64,640]{1,0:T(8,128)S(1)}, u32[]{:S(2)}, u32[]{:S(2)}) collective-permute-start(f32[64,640]{1,0:T(8,128)S(1)} %bitcast.16), channel_id=1, source_target_pairs={{0,2},{1,3},{2,0},{3,1},{4,6},{5,7},{6,4},{7,5},{8,10},{9,11},{10,... | collective-permute-start | bytes 491528 | tf_op jit(solution)/shard_map/ppermute | solution.py:317
  35.3 1.5 %collective-permute-start.4 = (f32[128,256]{1,0:T(8,128)S(1)}, f32[128,256]{1,0:T(8,128)S(1)}, u32[]{:S(2)}, u32[]{:S(2)}) collective-permute-start(f32[128,256]{1,0:T(8,128)S(1)} %dynamic-slice_bitcast_fusion), channel_id=1, source_target_pairs={{0,8},{4,12},{8,0},{12,4},{16,24},{20,28},{24,16},{28,20},{1,9},{5... | collective-permute-start | bytes 393224 | tf_op jit(solution)/shard_map/ppermute | solution.py:317
  36.9 2.3 %collective-permute-done.1.refs_2_ = f32[64,640]{1,0:T(8,128)S(1)} collective-permute-done((f32[64,640]{1,0:T(8,128)S(1)}, f32[64,640]{1,0:T(8,128)S(1)}, u32[]{:S(2)}, u32[]{:S(2)}) %collective-permute-start.1) | collective-permute-done | bytes 163872 | tf_op jit(solution)/shard_map/ppermute | solution.py:317
  39.2 1.2 %collective-permute-done.4 = f32[128,256]{1,0:T(8,128)S(1)} collective-permute-done((f32[128,256]{1,0:T(8,128)S(1)}, f32[128,256]{1,0:T(8,128)S(1)}, u32[]{:S(2)}, u32[]{:S(2)}) %collective-permute-start.4) | collective-permute-done | bytes 131104 | tf_op jit(solution)/shard_map/ppermute | solution.py:317
  40.6 2.4 %collective-permute-start.5 = (f32[64,256]{1,0:T(8,128)S(1)}, f32[64,256]{1,0:T(8,128)S(1)}, u32[]{:S(2)}, u32[]{:S(2)}) collective-permute-start(f32[64,256]{1,0:T(8,128)S(1)} %dynamic-slice_bitcast_fusion.1), channel_id=1, source_target_pairs={{0,16},{4,20},{8,24},{12,28},{16,0},{20,4},{24,8},{28,12},{1,17},{... | collective-permute-start | bytes 196616 | tf_op jit(solution)/shard_map/ppermute | solution.py:317
  42.9 5.0 %block_0.1 = (f32[512,512]{1,0:T(8,128)S(1)}, f32[512,1]{1,0:T(8,128)S(1)}) custom-call(s32[1]{0:T(128)} %bitcast.cell_ref.where_ref, f32[64,640]{1,0:T(8,128)S(1)} %bitcast.18, f32[64,640]{1,0:T(8,128)S(1)} %collective-permute-done.2.refs_1_, f32[64,640]{1,0:T(8,128)S(1)} %collective-permute-done.1.refs_2_, f32[64,640]{1,0:T(8,128)S(1)} %collective-permute-done.3.refs_3_), custom_call_target="tpu_custom_call" | custom-call | flops 1000000000 | bytes 1048576 | tf_op jit(solution)/shard_map/block_0/pallas_call | solution.py:210
  48.6 4.8 %block_1.1.in_ref = f32[512,512]{1,0:T(8,128)S(1)} custom-call(f32[512,512]{1,0:T(8,128)S(1)} %get-tuple-element.46.in_ref), custom_call_target="tpu_custom_call", output_to_operand_aliasing={{}: (0, {})} | custom-call | flops 1000000000 | bytes 1048576 | tf_op jit(solution)/shard_map/block_1/pallas_call | solution.py:225
  53.4 1.0 %collective-permute-done.6 = f32[64,256]{1,0:T(8,128)S(1)} collective-permute-done((f32[64,256]{1,0:T(8,128)S(1)}, f32[64,256]{1,0:T(8,128)S(1)}, u32[]{:S(2)}, u32[]{:S(2)}) %collective-permute-start.6) | collective-permute-done | bytes 65568 | tf_op jit(solution)/shard_map/ppermute | solution.py:317
  54.4 1.4 %collective-permute-start.7 = (f32[128,256]{1,0:T(8,128)S(1)}, f32[128,256]{1,0:T(8,128)S(1)}, u32[]{:S(2)}, u32[]{:S(2)}) collective-permute-start(f32[128,256]{1,0:T(8,128)S(1)} %pad_maximum_fusion.refs_0_), channel_id=1, source_target_pairs={{0,8},{4,12},{8,0},{12,4},{16,24},{20,28},{24,16},{28,20},{1,9},{5... | collective-permute-start | bytes 393224 | tf_op jit(solution)/shard_map/ppermute | solution.py:317
  56.6 5.0 %block_2.1.in_ref = f32[512,512]{1,0:T(8,128)S(1)} custom-call(f32[512,512]{1,0:T(8,128)S(1)} %block_1.1.in_ref), custom_call_target="tpu_custom_call", output_to_operand_aliasing={{}: (0, {})} | custom-call | flops 1000000000 | bytes 1048576 | tf_op jit(solution)/shard_map/block_2/pallas_call | solution.py:225
  61.7 1.3 %collective-permute-start.9 = (f32[128,256]{1,0:T(8,128)S(1)}, f32[128,256]{1,0:T(8,128)S(1)}, u32[]{:S(2)}, u32[]{:S(2)}) collective-permute-start(f32[128,256]{1,0:T(8,128)S(1)} %collective-permute-done.7.refs_1_), channel_id=1, source_target_pairs={{0,4},{4,0},{8,12},{12,8},{16,20},{20,16},{24,28},{28,24},{1,5},{5... | collective-permute-start | bytes 393224 | tf_op jit(solution)/shard_map/ppermute | solution.py:317
  63.1 4.7 %block_3.1.inverse_ref = f32[512,512]{1,0:T(8,128)S(1)} custom-call(f32[512,512]{1,0:T(8,128)S(1)} %block_2.1.in_ref), custom_call_target="tpu_custom_call", output_to_operand_aliasing={{}: (0, {})} | custom-call | flops 1000000000 | bytes 1048576 | tf_op jit(solution)/shard_map/block_3/pallas_call | solution.py:225
  67.8 1.5 %solve_far.1 = (f32[128,256]{1,0:T(8,128)S(1)}, f32[128,256]{1,0:T(8,128)S(1)}, f32[128,256]{1,0:T(8,128)S(1)}) custom-call(s32[2]{0:T(128)S(1)} %pad_add_fusion.where_ref, s32[8]{0:T(128)S(1)} %copy-done.3, f32[512,512]{1,0:T(8,128)S(1)} %block_3.1.inverse_ref, f32[512,1]{1,0:T(8,128)S(1)} %get-tuple-element.51.scale_ref, ...), custom_call_target="tpu_custom_call" | custom-call | flops 1000000000 | bytes 1048576 | tf_op jit(solution)/shard_map/solve_far/pallas_call | solution.py:284
  69.4 1.5 %collective-permute-start.11 = (f32[128,256]{1,0:T(8,128)S(1)}, f32[128,256]{1,0:T(8,128)S(1)}, u32[]{:S(2)}, u32[]{:S(2)}) collective-permute-start(f32[128,256]{1,0:T(8,128)S(1)} %get-tuple-element.56.refs_5_), channel_id=1, source_target_pairs={{0,2},{1,3},{2,0},{3,1},{4,6},{5,7},{6,4},{7,5},{8,10},{9,11},{10,... | collective-permute-start | bytes 393224 | tf_op jit(solution)/shard_map/ppermute | solution.py:317
  71.3 1.8 %solve_near.1 = (f32[128,256]{1,0:T(8,128)S(1)}, f32[8,256]{1,0:T(8,128)}) custom-call(s32[2]{0:T(128)S(1)} %pad_add_fusion.where_ref, s32[8]{0:T(128)S(1)} %copy-done.3, f32[512,512]{1,0:T(8,128)S(1)} %block_3.1.inverse_ref, f32[512,1]{1,0:T(8,128)S(1)} %get-tuple-element.51.scale_ref, f32[128,256]{1,0:T(8,128)S(1)} %pad_maximum_fusion.refs_0_, ...), custom_call_target="tpu_custom_call" | custom-call | flops 5000000000 | bytes 1048576 | tf_op jit(solution)/shard_map/solve_near/pallas_call | solution.py:284
  73.1 2.7 %collective-permute-done.11.refs_2_ = f32[128,256]{1,0:T(8,128)S(1)} collective-permute-done((f32[128,256]{1,0:T(8,128)S(1)}, f32[128,256]{1,0:T(8,128)S(1)}, u32[]{:S(2)}, u32[]{:S(2)}) %collective-permute-start.11) | collective-permute-done | bytes 131104 | tf_op jit(solution)/shard_map/ppermute | solution.py:317
  75.8 1.9 %collective-permute-done.12.refs_3_ = f32[128,256]{1,0:T(8,128)S(1)} collective-permute-done((f32[128,256]{1,0:T(8,128)S(1)}, f32[128,256]{1,0:T(8,128)S(1)}, u32[]{:S(2)}, u32[]{:S(2)}) %collective-permute-start.12) | collective-permute-done | bytes 131104 | tf_op jit(solution)/shard_map/ppermute | solution.py:317
  (32 shorter events, 6.0 us)
Async XLA Ops:
  0.6 0.9 %copy-start.1 = (f32[24,2048]{1,0:T(8,128)S(1)}, f32[24,2048]{1,0:T(8,128)}, u32[]{:S(2)}) copy-start(f32[24,2048]{1,0:T(8,128)} %points_ref.1) | copy-start | bytes 589828
  1.6 0.7 copy-start.2
  5.9 14.8 %all-to-all-start = ((f32[8,8,640]{2,1,0:T(8,128)}), f32[8,8,640]{2,1,0:T(8,128)S(1)}, u32[]{:S(2)}, u32[]{:S(2)}) async-start(f32[8,8,640]{2,1,0:T(8,128)} %bitcast.3), calls=%async_computation | async-start | bytes 327680 | tf_op jit(solution)/shard_map/all_to_all | solution.py:331
  13.2 1.2 %copy-start = (bf16[2048,256]{1,0:T(8,128)(2,1)S(1)}, bf16[2048,256]{1,0:T(8,128)(2,1)}, u32[]{:S(2)}) copy-start(bf16[2048,256]{1,0:T(8,128)(2,1)} %yields_ref.1) | copy-start | bytes 3145732
  21.5 12.3 %all-to-all-start.1 = ((f32[8,8,640]{2,1,0:T(8,128)}), f32[8,8,640]{2,1,0:T(8,128)S(1)}, u32[]{:S(2)}, u32[]{:S(2)}) async-start(f32[8,8,640]{2,1,0:T(8,128)} %broadcast_in_dim.2), calls=%async_computation.1 | async-start | bytes 327680 | tf_op jit(solution)/shard_map/all_to_all | solution.py:331
  25.0 8.7 %collective-permute-start = (f32[256,256]{1,0:T(8,128)S(1)}, f32[256,256]{1,0:T(8,128)S(1)}, u32[]{:S(2)}, u32[]{:S(2)}) collective-permute-start(f32[256,256]{1,0:T(8,128)S(1)} %get-tuple-element.37), channel_id=1, source_target_pairs={{0,4},{4,0},{8,12},{12,8},{16,20},{20,16},{24,28},{28,24},{1,5},{5... | collective-permute-start | bytes 786440 | tf_op jit(solution)/shard_map/ppermute | solution.py:317
  33.8 5.4 %collective-permute-start.1 = (f32[64,640]{1,0:T(8,128)S(1)}, f32[64,640]{1,0:T(8,128)S(1)}, u32[]{:S(2)}, u32[]{:S(2)}) collective-permute-start(f32[64,640]{1,0:T(8,128)S(1)} %bitcast.16), channel_id=1, source_target_pairs={{0,2},{1,3},{2,0},{3,1},{4,6},{5,7},{6,4},{7,5},{8,10},{9,11},{10,... | collective-permute-start | bytes 491528 | tf_op jit(solution)/shard_map/ppermute | solution.py:317
  35.3 5.0 %collective-permute-start.4 = (f32[128,256]{1,0:T(8,128)S(1)}, f32[128,256]{1,0:T(8,128)S(1)}, u32[]{:S(2)}, u32[]{:S(2)}) collective-permute-start(f32[128,256]{1,0:T(8,128)S(1)} %dynamic-slice_bitcast_fusion), channel_id=1, source_target_pairs={{0,8},{4,12},{8,0},{12,4},{16,24},{20,28},{24,16},{28,20},{1,9},{5... | collective-permute-start | bytes 393224 | tf_op jit(solution)/shard_map/ppermute | solution.py:317
  36.9 3.5 %collective-permute-start.2 = (f32[64,640]{1,0:T(8,128)S(1)}, f32[64,640]{1,0:T(8,128)S(1)}, u32[]{:S(2)}, u32[]{:S(2)}) collective-permute-start(f32[64,640]{1,0:T(8,128)S(1)} %bitcast.17), channel_id=1, source_target_pairs={{0,1},{1,0},{2,3},{3,2},{4,5},{5,4},{6,7},{7,6},{8,9},{9,8},{10,11... | collective-permute-start | bytes 491528 | tf_op jit(solution)/shard_map/ppermute | solution.py:317
  39.2 1.4 %collective-permute-start.3 = (f32[64,640]{1,0:T(8,128)S(1)}, f32[64,640]{1,0:T(8,128)S(1)}, u32[]{:S(2)}, u32[]{:S(2)}) collective-permute-start(f32[64,640]{1,0:T(8,128)S(1)} %collective-permute-done.1.refs_2_), channel_id=1, source_target_pairs={{0,1},{1,0},{2,3},{3,2},{4,5},{5,4},{6,7},{7,6},{8,9},{9,8},{10,11... | collective-permute-start | bytes 491528 | tf_op jit(solution)/shard_map/ppermute | solution.py:317
  40.6 7.4 %collective-permute-start.5 = (f32[64,256]{1,0:T(8,128)S(1)}, f32[64,256]{1,0:T(8,128)S(1)}, u32[]{:S(2)}, u32[]{:S(2)}) collective-permute-start(f32[64,256]{1,0:T(8,128)S(1)} %dynamic-slice_bitcast_fusion.1), channel_id=1, source_target_pairs={{0,16},{4,20},{8,24},{12,28},{16,0},{20,4},{24,8},{28,12},{1,17},{... | collective-permute-start | bytes 196616 | tf_op jit(solution)/shard_map/ppermute | solution.py:317
  48.0 6.4 %collective-permute-start.6 = (f32[64,256]{1,0:T(8,128)S(1)}, f32[64,256]{1,0:T(8,128)S(1)}, u32[]{:S(2)}, u32[]{:S(2)}) collective-permute-start(f32[64,256]{1,0:T(8,128)S(1)} %bitcast_add_fusion.1), channel_id=1, source_target_pairs={{0,16},{4,20},{8,24},{12,28},{16,0},{20,4},{24,8},{28,12},{1,17},{... | collective-permute-start | bytes 196616 | tf_op jit(solution)/shard_map/ppermute | solution.py:317
  54.4 7.2 %collective-permute-start.7 = (f32[128,256]{1,0:T(8,128)S(1)}, f32[128,256]{1,0:T(8,128)S(1)}, u32[]{:S(2)}, u32[]{:S(2)}) collective-permute-start(f32[128,256]{1,0:T(8,128)S(1)} %pad_maximum_fusion.refs_0_), channel_id=1, source_target_pairs={{0,8},{4,12},{8,0},{12,4},{16,24},{20,28},{24,16},{28,20},{1,9},{5... | collective-permute-start | bytes 393224 | tf_op jit(solution)/shard_map/ppermute | solution.py:317
  55.8 5.9 %collective-permute-start.8 = (f32[128,256]{1,0:T(8,128)S(1)}, f32[128,256]{1,0:T(8,128)S(1)}, u32[]{:S(2)}, u32[]{:S(2)}) collective-permute-start(f32[128,256]{1,0:T(8,128)S(1)} %pad_maximum_fusion.refs_0_), channel_id=1, source_target_pairs={{0,4},{4,0},{8,12},{12,8},{16,20},{20,16},{24,28},{28,24},{1,5},{5... | collective-permute-start | bytes 393224 | tf_op jit(solution)/shard_map/ppermute | solution.py:317
  61.7 6.1 %copy-start.3 = (s32[8]{0:T(128)S(1)}, s32[8]{0:T(128)}, u32[]{:S(2)}) copy-start(s32[8]{0:T(128)} %group_ref.3) | copy-start | bytes 100
  61.7 6.1 %collective-permute-start.9 = (f32[128,256]{1,0:T(8,128)S(1)}, f32[128,256]{1,0:T(8,128)S(1)}, u32[]{:S(2)}, u32[]{:S(2)}) collective-permute-start(f32[128,256]{1,0:T(8,128)S(1)} %collective-permute-done.7.refs_1_), channel_id=1, source_target_pairs={{0,4},{4,0},{8,12},{12,8},{16,20},{20,16},{24,28},{28,24},{1,5},{5... | collective-permute-start | bytes 393224 | tf_op jit(solution)/shard_map/ppermute | solution.py:317
  69.3 3.7 %collective-permute-start.10 = (f32[128,256]{1,0:T(8,128)S(1)}, f32[128,256]{1,0:T(8,128)S(1)}, u32[]{:S(2)}, u32[]{:S(2)}) collective-permute-start(f32[128,256]{1,0:T(8,128)S(1)} %get-tuple-element.55.refs_4_), channel_id=1, source_target_pairs={{0,1},{1,0},{2,3},{3,2},{4,5},{5,4},{6,7},{7,6},{8,9},{9,8},{10,11... | collective-permute-start | bytes 393224 | tf_op jit(solution)/shard_map/ppermute | solution.py:317
  69.4 6.4 %collective-permute-start.11 = (f32[128,256]{1,0:T(8,128)S(1)}, f32[128,256]{1,0:T(8,128)S(1)}, u32[]{:S(2)}, u32[]{:S(2)}) collective-permute-start(f32[128,256]{1,0:T(8,128)S(1)} %get-tuple-element.56.refs_5_), channel_id=1, source_target_pairs={{0,2},{1,3},{2,0},{3,1},{4,6},{5,7},{6,4},{7,5},{8,10},{9,11},{10,... | collective-permute-start | bytes 393224 | tf_op jit(solution)/shard_map/ppermute | solution.py:317
  70.9 6.7 %collective-permute-start.12 = (f32[128,256]{1,0:T(8,128)S(1)}, f32[128,256]{1,0:T(8,128)S(1)}, u32[]{:S(2)}, u32[]{:S(2)}) collective-permute-start(f32[128,256]{1,0:T(8,128)S(1)} %get-tuple-element.57.refs_6_), channel_id=1, source_target_pairs={{0,3},{1,2},{2,1},{3,0},{4,7},{5,6},{6,5},{7,4},{8,11},{9,10},{10,... | collective-permute-start | bytes 393224 | tf_op jit(solution)/shard_map/ppermute | solution.py:317

commit v4 on v3

--- a/solution.py
+++ b/solution.py
@@ -121,6 +121,13 @@
     return jnp.broadcast_to(values[at:at + 1, :], values.shape)
 
 
+def stacked_outer(left, right):
+    a, b = split3(left), split3(right)
+    left = jnp.concatenate([a[0], a[0], a[1], a[1], a[0], a[2]], axis=0).astype(jnp.bfloat16)
+    right = jnp.concatenate([b[0], b[1], b[0], b[1], b[2], b[0]], axis=0).astype(jnp.bfloat16)
+    return lax.dot_general(left, right, (((0,), (0,)), ((), ())), preferred_element_type=jnp.float32)
+
+
 def sweep_tile(bands):
     bands = list(bands)
     shape = bands[0].shape
@@ -138,12 +145,15 @@
             for k in range(p + 1, 8):
                 columns[k] = columns[k] - factor * row_of(columns[k], p)
             fresh = fresh - factor * row_of(fresh, p)
-        rows = [row_of(fresh, k) for k in range(8)]
-        for step in range(1, len(bands)):
-            other = (at + step) % len(bands)
+        delta = stacked_outer(own, fresh)
+        following = (at + 1) % len(bands)
+        for other in range(len(bands)):
             value = jnp.where(inside, 0.0, bands[other])
-            for k in range(8):
-                value = value - lane_of(bands[other], base + k) * rows[k]
+            if other == following:
+                for k in range(8):
+                    value = value - lane_of(bands[other], base + k) * row_of(fresh, k)
+            else:
+                value = value - delta[8 * other:8 * other + 8]
             bands[other] = value
         bands[at] = fresh
     return bands

time: 78.9 us -> 76.2 us (0.966)
  Pallas kernels: 28.1 us -> 25.3 us
  waiting for transfers between devices: 21.8 us -> 22.8 us
  starting transfers between devices: 24 us -> 23.2 us
    pallas_call x3, Pallas kernels: 14.6 us -> 11.9 us  [next_block(): pl.pallas_call(functools.partial(next_kernel, block), out_shape=jax.Shape...]
    ppermute x13, waiting for transfers between devices: 16.2 us -> 17.2 us  [swap(): return lax.ppermute(values, axis, [(at, at ^ step) for at in range(size)])]
    ppermute x13, starting transfers between devices: 13.2 us -> 12.4 us  [swap(): return lax.ppermute(values, axis, [(at, at ^ step) for at in range(size)])]
  transfers between devices with their start and end apart: 15 -> 15, of which waited for: 8 -> 9; matrix products, arithmetic and copies ran while one was open for 0% -> 0% of each run, Pallas kernels for 28% -> 25%
where the time goes in v4:
time: 76.2 us; the launch traced here: 75.8 us
  Pallas kernels  25.3 us (33%)
  starting transfers between devices  23.2 us (30%)
  waiting for transfers between devices  22.8 us (30%)
  local copies, waits for them, and re-layouts  3.53 us (5%)
  between operations  0.8 us (1%)
    ppermute x13, waiting for transfers between devices, swap(): return lax.ppermute(values, axis, [(at, at ^ step) for at in range(size)])  17.2 us
    ppermute x13, starting transfers between devices, swap(): return lax.ppermute(values, axis, [(at, at ^ step) for at in range(size)])  12.4 us
    pallas_call x3, Pallas kernels, next_block(): pl.pallas_call(functools.partial(next_kernel, block), out_shape=jax.Shape...  11.9 us
    all_to_all x2, starting transfers between devices, exchange(): return lax.all_to_all(pieces, 'samp', split_axis=0, concat_axis=0)  10.8 us
    all_to_all x2, waiting for transfers between devices, exchange(): return lax.all_to_all(pieces, 'samp', split_axis=0, concat_axis=0)  5.63 us
    pallas_call x1, Pallas kernels, first_block(): pl.pallas_call(first_kernel, out_shape=(jax.ShapeDtypeStruct((terms, term...  4.93 us
    pallas_call x1, Pallas kernels, design(): pl.pallas_call(functools.partial(design_kernel, 512), out_shape=(jax.Shap...  3.68 us
    pallas_call x2, Pallas kernels, solve(): pl.pallas_call(functools.partial(solve_kernel, samples, steps, rows, fini...  3.3 us
  transfers between devices with their start and end apart: 15, of which 9 were waited for; matrix products, arithmetic and copies ran while one was open for 0% of the time, Pallas kernels for 25%

profile of v4, /device:TPU:0, one launch (start us, length us, event | category | flops | bytes accessed | tf_op | source)
XLA Modules:
  0.0 75.8 jit_solution(9994404131300878318)
XLA Ops:
  0.6 0.9 %copy-done.1 = f32[24,2048]{1,0:T(8,128)S(1)} copy-done((f32[24,2048]{1,0:T(8,128)S(1)}, f32[24,2048]{1,0:T(8,128)}, u32[]{:S(2)}) %copy-start.1) | copy-done | bytes 196632
  2.2 3.7 %design.1 = (bf16[512,2048]{1,0:T(8,128)(2,1)S(1)}, f32[64,640]{1,0:T(8,128)}) custom-call(s32[1]{0:T(128)} %bitcast.cell_ref.where_ref, s32[2,512]{1,0:T(2,128)S(1)} %bitcast.19, f32[24,2048]{1,0:T(8,128)S(1)} %copy-done.1), custom_call_target="tpu_custom_call" | custom-call | tf_op jit(solution)/shard_map/design/pallas_call | solution.py:80
  5.9 7.3 %all-to-all-start = ((f32[8,8,640]{2,1,0:T(8,128)}), f32[8,8,640]{2,1,0:T(8,128)S(1)}, u32[]{:S(2)}, u32[]{:S(2)}) async-start(f32[8,8,640]{2,1,0:T(8,128)} %bitcast.3), calls=%async_computation | async-start | bytes 327680 | tf_op jit(solution)/shard_map/all_to_all | solution.py:341
  13.2 1.2 %copy-done = bf16[2048,256]{1,0:T(8,128)(2,1)S(1)} copy-done((bf16[2048,256]{1,0:T(8,128)(2,1)S(1)}, bf16[2048,256]{1,0:T(8,128)(2,1)}, u32[]{:S(2)}) %copy-start) | copy-done | bytes 1048600
  15.2 5.6 %all-to-all-done = f32[8,8,640]{2,1,0:T(8,128)S(1)} async-done(((f32[8,8,640]{2,1,0:T(8,128)}), f32[8,8,640]{2,1,0:T(8,128)S(1)}, u32[]{:S(2)}, u32[]{:S(2)}) %all-to-all-start) | async-done | bytes 163872 | tf_op jit(solution)/shard_map/all_to_all | solution.py:341
  21.5 3.6 %all-to-all-start.1 = ((f32[8,8,640]{2,1,0:T(8,128)}), f32[8,8,640]{2,1,0:T(8,128)S(1)}, u32[]{:S(2)}, u32[]{:S(2)}) async-start(f32[8,8,640]{2,1,0:T(8,128)} %broadcast_in_dim.2), calls=%async_computation.1 | async-start | bytes 327680 | tf_op jit(solution)/shard_map/all_to_all | solution.py:341
  25.0 1.7 %collective-permute-start = (f32[256,256]{1,0:T(8,128)S(1)}, f32[256,256]{1,0:T(8,128)S(1)}, u32[]{:S(2)}, u32[]{:S(2)}) collective-permute-start(f32[256,256]{1,0:T(8,128)S(1)} %get-tuple-element.37), channel_id=1, source_target_pairs={{0,4},{4,0},{8,12},{12,8},{16,20},{20,16},{24,28},{28,24},{1,5},{5... | collective-permute-start | bytes 786440 | tf_op jit(solution)/shard_map/ppermute | solution.py:327
  26.8 6.9 %collective-permute-done = f32[256,256]{1,0:T(8,128)S(1)} collective-permute-done((f32[256,256]{1,0:T(8,128)S(1)}, f32[256,256]{1,0:T(8,128)S(1)}, u32[]{:S(2)}, u32[]{:S(2)}) %collective-permute-start) | collective-permute-done | bytes 262176 | tf_op jit(solution)/shard_map/ppermute | solution.py:327
  33.8 1.5 %collective-permute-start.1 = (f32[64,640]{1,0:T(8,128)S(1)}, f32[64,640]{1,0:T(8,128)S(1)}, u32[]{:S(2)}, u32[]{:S(2)}) collective-permute-start(f32[64,640]{1,0:T(8,128)S(1)} %bitcast.16), channel_id=1, source_target_pairs={{0,2},{1,3},{2,0},{3,1},{4,6},{5,7},{6,4},{7,5},{8,10},{9,11},{10,... | collective-permute-start | bytes 491528 | tf_op jit(solution)/shard_map/ppermute | solution.py:327
  35.3 1.5 %collective-permute-start.4 = (f32[128,256]{1,0:T(8,128)S(1)}, f32[128,256]{1,0:T(8,128)S(1)}, u32[]{:S(2)}, u32[]{:S(2)}) collective-permute-start(f32[128,256]{1,0:T(8,128)S(1)} %dynamic-slice_bitcast_fusion), channel_id=1, source_target_pairs={{0,8},{4,12},{8,0},{12,4},{16,24},{20,28},{24,16},{28,20},{1,9},{5... | collective-permute-start | bytes 393224 | tf_op jit(solution)/shard_map/ppermute | solution.py:327
  36.9 2.3 %collective-permute-done.1.refs_2_ = f32[64,640]{1,0:T(8,128)S(1)} collective-permute-done((f32[64,640]{1,0:T(8,128)S(1)}, f32[64,640]{1,0:T(8,128)S(1)}, u32[]{:S(2)}, u32[]{:S(2)}) %collective-permute-start.1) | collective-permute-done | bytes 163872 | tf_op jit(solution)/shard_map/ppermute | solution.py:327
  39.2 1.2 %collective-permute-done.4 = f32[128,256]{1,0:T(8,128)S(1)} collective-permute-done((f32[128,256]{1,0:T(8,128)S(1)}, f32[128,256]{1,0:T(8,128)S(1)}, u32[]{:S(2)}, u32[]{:S(2)}) %collective-permute-start.4) | collective-permute-done | bytes 131104 | tf_op jit(solution)/shard_map/ppermute | solution.py:327
  40.6 2.4 %collective-permute-start.5 = (f32[64,256]{1,0:T(8,128)S(1)}, f32[64,256]{1,0:T(8,128)S(1)}, u32[]{:S(2)}, u32[]{:S(2)}) collective-permute-start(f32[64,256]{1,0:T(8,128)S(1)} %dynamic-slice_bitcast_fusion.1), channel_id=1, source_target_pairs={{0,16},{4,20},{8,24},{12,28},{16,0},{20,4},{24,8},{28,12},{1,17},{... | collective-permute-start | bytes 196616 | tf_op jit(solution)/shard_map/ppermute | solution.py:327
  42.9 4.9 %block_0.1 = (f32[512,512]{1,0:T(8,128)S(1)}, f32[512,1]{1,0:T(8,128)S(1)}) custom-call(s32[1]{0:T(128)} %bitcast.cell_ref.where_ref, f32[64,640]{1,0:T(8,128)S(1)} %bitcast.18, f32[64,640]{1,0:T(8,128)S(1)} %collective-permute-done.2.refs_1_, f32[64,640]{1,0:T(8,128)S(1)} %collective-permute-done.1.refs_2_, f32[64,640]{1,0:T(8,128)S(1)} %collective-permute-done.3.refs_3_), custom_call_target="tpu_custom_call" | custom-call | flops 1000000000 | bytes 1048576 | tf_op jit(solution)/shard_map/block_0/pallas_call | solution.py:220
  48.5 4.0 %block_1.1.in_ref = f32[512,512]{1,0:T(8,128)S(1)} custom-call(f32[512,512]{1,0:T(8,128)S(1)} %get-tuple-element.46.in_ref), custom_call_target="tpu_custom_call", output_to_operand_aliasing={{}: (0, {})} | custom-call | flops 1000000000 | bytes 1048576 | tf_op jit(solution)/shard_map/block_1/pallas_call | solution.py:235
  52.5 1.8 %collective-permute-done.6 = f32[64,256]{1,0:T(8,128)S(1)} collective-permute-done((f32[64,256]{1,0:T(8,128)S(1)}, f32[64,256]{1,0:T(8,128)S(1)}, u32[]{:S(2)}, u32[]{:S(2)}) %collective-permute-start.6) | collective-permute-done | bytes 65568 | tf_op jit(solution)/shard_map/ppermute | solution.py:327
  55.8 4.0 %block_2.1.in_ref = f32[512,512]{1,0:T(8,128)S(1)} custom-call(f32[512,512]{1,0:T(8,128)S(1)} %block_1.1.in_ref), custom_call_target="tpu_custom_call", output_to_operand_aliasing={{}: (0, {})} | custom-call | flops 1000000000 | bytes 1048576 | tf_op jit(solution)/shard_map/block_2/pallas_call | solution.py:235
  59.9 1.1 %collective-permute-start.9 = (f32[128,256]{1,0:T(8,128)S(1)}, f32[128,256]{1,0:T(8,128)S(1)}, u32[]{:S(2)}, u32[]{:S(2)}) collective-permute-start(f32[128,256]{1,0:T(8,128)S(1)} %collective-permute-done.7.refs_1_), channel_id=1, source_target_pairs={{0,4},{4,0},{8,12},{12,8},{16,20},{20,16},{24,28},{28,24},{1,5},{5... | collective-permute-start | bytes 393224 | tf_op jit(solution)/shard_map/ppermute | solution.py:327
  61.2 3.9 %block_3.1.inverse_ref = f32[512,512]{1,0:T(8,128)S(1)} custom-call(f32[512,512]{1,0:T(8,128)S(1)} %block_2.1.in_ref), custom_call_target="tpu_custom_call", output_to_operand_aliasing={{}: (0, {})} | custom-call | flops 1000000000 | bytes 1048576 | tf_op jit(solution)/shard_map/block_3/pallas_call | solution.py:235
  65.1 1.5 %solve_far.1 = (f32[128,256]{1,0:T(8,128)S(1)}, f32[128,256]{1,0:T(8,128)S(1)}, f32[128,256]{1,0:T(8,128)S(1)}) custom-call(s32[2]{0:T(128)S(1)} %pad_add_fusion.where_ref, s32[8]{0:T(128)S(1)} %copy-done.3, f32[512,512]{1,0:T(8,128)S(1)} %block_3.1.inverse_ref, f32[512,1]{1,0:T(8,128)S(1)} %get-tuple-element.51.scale_ref, ...), custom_call_target="tpu_custom_call" | custom-call | flops 1000000000 | bytes 1048576 | tf_op jit(solution)/shard_map/solve_far/pallas_call | solution.py:294
  66.7 1.6 %collective-permute-start.11 = (f32[128,256]{1,0:T(8,128)S(1)}, f32[128,256]{1,0:T(8,128)S(1)}, u32[]{:S(2)}, u32[]{:S(2)}) collective-permute-start(f32[128,256]{1,0:T(8,128)S(1)} %get-tuple-element.56.refs_5_), channel_id=1, source_target_pairs={{0,2},{1,3},{2,0},{3,1},{4,6},{5,7},{6,4},{7,5},{8,10},{9,11},{10,... | collective-permute-start | bytes 393224 | tf_op jit(solution)/shard_map/ppermute | solution.py:327
  68.6 1.8 %solve_near.1 = (f32[128,256]{1,0:T(8,128)S(1)}, f32[8,256]{1,0:T(8,128)}) custom-call(s32[2]{0:T(128)S(1)} %pad_add_fusion.where_ref, s32[8]{0:T(128)S(1)} %copy-done.3, f32[512,512]{1,0:T(8,128)S(1)} %block_3.1.inverse_ref, f32[512,1]{1,0:T(8,128)S(1)} %get-tuple-element.51.scale_ref, f32[128,256]{1,0:T(8,128)S(1)} %pad_maximum_fusion.refs_0_, ...), custom_call_target="tpu_custom_call" | custom-call | flops 5000000000 | bytes 1048576 | tf_op jit(solution)/shard_map/solve_near/pallas_call | solution.py:294
  70.4 2.7 %collective-permute-done.11.refs_2_ = f32[128,256]{1,0:T(8,128)S(1)} collective-permute-done((f32[128,256]{1,0:T(8,128)S(1)}, f32[128,256]{1,0:T(8,128)S(1)}, u32[]{:S(2)}, u32[]{:S(2)}) %collective-permute-start.11) | collective-permute-done | bytes 131104 | tf_op jit(solution)/shard_map/ppermute | solution.py:327
  73.1 1.9 %collective-permute-done.12.refs_3_ = f32[128,256]{1,0:T(8,128)S(1)} collective-permute-done((f32[128,256]{1,0:T(8,128)S(1)}, f32[128,256]{1,0:T(8,128)S(1)}, u32[]{:S(2)}, u32[]{:S(2)}) %collective-permute-start.12) | collective-permute-done | bytes 131104 | tf_op jit(solution)/shard_map/ppermute | solution.py:327
  (32 shorter events, 5.9 us)
Async XLA Ops:
  0.6 0.9 %copy-start.1 = (f32[24,2048]{1,0:T(8,128)S(1)}, f32[24,2048]{1,0:T(8,128)}, u32[]{:S(2)}) copy-start(f32[24,2048]{1,0:T(8,128)} %points_ref.1) | copy-start | bytes 589828
  1.6 0.7 copy-start.2
  5.9 14.8 %all-to-all-start = ((f32[8,8,640]{2,1,0:T(8,128)}), f32[8,8,640]{2,1,0:T(8,128)S(1)}, u32[]{:S(2)}, u32[]{:S(2)}) async-start(f32[8,8,640]{2,1,0:T(8,128)} %bitcast.3), calls=%async_computation | async-start | bytes 327680 | tf_op jit(solution)/shard_map/all_to_all | solution.py:341
  13.2 1.2 %copy-start = (bf16[2048,256]{1,0:T(8,128)(2,1)S(1)}, bf16[2048,256]{1,0:T(8,128)(2,1)}, u32[]{:S(2)}) copy-start(bf16[2048,256]{1,0:T(8,128)(2,1)} %yields_ref.1) | copy-start | bytes 3145732
  21.5 12.3 %all-to-all-start.1 = ((f32[8,8,640]{2,1,0:T(8,128)}), f32[8,8,640]{2,1,0:T(8,128)S(1)}, u32[]{:S(2)}, u32[]{:S(2)}) async-start(f32[8,8,640]{2,1,0:T(8,128)} %broadcast_in_dim.2), calls=%async_computation.1 | async-start | bytes 327680 | tf_op jit(solution)/shard_map/all_to_all | solution.py:341
  25.0 8.7 %collective-permute-start = (f32[256,256]{1,0:T(8,128)S(1)}, f32[256,256]{1,0:T(8,128)S(1)}, u32[]{:S(2)}, u32[]{:S(2)}) collective-permute-start(f32[256,256]{1,0:T(8,128)S(1)} %get-tuple-element.37), channel_id=1, source_target_pairs={{0,4},{4,0},{8,12},{12,8},{16,20},{20,16},{24,28},{28,24},{1,5},{5... | collective-permute-start | bytes 786440 | tf_op jit(solution)/shard_map/ppermute | solution.py:327
  33.8 5.4 %collective-permute-start.1 = (f32[64,640]{1,0:T(8,128)S(1)}, f32[64,640]{1,0:T(8,128)S(1)}, u32[]{:S(2)}, u32[]{:S(2)}) collective-permute-start(f32[64,640]{1,0:T(8,128)S(1)} %bitcast.16), channel_id=1, source_target_pairs={{0,2},{1,3},{2,0},{3,1},{4,6},{5,7},{6,4},{7,5},{8,10},{9,11},{10,... | collective-permute-start | bytes 491528 | tf_op jit(solution)/shard_map/ppermute | solution.py:327
  35.3 5.0 %collective-permute-start.4 = (f32[128,256]{1,0:T(8,128)S(1)}, f32[128,256]{1,0:T(8,128)S(1)}, u32[]{:S(2)}, u32[]{:S(2)}) collective-permute-start(f32[128,256]{1,0:T(8,128)S(1)} %dynamic-slice_bitcast_fusion), channel_id=1, source_target_pairs={{0,8},{4,12},{8,0},{12,4},{16,24},{20,28},{24,16},{28,20},{1,9},{5... | collective-permute-start | bytes 393224 | tf_op jit(solution)/shard_map/ppermute | solution.py:327
  36.9 3.5 %collective-permute-start.2 = (f32[64,640]{1,0:T(8,128)S(1)}, f32[64,640]{1,0:T(8,128)S(1)}, u32[]{:S(2)}, u32[]{:S(2)}) collective-permute-start(f32[64,640]{1,0:T(8,128)S(1)} %bitcast.17), channel_id=1, source_target_pairs={{0,1},{1,0},{2,3},{3,2},{4,5},{5,4},{6,7},{7,6},{8,9},{9,8},{10,11... | collective-permute-start | bytes 491528 | tf_op jit(solution)/shard_map/ppermute | solution.py:327
  39.2 1.4 %collective-permute-start.3 = (f32[64,640]{1,0:T(8,128)S(1)}, f32[64,640]{1,0:T(8,128)S(1)}, u32[]{:S(2)}, u32[]{:S(2)}) collective-permute-start(f32[64,640]{1,0:T(8,128)S(1)} %collective-permute-done.1.refs_2_), channel_id=1, source_target_pairs={{0,1},{1,0},{2,3},{3,2},{4,5},{5,4},{6,7},{7,6},{8,9},{9,8},{10,11... | collective-permute-start | bytes 491528 | tf_op jit(solution)/shard_map/ppermute | solution.py:327
  40.6 7.3 %collective-permute-start.5 = (f32[64,256]{1,0:T(8,128)S(1)}, f32[64,256]{1,0:T(8,128)S(1)}, u32[]{:S(2)}, u32[]{:S(2)}) collective-permute-start(f32[64,256]{1,0:T(8,128)S(1)} %dynamic-slice_bitcast_fusion.1), channel_id=1, source_target_pairs={{0,16},{4,20},{8,24},{12,28},{16,0},{20,4},{24,8},{28,12},{1,17},{... | collective-permute-start | bytes 196616 | tf_op jit(solution)/shard_map/ppermute | solution.py:327
  47.9 6.4 %collective-permute-start.6 = (f32[64,256]{1,0:T(8,128)S(1)}, f32[64,256]{1,0:T(8,128)S(1)}, u32[]{:S(2)}, u32[]{:S(2)}) collective-permute-start(f32[64,256]{1,0:T(8,128)S(1)} %bitcast_add_fusion.1), channel_id=1, source_target_pairs={{0,16},{4,20},{8,24},{12,28},{16,0},{20,4},{24,8},{28,12},{1,17},{... | collective-permute-start | bytes 196616 | tf_op jit(solution)/shard_map/ppermute | solution.py:327
  54.3 5.5 %collective-permute-start.7 = (f32[128,256]{1,0:T(8,128)S(1)}, f32[128,256]{1,0:T(8,128)S(1)}, u32[]{:S(2)}, u32[]{:S(2)}) collective-permute-start(f32[128,256]{1,0:T(8,128)S(1)} %pad_maximum_fusion.refs_0_), channel_id=1, source_target_pairs={{0,8},{4,12},{8,0},{12,4},{16,24},{20,28},{24,16},{28,20},{1,9},{5... | collective-permute-start | bytes 393224 | tf_op jit(solution)/shard_map/ppermute | solution.py:327
  55.0 5.0 %collective-permute-start.8 = (f32[128,256]{1,0:T(8,128)S(1)}, f32[128,256]{1,0:T(8,128)S(1)}, u32[]{:S(2)}, u32[]{:S(2)}) collective-permute-start(f32[128,256]{1,0:T(8,128)S(1)} %pad_maximum_fusion.refs_0_), channel_id=1, source_target_pairs={{0,4},{4,0},{8,12},{12,8},{16,20},{20,16},{24,28},{28,24},{1,5},{5... | collective-permute-start | bytes 393224 | tf_op jit(solution)/shard_map/ppermute | solution.py:327
  59.8 5.3 %copy-start.3 = (s32[8]{0:T(128)S(1)}, s32[8]{0:T(128)}, u32[]{:S(2)}) copy-start(s32[8]{0:T(128)} %group_ref.3) | copy-start | bytes 100
  59.9 5.1 %collective-permute-start.9 = (f32[128,256]{1,0:T(8,128)S(1)}, f32[128,256]{1,0:T(8,128)S(1)}, u32[]{:S(2)}, u32[]{:S(2)}) collective-permute-start(f32[128,256]{1,0:T(8,128)S(1)} %collective-permute-done.7.refs_1_), channel_id=1, source_target_pairs={{0,4},{4,0},{8,12},{12,8},{16,20},{20,16},{24,28},{28,24},{1,5},{5... | collective-permute-start | bytes 393224 | tf_op jit(solution)/shard_map/ppermute | solution.py:327
  66.6 3.7 %collective-permute-start.10 = (f32[128,256]{1,0:T(8,128)S(1)}, f32[128,256]{1,0:T(8,128)S(1)}, u32[]{:S(2)}, u32[]{:S(2)}) collective-permute-start(f32[128,256]{1,0:T(8,128)S(1)} %get-tuple-element.55.refs_4_), channel_id=1, source_target_pairs={{0,1},{1,0},{2,3},{3,2},{4,5},{5,4},{6,7},{7,6},{8,9},{9,8},{10,11... | collective-permute-start | bytes 393224 | tf_op jit(solution)/shard_map/ppermute | solution.py:327
  66.7 6.4 %collective-permute-start.11 = (f32[128,256]{1,0:T(8,128)S(1)}, f32[128,256]{1,0:T(8,128)S(1)}, u32[]{:S(2)}, u32[]{:S(2)}) collective-permute-start(f32[128,256]{1,0:T(8,128)S(1)} %get-tuple-element.56.refs_5_), channel_id=1, source_target_pairs={{0,2},{1,3},{2,0},{3,1},{4,6},{5,7},{6,4},{7,5},{8,10},{9,11},{10,... | collective-permute-start | bytes 393224 | tf_op jit(solution)/shard_map/ppermute | solution.py:327
  68.3 6.7 %collective-permute-start.12 = (f32[128,256]{1,0:T(8,128)S(1)}, f32[128,256]{1,0:T(8,128)S(1)}, u32[]{:S(2)}, u32[]{:S(2)}) collective-permute-start(f32[128,256]{1,0:T(8,128)S(1)} %get-tuple-element.57.refs_6_), channel_id=1, source_target_pairs={{0,3},{1,2},{2,1},{3,0},{4,7},{5,6},{6,5},{7,4},{8,11},{9,10},{10,... | collective-permute-start | bytes 393224 | tf_op jit(solution)/shard_map/ppermute | solution.py:327

commit v5 on v4

--- a/solution.py
+++ b/solution.py
@@ -167,50 +167,64 @@
     return jnp.dot(left, right, preferred_element_type=jnp.float32)
 
 
-def sweep_block(gram_ref, block):
+def sweep_block(gram, out_ref, minus, block):
+    terms = out_ref.shape[0]
     band = slice(block * TILE, (block + 1) * TILE)
-    bands = sweep_tile(gram_ref[block * TILE + at:block * TILE + at + 8, band] for at in range(0, TILE, 8))
-    minus = jnp.concatenate(bands, axis=0)
-    old = gram_ref[band, :]
-    columns = gram_ref[:, band]
-    fresh = -stacked_dot(minus, old)
-    gram_ref[...] -= stacked_dot(columns, fresh)
-    gram_ref[band, :] = fresh
-    gram_ref[:, band] = fresh.T
-    gram_ref[band, band] = minus
+    whole = slice(0, terms)
+    fresh = -stacked_dot(minus, gram(band, whole))
+    parts = [minus if at == block * TILE else fresh[:, at:at + TILE] for at in range(0, terms, TILE)]
+    fresh = jnp.concatenate(parts, axis=1)
+    change = stacked_dot(gram(whole, band), fresh)
+    inside = (lax.broadcasted_iota(jnp.int32, (TILE, terms), 1) // TILE) == block
+    for at in range(0, terms, TILE):
+        rows = slice(at, at + TILE)
+        if at == block * TILE:
+            out_ref[rows, :] = fresh
+        else:
+            out_ref[rows, :] = jnp.where(inside, 0.0, gram(rows, whole)) - change[rows, :]
+
+
+def sweep(tile):
+    return jnp.concatenate(sweep_tile([tile[at:at + 8, :] for at in range(0, TILE, 8)]), axis=0)
 
 
 def first_kernel(where_ref, *refs):
-    out_ref, scale_ref = refs[-2:]
+    out_ref, scale_ref, gram_ref = refs[-3:]
     terms = out_ref.shape[0]
     blocks = terms // TILE
-    for step, ref in enumerate(refs[:-2]):
+    for step, ref in enumerate(refs[:-3]):
         piece = ref.shape[0] // 2
         start = pl.multiple_of((where_ref[0] ^ step) * piece, piece)
         for block in range(blocks):
             half, lane = fold_place(block, blocks)
             reach = (block + 1) * TILE
-            out_ref[pl.ds(start + block * TILE, piece), 0:reach] = (
+            gram_ref[pl.ds(start + block * TILE, piece), 0:reach] = (
                 ref[half * piece:(half + 1) * piece, lane:lane + reach]
             )
-    for block in range(blocks):
-        for other in range(block):
-            tile = out_ref[block * TILE:(block + 1) * TILE, other * TILE:(other + 1) * TILE]
-            out_ref[other * TILE:(other + 1) * TILE, block * TILE:(block + 1) * TILE] = tile.T
     diagonal = lax.broadcasted_iota(jnp.int32, (TILE, TILE), 0) == lax.broadcasted_iota(jnp.int32, (TILE, TILE), 1)
-    across = []
-    for block in range(blocks):
-        band = slice(block * TILE, (block + 1) * TILE)
-        only = jnp.where(diagonal, out_ref[band, band], 0.0)
-        scale_ref[band, :] = lax.rsqrt(jnp.sum(only, axis=1, keepdims=True))
+    bands = [slice(block * TILE, (block + 1) * TILE) for block in range(blocks)]
+    across, down = [], []
+    for band in bands:
+        only = jnp.where(diagonal, gram_ref[band, band], 0.0)
+        down.append(lax.rsqrt(jnp.sum(only, axis=1, keepdims=True)))
         across.append(lax.rsqrt(jnp.sum(only, axis=0, keepdims=True)))
-    out_ref[...] = out_ref[...] * scale_ref[...] * jnp.concatenate(across, axis=1)
-    sweep_block(out_ref, 0)
+    tiles = {}
+    for i, band in enumerate(bands):
+        scale_ref[band, :] = down[i]
+        for j in range(i + 1):
+            tiles[i, j] = gram_ref[band, bands[j]] * down[i] * across[j]
+    minus = sweep(tiles[0, 0])
+    for i, band in enumerate(bands):
+        for j in range(i + 1):
+            gram_ref[band, bands[j]] = tiles[i, j]
+            if j < i:
+                gram_ref[bands[j], band] = tiles[i, j].T
+    sweep_block(lambda rows, lanes: gram_ref[rows, lanes], out_ref, minus, 0)
 
 
 def next_kernel(block, in_ref, out_ref):
-    out_ref[...] = in_ref[...]
-    sweep_block(out_ref, block)
+    band = slice(block * TILE, (block + 1) * TILE)
+    sweep_block(lambda rows, lanes: in_ref[rows, lanes], out_ref, sweep(in_ref[band, band]), block)
 
 
 STEP_COST = pl.CostEstimate(flops=10**9, bytes_accessed=2**20, transcendentals=512)
@@ -225,6 +239,7 @@
         ),
         in_specs=[SMEM] + [VMEM] * len(pieces),
         out_specs=(VMEM, VMEM),
+        scratch_shapes=[pltpu.VMEM((terms, terms), jnp.float32)],
         compiler_params=BIG,
         cost_estimate=STEP_COST,
         name="block_0",
@@ -237,7 +252,6 @@
         out_shape=jax.ShapeDtypeStruct(gram.shape, jnp.float32),
         in_specs=[VMEM],
         out_specs=VMEM,
-        input_output_aliases={0: 0},
         compiler_params=BIG,
         cost_estimate=STEP_COST,
         name="block_%d" % block,

time: 76.2 us -> 76.1 us (level)
  no operation moved by 1% of the time
where the time goes in v5:
time: 76.1 us; the launch traced here: 75.7 us
  Pallas kernels  24.6 us (32%)
  starting transfers between devices  23.8 us (31%)
  waiting for transfers between devices  22.7 us (30%)
  local copies, waits for them, and re-layouts  3.53 us (5%)
  between operations  0.8 us (1%)
    ppermute x13, waiting for transfers between devices, swap(): return lax.ppermute(values, axis, [(at, at ^ step) for at in range(size)])  17.1 us
    ppermute x13, starting transfers between devices, swap(): return lax.ppermute(values, axis, [(at, at ^ step) for at in range(size)])  13 us
    pallas_call x3, Pallas kernels, next_block(): pl.pallas_call(functools.partial(next_kernel, block), out_shape=jax.Shape...  11.7 us
    all_to_all x2, starting transfers between devices, exchange(): return lax.all_to_all(pieces, 'samp', split_axis=0, concat_axis=0)  10.8 us
    all_to_all x2, waiting for transfers between devices, exchange(): return lax.all_to_all(pieces, 'samp', split_axis=0, concat_axis=0)  5.63 us
    pallas_call x1, Pallas kernels, first_block(): pl.pallas_call(first_kernel, out_shape=(jax.ShapeDtypeStruct((terms, term...  4.38 us
    pallas_call x1, Pallas kernels, design(): pl.pallas_call(functools.partial(design_kernel, 512), out_shape=(jax.Shap...  3.68 us
    pallas_call x2, Pallas kernels, solve(): pl.pallas_call(functools.partial(solve_kernel, samples, steps, rows, fini...  3.3 us
  transfers between devices with their start and end apart: 15, of which 9 were waited for; matrix products, arithmetic and copies ran while one was open for 0% of the time, Pallas kernels for 25%

profile of v5, /device:TPU:0, one launch (start us, length us, event | category | flops | bytes accessed | tf_op | source)
XLA Modules:
  0.0 75.7 jit_solution(1369596469111958147)
XLA Ops:
  2.2 3.7 %design.1 = (bf16[512,2048]{1,0:T(8,128)(2,1)S(1)}, f32[64,640]{1,0:T(8,128)}) custom-call(s32[1]{0:T(128)} %bitcast.cell_ref.where_ref, s32[2,512]{1,0:T(2,128)S(1)} %bitcast.19, f32[24,2048]{1,0:T(8,128)S(1)} %copy-done.1), custom_call_target="tpu_custom_call" | custom-call | tf_op jit(solution)/shard_map/design/pallas_call | solution.py:80
  5.9 7.3 %all-to-all-start = ((f32[8,8,640]{2,1,0:T(8,128)}), f32[8,8,640]{2,1,0:T(8,128)S(1)}, u32[]{:S(2)}, u32[]{:S(2)}) async-start(f32[8,8,640]{2,1,0:T(8,128)} %bitcast.3), calls=%async_computation | async-start | bytes 327680 | tf_op jit(solution)/shard_map/all_to_all | solution.py:355
  13.2 1.2 %copy-done = bf16[2048,256]{1,0:T(8,128)(2,1)S(1)} copy-done((bf16[2048,256]{1,0:T(8,128)(2,1)S(1)}, bf16[2048,256]{1,0:T(8,128)(2,1)}, u32[]{:S(2)}) %copy-start) | copy-done | bytes 1048600
  15.2 5.6 %all-to-all-done = f32[8,8,640]{2,1,0:T(8,128)S(1)} async-done(((f32[8,8,640]{2,1,0:T(8,128)}), f32[8,8,640]{2,1,0:T(8,128)S(1)}, u32[]{:S(2)}, u32[]{:S(2)}) %all-to-all-start) | async-done | bytes 163872 | tf_op jit(solution)/shard_map/all_to_all | solution.py:355
  21.5 3.6 %all-to-all-start.1 = ((f32[8,8,640]{2,1,0:T(8,128)}), f32[8,8,640]{2,1,0:T(8,128)S(1)}, u32[]{:S(2)}, u32[]{:S(2)}) async-start(f32[8,8,640]{2,1,0:T(8,128)} %broadcast_in_dim.2), calls=%async_computation.1 | async-start | bytes 327680 | tf_op jit(solution)/shard_map/all_to_all | solution.py:355
  25.0 1.7 %collective-permute-start = (f32[256,256]{1,0:T(8,128)S(1)}, f32[256,256]{1,0:T(8,128)S(1)}, u32[]{:S(2)}, u32[]{:S(2)}) collective-permute-start(f32[256,256]{1,0:T(8,128)S(1)} %get-tuple-element.37), channel_id=1, source_target_pairs={{0,4},{4,0},{8,12},{12,8},{16,20},{20,16},{24,28},{28,24},{1,5},{5... | collective-permute-start | bytes 786440 | tf_op jit(solution)/shard_map/ppermute | solution.py:341
  26.8 6.9 %collective-permute-done = f32[256,256]{1,0:T(8,128)S(1)} collective-permute-done((f32[256,256]{1,0:T(8,128)S(1)}, f32[256,256]{1,0:T(8,128)S(1)}, u32[]{:S(2)}, u32[]{:S(2)}) %collective-permute-start) | collective-permute-done | bytes 262176 | tf_op jit(solution)/shard_map/ppermute | solution.py:341
  33.8 1.5 %collective-permute-start.1 = (f32[64,640]{1,0:T(8,128)S(1)}, f32[64,640]{1,0:T(8,128)S(1)}, u32[]{:S(2)}, u32[]{:S(2)}) collective-permute-start(f32[64,640]{1,0:T(8,128)S(1)} %bitcast.16), channel_id=1, source_target_pairs={{0,2},{1,3},{2,0},{3,1},{4,6},{5,7},{6,4},{7,5},{8,10},{9,11},{10,... | collective-permute-start | bytes 491528 | tf_op jit(solution)/shard_map/ppermute | solution.py:341
  35.3 1.5 %collective-permute-start.4 = (f32[128,256]{1,0:T(8,128)S(1)}, f32[128,256]{1,0:T(8,128)S(1)}, u32[]{:S(2)}, u32[]{:S(2)}) collective-permute-start(f32[128,256]{1,0:T(8,128)S(1)} %dynamic-slice_bitcast_fusion), channel_id=1, source_target_pairs={{0,8},{4,12},{8,0},{12,4},{16,24},{20,28},{24,16},{28,20},{1,9},{5... | collective-permute-start | bytes 393224 | tf_op jit(solution)/shard_map/ppermute | solution.py:341
  36.9 2.3 %collective-permute-done.1.refs_2_ = f32[64,640]{1,0:T(8,128)S(1)} collective-permute-done((f32[64,640]{1,0:T(8,128)S(1)}, f32[64,640]{1,0:T(8,128)S(1)}, u32[]{:S(2)}, u32[]{:S(2)}) %collective-permute-start.1) | collective-permute-done | bytes 163872 | tf_op jit(solution)/shard_map/ppermute | solution.py:341
  39.2 1.2 %collective-permute-done.4 = f32[128,256]{1,0:T(8,128)S(1)} collective-permute-done((f32[128,256]{1,0:T(8,128)S(1)}, f32[128,256]{1,0:T(8,128)S(1)}, u32[]{:S(2)}, u32[]{:S(2)}) %collective-permute-start.4) | collective-permute-done | bytes 131104 | tf_op jit(solution)/shard_map/ppermute | solution.py:341
  40.6 2.4 %collective-permute-start.5 = (f32[64,256]{1,0:T(8,128)S(1)}, f32[64,256]{1,0:T(8,128)S(1)}, u32[]{:S(2)}, u32[]{:S(2)}) collective-permute-start(f32[64,256]{1,0:T(8,128)S(1)} %dynamic-slice_bitcast_fusion.1), channel_id=1, source_target_pairs={{0,16},{4,20},{8,24},{12,28},{16,0},{20,4},{24,8},{28,12},{1,17},{... | collective-permute-start | bytes 196616 | tf_op jit(solution)/shard_map/ppermute | solution.py:341
  42.9 4.4 %block_0.1 = (f32[512,512]{1,0:T(8,128)S(1)}, f32[512,1]{1,0:T(8,128)S(1)}) custom-call(s32[1]{0:T(128)} %bitcast.cell_ref.where_ref, f32[64,640]{1,0:T(8,128)S(1)} %bitcast.18, f32[64,640]{1,0:T(8,128)S(1)} %collective-permute-done.2.refs_1_, f32[64,640]{1,0:T(8,128)S(1)} %collective-permute-done.1.refs_2_, f32[64,640]{1,0:T(8,128)S(1)} %collective-permute-done.3.refs_3_), custom_call_target="tpu_custom_call" | custom-call | flops 1000000000 | bytes 1048576 | tf_op jit(solution)/shard_map/block_0/pallas_call | solution.py:234
  48.2 3.9 %block_1.1.in_ref = f32[512,512]{1,0:T(8,128)S(1)} custom-call(f32[512,512]{1,0:T(8,128)S(1)} %get-tuple-element.46.in_ref), custom_call_target="tpu_custom_call" | custom-call | flops 1000000000 | bytes 1048576 | tf_op jit(solution)/shard_map/block_1/pallas_call | solution.py:250
  52.1 1.7 %collective-permute-done.6 = f32[64,256]{1,0:T(8,128)S(1)} collective-permute-done((f32[64,256]{1,0:T(8,128)S(1)}, f32[64,256]{1,0:T(8,128)S(1)}, u32[]{:S(2)}, u32[]{:S(2)}) %collective-permute-start.6) | collective-permute-done | bytes 65568 | tf_op jit(solution)/shard_map/ppermute | solution.py:341
  53.8 1.1 %collective-permute-start.7 = (f32[128,256]{1,0:T(8,128)S(1)}, f32[128,256]{1,0:T(8,128)S(1)}, u32[]{:S(2)}, u32[]{:S(2)}) collective-permute-start(f32[128,256]{1,0:T(8,128)S(1)} %pad_maximum_fusion.refs_0_), channel_id=1, source_target_pairs={{0,8},{4,12},{8,0},{12,4},{16,24},{20,28},{24,16},{28,20},{1,9},{5... | collective-permute-start | bytes 393224 | tf_op jit(solution)/shard_map/ppermute | solution.py:341
  55.7 3.9 %block_2.1.in_ref = f32[512,512]{1,0:T(8,128)S(1)} custom-call(f32[512,512]{1,0:T(8,128)S(1)} %block_1.1.in_ref), custom_call_target="tpu_custom_call" | custom-call | flops 1000000000 | bytes 1048576 | tf_op jit(solution)/shard_map/block_2/pallas_call | solution.py:250
  59.9 1.1 %collective-permute-start.9 = (f32[128,256]{1,0:T(8,128)S(1)}, f32[128,256]{1,0:T(8,128)S(1)}, u32[]{:S(2)}, u32[]{:S(2)}) collective-permute-start(f32[128,256]{1,0:T(8,128)S(1)} %collective-permute-done.7.refs_1_), channel_id=1, source_target_pairs={{0,4},{4,0},{8,12},{12,8},{16,20},{20,16},{24,28},{28,24},{1,5},{5... | collective-permute-start | bytes 393224 | tf_op jit(solution)/shard_map/ppermute | solution.py:341
  61.0 3.9 %block_3.1.inverse_ref = f32[512,512]{1,0:T(8,128)S(1)} custom-call(f32[512,512]{1,0:T(8,128)S(1)} %block_2.1.in_ref), custom_call_target="tpu_custom_call" | custom-call | flops 1000000000 | bytes 1048576 | tf_op jit(solution)/shard_map/block_3/pallas_call | solution.py:250
  65.0 1.5 %solve_far.1 = (f32[128,256]{1,0:T(8,128)S(1)}, f32[128,256]{1,0:T(8,128)S(1)}, f32[128,256]{1,0:T(8,128)S(1)}) custom-call(s32[2]{0:T(128)S(1)} %pad_add_fusion.where_ref, s32[8]{0:T(128)S(1)} %copy-done.3, f32[512,512]{1,0:T(8,128)S(1)} %block_3.1.inverse_ref, f32[512,1]{1,0:T(8,128)S(1)} %get-tuple-element.51.scale_ref, ...), custom_call_target="tpu_custom_call" | custom-call | flops 1000000000 | bytes 1048576 | tf_op jit(solution)/shard_map/solve_far/pallas_call | solution.py:308
  66.6 1.6 %collective-permute-start.11 = (f32[128,256]{1,0:T(8,128)S(1)}, f32[128,256]{1,0:T(8,128)S(1)}, u32[]{:S(2)}, u32[]{:S(2)}) collective-permute-start(f32[128,256]{1,0:T(8,128)S(1)} %get-tuple-element.56.refs_5_), channel_id=1, source_target_pairs={{0,2},{1,3},{2,0},{3,1},{4,6},{5,7},{6,4},{7,5},{8,10},{9,11},{10,... | collective-permute-start | bytes 393224 | tf_op jit(solution)/shard_map/ppermute | solution.py:341
  68.4 1.8 %solve_near.1 = (f32[128,256]{1,0:T(8,128)S(1)}, f32[8,256]{1,0:T(8,128)}) custom-call(s32[2]{0:T(128)S(1)} %pad_add_fusion.where_ref, s32[8]{0:T(128)S(1)} %copy-done.3, f32[512,512]{1,0:T(8,128)S(1)} %block_3.1.inverse_ref, f32[512,1]{1,0:T(8,128)S(1)} %get-tuple-element.51.scale_ref, f32[128,256]{1,0:T(8,128)S(1)} %pad_maximum_fusion.refs_0_, ...), custom_call_target="tpu_custom_call" | custom-call | flops 5000000000 | bytes 1048576 | tf_op jit(solution)/shard_map/solve_near/pallas_call | solution.py:308
  70.2 2.7 %collective-permute-done.11.refs_2_ = f32[128,256]{1,0:T(8,128)S(1)} collective-permute-done((f32[128,256]{1,0:T(8,128)S(1)}, f32[128,256]{1,0:T(8,128)S(1)}, u32[]{:S(2)}, u32[]{:S(2)}) %collective-permute-start.11) | collective-permute-done | bytes 131104 | tf_op jit(solution)/shard_map/ppermute | solution.py:341
  72.9 1.9 %collective-permute-done.12.refs_3_ = f32[128,256]{1,0:T(8,128)S(1)} collective-permute-done((f32[128,256]{1,0:T(8,128)S(1)}, f32[128,256]{1,0:T(8,128)S(1)}, u32[]{:S(2)}, u32[]{:S(2)}) %collective-permute-start.12) | collective-permute-done | bytes 131104 | tf_op jit(solution)/shard_map/ppermute | solution.py:341
  (32 shorter events, 6.4 us)
Async XLA Ops:
  0.6 0.9 %copy-start.1 = (f32[24,2048]{1,0:T(8,128)S(1)}, f32[24,2048]{1,0:T(8,128)}, u32[]{:S(2)}) copy-start(f32[24,2048]{1,0:T(8,128)} %points_ref.1) | copy-start | bytes 589828
  1.6 0.7 copy-start.2
  5.9 14.8 %all-to-all-start = ((f32[8,8,640]{2,1,0:T(8,128)}), f32[8,8,640]{2,1,0:T(8,128)S(1)}, u32[]{:S(2)}, u32[]{:S(2)}) async-start(f32[8,8,640]{2,1,0:T(8,128)} %bitcast.3), calls=%async_computation | async-start | bytes 327680 | tf_op jit(solution)/shard_map/all_to_all | solution.py:355
  13.2 1.2 %copy-start = (bf16[2048,256]{1,0:T(8,128)(2,1)S(1)}, bf16[2048,256]{1,0:T(8,128)(2,1)}, u32[]{:S(2)}) copy-start(bf16[2048,256]{1,0:T(8,128)(2,1)} %yields_ref.1) | copy-start | bytes 3145732
  21.5 12.3 %all-to-all-start.1 = ((f32[8,8,640]{2,1,0:T(8,128)}), f32[8,8,640]{2,1,0:T(8,128)S(1)}, u32[]{:S(2)}, u32[]{:S(2)}) async-start(f32[8,8,640]{2,1,0:T(8,128)} %broadcast_in_dim.2), calls=%async_computation.1 | async-start | bytes 327680 | tf_op jit(solution)/shard_map/all_to_all | solution.py:355
  25.0 8.7 %collective-permute-start = (f32[256,256]{1,0:T(8,128)S(1)}, f32[256,256]{1,0:T(8,128)S(1)}, u32[]{:S(2)}, u32[]{:S(2)}) collective-permute-start(f32[256,256]{1,0:T(8,128)S(1)} %get-tuple-element.37), channel_id=1, source_target_pairs={{0,4},{4,0},{8,12},{12,8},{16,20},{20,16},{24,28},{28,24},{1,5},{5... | collective-permute-start | bytes 786440 | tf_op jit(solution)/shard_map/ppermute | solution.py:341
  33.8 5.4 %collective-permute-start.1 = (f32[64,640]{1,0:T(8,128)S(1)}, f32[64,640]{1,0:T(8,128)S(1)}, u32[]{:S(2)}, u32[]{:S(2)}) collective-permute-start(f32[64,640]{1,0:T(8,128)S(1)} %bitcast.16), channel_id=1, source_target_pairs={{0,2},{1,3},{2,0},{3,1},{4,6},{5,7},{6,4},{7,5},{8,10},{9,11},{10,... | collective-permute-start | bytes 491528 | tf_op jit(solution)/shard_map/ppermute | solution.py:341
  35.3 5.0 %collective-permute-start.4 = (f32[128,256]{1,0:T(8,128)S(1)}, f32[128,256]{1,0:T(8,128)S(1)}, u32[]{:S(2)}, u32[]{:S(2)}) collective-permute-start(f32[128,256]{1,0:T(8,128)S(1)} %dynamic-slice_bitcast_fusion), channel_id=1, source_target_pairs={{0,8},{4,12},{8,0},{12,4},{16,24},{20,28},{24,16},{28,20},{1,9},{5... | collective-permute-start | bytes 393224 | tf_op jit(solution)/shard_map/ppermute | solution.py:341
  36.9 3.5 %collective-permute-start.2 = (f32[64,640]{1,0:T(8,128)S(1)}, f32[64,640]{1,0:T(8,128)S(1)}, u32[]{:S(2)}, u32[]{:S(2)}) collective-permute-start(f32[64,640]{1,0:T(8,128)S(1)} %bitcast.17), channel_id=1, source_target_pairs={{0,1},{1,0},{2,3},{3,2},{4,5},{5,4},{6,7},{7,6},{8,9},{9,8},{10,11... | collective-permute-start | bytes 491528 | tf_op jit(solution)/shard_map/ppermute | solution.py:341
  39.2 1.4 %collective-permute-start.3 = (f32[64,640]{1,0:T(8,128)S(1)}, f32[64,640]{1,0:T(8,128)S(1)}, u32[]{:S(2)}, u32[]{:S(2)}) collective-permute-start(f32[64,640]{1,0:T(8,128)S(1)} %collective-permute-done.1.refs_2_), channel_id=1, source_target_pairs={{0,1},{1,0},{2,3},{3,2},{4,5},{5,4},{6,7},{7,6},{8,9},{9,8},{10,11... | collective-permute-start | bytes 491528 | tf_op jit(solution)/shard_map/ppermute | solution.py:341
  40.6 6.7 %collective-permute-start.5 = (f32[64,256]{1,0:T(8,128)S(1)}, f32[64,256]{1,0:T(8,128)S(1)}, u32[]{:S(2)}, u32[]{:S(2)}) collective-permute-start(f32[64,256]{1,0:T(8,128)S(1)} %dynamic-slice_bitcast_fusion.1), channel_id=1, source_target_pairs={{0,16},{4,20},{8,24},{12,28},{16,0},{20,4},{24,8},{28,12},{1,17},{... | collective-permute-start | bytes 196616 | tf_op jit(solution)/shard_map/ppermute | solution.py:341
  47.3 6.4 %collective-permute-start.6 = (f32[64,256]{1,0:T(8,128)S(1)}, f32[64,256]{1,0:T(8,128)S(1)}, u32[]{:S(2)}, u32[]{:S(2)}) collective-permute-start(f32[64,256]{1,0:T(8,128)S(1)} %bitcast_add_fusion.1), channel_id=1, source_target_pairs={{0,16},{4,20},{8,24},{12,28},{16,0},{20,4},{24,8},{28,12},{1,17},{... | collective-permute-start | bytes 196616 | tf_op jit(solution)/shard_map/ppermute | solution.py:341
  53.8 5.9 %collective-permute-start.7 = (f32[128,256]{1,0:T(8,128)S(1)}, f32[128,256]{1,0:T(8,128)S(1)}, u32[]{:S(2)}, u32[]{:S(2)}) collective-permute-start(f32[128,256]{1,0:T(8,128)S(1)} %pad_maximum_fusion.refs_0_), channel_id=1, source_target_pairs={{0,8},{4,12},{8,0},{12,4},{16,24},{20,28},{24,16},{28,20},{1,9},{5... | collective-permute-start | bytes 393224 | tf_op jit(solution)/shard_map/ppermute | solution.py:341
  54.9 5.0 %collective-permute-start.8 = (f32[128,256]{1,0:T(8,128)S(1)}, f32[128,256]{1,0:T(8,128)S(1)}, u32[]{:S(2)}, u32[]{:S(2)}) collective-permute-start(f32[128,256]{1,0:T(8,128)S(1)} %pad_maximum_fusion.refs_0_), channel_id=1, source_target_pairs={{0,4},{4,0},{8,12},{12,8},{16,20},{20,16},{24,28},{28,24},{1,5},{5... | collective-permute-start | bytes 393224 | tf_op jit(solution)/shard_map/ppermute | solution.py:341
  59.7 5.3 %copy-start.3 = (s32[8]{0:T(128)S(1)}, s32[8]{0:T(128)}, u32[]{:S(2)}) copy-start(s32[8]{0:T(128)} %group_ref.3) | copy-start | bytes 100
  59.9 5.1 %collective-permute-start.9 = (f32[128,256]{1,0:T(8,128)S(1)}, f32[128,256]{1,0:T(8,128)S(1)}, u32[]{:S(2)}, u32[]{:S(2)}) collective-permute-start(f32[128,256]{1,0:T(8,128)S(1)} %collective-permute-done.7.refs_1_), channel_id=1, source_target_pairs={{0,4},{4,0},{8,12},{12,8},{16,20},{20,16},{24,28},{28,24},{1,5},{5... | collective-permute-start | bytes 393224 | tf_op jit(solution)/shard_map/ppermute | solution.py:341
  66.5 3.7 %collective-permute-start.10 = (f32[128,256]{1,0:T(8,128)S(1)}, f32[128,256]{1,0:T(8,128)S(1)}, u32[]{:S(2)}, u32[]{:S(2)}) collective-permute-start(f32[128,256]{1,0:T(8,128)S(1)} %get-tuple-element.55.refs_4_), channel_id=1, source_target_pairs={{0,1},{1,0},{2,3},{3,2},{4,5},{5,4},{6,7},{7,6},{8,9},{9,8},{10,11... | collective-permute-start | bytes 393224 | tf_op jit(solution)/shard_map/ppermute | solution.py:341
  66.6 6.4 %collective-permute-start.11 = (f32[128,256]{1,0:T(8,128)S(1)}, f32[128,256]{1,0:T(8,128)S(1)}, u32[]{:S(2)}, u32[]{:S(2)}) collective-permute-start(f32[128,256]{1,0:T(8,128)S(1)} %get-tuple-element.56.refs_5_), channel_id=1, source_target_pairs={{0,2},{1,3},{2,0},{3,1},{4,6},{5,7},{6,4},{7,5},{8,10},{9,11},{10,... | collective-permute-start | bytes 393224 | tf_op jit(solution)/shard_map/ppermute | solution.py:341
  68.1 6.7 %collective-permute-start.12 = (f32[128,256]{1,0:T(8,128)S(1)}, f32[128,256]{1,0:T(8,128)S(1)}, u32[]{:S(2)}, u32[]{:S(2)}) collective-permute-start(f32[128,256]{1,0:T(8,128)S(1)} %get-tuple-element.57.refs_6_), channel_id=1, source_target_pairs={{0,3},{1,2},{2,1},{3,0},{4,7},{5,6},{6,5},{7,4},{8,11},{9,10},{10,... | collective-permute-start | bytes 393224 | tf_op jit(solution)/shard_map/ppermute | solution.py:341

commit v6 on v5

--- a/solution.py
+++ b/solution.py
@@ -189,17 +189,21 @@
 
 
 def first_kernel(where_ref, *refs):
-    out_ref, scale_ref, gram_ref = refs[-3:]
+    out_ref, scale_ref, gram_ref, fold_ref = refs[-4:]
     terms = out_ref.shape[0]
     blocks = terms // TILE
-    for step, ref in enumerate(refs[:-3]):
+    for step, ref in enumerate(refs[:-4]):
         piece = ref.shape[0] // 2
-        start = pl.multiple_of((where_ref[0] ^ step) * piece, piece)
+        eighth = ref.shape[0] // 8
+        for at in range(8):
+            row = pl.multiple_of((where_ref[0] ^ at) * eighth, eighth)
+            fold_ref[pl.ds(row, eighth), :] = ref[at * eighth:(at + 1) * eighth, :]
+        start = pl.multiple_of((where_ref[1] ^ step) * piece, piece)
         for block in range(blocks):
             half, lane = fold_place(block, blocks)
             reach = (block + 1) * TILE
             gram_ref[pl.ds(start + block * TILE, piece), 0:reach] = (
-                ref[half * piece:(half + 1) * piece, lane:lane + reach]
+                fold_ref[half * piece:(half + 1) * piece, lane:lane + reach]
             )
     diagonal = lax.broadcasted_iota(jnp.int32, (TILE, TILE), 0) == lax.broadcasted_iota(jnp.int32, (TILE, TILE), 1)
     bands = [slice(block * TILE, (block + 1) * TILE) for block in range(blocks)]
@@ -239,7 +243,7 @@
         ),
         in_specs=[SMEM] + [VMEM] * len(pieces),
         out_specs=(VMEM, VMEM),
-        scratch_shapes=[pltpu.VMEM((terms, terms), jnp.float32)],
+        scratch_shapes=[pltpu.VMEM((terms, terms), jnp.float32), pltpu.VMEM(pieces[0].shape, jnp.float32)],
         compiler_params=BIG,
         cost_estimate=STEP_COST,
         name="block_0",
@@ -351,12 +355,16 @@
     return pick(halves, mine) + swap(pick(halves, mine ^ 1), "samp", 1 << bit)
 
 
-def exchange(pieces):
-    return lax.all_to_all(pieces, "samp", split_axis=0, concat_axis=0)
-
-
-def spread(piece):
-    return jnp.broadcast_to(piece[None], (lax.axis_size("samp"),) + piece.shape)
+def join(values, step):
+    return jnp.concatenate([values, swap(values, "samp", step)], axis=0)
+
+
+def add_rest(values):
+    step = 8
+    while step < lax.axis_size("samp"):
+        values = values + swap(values, "samp", step)
+        step *= 2
+    return values
 
 
 def on_device(points, yields, term_index, block_group):
@@ -365,41 +373,36 @@
     me, cell = lax.axis_index("samp"), lax.axis_index("cell")
     blocks = term_index.shape[0] // TILE
     psi, fold = design(points, term_index, cell, n_cell)
-    pieces = fold.reshape((n_samp, 8, -1) if fold.shape[0] % (8 * n_samp) else (n_samp, -1, fold.shape[1]))
-    came = exchange(pieces)
+    spot = ((me & 1) << 2) | (me & 2) | ((me >> 2) & 1)
+    fold = halve(fold, me, 0)
     kept, sent = cross_halves(psi, yields, me & 1)
-    came, kept, sent = lax.optimization_barrier((came, kept, sent))
-    half = kept + swap(sent, "samp", 1)
-    fold = exchange(spread(jnp.sum(came, axis=0))).reshape(fold.shape)
-    fold, half = lax.optimization_barrier((fold, half))
-    part = halve(half, me, 1)
+    fold, kept, sent = lax.optimization_barrier((fold, kept, sent))
+    part = kept + swap(sent, "samp", 1)
+    fold = add_rest(halve(halve(fold, me, 1), me, 2))
+    fold, part = lax.optimization_barrier((fold, part))
+    part = halve(part, me, 1)
+    fold = join(join(fold, 4), 2)
+    fold, part = lax.optimization_barrier((fold, part))
+    part = add_rest(halve(part, me, 2))
+    rows = part.shape[0]
+    fold = join(fold, 1)
+    fold, part = lax.optimization_barrier((fold, part))
+    pair = join(part, 4)
     held, order = [fold], [0]
     step = n_cell // 2
     while step:
         held = held + [swap(value, "cell", step) for value in held]
         order = order + [value ^ step for value in order]
         step //= 2
-    held, part = lax.optimization_barrier((held, part))
-    gram, scale = first_block(cell.reshape(1), [held[order.index(at)] for at in range(n_cell)], term_index.shape[0])
-    part = halve(part, me, 2)
-    bit = 8
-    while bit < n_samp:
-        part = part + swap(part, "samp", bit)
-        bit *= 2
-    rows = part.shape[0]
+    held, pair = lax.optimization_barrier((held, pair))
+    where = jnp.stack([spot, cell])
+    gram, scale = first_block(where, [held[order.index(at)] for at in range(n_cell)], term_index.shape[0])
+    pieces = [pair, swap(pair, "samp", 2), swap(pair, "samp", 1)]
     for block in range(1, blocks):
         if block == 1:
-            gram, part = lax.optimization_barrier((gram, part))
-            pair = jnp.concatenate([part, swap(part, "samp", 4)], axis=0)
-        elif block == 2:
-            gram, pair = lax.optimization_barrier((gram, pair))
-            pieces = [pair, swap(pair, "samp", 2), swap(pair, "samp", 1)]
-        elif block == 3:
             gram, pieces = lax.optimization_barrier((gram, pieces))
             pieces = pieces + [swap(pieces[1], "samp", 1)]
         gram = next_block(gram, block)
-    spot = ((me & 1) << 2) | (me & 2) | ((me >> 2) & 1)
-    where = jnp.stack([spot, cell])
     given = (where, gram, scale, pieces, rows, block_group, points.shape[1] * n_samp, n_cell)
     far = list(solve(*given, tuple(range(1, n_cell))))
     came = [swap(value, "cell", 1 + at) for at, value in enumerate(far)]

time: 76.1 us -> 76.9 us (1.011)
  starting transfers between devices: 23.8 us -> 25.7 us
    ppermute x13 -> x19, starting transfers between devices: 13 us -> 25.7 us  [swap(): return lax.ppermute(values, axis, [(at, at ^ step) for at in range(size)])]
    all_to_all x2 -> x0, starting transfers between devices: 10.8 us -> none  [exchange(): return lax.all_to_all(pieces, 'samp', split_axis=0, concat_axis=0)]
    all_to_all x2 -> x0, waiting for transfers between devices: 5.63 us -> none  [exchange(): return lax.all_to_all(pieces, 'samp', split_axis=0, concat_axis=0)]
    ppermute x13 -> x19, waiting for transfers between devices: 17.1 us -> 22.3 us  [swap(): return lax.ppermute(values, axis, [(at, at ^ step) for at in range(size)])]
  transfers between devices with their start and end apart: 15 -> 19, of which waited for: 9 -> 11; matrix products, arithmetic and copies ran while one was open for 0% -> 0% of each run, Pallas kernels for 25% -> 20%
where the time goes in v6:
time: 76.9 us; the launch traced here: 76.6 us
  starting transfers between devices  25.7 us (33%)
  Pallas kernels  24.7 us (32%)
  waiting for transfers between devices  22.3 us (29%)
  local copies, waits for them, and re-layouts  2.91 us (4%)
  between operations  0.86 us (1%)
    ppermute x19, starting transfers between devices, swap(): return lax.ppermute(values, axis, [(at, at ^ step) for at in range(size)])  25.7 us
    ppermute x19, waiting for transfers between devices, swap(): return lax.ppermute(values, axis, [(at, at ^ step) for at in range(size)])  22.3 us
    pallas_call x3, Pallas kernels, next_block(): pl.pallas_call(functools.partial(next_kernel, block), out_shape=jax.Shape...  11.9 us
    pallas_call x1, Pallas kernels, first_block(): pl.pallas_call(first_kernel, out_shape=(jax.ShapeDtypeStruct((terms, term...  4.98 us
    pallas_call x2, Pallas kernels, solve(): pl.pallas_call(functools.partial(solve_kernel, samples, steps, rows, fini...  3.3 us
    pallas_call x1, Pallas kernels, design(): pl.pallas_call(functools.partial(design_kernel, 512), out_shape=(jax.Shap...  2.97 us
    unnamed x8, local copies, waits for them, and re-layouts  2.84 us
  transfers between devices with their start and end apart: 19, of which 11 were waited for; matrix products, arithmetic and copies ran while one was open for 0% of the time, Pallas kernels for 20%

profile of v6, /device:TPU:0, one launch (start us, length us, event | category | flops | bytes accessed | tf_op | source)
XLA Modules:
  0.0 76.6 jit_solution(18172537698068498523)
XLA Ops:
  2.3 3.0 %design.1 = (bf16[512,2048]{1,0:T(8,128)(2,1)S(1)}, f32[64,640]{1,0:T(8,128)S(1)}) custom-call(s32[1]{0:T(128)} %bitcast.cell_ref.where_ref, s32[2,512]{1,0:T(2,128)S(1)} %bitcast.34, f32[24,2048]{1,0:T(8,128)S(1)} %copy-done.1), custom_call_target="tpu_custom_call" | custom-call | tf_op jit(solution)/shard_map/design/pallas_call | solution.py:80
  5.3 3.0 %collective-permute-start = (f32[32,640]{1,0:T(8,128)S(1)}, f32[32,640]{1,0:T(8,128)S(1)}, u32[]{:S(2)}, u32[]{:S(2)}) collective-permute-start(f32[32,640]{1,0:T(8,128)S(1)} %dynamic-slice_bitcast_fusion.1), channel_id=1, source_target_pairs={{0,4},{4,0},{8,12},{12,8},{16,20},{20,16},{24,28},{28,24},{1,5},{5... | collective-permute-start | bytes 245768 | tf_op jit(solution)/shard_map/ppermute | solution.py:345
  10.8 2.1 %collective-permute-start.1 = (f32[16,640]{1,0:T(8,128)S(1)}, f32[16,640]{1,0:T(8,128)S(1)}, u32[]{:S(2)}, u32[]{:S(2)}) collective-permute-start(f32[16,640]{1,0:T(8,128)S(1)} %dynamic-slice_bitcast_fusion.3), channel_id=1, source_target_pairs={{0,8},{4,12},{8,0},{12,4},{16,24},{20,28},{24,16},{28,20},{1,9},{5... | collective-permute-start | bytes 122888 | tf_op jit(solution)/shard_map/ppermute | solution.py:345
  12.9 1.5 %collective-permute-start.3 = (f32[256,256]{1,0:T(8,128)S(1)}, f32[256,256]{1,0:T(8,128)S(1)}, u32[]{:S(2)}, u32[]{:S(2)}) collective-permute-start(f32[256,256]{1,0:T(8,128)S(1)} %get-tuple-element.37), channel_id=1, source_target_pairs={{0,4},{4,0},{8,12},{12,8},{16,20},{20,16},{24,28},{28,24},{1,5},{5... | collective-permute-start | bytes 786440 | tf_op jit(solution)/shard_map/ppermute | solution.py:345
  14.9 3.1 %collective-permute-start.2 = (f32[8,640]{1,0:T(8,128)S(1)}, f32[8,640]{1,0:T(8,128)S(1)}, u32[]{:S(2)}, u32[]{:S(2)}) collective-permute-start(f32[8,640]{1,0:T(8,128)S(1)} %dynamic-slice_bitcast_fusion.4), channel_id=1, source_target_pairs={{0,16},{4,20},{8,24},{12,28},{16,0},{20,4},{24,8},{28,12},{1,17},{... | collective-permute-start | bytes 61448 | tf_op jit(solution)/shard_map/ppermute | solution.py:345
  18.0 1.8 %collective-permute-done.2 = f32[8,640]{1,0:T(8,128)S(1)} collective-permute-done((f32[8,640]{1,0:T(8,128)S(1)}, f32[8,640]{1,0:T(8,128)S(1)}, u32[]{:S(2)}, u32[]{:S(2)}) %collective-permute-start.2) | collective-permute-done | bytes 20512 | tf_op jit(solution)/shard_map/ppermute | solution.py:345
  19.8 3.0 %collective-permute-start.4 = (f32[8,640]{1,0:T(8,128)S(1)}, f32[8,640]{1,0:T(8,128)S(1)}, u32[]{:S(2)}, u32[]{:S(2)}) collective-permute-start(f32[8,640]{1,0:T(8,128)S(1)} %bitcast_add_fusion.4), channel_id=1, source_target_pairs={{0,16},{4,20},{8,24},{12,28},{16,0},{20,4},{24,8},{28,12},{1,17},{... | collective-permute-start | bytes 61448 | tf_op jit(solution)/shard_map/ppermute | solution.py:345
  22.8 1.9 %collective-permute-done.4 = f32[8,640]{1,0:T(8,128)S(1)} collective-permute-done((f32[8,640]{1,0:T(8,128)S(1)}, f32[8,640]{1,0:T(8,128)S(1)}, u32[]{:S(2)}, u32[]{:S(2)}) %collective-permute-start.4) | collective-permute-done | bytes 20512 | tf_op jit(solution)/shard_map/ppermute | solution.py:345
  24.7 1.8 %collective-permute-start.5 = (f32[16,640]{1,0:T(8,128)S(1)}, f32[16,640]{1,0:T(8,128)S(1)}, u32[]{:S(2)}, u32[]{:S(2)}) collective-permute-start(f32[16,640]{1,0:T(8,128)S(1)} %pad_maximum_fusion.3), channel_id=1, source_target_pairs={{0,8},{4,12},{8,0},{12,4},{16,24},{20,28},{24,16},{28,20},{1,9},{5... | collective-permute-start | bytes 122888 | tf_op jit(solution)/shard_map/ppermute | solution.py:345
  26.8 1.9 %collective-permute-done.5 = f32[16,640]{1,0:T(8,128)S(1)} collective-permute-done((f32[16,640]{1,0:T(8,128)S(1)}, f32[16,640]{1,0:T(8,128)S(1)}, u32[]{:S(2)}, u32[]{:S(2)}) %collective-permute-start.5) | collective-permute-done | bytes 40992 | tf_op jit(solution)/shard_map/ppermute | solution.py:345
  28.7 3.0 %collective-permute-done.6 = f32[128,256]{1,0:T(8,128)S(1)} collective-permute-done((f32[128,256]{1,0:T(8,128)S(1)}, f32[128,256]{1,0:T(8,128)S(1)}, u32[]{:S(2)}, u32[]{:S(2)}) %collective-permute-start.6) | collective-permute-done | bytes 131104 | tf_op jit(solution)/shard_map/ppermute | solution.py:345
  31.8 2.7 %collective-permute-start.8 = (f32[64,256]{1,0:T(8,128)S(1)}, f32[64,256]{1,0:T(8,128)S(1)}, u32[]{:S(2)}, u32[]{:S(2)}) collective-permute-start(f32[64,256]{1,0:T(8,128)S(1)} %dynamic-slice_bitcast_fusion.2), channel_id=1, source_target_pairs={{0,16},{4,20},{8,24},{12,28},{16,0},{20,4},{24,8},{28,12},{1,17},{... | collective-permute-start | bytes 196616 | tf_op jit(solution)/shard_map/ppermute | solution.py:345
  34.4 1.5 %collective-permute-start.7 = (f32[32,640]{1,0:T(8,128)S(1)}, f32[32,640]{1,0:T(8,128)S(1)}, u32[]{:S(2)}, u32[]{:S(2)}) collective-permute-start(f32[32,640]{1,0:T(8,128)S(1)} %pad_maximum_fusion.2), channel_id=1, source_target_pairs={{0,4},{4,0},{8,12},{12,8},{16,20},{20,16},{24,28},{28,24},{1,5},{5... | collective-permute-start | bytes 245768 | tf_op jit(solution)/shard_map/ppermute | solution.py:345
  35.9 3.1 %collective-permute-done.8 = f32[64,256]{1,0:T(8,128)S(1)} collective-permute-done((f32[64,256]{1,0:T(8,128)S(1)}, f32[64,256]{1,0:T(8,128)S(1)}, u32[]{:S(2)}, u32[]{:S(2)}) %collective-permute-start.8) | collective-permute-done | bytes 65568 | tf_op jit(solution)/shard_map/ppermute | solution.py:345
  41.3 3.2 %collective-permute-done.9.refs_2_ = f32[64,640]{1,0:T(8,128)S(1)} collective-permute-done((f32[64,640]{1,0:T(8,128)S(1)}, f32[64,640]{1,0:T(8,128)S(1)}, u32[]{:S(2)}, u32[]{:S(2)}) %collective-permute-start.9) | collective-permute-done | bytes 163872 | tf_op jit(solution)/shard_map/ppermute | solution.py:345
  44.5 1.8 %collective-permute-done.12 = f32[64,256]{1,0:T(8,128)S(1)} collective-permute-done((f32[64,256]{1,0:T(8,128)S(1)}, f32[64,256]{1,0:T(8,128)S(1)}, u32[]{:S(2)}, u32[]{:S(2)}) %collective-permute-start.12) | collective-permute-done | bytes 65568 | tf_op jit(solution)/shard_map/ppermute | solution.py:345
  46.3 1.6 %collective-permute-start.14 = (f32[128,256]{1,0:T(8,128)S(1)}, f32[128,256]{1,0:T(8,128)S(1)}, u32[]{:S(2)}, u32[]{:S(2)}) collective-permute-start(f32[128,256]{1,0:T(8,128)S(1)} %pad_maximum_fusion.1.refs_0_), channel_id=1, source_target_pairs={{0,4},{4,0},{8,12},{12,8},{16,20},{20,16},{24,28},{28,24},{1,5},{5... | collective-permute-start | bytes 393224 | tf_op jit(solution)/shard_map/ppermute | solution.py:345
  48.4 5.0 %block_0.1 = (f32[512,512]{1,0:T(8,128)S(1)}, f32[512,1]{1,0:T(8,128)S(1)}) custom-call(s32[2]{0:T(128)S(1)} %pad_add_fusion.where_ref, f32[64,640]{1,0:T(8,128)S(1)} %pad_maximum_fusion.refs_0_, f32[64,640]{1,0:T(8,128)S(1)} %collective-permute-done.10.refs_1_, f32[64,640]{1,0:T(8,128)S(1)} %collective-permute-done.9.refs_2_, ...), custom_call_target="tpu_custom_call" | custom-call | flops 1000000000 | bytes 1048576 | tf_op jit(solution)/shard_map/block_0/pallas_call | solution.py:238
  53.4 3.9 %block_1.1.in_ref = f32[512,512]{1,0:T(8,128)S(1)} custom-call(f32[512,512]{1,0:T(8,128)S(1)} %get-tuple-element.50.in_ref), custom_call_target="tpu_custom_call" | custom-call | flops 1000000000 | bytes 1048576 | tf_op jit(solution)/shard_map/block_1/pallas_call | solution.py:254
  57.9 3.9 %block_2.1.in_ref = f32[512,512]{1,0:T(8,128)S(1)} custom-call(f32[512,512]{1,0:T(8,128)S(1)} %block_1.1.in_ref), custom_call_target="tpu_custom_call" | custom-call | flops 1000000000 | bytes 1048576 | tf_op jit(solution)/shard_map/block_2/pallas_call | solution.py:254
  61.8 4.1 %block_3.1.inverse_ref = f32[512,512]{1,0:T(8,128)S(1)} custom-call(f32[512,512]{1,0:T(8,128)S(1)} %block_2.1.in_ref), custom_call_target="tpu_custom_call" | custom-call | flops 1000000000 | bytes 1048576 | tf_op jit(solution)/shard_map/block_3/pallas_call | solution.py:254
  69.4 1.8 %solve_near.1 = (f32[128,256]{1,0:T(8,128)S(1)}, f32[8,256]{1,0:T(8,128)}) custom-call(s32[2]{0:T(128)S(1)} %pad_add_fusion.where_ref, s32[8]{0:T(128)S(1)} %copy-done.3, f32[512,512]{1,0:T(8,128)S(1)} %block_3.1.inverse_ref, f32[512,1]{1,0:T(8,128)S(1)} %get-tuple-element.51.scale_ref, f32[128,256]{1,0:T(8,128)S(1)} %pad_maximum_fusion.1.refs_0_, ...), custom_call_target="tpu_custom_call" | custom-call | flops 5000000000 | bytes 1048576 | tf_op jit(solution)/shard_map/solve_near/pallas_call | solution.py:312
  71.2 2.7 %collective-permute-done.17.refs_2_ = f32[128,256]{1,0:T(8,128)S(1)} collective-permute-done((f32[128,256]{1,0:T(8,128)S(1)}, f32[128,256]{1,0:T(8,128)S(1)}, u32[]{:S(2)}, u32[]{:S(2)}) %collective-permute-start.17) | collective-permute-done | bytes 131104 | tf_op jit(solution)/shard_map/ppermute | solution.py:345
  73.9 1.9 %collective-permute-done.18.refs_3_ = f32[128,256]{1,0:T(8,128)S(1)} collective-permute-done((f32[128,256]{1,0:T(8,128)S(1)}, f32[128,256]{1,0:T(8,128)S(1)}, u32[]{:S(2)}, u32[]{:S(2)}) %collective-permute-start.18) | collective-permute-done | bytes 131104 | tf_op jit(solution)/shard_map/ppermute | solution.py:345
  (47 shorter events, 12.5 us)
Async XLA Ops:
  0.6 0.9 %copy-start.1 = (f32[24,2048]{1,0:T(8,128)S(1)}, f32[24,2048]{1,0:T(8,128)}, u32[]{:S(2)}) copy-start(f32[24,2048]{1,0:T(8,128)} %points_ref.1) | copy-start | bytes 589828
  1.6 0.7 copy-start.2
  5.3 5.5 %collective-permute-start = (f32[32,640]{1,0:T(8,128)S(1)}, f32[32,640]{1,0:T(8,128)S(1)}, u32[]{:S(2)}, u32[]{:S(2)}) collective-permute-start(f32[32,640]{1,0:T(8,128)S(1)} %dynamic-slice_bitcast_fusion.1), channel_id=1, source_target_pairs={{0,4},{4,0},{8,12},{12,8},{16,20},{20,16},{24,28},{28,24},{1,5},{5... | collective-permute-start | bytes 245768 | tf_op jit(solution)/shard_map/ppermute | solution.py:345
  8.3 1.2 %copy-start = (bf16[2048,256]{1,0:T(8,128)(2,1)S(1)}, bf16[2048,256]{1,0:T(8,128)(2,1)}, u32[]{:S(2)}) copy-start(bf16[2048,256]{1,0:T(8,128)(2,1)} %yields_ref.1) | copy-start | bytes 3145732
  10.8 4.1 %collective-permute-start.1 = (f32[16,640]{1,0:T(8,128)S(1)}, f32[16,640]{1,0:T(8,128)S(1)}, u32[]{:S(2)}, u32[]{:S(2)}) collective-permute-start(f32[16,640]{1,0:T(8,128)S(1)} %dynamic-slice_bitcast_fusion.3), channel_id=1, source_target_pairs={{0,8},{4,12},{8,0},{12,4},{16,24},{20,28},{24,16},{28,20},{1,9},{5... | collective-permute-start | bytes 122888 | tf_op jit(solution)/shard_map/ppermute | solution.py:345
  12.9 6.9 %collective-permute-start.3 = (f32[256,256]{1,0:T(8,128)S(1)}, f32[256,256]{1,0:T(8,128)S(1)}, u32[]{:S(2)}, u32[]{:S(2)}) collective-permute-start(f32[256,256]{1,0:T(8,128)S(1)} %get-tuple-element.37), channel_id=1, source_target_pairs={{0,4},{4,0},{8,12},{12,8},{16,20},{20,16},{24,28},{28,24},{1,5},{5... | collective-permute-start | bytes 786440 | tf_op jit(solution)/shard_map/ppermute | solution.py:345
  14.9 4.9 %collective-permute-start.2 = (f32[8,640]{1,0:T(8,128)S(1)}, f32[8,640]{1,0:T(8,128)S(1)}, u32[]{:S(2)}, u32[]{:S(2)}) collective-permute-start(f32[8,640]{1,0:T(8,128)S(1)} %dynamic-slice_bitcast_fusion.4), channel_id=1, source_target_pairs={{0,16},{4,20},{8,24},{12,28},{16,0},{20,4},{24,8},{28,12},{1,17},{... | collective-permute-start | bytes 61448 | tf_op jit(solution)/shard_map/ppermute | solution.py:345
  19.8 4.9 %collective-permute-start.4 = (f32[8,640]{1,0:T(8,128)S(1)}, f32[8,640]{1,0:T(8,128)S(1)}, u32[]{:S(2)}, u32[]{:S(2)}) collective-permute-start(f32[8,640]{1,0:T(8,128)S(1)} %bitcast_add_fusion.4), channel_id=1, source_target_pairs={{0,16},{4,20},{8,24},{12,28},{16,0},{20,4},{24,8},{28,12},{1,17},{... | collective-permute-start | bytes 61448 | tf_op jit(solution)/shard_map/ppermute | solution.py:345
  24.7 4.0 %collective-permute-start.5 = (f32[16,640]{1,0:T(8,128)S(1)}, f32[16,640]{1,0:T(8,128)S(1)}, u32[]{:S(2)}, u32[]{:S(2)}) collective-permute-start(f32[16,640]{1,0:T(8,128)S(1)} %pad_maximum_fusion.3), channel_id=1, source_target_pairs={{0,8},{4,12},{8,0},{12,4},{16,24},{20,28},{24,16},{28,20},{1,9},{5... | collective-permute-start | bytes 122888 | tf_op jit(solution)/shard_map/ppermute | solution.py:345
  26.5 5.2 %collective-permute-start.6 = (f32[128,256]{1,0:T(8,128)S(1)}, f32[128,256]{1,0:T(8,128)S(1)}, u32[]{:S(2)}, u32[]{:S(2)}) collective-permute-start(f32[128,256]{1,0:T(8,128)S(1)} %dynamic-slice_bitcast_fusion), channel_id=1, source_target_pairs={{0,8},{4,12},{8,0},{12,4},{16,24},{20,28},{24,16},{28,20},{1,9},{5... | collective-permute-start | bytes 393224 | tf_op jit(solution)/shard_map/ppermute | solution.py:345
  31.8 7.3 %collective-permute-start.8 = (f32[64,256]{1,0:T(8,128)S(1)}, f32[64,256]{1,0:T(8,128)S(1)}, u32[]{:S(2)}, u32[]{:S(2)}) collective-permute-start(f32[64,256]{1,0:T(8,128)S(1)} %dynamic-slice_bitcast_fusion.2), channel_id=1, source_target_pairs={{0,16},{4,20},{8,24},{12,28},{16,0},{20,4},{24,8},{28,12},{1,17},{... | collective-permute-start | bytes 196616 | tf_op jit(solution)/shard_map/ppermute | solution.py:345
  34.4 4.7 %collective-permute-start.7 = (f32[32,640]{1,0:T(8,128)S(1)}, f32[32,640]{1,0:T(8,128)S(1)}, u32[]{:S(2)}, u32[]{:S(2)}) collective-permute-start(f32[32,640]{1,0:T(8,128)S(1)} %pad_maximum_fusion.2), channel_id=1, source_target_pairs={{0,4},{4,0},{8,12},{12,8},{16,20},{20,16},{24,28},{28,24},{1,5},{5... | collective-permute-start | bytes 245768 | tf_op jit(solution)/shard_map/ppermute | solution.py:345
  39.1 5.4 %collective-permute-start.9 = (f32[64,640]{1,0:T(8,128)S(1)}, f32[64,640]{1,0:T(8,128)S(1)}, u32[]{:S(2)}, u32[]{:S(2)}) collective-permute-start(f32[64,640]{1,0:T(8,128)S(1)} %pad_maximum_fusion.refs_0_), channel_id=1, source_target_pairs={{0,2},{1,3},{2,0},{3,1},{4,6},{5,7},{6,4},{7,5},{8,10},{9,11},{10,... | collective-permute-start | bytes 491528 | tf_op jit(solution)/shard_map/ppermute | solution.py:345
  40.4 5.9 %collective-permute-start.12 = (f32[64,256]{1,0:T(8,128)S(1)}, f32[64,256]{1,0:T(8,128)S(1)}, u32[]{:S(2)}, u32[]{:S(2)}) collective-permute-start(f32[64,256]{1,0:T(8,128)S(1)} %bitcast_add_fusion.2), channel_id=1, source_target_pairs={{0,16},{4,20},{8,24},{12,28},{16,0},{20,4},{24,8},{28,12},{1,17},{... | collective-permute-start | bytes 196616 | tf_op jit(solution)/shard_map/ppermute | solution.py:345
  41.3 5.0 %collective-permute-start.10 = (f32[64,640]{1,0:T(8,128)S(1)}, f32[64,640]{1,0:T(8,128)S(1)}, u32[]{:S(2)}, u32[]{:S(2)}) collective-permute-start(f32[64,640]{1,0:T(8,128)S(1)} %pad_maximum_fusion.refs_0_), channel_id=1, source_target_pairs={{0,1},{1,0},{2,3},{3,2},{4,5},{5,4},{6,7},{7,6},{8,9},{9,8},{10,11... | collective-permute-start | bytes 491528 | tf_op jit(solution)/shard_map/ppermute | solution.py:345
  44.5 1.8 %collective-permute-start.11 = (f32[64,640]{1,0:T(8,128)S(1)}, f32[64,640]{1,0:T(8,128)S(1)}, u32[]{:S(2)}, u32[]{:S(2)}) collective-permute-start(f32[64,640]{1,0:T(8,128)S(1)} %collective-permute-done.9.refs_2_), channel_id=1, source_target_pairs={{0,1},{1,0},{2,3},{3,2},{4,5},{5,4},{6,7},{7,6},{8,9},{9,8},{10,11... | collective-permute-start | bytes 491528 | tf_op jit(solution)/shard_map/ppermute | solution.py:345
  46.3 7.1 %collective-permute-start.14 = (f32[128,256]{1,0:T(8,128)S(1)}, f32[128,256]{1,0:T(8,128)S(1)}, u32[]{:S(2)}, u32[]{:S(2)}) collective-permute-start(f32[128,256]{1,0:T(8,128)S(1)} %pad_maximum_fusion.1.refs_0_), channel_id=1, source_target_pairs={{0,4},{4,0},{8,12},{12,8},{16,20},{20,16},{24,28},{28,24},{1,5},{5... | collective-permute-start | bytes 393224 | tf_op jit(solution)/shard_map/ppermute | solution.py:345
  47.9 5.5 %collective-permute-start.13 = (f32[128,256]{1,0:T(8,128)S(1)}, f32[128,256]{1,0:T(8,128)S(1)}, u32[]{:S(2)}, u32[]{:S(2)}) collective-permute-start(f32[128,256]{1,0:T(8,128)S(1)} %pad_maximum_fusion.1.refs_0_), channel_id=1, source_target_pairs={{0,8},{4,12},{8,0},{12,4},{16,24},{20,28},{24,16},{28,20},{1,9},{5... | collective-permute-start | bytes 393224 | tf_op jit(solution)/shard_map/ppermute | solution.py:345
  57.3 8.6 %collective-permute-start.15 = (f32[128,256]{1,0:T(8,128)S(1)}, f32[128,256]{1,0:T(8,128)S(1)}, u32[]{:S(2)}, u32[]{:S(2)}) collective-permute-start(f32[128,256]{1,0:T(8,128)S(1)} %collective-permute-done.13.refs_1_), channel_id=1, source_target_pairs={{0,4},{4,0},{8,12},{12,8},{16,20},{20,16},{24,28},{28,24},{1,5},{5... | collective-permute-start | bytes 393224 | tf_op jit(solution)/shard_map/ppermute | solution.py:345
  61.8 4.1 %copy-start.3 = (s32[8]{0:T(128)S(1)}, s32[8]{0:T(128)}, u32[]{:S(2)}) copy-start(s32[8]{0:T(128)} %group_ref.3) | copy-start | bytes 100
  67.5 3.7 %collective-permute-start.16 = (f32[128,256]{1,0:T(8,128)S(1)}, f32[128,256]{1,0:T(8,128)S(1)}, u32[]{:S(2)}, u32[]{:S(2)}) collective-permute-start(f32[128,256]{1,0:T(8,128)S(1)} %get-tuple-element.55.refs_4_), channel_id=1, source_target_pairs={{0,1},{1,0},{2,3},{3,2},{4,5},{5,4},{6,7},{7,6},{8,9},{9,8},{10,11... | collective-permute-start | bytes 393224 | tf_op jit(solution)/shard_map/ppermute | solution.py:345
  67.6 6.4 %collective-permute-start.17 = (f32[128,256]{1,0:T(8,128)S(1)}, f32[128,256]{1,0:T(8,128)S(1)}, u32[]{:S(2)}, u32[]{:S(2)}) collective-permute-start(f32[128,256]{1,0:T(8,128)S(1)} %get-tuple-element.56.refs_5_), channel_id=1, source_target_pairs={{0,2},{1,3},{2,0},{3,1},{4,6},{5,7},{6,4},{7,5},{8,10},{9,11},{10,... | collective-permute-start | bytes 393224 | tf_op jit(solution)/shard_map/ppermute | solution.py:345
  69.0 6.9 %collective-permute-start.18 = (f32[128,256]{1,0:T(8,128)S(1)}, f32[128,256]{1,0:T(8,128)S(1)}, u32[]{:S(2)}, u32[]{:S(2)}) collective-permute-start(f32[128,256]{1,0:T(8,128)S(1)} %get-tuple-element.57.refs_6_), channel_id=1, source_target_pairs={{0,3},{1,2},{2,1},{3,0},{4,7},{5,6},{6,5},{7,4},{8,11},{9,10},{10,... | collective-permute-start | bytes 393224 | tf_op jit(solution)/shard_map/ppermute | solution.py:345

commit v7 on v6

--- a/solution.py
+++ b/solution.py
@@ -139,12 +139,20 @@
         inside = (lanes >= base) & (lanes < base + 8)
         columns = [lane_of(own, base + k) for k in range(8)]
         fresh = jnp.where(inside, jnp.where(lanes == subs + base, -1.0, 0.0), own)
-        for p in range(8):
-            inverse = 1.0 / row_of(columns[p], p)
-            factor = jnp.where(subs == p, 1.0 - inverse, columns[p] * inverse)
-            for k in range(p + 1, 8):
-                columns[k] = columns[k] - factor * row_of(columns[k], p)
-            fresh = fresh - factor * row_of(fresh, p)
+        for p in range(0, 8, 2):
+            q = p + 1
+            a, b, d = row_of(columns[p], p), row_of(columns[p], q), row_of(columns[q], q)
+            det = a * d - b * b
+            first = d * columns[p] - b * columns[q]
+            second = a * columns[q] - b * columns[p]
+            first = jnp.where(subs == p, det - d, jnp.where(subs == q, b, first))
+            second = jnp.where(subs == p, b, jnp.where(subs == q, det - a, second))
+            inverse = 1.0 / det
+            for k in range(q + 1, 8):
+                less = first * row_of(columns[k], p) + second * row_of(columns[k], q)
+                columns[k] = columns[k] - less * inverse
+            less = first * row_of(fresh, p) + second * row_of(fresh, q)
+            fresh = fresh - less * inverse
         delta = stacked_outer(own, fresh)
         following = (at + 1) % len(bands)
         for other in range(len(bands)):
@@ -317,7 +325,7 @@
         scratch_shapes=[pltpu.VMEM((terms, cells), jnp.float32)],
         compiler_params=BIG,
         cost_estimate=pl.CostEstimate(flops=(5 if finish else 1) * 10**9, bytes_accessed=2**20, transcendentals=0),
-        name="solve_near" if finish else "solve_far",
+        name="solve_near" if finish else "solve_far_%d" % steps[0],
     )(where, block_group, inverse, scale, *pieces, *others)
 
 
@@ -381,11 +389,11 @@
     fold = add_rest(halve(halve(fold, me, 1), me, 2))
     fold, part = lax.optimization_barrier((fold, part))
     part = halve(part, me, 1)
-    fold = join(join(fold, 4), 2)
+    fold = join(fold, 4)
     fold, part = lax.optimization_barrier((fold, part))
     part = add_rest(halve(part, me, 2))
     rows = part.shape[0]
-    fold = join(fold, 1)
+    fold = join(join(fold, 2), 1)
     fold, part = lax.optimization_barrier((fold, part))
     pair = join(part, 4)
     held, order = [fold], [0]
@@ -404,9 +412,11 @@
             pieces = pieces + [swap(pieces[1], "samp", 1)]
         gram = next_block(gram, block)
     given = (where, gram, scale, pieces, rows, block_group, points.shape[1] * n_samp, n_cell)
-    far = list(solve(*given, tuple(range(1, n_cell))))
-    came = [swap(value, "cell", 1 + at) for at, value in enumerate(far)]
-    near, sobol = solve(*given, (0,), far)
+    far = [None] * n_cell
+    for step in range(n_cell - 1, 0, -1):
+        far[step], = solve(*given, (step,))
+    came = [swap(far[step], "cell", step) for step in range(1, n_cell)]
+    near, sobol = solve(*given, (0,), far[1:])
     shares = [near] + came
     return (join_columns(cell.reshape(1), shares), sobol)
 

time: 76.9 us -> 75 us (0.975)
  waiting for transfers between devices: 22.3 us -> 18.6 us
  starting transfers between devices: 25.7 us -> 27.2 us
    ppermute x19, waiting for transfers between devices: 22.3 us -> 18.6 us  [swap(): return lax.ppermute(values, axis, [(at, at ^ step) for at in range(size)])]
    pallas_call x2 -> x4, Pallas kernels: 3.3 us -> 5.06 us  [solve(): pl.pallas_call(functools.partial(solve_kernel, samples, steps, rows, fini...]
    ppermute x19, starting transfers between devices: 25.7 us -> 27.2 us  [swap(): return lax.ppermute(values, axis, [(at, at ^ step) for at in range(size)])]
    pallas_call x3, Pallas kernels: 11.9 us -> 11 us  [next_block(): pl.pallas_call(functools.partial(next_kernel, block), out_shape=jax.Shape...]
  transfers between devices with their start and end apart: 19 -> 19, of which waited for: 11 -> 11; matrix products, arithmetic and copies ran while one was open for 0% -> 0% of each run, Pallas kernels for 20% -> 22%
where the time goes in v7:
time: 75 us; the launch traced here: 74.8 us
  starting transfers between devices  27.2 us (36%)
  Pallas kernels  25 us (33%)
  waiting for transfers between devices  18.6 us (25%)
  local copies, waits for them, and re-layouts  2.9 us (4%)
  between operations  0.86 us (1%)
    ppermute x19, starting transfers between devices, swap(): return lax.ppermute(values, axis, [(at, at ^ step) for at in range(size)])  27.2 us
    ppermute x19, waiting for transfers between devices, swap(): return lax.ppermute(values, axis, [(at, at ^ step) for at in range(size)])  18.6 us
    pallas_call x3, Pallas kernels, next_block(): pl.pallas_call(functools.partial(next_kernel, block), out_shape=jax.Shape...  11 us
    pallas_call x4, Pallas kernels, solve(): pl.pallas_call(functools.partial(solve_kernel, samples, steps, rows, fini...  5.06 us
    pallas_call x1, Pallas kernels, first_block(): pl.pallas_call(first_kernel, out_shape=(jax.ShapeDtypeStruct((terms, term...  4.45 us
    pallas_call x1, Pallas kernels, design(): pl.pallas_call(functools.partial(design_kernel, 512), out_shape=(jax.Shap...  2.97 us
    unnamed x8, local copies, waits for them, and re-layouts  2.84 us
  transfers between devices with their start and end apart: 19, of which 11 were waited for; matrix products, arithmetic and copies ran while one was open for 0% of the time, Pallas kernels for 22%

profile of v7, /device:TPU:0, one launch (start us, length us, event | category | flops | bytes accessed | tf_op | source)
XLA Modules:
  0.0 74.8 jit_solution(17871750102990329023)
XLA Ops:
  2.3 3.0 %design.1 = (bf16[512,2048]{1,0:T(8,128)(2,1)S(1)}, f32[64,640]{1,0:T(8,128)S(1)}) custom-call(s32[1]{0:T(128)} %bitcast.cell_ref.where_ref, s32[2,512]{1,0:T(2,128)S(1)} %bitcast.34, f32[24,2048]{1,0:T(8,128)S(1)} %copy-done.1), custom_call_target="tpu_custom_call" | custom-call | tf_op jit(solution)/shard_map/design/pallas_call | solution.py:80
  5.3 3.0 %collective-permute-start = (f32[32,640]{1,0:T(8,128)S(1)}, f32[32,640]{1,0:T(8,128)S(1)}, u32[]{:S(2)}, u32[]{:S(2)}) collective-permute-start(f32[32,640]{1,0:T(8,128)S(1)} %dynamic-slice_bitcast_fusion.1), channel_id=1, source_target_pairs={{0,4},{4,0},{8,12},{12,8},{16,20},{20,16},{24,28},{28,24},{1,5},{5... | collective-permute-start | bytes 245768 | tf_op jit(solution)/shard_map/ppermute | solution.py:353
  10.8 2.1 %collective-permute-start.1 = (f32[16,640]{1,0:T(8,128)S(1)}, f32[16,640]{1,0:T(8,128)S(1)}, u32[]{:S(2)}, u32[]{:S(2)}) collective-permute-start(f32[16,640]{1,0:T(8,128)S(1)} %dynamic-slice_bitcast_fusion.3), channel_id=1, source_target_pairs={{0,8},{4,12},{8,0},{12,4},{16,24},{20,28},{24,16},{28,20},{1,9},{5... | collective-permute-start | bytes 122888 | tf_op jit(solution)/shard_map/ppermute | solution.py:353
  12.9 1.5 %collective-permute-start.3 = (f32[256,256]{1,0:T(8,128)S(1)}, f32[256,256]{1,0:T(8,128)S(1)}, u32[]{:S(2)}, u32[]{:S(2)}) collective-permute-start(f32[256,256]{1,0:T(8,128)S(1)} %get-tuple-element.34), channel_id=1, source_target_pairs={{0,4},{4,0},{8,12},{12,8},{16,20},{20,16},{24,28},{28,24},{1,5},{5... | collective-permute-start | bytes 786440 | tf_op jit(solution)/shard_map/ppermute | solution.py:353
  14.9 3.1 %collective-permute-start.2 = (f32[8,640]{1,0:T(8,128)S(1)}, f32[8,640]{1,0:T(8,128)S(1)}, u32[]{:S(2)}, u32[]{:S(2)}) collective-permute-start(f32[8,640]{1,0:T(8,128)S(1)} %dynamic-slice_bitcast_fusion.4), channel_id=1, source_target_pairs={{0,16},{4,20},{8,24},{12,28},{16,0},{20,4},{24,8},{28,12},{1,17},{... | collective-permute-start | bytes 61448 | tf_op jit(solution)/shard_map/ppermute | solution.py:353
  18.0 1.8 %collective-permute-done.2 = f32[8,640]{1,0:T(8,128)S(1)} collective-permute-done((f32[8,640]{1,0:T(8,128)S(1)}, f32[8,640]{1,0:T(8,128)S(1)}, u32[]{:S(2)}, u32[]{:S(2)}) %collective-permute-start.2) | collective-permute-done | bytes 20512 | tf_op jit(solution)/shard_map/ppermute | solution.py:353
  19.8 3.0 %collective-permute-start.4 = (f32[8,640]{1,0:T(8,128)S(1)}, f32[8,640]{1,0:T(8,128)S(1)}, u32[]{:S(2)}, u32[]{:S(2)}) collective-permute-start(f32[8,640]{1,0:T(8,128)S(1)} %bitcast_add_fusion.4), channel_id=1, source_target_pairs={{0,16},{4,20},{8,24},{12,28},{16,0},{20,4},{24,8},{28,12},{1,17},{... | collective-permute-start | bytes 61448 | tf_op jit(solution)/shard_map/ppermute | solution.py:353
  22.8 1.8 %collective-permute-start.5 = (f32[128,256]{1,0:T(8,128)S(1)}, f32[128,256]{1,0:T(8,128)S(1)}, u32[]{:S(2)}, u32[]{:S(2)}) collective-permute-start(f32[128,256]{1,0:T(8,128)S(1)} %dynamic-slice_bitcast_fusion), channel_id=1, source_target_pairs={{0,8},{4,12},{8,0},{12,4},{16,24},{20,28},{24,16},{28,20},{1,9},{5... | collective-permute-start | bytes 393224 | tf_op jit(solution)/shard_map/ppermute | solution.py:353
  24.7 3.2 %collective-permute-done.5 = f32[128,256]{1,0:T(8,128)S(1)} collective-permute-done((f32[128,256]{1,0:T(8,128)S(1)}, f32[128,256]{1,0:T(8,128)S(1)}, u32[]{:S(2)}, u32[]{:S(2)}) %collective-permute-start.5) | collective-permute-done | bytes 131104 | tf_op jit(solution)/shard_map/ppermute | solution.py:353
  27.9 1.9 %collective-permute-start.6 = (f32[16,640]{1,0:T(8,128)S(1)}, f32[16,640]{1,0:T(8,128)S(1)}, u32[]{:S(2)}, u32[]{:S(2)}) collective-permute-start(f32[16,640]{1,0:T(8,128)S(1)} %pad_maximum_fusion.3), channel_id=1, source_target_pairs={{0,8},{4,12},{8,0},{12,4},{16,24},{20,28},{24,16},{28,20},{1,9},{5... | collective-permute-start | bytes 122888 | tf_op jit(solution)/shard_map/ppermute | solution.py:353
  32.0 1.5 %collective-permute-start.7 = (f32[32,640]{1,0:T(8,128)S(1)}, f32[32,640]{1,0:T(8,128)S(1)}, u32[]{:S(2)}, u32[]{:S(2)}) collective-permute-start(f32[32,640]{1,0:T(8,128)S(1)} %pad_maximum_fusion.2), channel_id=1, source_target_pairs={{0,4},{4,0},{8,12},{12,8},{16,20},{20,16},{24,28},{28,24},{1,5},{5... | collective-permute-start | bytes 245768 | tf_op jit(solution)/shard_map/ppermute | solution.py:353
  33.5 3.2 %collective-permute-done.8 = f32[64,256]{1,0:T(8,128)S(1)} collective-permute-done((f32[64,256]{1,0:T(8,128)S(1)}, f32[64,256]{1,0:T(8,128)S(1)}, u32[]{:S(2)}, u32[]{:S(2)}) %collective-permute-start.8) | collective-permute-done | bytes 65568 | tf_op jit(solution)/shard_map/ppermute | solution.py:353
  36.7 1.2 %collective-permute-start.9 = (f32[64,640]{1,0:T(8,128)S(1)}, f32[64,640]{1,0:T(8,128)S(1)}, u32[]{:S(2)}, u32[]{:S(2)}) collective-permute-start(f32[64,640]{1,0:T(8,128)S(1)} %pad_maximum_fusion.refs_0_), channel_id=1, source_target_pairs={{0,2},{1,3},{2,0},{3,1},{4,6},{5,7},{6,4},{7,5},{8,10},{9,11},{10,... | collective-permute-start | bytes 491528 | tf_op jit(solution)/shard_map/ppermute | solution.py:353
  38.9 3.3 %collective-permute-done.9.refs_2_ = f32[64,640]{1,0:T(8,128)S(1)} collective-permute-done((f32[64,640]{1,0:T(8,128)S(1)}, f32[64,640]{1,0:T(8,128)S(1)}, u32[]{:S(2)}, u32[]{:S(2)}) %collective-permute-start.9) | collective-permute-done | bytes 163872 | tf_op jit(solution)/shard_map/ppermute | solution.py:353
  43.5 1.5 %collective-permute-start.14 = (f32[128,256]{1,0:T(8,128)S(1)}, f32[128,256]{1,0:T(8,128)S(1)}, u32[]{:S(2)}, u32[]{:S(2)}) collective-permute-start(f32[128,256]{1,0:T(8,128)S(1)} %pad_maximum_fusion.1.refs_0_), channel_id=1, source_target_pairs={{0,4},{4,0},{8,12},{12,8},{16,20},{20,16},{24,28},{28,24},{1,5},{5... | collective-permute-start | bytes 393224 | tf_op jit(solution)/shard_map/ppermute | solution.py:353
  45.0 2.0 %collective-permute-start.13 = (f32[128,256]{1,0:T(8,128)S(1)}, f32[128,256]{1,0:T(8,128)S(1)}, u32[]{:S(2)}, u32[]{:S(2)}) collective-permute-start(f32[128,256]{1,0:T(8,128)S(1)} %pad_maximum_fusion.1.refs_0_), channel_id=1, source_target_pairs={{0,8},{4,12},{8,0},{12,4},{16,24},{20,28},{24,16},{28,20},{1,9},{5... | collective-permute-start | bytes 393224 | tf_op jit(solution)/shard_map/ppermute | solution.py:353
  47.1 4.4 %block_0.1 = (f32[512,512]{1,0:T(8,128)S(1)}, f32[512,1]{1,0:T(8,128)S(1)}) custom-call(s32[2]{0:T(128)S(1)} %pad_add_fusion.where_ref, f32[64,640]{1,0:T(8,128)S(1)} %pad_maximum_fusion.refs_0_, f32[64,640]{1,0:T(8,128)S(1)} %collective-permute-done.10.refs_1_, f32[64,640]{1,0:T(8,128)S(1)} %collective-permute-done.9.refs_2_, ...), custom_call_target="tpu_custom_call" | custom-call | flops 1000000000 | bytes 1048576 | tf_op jit(solution)/shard_map/block_0/pallas_call | solution.py:246
  51.6 3.6 %block_1.1.in_ref = f32[512,512]{1,0:T(8,128)S(1)} custom-call(f32[512,512]{1,0:T(8,128)S(1)} %get-tuple-element.47.in_ref), custom_call_target="tpu_custom_call" | custom-call | flops 1000000000 | bytes 1048576 | tf_op jit(solution)/shard_map/block_1/pallas_call | solution.py:262
  55.7 3.6 %block_2.1.in_ref = f32[512,512]{1,0:T(8,128)S(1)} custom-call(f32[512,512]{1,0:T(8,128)S(1)} %block_1.1.in_ref), custom_call_target="tpu_custom_call" | custom-call | flops 1000000000 | bytes 1048576 | tf_op jit(solution)/shard_map/block_2/pallas_call | solution.py:262
  59.3 3.8 %block_3.1.inverse_ref = f32[512,512]{1,0:T(8,128)S(1)} custom-call(f32[512,512]{1,0:T(8,128)S(1)} %block_2.1.in_ref), custom_call_target="tpu_custom_call" | custom-call | flops 1000000000 | bytes 1048576 | tf_op jit(solution)/shard_map/block_3/pallas_call | solution.py:262
  65.4 1.5 %collective-permute-start.17 = (f32[128,256]{1,0:T(8,128)S(1)}, f32[128,256]{1,0:T(8,128)S(1)}, u32[]{:S(2)}, u32[]{:S(2)}) collective-permute-start(f32[128,256]{1,0:T(8,128)S(1)} %solve_far_2.1.refs_5_), channel_id=1, source_target_pairs={{0,2},{1,3},{2,0},{3,1},{4,6},{5,7},{6,4},{7,5},{8,10},{9,11},{10,... | collective-permute-start | bytes 393224 | tf_op jit(solution)/shard_map/ppermute | solution.py:353
  68.5 1.8 %solve_near.1 = (f32[128,256]{1,0:T(8,128)S(1)}, f32[8,256]{1,0:T(8,128)}) custom-call(s32[2]{0:T(128)S(1)} %pad_add_fusion.where_ref, s32[8]{0:T(128)S(1)} %copy-done.3, f32[512,512]{1,0:T(8,128)S(1)} %block_3.1.inverse_ref, f32[512,1]{1,0:T(8,128)S(1)} %get-tuple-element.48.scale_ref, f32[128,256]{1,0:T(8,128)S(1)} %pad_maximum_fusion.1.refs_0_, ...), custom_call_target="tpu_custom_call" | custom-call | flops 5000000000 | bytes 1048576 | tf_op jit(solution)/shard_map/solve_near/pallas_call | solution.py:320
  70.3 1.3 %collective-permute-done.17.refs_2_ = f32[128,256]{1,0:T(8,128)S(1)} collective-permute-done((f32[128,256]{1,0:T(8,128)S(1)}, f32[128,256]{1,0:T(8,128)S(1)}, u32[]{:S(2)}, u32[]{:S(2)}) %collective-permute-start.17) | collective-permute-done | bytes 131104 | tf_op jit(solution)/shard_map/ppermute | solution.py:353
  71.6 2.3 %collective-permute-done.18.refs_3_ = f32[128,256]{1,0:T(8,128)S(1)} collective-permute-done((f32[128,256]{1,0:T(8,128)S(1)}, f32[128,256]{1,0:T(8,128)S(1)}, u32[]{:S(2)}, u32[]{:S(2)}) %collective-permute-start.18) | collective-permute-done | bytes 131104 | tf_op jit(solution)/shard_map/ppermute | solution.py:353
  (49 shorter events, 14.2 us)
Async XLA Ops:
  0.6 0.9 %copy-start.1 = (f32[24,2048]{1,0:T(8,128)S(1)}, f32[24,2048]{1,0:T(8,128)}, u32[]{:S(2)}) copy-start(f32[24,2048]{1,0:T(8,128)} %points_ref.1) | copy-start | bytes 589828
  1.6 0.7 copy-start.2
  5.3 5.5 %collective-permute-start = (f32[32,640]{1,0:T(8,128)S(1)}, f32[32,640]{1,0:T(8,128)S(1)}, u32[]{:S(2)}, u32[]{:S(2)}) collective-permute-start(f32[32,640]{1,0:T(8,128)S(1)} %dynamic-slice_bitcast_fusion.1), channel_id=1, source_target_pairs={{0,4},{4,0},{8,12},{12,8},{16,20},{20,16},{24,28},{28,24},{1,5},{5... | collective-permute-start | bytes 245768 | tf_op jit(solution)/shard_map/ppermute | solution.py:353
  8.3 1.2 %copy-start = (bf16[2048,256]{1,0:T(8,128)(2,1)S(1)}, bf16[2048,256]{1,0:T(8,128)(2,1)}, u32[]{:S(2)}) copy-start(bf16[2048,256]{1,0:T(8,128)(2,1)} %yields_ref.1) | copy-start | bytes 3145732
  10.8 4.1 %collective-permute-start.1 = (f32[16,640]{1,0:T(8,128)S(1)}, f32[16,640]{1,0:T(8,128)S(1)}, u32[]{:S(2)}, u32[]{:S(2)}) collective-permute-start(f32[16,640]{1,0:T(8,128)S(1)} %dynamic-slice_bitcast_fusion.3), channel_id=1, source_target_pairs={{0,8},{4,12},{8,0},{12,4},{16,24},{20,28},{24,16},{28,20},{1,9},{5... | collective-permute-start | bytes 122888 | tf_op jit(solution)/shard_map/ppermute | solution.py:353
  12.9 6.9 %collective-permute-start.3 = (f32[256,256]{1,0:T(8,128)S(1)}, f32[256,256]{1,0:T(8,128)S(1)}, u32[]{:S(2)}, u32[]{:S(2)}) collective-permute-start(f32[256,256]{1,0:T(8,128)S(1)} %get-tuple-element.34), channel_id=1, source_target_pairs={{0,4},{4,0},{8,12},{12,8},{16,20},{20,16},{24,28},{28,24},{1,5},{5... | collective-permute-start | bytes 786440 | tf_op jit(solution)/shard_map/ppermute | solution.py:353
  14.9 4.9 %collective-permute-start.2 = (f32[8,640]{1,0:T(8,128)S(1)}, f32[8,640]{1,0:T(8,128)S(1)}, u32[]{:S(2)}, u32[]{:S(2)}) collective-permute-start(f32[8,640]{1,0:T(8,128)S(1)} %dynamic-slice_bitcast_fusion.4), channel_id=1, source_target_pairs={{0,16},{4,20},{8,24},{12,28},{16,0},{20,4},{24,8},{28,12},{1,17},{... | collective-permute-start | bytes 61448 | tf_op jit(solution)/shard_map/ppermute | solution.py:353
  19.8 4.8 %collective-permute-start.4 = (f32[8,640]{1,0:T(8,128)S(1)}, f32[8,640]{1,0:T(8,128)S(1)}, u32[]{:S(2)}, u32[]{:S(2)}) collective-permute-start(f32[8,640]{1,0:T(8,128)S(1)} %bitcast_add_fusion.4), channel_id=1, source_target_pairs={{0,16},{4,20},{8,24},{12,28},{16,0},{20,4},{24,8},{28,12},{1,17},{... | collective-permute-start | bytes 61448 | tf_op jit(solution)/shard_map/ppermute | solution.py:353
  22.8 5.0 %collective-permute-start.5 = (f32[128,256]{1,0:T(8,128)S(1)}, f32[128,256]{1,0:T(8,128)S(1)}, u32[]{:S(2)}, u32[]{:S(2)}) collective-permute-start(f32[128,256]{1,0:T(8,128)S(1)} %dynamic-slice_bitcast_fusion), channel_id=1, source_target_pairs={{0,8},{4,12},{8,0},{12,4},{16,24},{20,28},{24,16},{28,20},{1,9},{5... | collective-permute-start | bytes 393224 | tf_op jit(solution)/shard_map/ppermute | solution.py:353
  27.9 4.1 %collective-permute-start.6 = (f32[16,640]{1,0:T(8,128)S(1)}, f32[16,640]{1,0:T(8,128)S(1)}, u32[]{:S(2)}, u32[]{:S(2)}) collective-permute-start(f32[16,640]{1,0:T(8,128)S(1)} %pad_maximum_fusion.3), channel_id=1, source_target_pairs={{0,8},{4,12},{8,0},{12,4},{16,24},{20,28},{24,16},{28,20},{1,9},{5... | collective-permute-start | bytes 122888 | tf_op jit(solution)/shard_map/ppermute | solution.py:353
  29.8 6.9 %collective-permute-start.8 = (f32[64,256]{1,0:T(8,128)S(1)}, f32[64,256]{1,0:T(8,128)S(1)}, u32[]{:S(2)}, u32[]{:S(2)}) collective-permute-start(f32[64,256]{1,0:T(8,128)S(1)} %dynamic-slice_bitcast_fusion.2), channel_id=1, source_target_pairs={{0,16},{4,20},{8,24},{12,28},{16,0},{20,4},{24,8},{28,12},{1,17},{... | collective-permute-start | bytes 196616 | tf_op jit(solution)/shard_map/ppermute | solution.py:353
  32.0 4.7 %collective-permute-start.7 = (f32[32,640]{1,0:T(8,128)S(1)}, f32[32,640]{1,0:T(8,128)S(1)}, u32[]{:S(2)}, u32[]{:S(2)}) collective-permute-start(f32[32,640]{1,0:T(8,128)S(1)} %pad_maximum_fusion.2), channel_id=1, source_target_pairs={{0,4},{4,0},{8,12},{12,8},{16,20},{20,16},{24,28},{28,24},{1,5},{5... | collective-permute-start | bytes 245768 | tf_op jit(solution)/shard_map/ppermute | solution.py:353
  36.7 5.4 %collective-permute-start.9 = (f32[64,640]{1,0:T(8,128)S(1)}, f32[64,640]{1,0:T(8,128)S(1)}, u32[]{:S(2)}, u32[]{:S(2)}) collective-permute-start(f32[64,640]{1,0:T(8,128)S(1)} %pad_maximum_fusion.refs_0_), channel_id=1, source_target_pairs={{0,2},{1,3},{2,0},{3,1},{4,6},{5,7},{6,4},{7,5},{8,10},{9,11},{10,... | collective-permute-start | bytes 491528 | tf_op jit(solution)/shard_map/ppermute | solution.py:353
  38.0 5.2 %collective-permute-start.12 = (f32[64,256]{1,0:T(8,128)S(1)}, f32[64,256]{1,0:T(8,128)S(1)}, u32[]{:S(2)}, u32[]{:S(2)}) collective-permute-start(f32[64,256]{1,0:T(8,128)S(1)} %bitcast_add_fusion.2), channel_id=1, source_target_pairs={{0,16},{4,20},{8,24},{12,28},{16,0},{20,4},{24,8},{28,12},{1,17},{... | collective-permute-start | bytes 196616 | tf_op jit(solution)/shard_map/ppermute | solution.py:353
  38.9 4.3 %collective-permute-start.10 = (f32[64,640]{1,0:T(8,128)S(1)}, f32[64,640]{1,0:T(8,128)S(1)}, u32[]{:S(2)}, u32[]{:S(2)}) collective-permute-start(f32[64,640]{1,0:T(8,128)S(1)} %pad_maximum_fusion.refs_0_), channel_id=1, source_target_pairs={{0,1},{1,0},{2,3},{3,2},{4,5},{5,4},{6,7},{7,6},{8,9},{9,8},{10,11... | collective-permute-start | bytes 491528 | tf_op jit(solution)/shard_map/ppermute | solution.py:353
  42.1 1.4 %collective-permute-start.11 = (f32[64,640]{1,0:T(8,128)S(1)}, f32[64,640]{1,0:T(8,128)S(1)}, u32[]{:S(2)}, u32[]{:S(2)}) collective-permute-start(f32[64,640]{1,0:T(8,128)S(1)} %collective-permute-done.9.refs_2_), channel_id=1, source_target_pairs={{0,1},{1,0},{2,3},{3,2},{4,5},{5,4},{6,7},{7,6},{8,9},{9,8},{10,11... | collective-permute-start | bytes 491528 | tf_op jit(solution)/shard_map/ppermute | solution.py:353
  43.5 8.1 %collective-permute-start.14 = (f32[128,256]{1,0:T(8,128)S(1)}, f32[128,256]{1,0:T(8,128)S(1)}, u32[]{:S(2)}, u32[]{:S(2)}) collective-permute-start(f32[128,256]{1,0:T(8,128)S(1)} %pad_maximum_fusion.1.refs_0_), channel_id=1, source_target_pairs={{0,4},{4,0},{8,12},{12,8},{16,20},{20,16},{24,28},{28,24},{1,5},{5... | collective-permute-start | bytes 393224 | tf_op jit(solution)/shard_map/ppermute | solution.py:353
  45.0 6.6 %collective-permute-start.13 = (f32[128,256]{1,0:T(8,128)S(1)}, f32[128,256]{1,0:T(8,128)S(1)}, u32[]{:S(2)}, u32[]{:S(2)}) collective-permute-start(f32[128,256]{1,0:T(8,128)S(1)} %pad_maximum_fusion.1.refs_0_), channel_id=1, source_target_pairs={{0,8},{4,12},{8,0},{12,4},{16,24},{20,28},{24,16},{28,20},{1,9},{5... | collective-permute-start | bytes 393224 | tf_op jit(solution)/shard_map/ppermute | solution.py:353
  55.3 7.9 %collective-permute-start.15 = (f32[128,256]{1,0:T(8,128)S(1)}, f32[128,256]{1,0:T(8,128)S(1)}, u32[]{:S(2)}, u32[]{:S(2)}) collective-permute-start(f32[128,256]{1,0:T(8,128)S(1)} %collective-permute-done.13.refs_1_), channel_id=1, source_target_pairs={{0,4},{4,0},{8,12},{12,8},{16,20},{20,16},{24,28},{28,24},{1,5},{5... | collective-permute-start | bytes 393224 | tf_op jit(solution)/shard_map/ppermute | solution.py:353
  59.3 3.8 %copy-start.3 = (s32[8]{0:T(128)S(1)}, s32[8]{0:T(128)}, u32[]{:S(2)}) copy-start(s32[8]{0:T(128)} %group_ref.7) | copy-start | bytes 100
  64.3 6.0 %collective-permute-start.16 = (f32[128,256]{1,0:T(8,128)S(1)}, f32[128,256]{1,0:T(8,128)S(1)}, u32[]{:S(2)}, u32[]{:S(2)}) collective-permute-start(f32[128,256]{1,0:T(8,128)S(1)} %solve_far_1.1.refs_4_), channel_id=1, source_target_pairs={{0,1},{1,0},{2,3},{3,2},{4,5},{5,4},{6,7},{7,6},{8,9},{9,8},{10,11... | collective-permute-start | bytes 393224 | tf_op jit(solution)/shard_map/ppermute | solution.py:353
  65.4 6.2 %collective-permute-start.17 = (f32[128,256]{1,0:T(8,128)S(1)}, f32[128,256]{1,0:T(8,128)S(1)}, u32[]{:S(2)}, u32[]{:S(2)}) collective-permute-start(f32[128,256]{1,0:T(8,128)S(1)} %solve_far_2.1.refs_5_), channel_id=1, source_target_pairs={{0,2},{1,3},{2,0},{3,1},{4,6},{5,7},{6,4},{7,5},{8,10},{9,11},{10,... | collective-permute-start | bytes 393224 | tf_op jit(solution)/shard_map/ppermute | solution.py:353
  68.0 5.9 %collective-permute-start.18 = (f32[128,256]{1,0:T(8,128)S(1)}, f32[128,256]{1,0:T(8,128)S(1)}, u32[]{:S(2)}, u32[]{:S(2)}) collective-permute-start(f32[128,256]{1,0:T(8,128)S(1)} %solve_far_3.1.refs_6_), channel_id=1, source_target_pairs={{0,3},{1,2},{2,1},{3,0},{4,7},{5,6},{6,5},{7,4},{8,11},{9,10},{10,... | collective-permute-start | bytes 393224 | tf_op jit(solution)/shard_map/ppermute | solution.py:353

commit v8 on v7

--- a/solution.py
+++ b/solution.py
@@ -204,9 +204,9 @@
         piece = ref.shape[0] // 2
         eighth = ref.shape[0] // 8
         for at in range(8):
-            row = pl.multiple_of((where_ref[0] ^ at) * eighth, eighth)
-            fold_ref[pl.ds(row, eighth), :] = ref[at * eighth:(at + 1) * eighth, :]
-        start = pl.multiple_of((where_ref[1] ^ step) * piece, piece)
+            row = ((at & 1) * 4 + (at & 2) + (at >> 2)) * eighth
+            fold_ref[row:row + eighth, :] = ref[at * eighth:(at + 1) * eighth, :]
+        start = pl.multiple_of((where_ref[0] ^ step) * piece, piece)
         for block in range(blocks):
             half, lane = fold_place(block, blocks)
             reach = (block + 1) * TILE
@@ -272,8 +272,8 @@
 
 def solve_kernel(samples, steps, rows, finish, where_ref, group_ref, inverse_ref, scale_ref, *refs):
     count = len(steps)
-    pieces = refs[:4]
-    others = refs[4:-(count + finish + 1)]
+    pieces = refs[:2]
+    others = refs[2:-(count + finish + 1)]
     cross_ref = refs[-1]
     shares = refs[-(count + finish + 1):-(finish + 1)]
     step = 0
@@ -325,7 +325,7 @@
         scratch_shapes=[pltpu.VMEM((terms, cells), jnp.float32)],
         compiler_params=BIG,
         cost_estimate=pl.CostEstimate(flops=(5 if finish else 1) * 10**9, bytes_accessed=2**20, transcendentals=0),
-        name="solve_near" if finish else "solve_far_%d" % steps[0],
+        name="solve_near" if finish else "solve_far",
     )(where, block_group, inverse, scale, *pieces, *others)
 
 
@@ -389,34 +389,30 @@
     fold = add_rest(halve(halve(fold, me, 1), me, 2))
     fold, part = lax.optimization_barrier((fold, part))
     part = halve(part, me, 1)
-    fold = join(fold, 4)
+    copies = jnp.broadcast_to(fold[None], (n_samp,) + fold.shape)
+    fold = lax.all_to_all(copies, "samp", split_axis=0, concat_axis=0)[:8].reshape(-1, fold.shape[1])
     fold, part = lax.optimization_barrier((fold, part))
     part = add_rest(halve(part, me, 2))
     rows = part.shape[0]
-    fold = join(join(fold, 2), 1)
-    fold, part = lax.optimization_barrier((fold, part))
-    pair = join(part, 4)
     held, order = [fold], [0]
     step = n_cell // 2
     while step:
         held = held + [swap(value, "cell", step) for value in held]
         order = order + [value ^ step for value in order]
         step //= 2
-    held, pair = lax.optimization_barrier((held, pair))
+    held, part = lax.optimization_barrier((held, part))
+    gram, scale = first_block(cell.reshape(1), [held[order.index(at)] for at in range(n_cell)], term_index.shape[0])
+    for block in range(1, blocks):
+        if block <= 2:
+            part = join(part, 8 >> block)
+            gram, part = lax.optimization_barrier((gram, part))
+        gram = next_block(gram, block)
+    pieces = [part, swap(part, "samp", 1)]
     where = jnp.stack([spot, cell])
-    gram, scale = first_block(where, [held[order.index(at)] for at in range(n_cell)], term_index.shape[0])
-    pieces = [pair, swap(pair, "samp", 2), swap(pair, "samp", 1)]
-    for block in range(1, blocks):
-        if block == 1:
-            gram, pieces = lax.optimization_barrier((gram, pieces))
-            pieces = pieces + [swap(pieces[1], "samp", 1)]
-        gram = next_block(gram, block)
     given = (where, gram, scale, pieces, rows, block_group, points.shape[1] * n_samp, n_cell)
-    far = [None] * n_cell
-    for step in range(n_cell - 1, 0, -1):
-        far[step], = solve(*given, (step,))
-    came = [swap(far[step], "cell", step) for step in range(1, n_cell)]
-    near, sobol = solve(*given, (0,), far[1:])
+    far = solve(*given, tuple(range(1, n_cell)))
+    came = [swap(value, "cell", 1 + at) for at, value in enumerate(far)]
+    near, sobol = solve(*given, (0,), far)
     shares = [near] + came
     return (join_columns(cell.reshape(1), shares), sobol)
 

time: 75 us -> 73.5 us (0.980)
  waiting for transfers between devices: 18.6 us -> 22.5 us
  starting transfers between devices: 27.2 us -> 23.5 us
  Pallas kernels: 25 us -> 22.5 us
    ppermute x19 -> x15, starting transfers between devices: 27.2 us -> 18.4 us  [swap(): return lax.ppermute(values, axis, [(at, at ^ step) for at in range(size)])]
    all_to_all x0 -> x1, waiting for transfers between devices: none -> 7.82 us  [on_device(): lax.all_to_all(copies, 'samp', split_axis=0, concat_axis=0)[:8]]
    all_to_all x0 -> x1, starting transfers between devices: none -> 5.08 us  [on_device(): lax.all_to_all(copies, 'samp', split_axis=0, concat_axis=0)[:8]]
    ppermute x19 -> x15, waiting for transfers between devices: 18.6 us -> 14.7 us  [swap(): return lax.ppermute(values, axis, [(at, at ^ step) for at in range(size)])]
    pallas_call x4 -> x2, Pallas kernels: 5.06 us -> 3.31 us  [solve(): pl.pallas_call(functools.partial(solve_kernel, samples, steps, rows, fini...]
  transfers between devices with their start and end apart: 19 -> 16, of which waited for: 11 -> 10; matrix products, arithmetic and copies ran while one was open for 0% -> 1% of each run, Pallas kernels for 22% -> 24%
where the time goes in v8:
time: 73.5 us; the launch traced here: 73.2 us
  starting transfers between devices  23.5 us (32%)
  Pallas kernels  22.5 us (31%)
  waiting for transfers between devices  22.5 us (31%)
  local copies, waits for them, and re-layouts  3.58 us (5%)
  between operations  0.85 us (1%)
    ppermute x15, starting transfers between devices, swap(): return lax.ppermute(values, axis, [(at, at ^ step) for at in range(size)])  18.4 us
    ppermute x15, waiting for transfers between devices, swap(): return lax.ppermute(values, axis, [(at, at ^ step) for at in range(size)])  14.7 us
    pallas_call x3, Pallas kernels, next_block(): pl.pallas_call(functools.partial(next_kernel, block), out_shape=jax.Shape...  10.9 us
    all_to_all x1, waiting for transfers between devices, on_device(): lax.all_to_all(copies, 'samp', split_axis=0, concat_axis=0)[:8]  7.82 us
    all_to_all x1, starting transfers between devices, on_device(): lax.all_to_all(copies, 'samp', split_axis=0, concat_axis=0)[:8]  5.08 us
    pallas_call x1, Pallas kernels, first_block(): pl.pallas_call(first_kernel, out_shape=(jax.ShapeDtypeStruct((terms, term...  3.85 us
    pallas_call x2, Pallas kernels, solve(): pl.pallas_call(functools.partial(solve_kernel, samples, steps, rows, fini...  3.31 us
    pallas_call x1, Pallas kernels, design(): pl.pallas_call(functools.partial(design_kernel, 512), out_shape=(jax.Shap...  2.97 us
  transfers between devices with their start and end apart: 16, of which 10 were waited for; matrix products, arithmetic and copies ran while one was open for 1% of the time, Pallas kernels for 24%

profile of v8, /device:TPU:0, one launch (start us, length us, event | category | flops | bytes accessed | tf_op | source)
XLA Modules:
  0.0 73.2 jit_solution(12887324290894408112)
XLA Ops:
  2.3 3.0 %design.1 = (bf16[512,2048]{1,0:T(8,128)(2,1)S(1)}, f32[64,640]{1,0:T(8,128)S(1)}) custom-call(s32[1]{0:T(128)} %bitcast.cell_ref.where_ref, s32[2,512]{1,0:T(2,128)S(1)} %bitcast.38, f32[24,2048]{1,0:T(8,128)S(1)} %copy-done.1), custom_call_target="tpu_custom_call" | custom-call | tf_op jit(solution)/shard_map/design/pallas_call | solution.py:80
  5.3 3.0 %collective-permute-start = (f32[32,640]{1,0:T(8,128)S(1)}, f32[32,640]{1,0:T(8,128)S(1)}, u32[]{:S(2)}, u32[]{:S(2)}) collective-permute-start(f32[32,640]{1,0:T(8,128)S(1)} %dynamic-slice_bitcast_fusion.1), channel_id=1, source_target_pairs={{0,4},{4,0},{8,12},{12,8},{16,20},{20,16},{24,28},{28,24},{1,5},{5... | collective-permute-start | bytes 245768 | tf_op jit(solution)/shard_map/ppermute | solution.py:353
  8.3 1.2 %copy-done = bf16[2048,256]{1,0:T(8,128)(2,1)S(1)} copy-done((bf16[2048,256]{1,0:T(8,128)(2,1)S(1)}, bf16[2048,256]{1,0:T(8,128)(2,1)}, u32[]{:S(2)}) %copy-start) | copy-done | bytes 1048600
  10.8 2.1 %collective-permute-start.1 = (f32[16,640]{1,0:T(8,128)S(1)}, f32[16,640]{1,0:T(8,128)S(1)}, u32[]{:S(2)}, u32[]{:S(2)}) collective-permute-start(f32[16,640]{1,0:T(8,128)S(1)} %dynamic-slice_bitcast_fusion.3), channel_id=1, source_target_pairs={{0,8},{4,12},{8,0},{12,4},{16,24},{20,28},{24,16},{28,20},{1,9},{5... | collective-permute-start | bytes 122888 | tf_op jit(solution)/shard_map/ppermute | solution.py:353
  12.9 1.5 %collective-permute-start.3 = (f32[256,256]{1,0:T(8,128)S(1)}, f32[256,256]{1,0:T(8,128)S(1)}, u32[]{:S(2)}, u32[]{:S(2)}) collective-permute-start(f32[256,256]{1,0:T(8,128)S(1)} %get-tuple-element.35), channel_id=1, source_target_pairs={{0,4},{4,0},{8,12},{12,8},{16,20},{20,16},{24,28},{28,24},{1,5},{5... | collective-permute-start | bytes 786440 | tf_op jit(solution)/shard_map/ppermute | solution.py:353
  14.9 3.1 %collective-permute-start.2 = (f32[8,640]{1,0:T(8,128)S(1)}, f32[8,640]{1,0:T(8,128)S(1)}, u32[]{:S(2)}, u32[]{:S(2)}) collective-permute-start(f32[8,640]{1,0:T(8,128)S(1)} %dynamic-slice_bitcast_fusion.4), channel_id=1, source_target_pairs={{0,16},{4,20},{8,24},{12,28},{16,0},{20,4},{24,8},{28,12},{1,17},{... | collective-permute-start | bytes 61448 | tf_op jit(solution)/shard_map/ppermute | solution.py:353
  18.0 1.8 %collective-permute-done.2 = f32[8,640]{1,0:T(8,128)S(1)} collective-permute-done((f32[8,640]{1,0:T(8,128)S(1)}, f32[8,640]{1,0:T(8,128)S(1)}, u32[]{:S(2)}, u32[]{:S(2)}) %collective-permute-start.2) | collective-permute-done | bytes 20512 | tf_op jit(solution)/shard_map/ppermute | solution.py:353
  19.8 2.0 %collective-permute-start.4 = (f32[128,256]{1,0:T(8,128)S(1)}, f32[128,256]{1,0:T(8,128)S(1)}, u32[]{:S(2)}, u32[]{:S(2)}) collective-permute-start(f32[128,256]{1,0:T(8,128)S(1)} %dynamic-slice_bitcast_fusion), channel_id=1, source_target_pairs={{0,8},{4,12},{8,0},{12,4},{16,24},{20,28},{24,16},{28,20},{1,9},{5... | collective-permute-start | bytes 393224 | tf_op jit(solution)/shard_map/ppermute | solution.py:353
  22.5 5.1 %all-to-all-start = ((f32[8,8,640]{2,1,0:T(8,128)}), f32[8,8,640]{2,1,0:T(8,128)S(1)}, u32[]{:S(2)}, u32[]{:S(2)}) async-start(f32[8,8,640]{2,1,0:T(8,128)} %broadcast_in_dim.2), calls=%async_computation | async-start | bytes 327680 | tf_op jit(solution)/shard_map/all_to_all | solution.py:393
  27.6 7.8 %all-to-all-done = f32[8,8,640]{2,1,0:T(8,128)S(1)} async-done(((f32[8,8,640]{2,1,0:T(8,128)}), f32[8,8,640]{2,1,0:T(8,128)S(1)}, u32[]{:S(2)}, u32[]{:S(2)}) %all-to-all-start) | async-done | bytes 163872 | tf_op jit(solution)/shard_map/all_to_all | solution.py:393
  35.4 1.8 %collective-permute-start.5 = (f32[64,640]{1,0:T(8,128)S(1)}, f32[64,640]{1,0:T(8,128)S(1)}, u32[]{:S(2)}, u32[]{:S(2)}) collective-permute-start(f32[64,640]{1,0:T(8,128)S(1)} %bitcast.33), channel_id=1, source_target_pairs={{0,2},{1,3},{2,0},{3,1},{4,6},{5,7},{6,4},{7,5},{8,10},{9,11},{10,... | collective-permute-start | bytes 491528 | tf_op jit(solution)/shard_map/ppermute | solution.py:353
  38.0 2.8 %collective-permute-done.5.refs_2_ = f32[64,640]{1,0:T(8,128)S(1)} collective-permute-done((f32[64,640]{1,0:T(8,128)S(1)}, f32[64,640]{1,0:T(8,128)S(1)}, u32[]{:S(2)}, u32[]{:S(2)}) %collective-permute-start.5) | collective-permute-done | bytes 163872 | tf_op jit(solution)/shard_map/ppermute | solution.py:353
  40.8 2.1 %collective-permute-done.8 = f32[64,256]{1,0:T(8,128)S(1)} collective-permute-done((f32[64,256]{1,0:T(8,128)S(1)}, f32[64,256]{1,0:T(8,128)S(1)}, u32[]{:S(2)}, u32[]{:S(2)}) %collective-permute-start.8) | collective-permute-done | bytes 65568 | tf_op jit(solution)/shard_map/ppermute | solution.py:353
  43.2 3.9 %block_0.1 = (f32[512,512]{1,0:T(8,128)S(1)}, f32[512,1]{1,0:T(8,128)S(1)}) custom-call(s32[1]{0:T(128)} %bitcast.cell_ref.where_ref, f32[64,640]{1,0:T(8,128)S(1)} %bitcast.35, f32[64,640]{1,0:T(8,128)S(1)} %collective-permute-done.6.refs_1_, f32[64,640]{1,0:T(8,128)S(1)} %collective-permute-done.5.refs_2_, f32[64,640]{1,0:T(8,128)S(1)} %collective-permute-done.7.refs_3_), custom_call_target="tpu_custom_call" | custom-call | flops 1000000000 | bytes 1048576 | tf_op jit(solution)/shard_map/block_0/pallas_call | solution.py:246
  48.3 3.6 %block_1.1.in_ref = f32[512,512]{1,0:T(8,128)S(1)} custom-call(f32[512,512]{1,0:T(8,128)S(1)} %get-tuple-element.46.in_ref), custom_call_target="tpu_custom_call" | custom-call | flops 1000000000 | bytes 1048576 | tf_op jit(solution)/shard_map/block_1/pallas_call | solution.py:262
  51.9 1.3 %collective-permute-done.10 = f32[128,256]{1,0:T(8,128)S(1)} collective-permute-done((f32[128,256]{1,0:T(8,128)S(1)}, f32[128,256]{1,0:T(8,128)S(1)}, u32[]{:S(2)}, u32[]{:S(2)}) %collective-permute-start.10) | collective-permute-done | bytes 131104 | tf_op jit(solution)/shard_map/ppermute | solution.py:353
  53.2 1.5 %collective-permute-start.11 = (f32[256,256]{1,0:T(8,128)S(1)}, f32[256,256]{1,0:T(8,128)S(1)}, u32[]{:S(2)}, u32[]{:S(2)}) collective-permute-start(f32[256,256]{1,0:T(8,128)S(1)} %pad_maximum_fusion.refs_0_), channel_id=1, source_target_pairs={{0,4},{4,0},{8,12},{12,8},{16,20},{20,16},{24,28},{28,24},{1,5},{5... | collective-permute-start | bytes 786440 | tf_op jit(solution)/shard_map/ppermute | solution.py:353
  54.8 3.6 %block_2.1.in_ref = f32[512,512]{1,0:T(8,128)S(1)} custom-call(f32[512,512]{1,0:T(8,128)S(1)} %block_1.1.in_ref), custom_call_target="tpu_custom_call" | custom-call | flops 1000000000 | bytes 1048576 | tf_op jit(solution)/shard_map/block_2/pallas_call | solution.py:262
  58.4 3.6 %block_3.1.inverse_ref = f32[512,512]{1,0:T(8,128)S(1)} custom-call(f32[512,512]{1,0:T(8,128)S(1)} %block_2.1.in_ref), custom_call_target="tpu_custom_call" | custom-call | flops 1000000000 | bytes 1048576 | tf_op jit(solution)/shard_map/block_3/pallas_call | solution.py:262
  62.1 1.5 %solve_far.1 = (f32[128,256]{1,0:T(8,128)S(1)}, f32[128,256]{1,0:T(8,128)S(1)}, f32[128,256]{1,0:T(8,128)S(1)}) custom-call(s32[2]{0:T(128)S(1)} %pad_add_fusion.where_ref, s32[8]{0:T(128)S(1)} %copy-done.3, f32[512,512]{1,0:T(8,128)S(1)} %block_3.1.inverse_ref, f32[512,1]{1,0:T(8,128)S(1)} %get-tuple-element.49.scale_ref, ...), custom_call_target="tpu_custom_call" | custom-call | flops 1000000000 | bytes 1048576 | tf_op jit(solution)/shard_map/solve_far/pallas_call | solution.py:320
  63.7 2.0 %collective-permute-start.13 = (f32[128,256]{1,0:T(8,128)S(1)}, f32[128,256]{1,0:T(8,128)S(1)}, u32[]{:S(2)}, u32[]{:S(2)}) collective-permute-start(f32[128,256]{1,0:T(8,128)S(1)} %get-tuple-element.52.refs_3_), channel_id=1, source_target_pairs={{0,2},{1,3},{2,0},{3,1},{4,6},{5,7},{6,4},{7,5},{8,10},{9,11},{10,... | collective-permute-start | bytes 393224 | tf_op jit(solution)/shard_map/ppermute | solution.py:353
  65.8 1.8 %solve_near.1 = (f32[128,256]{1,0:T(8,128)S(1)}, f32[8,256]{1,0:T(8,128)}) custom-call(s32[2]{0:T(128)S(1)} %pad_add_fusion.where_ref, s32[8]{0:T(128)S(1)} %copy-done.3, f32[512,512]{1,0:T(8,128)S(1)} %block_3.1.inverse_ref, f32[512,1]{1,0:T(8,128)S(1)} %get-tuple-element.49.scale_ref, f32[256,256]{1,0:T(8,128)S(1)} %pad_maximum_fusion.refs_0_, ...), custom_call_target="tpu_custom_call" | custom-call | flops 5000000000 | bytes 1048576 | tf_op jit(solution)/shard_map/solve_near/pallas_call | solution.py:320
  67.6 2.5 %collective-permute-done.13.refs_2_ = f32[128,256]{1,0:T(8,128)S(1)} collective-permute-done((f32[128,256]{1,0:T(8,128)S(1)}, f32[128,256]{1,0:T(8,128)S(1)}, u32[]{:S(2)}, u32[]{:S(2)}) %collective-permute-start.13) | collective-permute-done | bytes 131104 | tf_op jit(solution)/shard_map/ppermute | solution.py:353
  70.1 2.2 %collective-permute-done.14.refs_3_ = f32[128,256]{1,0:T(8,128)S(1)} collective-permute-done((f32[128,256]{1,0:T(8,128)S(1)}, f32[128,256]{1,0:T(8,128)S(1)}, u32[]{:S(2)}, u32[]{:S(2)}) %collective-permute-start.14) | collective-permute-done | bytes 131104 | tf_op jit(solution)/shard_map/ppermute | solution.py:353
  (40 shorter events, 7.5 us)
Async XLA Ops:
  0.6 0.9 %copy-start.1 = (f32[24,2048]{1,0:T(8,128)S(1)}, f32[24,2048]{1,0:T(8,128)}, u32[]{:S(2)}) copy-start(f32[24,2048]{1,0:T(8,128)} %points_ref.1) | copy-start | bytes 589828
  1.6 0.7 copy-start.2
  5.3 5.5 %collective-permute-start = (f32[32,640]{1,0:T(8,128)S(1)}, f32[32,640]{1,0:T(8,128)S(1)}, u32[]{:S(2)}, u32[]{:S(2)}) collective-permute-start(f32[32,640]{1,0:T(8,128)S(1)} %dynamic-slice_bitcast_fusion.1), channel_id=1, source_target_pairs={{0,4},{4,0},{8,12},{12,8},{16,20},{20,16},{24,28},{28,24},{1,5},{5... | collective-permute-start | bytes 245768 | tf_op jit(solution)/shard_map/ppermute | solution.py:353
  8.3 1.2 %copy-start = (bf16[2048,256]{1,0:T(8,128)(2,1)S(1)}, bf16[2048,256]{1,0:T(8,128)(2,1)}, u32[]{:S(2)}) copy-start(bf16[2048,256]{1,0:T(8,128)(2,1)} %yields_ref.1) | copy-start | bytes 3145732
  10.8 4.1 %collective-permute-start.1 = (f32[16,640]{1,0:T(8,128)S(1)}, f32[16,640]{1,0:T(8,128)S(1)}, u32[]{:S(2)}, u32[]{:S(2)}) collective-permute-start(f32[16,640]{1,0:T(8,128)S(1)} %dynamic-slice_bitcast_fusion.3), channel_id=1, source_target_pairs={{0,8},{4,12},{8,0},{12,4},{16,24},{20,28},{24,16},{28,20},{1,9},{5... | collective-permute-start | bytes 122888 | tf_op jit(solution)/shard_map/ppermute | solution.py:353
  12.9 6.9 %collective-permute-start.3 = (f32[256,256]{1,0:T(8,128)S(1)}, f32[256,256]{1,0:T(8,128)S(1)}, u32[]{:S(2)}, u32[]{:S(2)}) collective-permute-start(f32[256,256]{1,0:T(8,128)S(1)} %get-tuple-element.35), channel_id=1, source_target_pairs={{0,4},{4,0},{8,12},{12,8},{16,20},{20,16},{24,28},{28,24},{1,5},{5... | collective-permute-start | bytes 786440 | tf_op jit(solution)/shard_map/ppermute | solution.py:353
  14.9 4.9 %collective-permute-start.2 = (f32[8,640]{1,0:T(8,128)S(1)}, f32[8,640]{1,0:T(8,128)S(1)}, u32[]{:S(2)}, u32[]{:S(2)}) collective-permute-start(f32[8,640]{1,0:T(8,128)S(1)} %dynamic-slice_bitcast_fusion.4), channel_id=1, source_target_pairs={{0,16},{4,20},{8,24},{12,28},{16,0},{20,4},{24,8},{28,12},{1,17},{... | collective-permute-start | bytes 61448 | tf_op jit(solution)/shard_map/ppermute | solution.py:353
  19.8 7.7 %collective-permute-start.4 = (f32[128,256]{1,0:T(8,128)S(1)}, f32[128,256]{1,0:T(8,128)S(1)}, u32[]{:S(2)}, u32[]{:S(2)}) collective-permute-start(f32[128,256]{1,0:T(8,128)S(1)} %dynamic-slice_bitcast_fusion), channel_id=1, source_target_pairs={{0,8},{4,12},{8,0},{12,4},{16,24},{20,28},{24,16},{28,20},{1,9},{5... | collective-permute-start | bytes 393224 | tf_op jit(solution)/shard_map/ppermute | solution.py:353
  22.5 12.9 %all-to-all-start = ((f32[8,8,640]{2,1,0:T(8,128)}), f32[8,8,640]{2,1,0:T(8,128)S(1)}, u32[]{:S(2)}, u32[]{:S(2)}) async-start(f32[8,8,640]{2,1,0:T(8,128)} %broadcast_in_dim.2), calls=%async_computation | async-start | bytes 327680 | tf_op jit(solution)/shard_map/all_to_all | solution.py:393
  35.4 5.3 %collective-permute-start.5 = (f32[64,640]{1,0:T(8,128)S(1)}, f32[64,640]{1,0:T(8,128)S(1)}, u32[]{:S(2)}, u32[]{:S(2)}) collective-permute-start(f32[64,640]{1,0:T(8,128)S(1)} %bitcast.33), channel_id=1, source_target_pairs={{0,2},{1,3},{2,0},{3,1},{4,6},{5,7},{6,4},{7,5},{8,10},{9,11},{10,... | collective-permute-start | bytes 491528 | tf_op jit(solution)/shard_map/ppermute | solution.py:353
  37.2 5.6 %collective-permute-start.8 = (f32[64,256]{1,0:T(8,128)S(1)}, f32[64,256]{1,0:T(8,128)S(1)}, u32[]{:S(2)}, u32[]{:S(2)}) collective-permute-start(f32[64,256]{1,0:T(8,128)S(1)} %dynamic-slice_bitcast_fusion.2), channel_id=1, source_target_pairs={{0,16},{4,20},{8,24},{12,28},{16,0},{20,4},{24,8},{28,12},{1,17},{... | collective-permute-start | bytes 196616 | tf_op jit(solution)/shard_map/ppermute | solution.py:353
  38.0 4.9 %collective-permute-start.6 = (f32[64,640]{1,0:T(8,128)S(1)}, f32[64,640]{1,0:T(8,128)S(1)}, u32[]{:S(2)}, u32[]{:S(2)}) collective-permute-start(f32[64,640]{1,0:T(8,128)S(1)} %bitcast.34), channel_id=1, source_target_pairs={{0,1},{1,0},{2,3},{3,2},{4,5},{5,4},{6,7},{7,6},{8,9},{9,8},{10,11... | collective-permute-start | bytes 491528 | tf_op jit(solution)/shard_map/ppermute | solution.py:353
  40.7 2.1 %collective-permute-start.7 = (f32[64,640]{1,0:T(8,128)S(1)}, f32[64,640]{1,0:T(8,128)S(1)}, u32[]{:S(2)}, u32[]{:S(2)}) collective-permute-start(f32[64,640]{1,0:T(8,128)S(1)} %collective-permute-done.5.refs_2_), channel_id=1, source_target_pairs={{0,1},{1,0},{2,3},{3,2},{4,5},{5,4},{6,7},{7,6},{8,9},{9,8},{10,11... | collective-permute-start | bytes 491528 | tf_op jit(solution)/shard_map/ppermute | solution.py:353
  42.9 5.3 %collective-permute-start.9 = (f32[64,256]{1,0:T(8,128)S(1)}, f32[64,256]{1,0:T(8,128)S(1)}, u32[]{:S(2)}, u32[]{:S(2)}) collective-permute-start(f32[64,256]{1,0:T(8,128)S(1)} %bitcast_add_fusion.2), channel_id=1, source_target_pairs={{0,16},{4,20},{8,24},{12,28},{16,0},{20,4},{24,8},{28,12},{1,17},{... | collective-permute-start | bytes 196616 | tf_op jit(solution)/shard_map/ppermute | solution.py:353
  48.2 5.0 %collective-permute-start.10 = (f32[128,256]{1,0:T(8,128)S(1)}, f32[128,256]{1,0:T(8,128)S(1)}, u32[]{:S(2)}, u32[]{:S(2)}) collective-permute-start(f32[128,256]{1,0:T(8,128)S(1)} %pad_maximum_fusion.1), channel_id=1, source_target_pairs={{0,8},{4,12},{8,0},{12,4},{16,24},{20,28},{24,16},{28,20},{1,9},{5... | collective-permute-start | bytes 393224 | tf_op jit(solution)/shard_map/ppermute | solution.py:353
  53.2 8.8 %collective-permute-start.11 = (f32[256,256]{1,0:T(8,128)S(1)}, f32[256,256]{1,0:T(8,128)S(1)}, u32[]{:S(2)}, u32[]{:S(2)}) collective-permute-start(f32[256,256]{1,0:T(8,128)S(1)} %pad_maximum_fusion.refs_0_), channel_id=1, source_target_pairs={{0,4},{4,0},{8,12},{12,8},{16,20},{20,16},{24,28},{28,24},{1,5},{5... | collective-permute-start | bytes 786440 | tf_op jit(solution)/shard_map/ppermute | solution.py:353
  58.4 3.7 %copy-start.3 = (s32[8]{0:T(128)S(1)}, s32[8]{0:T(128)}, u32[]{:S(2)}) copy-start(s32[8]{0:T(128)} %group_ref.3) | copy-start | bytes 100
  63.6 4.0 %collective-permute-start.12 = (f32[128,256]{1,0:T(8,128)S(1)}, f32[128,256]{1,0:T(8,128)S(1)}, u32[]{:S(2)}, u32[]{:S(2)}) collective-permute-start(f32[128,256]{1,0:T(8,128)S(1)} %get-tuple-element.51.refs_2_), channel_id=1, source_target_pairs={{0,1},{1,0},{2,3},{3,2},{4,5},{5,4},{6,7},{7,6},{8,9},{9,8},{10,11... | collective-permute-start | bytes 393224 | tf_op jit(solution)/shard_map/ppermute | solution.py:353
  63.7 6.4 %collective-permute-start.13 = (f32[128,256]{1,0:T(8,128)S(1)}, f32[128,256]{1,0:T(8,128)S(1)}, u32[]{:S(2)}, u32[]{:S(2)}) collective-permute-start(f32[128,256]{1,0:T(8,128)S(1)} %get-tuple-element.52.refs_3_), channel_id=1, source_target_pairs={{0,2},{1,3},{2,0},{3,1},{4,6},{5,7},{6,4},{7,5},{8,10},{9,11},{10,... | collective-permute-start | bytes 393224 | tf_op jit(solution)/shard_map/ppermute | solution.py:353
  65.7 6.6 %collective-permute-start.14 = (f32[128,256]{1,0:T(8,128)S(1)}, f32[128,256]{1,0:T(8,128)S(1)}, u32[]{:S(2)}, u32[]{:S(2)}) collective-permute-start(f32[128,256]{1,0:T(8,128)S(1)} %get-tuple-element.53.refs_4_), channel_id=1, source_target_pairs={{0,3},{1,2},{2,1},{3,0},{4,7},{5,6},{6,5},{7,4},{8,11},{9,10},{10,... | collective-permute-start | bytes 393224 | tf_op jit(solution)/shard_map/ppermute | solution.py:353

commit v9 on v8

--- a/solution.py
+++ b/solution.py
@@ -147,7 +147,7 @@
             second = a * columns[q] - b * columns[p]
             first = jnp.where(subs == p, det - d, jnp.where(subs == q, b, first))
             second = jnp.where(subs == p, b, jnp.where(subs == q, det - a, second))
-            inverse = 1.0 / det
+            inverse = pltpu.reciprocal(det, approx=True)
             for k in range(q + 1, 8):
                 less = first * row_of(columns[k], p) + second * row_of(columns[k], q)
                 columns[k] = columns[k] - less * inverse
@@ -158,8 +158,10 @@
         for other in range(len(bands)):
             value = jnp.where(inside, 0.0, bands[other])
             if other == following:
-                for k in range(8):
-                    value = value - lane_of(bands[other], base + k) * row_of(fresh, k)
+                terms = [lane_of(bands[other], base + k) * row_of(fresh, k) for k in range(8)]
+                while len(terms) > 1:
+                    terms = [terms[k] + terms[k + 1] for k in range(0, len(terms), 2)]
+                value = value - terms[0]
             else:
                 value = value - delta[8 * other:8 * other + 8]
             bands[other] = value
@@ -276,11 +278,11 @@
     others = refs[2:-(count + finish + 1)]
     cross_ref = refs[-1]
     shares = refs[-(count + finish + 1):-(finish + 1)]
-    step = 0
+    steps_back = [0, 1, 4, 5, 2, 3, 6, 7]
     for ref in pieces:
         for at in range(0, ref.shape[0], rows):
-            cross_ref[pl.ds(pl.multiple_of((where_ref[0] ^ step) * rows, rows), rows), :] = ref[at:at + rows, :]
-            step += 1
+            place = (where_ref[0] ^ steps_back.pop(0)) * rows
+            cross_ref[pl.ds(pl.multiple_of(place, rows), rows), :] = ref[at:at + rows, :]
     terms, cells = cross_ref.shape
     scaled = scale_ref[...] * cross_ref[...]
     size = jnp.sqrt(jnp.float32(samples))
@@ -404,10 +406,10 @@
     gram, scale = first_block(cell.reshape(1), [held[order.index(at)] for at in range(n_cell)], term_index.shape[0])
     for block in range(1, blocks):
         if block <= 2:
-            part = join(part, 8 >> block)
+            part = join(part, (4, 1)[block - 1])
             gram, part = lax.optimization_barrier((gram, part))
         gram = next_block(gram, block)
-    pieces = [part, swap(part, "samp", 1)]
+    pieces = [part, swap(part, "samp", 2)]
     where = jnp.stack([spot, cell])
     given = (where, gram, scale, pieces, rows, block_group, points.shape[1] * n_samp, n_cell)
     far = solve(*given, tuple(range(1, n_cell)))

time: 73.5 us -> 72.5 us (0.986)
  waiting for transfers between devices: 22.5 us -> 21.2 us
    ppermute x15, waiting for transfers between devices: 14.7 us -> 13.4 us  [swap(): return lax.ppermute(values, axis, [(at, at ^ step) for at in range(size)])]
  transfers between devices with their start and end apart: 16 -> 16, of which waited for: 10 -> 9; matrix products, arithmetic and copies ran while one was open for 1% -> 1% of each run, Pallas kernels for 24% -> 24%
where the time goes in v9:
time: 72.5 us; the launch traced here: 72.2 us
  starting transfers between devices  23.8 us (33%)
  Pallas kernels  22.6 us (31%)
  waiting for transfers between devices  21.2 us (29%)
  local copies, waits for them, and re-layouts  3.58 us (5%)
  between operations  0.85 us (1%)
    ppermute x15, starting transfers between devices, swap(): return lax.ppermute(values, axis, [(at, at ^ step) for at in range(size)])  18.7 us
    ppermute x15, waiting for transfers between devices, swap(): return lax.ppermute(values, axis, [(at, at ^ step) for at in range(size)])  13.4 us
    pallas_call x3, Pallas kernels, next_block(): pl.pallas_call(functools.partial(next_kernel, block), out_shape=jax.Shape...  10.9 us
    all_to_all x1, waiting for transfers between devices, on_device(): lax.all_to_all(copies, 'samp', split_axis=0, concat_axis=0)[:8]  7.82 us
    all_to_all x1, starting transfers between devices, on_device(): lax.all_to_all(copies, 'samp', split_axis=0, concat_axis=0)[:8]  5.08 us
    pallas_call x1, Pallas kernels, first_block(): pl.pallas_call(first_kernel, out_shape=(jax.ShapeDtypeStruct((terms, term...  3.91 us
    pallas_call x2, Pallas kernels, solve(): pl.pallas_call(functools.partial(solve_kernel, samples, steps, rows, fini...  3.31 us
    pallas_call x1, Pallas kernels, design(): pl.pallas_call(functools.partial(design_kernel, 512), out_shape=(jax.Shap...  2.97 us
  transfers between devices with their start and end apart: 16, of which 9 were waited for; matrix products, arithmetic and copies ran while one was open for 1% of the time, Pallas kernels for 24%

profile of v9, /device:TPU:0, one launch (start us, length us, event | category | flops | bytes accessed | tf_op | source)
XLA Modules:
  0.0 72.2 jit_solution(6731443392700916609)
XLA Ops:
  2.3 3.0 %design.1 = (bf16[512,2048]{1,0:T(8,128)(2,1)S(1)}, f32[64,640]{1,0:T(8,128)S(1)}) custom-call(s32[1]{0:T(128)} %bitcast.cell_ref.where_ref, s32[2,512]{1,0:T(2,128)S(1)} %bitcast.38, f32[24,2048]{1,0:T(8,128)S(1)} %copy-done.1), custom_call_target="tpu_custom_call" | custom-call | tf_op jit(solution)/shard_map/design/pallas_call | solution.py:80
  5.3 3.0 %collective-permute-start = (f32[32,640]{1,0:T(8,128)S(1)}, f32[32,640]{1,0:T(8,128)S(1)}, u32[]{:S(2)}, u32[]{:S(2)}) collective-permute-start(f32[32,640]{1,0:T(8,128)S(1)} %dynamic-slice_bitcast_fusion.1), channel_id=1, source_target_pairs={{0,4},{4,0},{8,12},{12,8},{16,20},{20,16},{24,28},{28,24},{1,5},{5... | collective-permute-start | bytes 245768 | tf_op jit(solution)/shard_map/ppermute | solution.py:355
  8.3 1.2 %copy-done = bf16[2048,256]{1,0:T(8,128)(2,1)S(1)} copy-done((bf16[2048,256]{1,0:T(8,128)(2,1)S(1)}, bf16[2048,256]{1,0:T(8,128)(2,1)}, u32[]{:S(2)}) %copy-start) | copy-done | bytes 1048600
  10.8 2.1 %collective-permute-start.1 = (f32[16,640]{1,0:T(8,128)S(1)}, f32[16,640]{1,0:T(8,128)S(1)}, u32[]{:S(2)}, u32[]{:S(2)}) collective-permute-start(f32[16,640]{1,0:T(8,128)S(1)} %dynamic-slice_bitcast_fusion.3), channel_id=1, source_target_pairs={{0,8},{4,12},{8,0},{12,4},{16,24},{20,28},{24,16},{28,20},{1,9},{5... | collective-permute-start | bytes 122888 | tf_op jit(solution)/shard_map/ppermute | solution.py:355
  12.9 1.5 %collective-permute-start.3 = (f32[256,256]{1,0:T(8,128)S(1)}, f32[256,256]{1,0:T(8,128)S(1)}, u32[]{:S(2)}, u32[]{:S(2)}) collective-permute-start(f32[256,256]{1,0:T(8,128)S(1)} %get-tuple-element.35), channel_id=1, source_target_pairs={{0,4},{4,0},{8,12},{12,8},{16,20},{20,16},{24,28},{28,24},{1,5},{5... | collective-permute-start | bytes 786440 | tf_op jit(solution)/shard_map/ppermute | solution.py:355
  14.9 3.1 %collective-permute-start.2 = (f32[8,640]{1,0:T(8,128)S(1)}, f32[8,640]{1,0:T(8,128)S(1)}, u32[]{:S(2)}, u32[]{:S(2)}) collective-permute-start(f32[8,640]{1,0:T(8,128)S(1)} %dynamic-slice_bitcast_fusion.4), channel_id=1, source_target_pairs={{0,16},{4,20},{8,24},{12,28},{16,0},{20,4},{24,8},{28,12},{1,17},{... | collective-permute-start | bytes 61448 | tf_op jit(solution)/shard_map/ppermute | solution.py:355
  18.0 1.8 %collective-permute-done.2 = f32[8,640]{1,0:T(8,128)S(1)} collective-permute-done((f32[8,640]{1,0:T(8,128)S(1)}, f32[8,640]{1,0:T(8,128)S(1)}, u32[]{:S(2)}, u32[]{:S(2)}) %collective-permute-start.2) | collective-permute-done | bytes 20512 | tf_op jit(solution)/shard_map/ppermute | solution.py:355
  19.8 2.0 %collective-permute-start.4 = (f32[128,256]{1,0:T(8,128)S(1)}, f32[128,256]{1,0:T(8,128)S(1)}, u32[]{:S(2)}, u32[]{:S(2)}) collective-permute-start(f32[128,256]{1,0:T(8,128)S(1)} %dynamic-slice_bitcast_fusion), channel_id=1, source_target_pairs={{0,8},{4,12},{8,0},{12,4},{16,24},{20,28},{24,16},{28,20},{1,9},{5... | collective-permute-start | bytes 393224 | tf_op jit(solution)/shard_map/ppermute | solution.py:355
  22.5 5.1 %all-to-all-start = ((f32[8,8,640]{2,1,0:T(8,128)}), f32[8,8,640]{2,1,0:T(8,128)S(1)}, u32[]{:S(2)}, u32[]{:S(2)}) async-start(f32[8,8,640]{2,1,0:T(8,128)} %broadcast_in_dim.2), calls=%async_computation | async-start | bytes 327680 | tf_op jit(solution)/shard_map/all_to_all | solution.py:395
  27.6 7.8 %all-to-all-done = f32[8,8,640]{2,1,0:T(8,128)S(1)} async-done(((f32[8,8,640]{2,1,0:T(8,128)}), f32[8,8,640]{2,1,0:T(8,128)S(1)}, u32[]{:S(2)}, u32[]{:S(2)}) %all-to-all-start) | async-done | bytes 163872 | tf_op jit(solution)/shard_map/all_to_all | solution.py:395
  35.4 1.8 %collective-permute-start.5 = (f32[64,640]{1,0:T(8,128)S(1)}, f32[64,640]{1,0:T(8,128)S(1)}, u32[]{:S(2)}, u32[]{:S(2)}) collective-permute-start(f32[64,640]{1,0:T(8,128)S(1)} %bitcast.33), channel_id=1, source_target_pairs={{0,2},{1,3},{2,0},{3,1},{4,6},{5,7},{6,4},{7,5},{8,10},{9,11},{10,... | collective-permute-start | bytes 491528 | tf_op jit(solution)/shard_map/ppermute | solution.py:355
  38.0 2.8 %collective-permute-done.5.refs_2_ = f32[64,640]{1,0:T(8,128)S(1)} collective-permute-done((f32[64,640]{1,0:T(8,128)S(1)}, f32[64,640]{1,0:T(8,128)S(1)}, u32[]{:S(2)}, u32[]{:S(2)}) %collective-permute-start.5) | collective-permute-done | bytes 163872 | tf_op jit(solution)/shard_map/ppermute | solution.py:355
  40.8 2.1 %collective-permute-done.8 = f32[64,256]{1,0:T(8,128)S(1)} collective-permute-done((f32[64,256]{1,0:T(8,128)S(1)}, f32[64,256]{1,0:T(8,128)S(1)}, u32[]{:S(2)}, u32[]{:S(2)}) %collective-permute-start.8) | collective-permute-done | bytes 65568 | tf_op jit(solution)/shard_map/ppermute | solution.py:355
  43.2 3.9 %block_0.1 = (f32[512,512]{1,0:T(8,128)S(1)}, f32[512,1]{1,0:T(8,128)S(1)}) custom-call(s32[1]{0:T(128)} %bitcast.cell_ref.where_ref, f32[64,640]{1,0:T(8,128)S(1)} %bitcast.35, f32[64,640]{1,0:T(8,128)S(1)} %collective-permute-done.6.refs_1_, f32[64,640]{1,0:T(8,128)S(1)} %collective-permute-done.5.refs_2_, f32[64,640]{1,0:T(8,128)S(1)} %collective-permute-done.7.refs_3_), custom_call_target="tpu_custom_call" | custom-call | flops 1000000000 | bytes 1048576 | tf_op jit(solution)/shard_map/block_0/pallas_call | solution.py:248
  47.2 1.0 %collective-permute-done.9 = f32[64,256]{1,0:T(8,128)S(1)} collective-permute-done((f32[64,256]{1,0:T(8,128)S(1)}, f32[64,256]{1,0:T(8,128)S(1)}, u32[]{:S(2)}, u32[]{:S(2)}) %collective-permute-start.9) | collective-permute-done | bytes 65568 | tf_op jit(solution)/shard_map/ppermute | solution.py:355
  48.2 1.4 %collective-permute-start.10 = (f32[128,256]{1,0:T(8,128)S(1)}, f32[128,256]{1,0:T(8,128)S(1)}, u32[]{:S(2)}, u32[]{:S(2)}) collective-permute-start(f32[128,256]{1,0:T(8,128)S(1)} %pad_maximum_fusion.1), channel_id=1, source_target_pairs={{0,4},{4,0},{8,12},{12,8},{16,20},{20,16},{24,28},{28,24},{1,5},{5... | collective-permute-start | bytes 393224 | tf_op jit(solution)/shard_map/ppermute | solution.py:355
  49.6 3.6 %block_1.1.in_ref = f32[512,512]{1,0:T(8,128)S(1)} custom-call(f32[512,512]{1,0:T(8,128)S(1)} %get-tuple-element.46.in_ref), custom_call_target="tpu_custom_call" | custom-call | flops 1000000000 | bytes 1048576 | tf_op jit(solution)/shard_map/block_1/pallas_call | solution.py:264
  53.6 3.6 %block_2.1.in_ref = f32[512,512]{1,0:T(8,128)S(1)} custom-call(f32[512,512]{1,0:T(8,128)S(1)} %block_1.1.in_ref), custom_call_target="tpu_custom_call" | custom-call | flops 1000000000 | bytes 1048576 | tf_op jit(solution)/shard_map/block_2/pallas_call | solution.py:264
  57.3 3.6 %block_3.1.inverse_ref = f32[512,512]{1,0:T(8,128)S(1)} custom-call(f32[512,512]{1,0:T(8,128)S(1)} %block_2.1.in_ref), custom_call_target="tpu_custom_call" | custom-call | flops 1000000000 | bytes 1048576 | tf_op jit(solution)/shard_map/block_3/pallas_call | solution.py:264
  60.9 1.5 %solve_far.1 = (f32[128,256]{1,0:T(8,128)S(1)}, f32[128,256]{1,0:T(8,128)S(1)}, f32[128,256]{1,0:T(8,128)S(1)}) custom-call(s32[2]{0:T(128)S(1)} %pad_add_fusion.where_ref, s32[8]{0:T(128)S(1)} %copy-done.3, f32[512,512]{1,0:T(8,128)S(1)} %block_3.1.inverse_ref, f32[512,1]{1,0:T(8,128)S(1)} %get-tuple-element.49.scale_ref, ...), custom_call_target="tpu_custom_call" | custom-call | flops 1000000000 | bytes 1048576 | tf_op jit(solution)/shard_map/solve_far/pallas_call | solution.py:322
  62.5 2.2 %collective-permute-start.13 = (f32[128,256]{1,0:T(8,128)S(1)}, f32[128,256]{1,0:T(8,128)S(1)}, u32[]{:S(2)}, u32[]{:S(2)}) collective-permute-start(f32[128,256]{1,0:T(8,128)S(1)} %get-tuple-element.52.refs_3_), channel_id=1, source_target_pairs={{0,2},{1,3},{2,0},{3,1},{4,6},{5,7},{6,4},{7,5},{8,10},{9,11},{10,... | collective-permute-start | bytes 393224 | tf_op jit(solution)/shard_map/ppermute | solution.py:355
  64.8 1.8 %solve_near.1 = (f32[128,256]{1,0:T(8,128)S(1)}, f32[8,256]{1,0:T(8,128)}) custom-call(s32[2]{0:T(128)S(1)} %pad_add_fusion.where_ref, s32[8]{0:T(128)S(1)} %copy-done.3, f32[512,512]{1,0:T(8,128)S(1)} %block_3.1.inverse_ref, f32[512,1]{1,0:T(8,128)S(1)} %get-tuple-element.49.scale_ref, f32[256,256]{1,0:T(8,128)S(1)} %pad_maximum_fusion.refs_0_, ...), custom_call_target="tpu_custom_call" | custom-call | flops 5000000000 | bytes 1048576 | tf_op jit(solution)/shard_map/solve_near/pallas_call | solution.py:322
  66.6 2.5 %collective-permute-done.13.refs_2_ = f32[128,256]{1,0:T(8,128)S(1)} collective-permute-done((f32[128,256]{1,0:T(8,128)S(1)}, f32[128,256]{1,0:T(8,128)S(1)}, u32[]{:S(2)}, u32[]{:S(2)}) %collective-permute-start.13) | collective-permute-done | bytes 131104 | tf_op jit(solution)/shard_map/ppermute | solution.py:355
  69.1 2.3 %collective-permute-done.14.refs_3_ = f32[128,256]{1,0:T(8,128)S(1)} collective-permute-done((f32[128,256]{1,0:T(8,128)S(1)}, f32[128,256]{1,0:T(8,128)S(1)}, u32[]{:S(2)}, u32[]{:S(2)}) %collective-permute-start.14) | collective-permute-done | bytes 131104 | tf_op jit(solution)/shard_map/ppermute | solution.py:355
  (40 shorter events, 6.6 us)
Async XLA Ops:
  0.6 0.9 %copy-start.1 = (f32[24,2048]{1,0:T(8,128)S(1)}, f32[24,2048]{1,0:T(8,128)}, u32[]{:S(2)}) copy-start(f32[24,2048]{1,0:T(8,128)} %points_ref.1) | copy-start | bytes 589828
  1.6 0.7 copy-start.2
  5.3 5.5 %collective-permute-start = (f32[32,640]{1,0:T(8,128)S(1)}, f32[32,640]{1,0:T(8,128)S(1)}, u32[]{:S(2)}, u32[]{:S(2)}) collective-permute-start(f32[32,640]{1,0:T(8,128)S(1)} %dynamic-slice_bitcast_fusion.1), channel_id=1, source_target_pairs={{0,4},{4,0},{8,12},{12,8},{16,20},{20,16},{24,28},{28,24},{1,5},{5... | collective-permute-start | bytes 245768 | tf_op jit(solution)/shard_map/ppermute | solution.py:355
  8.3 1.2 %copy-start = (bf16[2048,256]{1,0:T(8,128)(2,1)S(1)}, bf16[2048,256]{1,0:T(8,128)(2,1)}, u32[]{:S(2)}) copy-start(bf16[2048,256]{1,0:T(8,128)(2,1)} %yields_ref.1) | copy-start | bytes 3145732
  10.8 4.1 %collective-permute-start.1 = (f32[16,640]{1,0:T(8,128)S(1)}, f32[16,640]{1,0:T(8,128)S(1)}, u32[]{:S(2)}, u32[]{:S(2)}) collective-permute-start(f32[16,640]{1,0:T(8,128)S(1)} %dynamic-slice_bitcast_fusion.3), channel_id=1, source_target_pairs={{0,8},{4,12},{8,0},{12,4},{16,24},{20,28},{24,16},{28,20},{1,9},{5... | collective-permute-start | bytes 122888 | tf_op jit(solution)/shard_map/ppermute | solution.py:355
  12.9 6.9 %collective-permute-start.3 = (f32[256,256]{1,0:T(8,128)S(1)}, f32[256,256]{1,0:T(8,128)S(1)}, u32[]{:S(2)}, u32[]{:S(2)}) collective-permute-start(f32[256,256]{1,0:T(8,128)S(1)} %get-tuple-element.35), channel_id=1, source_target_pairs={{0,4},{4,0},{8,12},{12,8},{16,20},{20,16},{24,28},{28,24},{1,5},{5... | collective-permute-start | bytes 786440 | tf_op jit(solution)/shard_map/ppermute | solution.py:355
  14.9 4.9 %collective-permute-start.2 = (f32[8,640]{1,0:T(8,128)S(1)}, f32[8,640]{1,0:T(8,128)S(1)}, u32[]{:S(2)}, u32[]{:S(2)}) collective-permute-start(f32[8,640]{1,0:T(8,128)S(1)} %dynamic-slice_bitcast_fusion.4), channel_id=1, source_target_pairs={{0,16},{4,20},{8,24},{12,28},{16,0},{20,4},{24,8},{28,12},{1,17},{... | collective-permute-start | bytes 61448 | tf_op jit(solution)/shard_map/ppermute | solution.py:355
  19.8 7.7 %collective-permute-start.4 = (f32[128,256]{1,0:T(8,128)S(1)}, f32[128,256]{1,0:T(8,128)S(1)}, u32[]{:S(2)}, u32[]{:S(2)}) collective-permute-start(f32[128,256]{1,0:T(8,128)S(1)} %dynamic-slice_bitcast_fusion), channel_id=1, source_target_pairs={{0,8},{4,12},{8,0},{12,4},{16,24},{20,28},{24,16},{28,20},{1,9},{5... | collective-permute-start | bytes 393224 | tf_op jit(solution)/shard_map/ppermute | solution.py:355
  22.5 12.9 %all-to-all-start = ((f32[8,8,640]{2,1,0:T(8,128)}), f32[8,8,640]{2,1,0:T(8,128)S(1)}, u32[]{:S(2)}, u32[]{:S(2)}) async-start(f32[8,8,640]{2,1,0:T(8,128)} %broadcast_in_dim.2), calls=%async_computation | async-start | bytes 327680 | tf_op jit(solution)/shard_map/all_to_all | solution.py:395
  35.4 5.3 %collective-permute-start.5 = (f32[64,640]{1,0:T(8,128)S(1)}, f32[64,640]{1,0:T(8,128)S(1)}, u32[]{:S(2)}, u32[]{:S(2)}) collective-permute-start(f32[64,640]{1,0:T(8,128)S(1)} %bitcast.33), channel_id=1, source_target_pairs={{0,2},{1,3},{2,0},{3,1},{4,6},{5,7},{6,4},{7,5},{8,10},{9,11},{10,... | collective-permute-start | bytes 491528 | tf_op jit(solution)/shard_map/ppermute | solution.py:355
  37.2 5.6 %collective-permute-start.8 = (f32[64,256]{1,0:T(8,128)S(1)}, f32[64,256]{1,0:T(8,128)S(1)}, u32[]{:S(2)}, u32[]{:S(2)}) collective-permute-start(f32[64,256]{1,0:T(8,128)S(1)} %dynamic-slice_bitcast_fusion.2), channel_id=1, source_target_pairs={{0,16},{4,20},{8,24},{12,28},{16,0},{20,4},{24,8},{28,12},{1,17},{... | collective-permute-start | bytes 196616 | tf_op jit(solution)/shard_map/ppermute | solution.py:355
  38.0 4.9 %collective-permute-start.6 = (f32[64,640]{1,0:T(8,128)S(1)}, f32[64,640]{1,0:T(8,128)S(1)}, u32[]{:S(2)}, u32[]{:S(2)}) collective-permute-start(f32[64,640]{1,0:T(8,128)S(1)} %bitcast.34), channel_id=1, source_target_pairs={{0,1},{1,0},{2,3},{3,2},{4,5},{5,4},{6,7},{7,6},{8,9},{9,8},{10,11... | collective-permute-start | bytes 491528 | tf_op jit(solution)/shard_map/ppermute | solution.py:355
  40.7 2.1 %collective-permute-start.7 = (f32[64,640]{1,0:T(8,128)S(1)}, f32[64,640]{1,0:T(8,128)S(1)}, u32[]{:S(2)}, u32[]{:S(2)}) collective-permute-start(f32[64,640]{1,0:T(8,128)S(1)} %collective-permute-done.5.refs_2_), channel_id=1, source_target_pairs={{0,1},{1,0},{2,3},{3,2},{4,5},{5,4},{6,7},{7,6},{8,9},{9,8},{10,11... | collective-permute-start | bytes 491528 | tf_op jit(solution)/shard_map/ppermute | solution.py:355
  42.9 5.3 %collective-permute-start.9 = (f32[64,256]{1,0:T(8,128)S(1)}, f32[64,256]{1,0:T(8,128)S(1)}, u32[]{:S(2)}, u32[]{:S(2)}) collective-permute-start(f32[64,256]{1,0:T(8,128)S(1)} %bitcast_add_fusion.2), channel_id=1, source_target_pairs={{0,16},{4,20},{8,24},{12,28},{16,0},{20,4},{24,8},{28,12},{1,17},{... | collective-permute-start | bytes 196616 | tf_op jit(solution)/shard_map/ppermute | solution.py:355
  48.2 5.0 %collective-permute-start.10 = (f32[128,256]{1,0:T(8,128)S(1)}, f32[128,256]{1,0:T(8,128)S(1)}, u32[]{:S(2)}, u32[]{:S(2)}) collective-permute-start(f32[128,256]{1,0:T(8,128)S(1)} %pad_maximum_fusion.1), channel_id=1, source_target_pairs={{0,4},{4,0},{8,12},{12,8},{16,20},{20,16},{24,28},{28,24},{1,5},{5... | collective-permute-start | bytes 393224 | tf_op jit(solution)/shard_map/ppermute | solution.py:355
  53.2 7.7 %collective-permute-start.11 = (f32[256,256]{1,0:T(8,128)S(1)}, f32[256,256]{1,0:T(8,128)S(1)}, u32[]{:S(2)}, u32[]{:S(2)}) collective-permute-start(f32[256,256]{1,0:T(8,128)S(1)} %pad_maximum_fusion.refs_0_), channel_id=1, source_target_pairs={{0,8},{4,12},{8,0},{12,4},{16,24},{20,28},{24,16},{28,20},{1,9},{5... | collective-permute-start | bytes 786440 | tf_op jit(solution)/shard_map/ppermute | solution.py:355
  57.3 3.7 %copy-start.3 = (s32[8]{0:T(128)S(1)}, s32[8]{0:T(128)}, u32[]{:S(2)}) copy-start(s32[8]{0:T(128)} %group_ref.3) | copy-start | bytes 100
  62.5 4.2 %collective-permute-start.12 = (f32[128,256]{1,0:T(8,128)S(1)}, f32[128,256]{1,0:T(8,128)S(1)}, u32[]{:S(2)}, u32[]{:S(2)}) collective-permute-start(f32[128,256]{1,0:T(8,128)S(1)} %get-tuple-element.51.refs_2_), channel_id=1, source_target_pairs={{0,1},{1,0},{2,3},{3,2},{4,5},{5,4},{6,7},{7,6},{8,9},{9,8},{10,11... | collective-permute-start | bytes 393224 | tf_op jit(solution)/shard_map/ppermute | solution.py:355
  62.5 6.6 %collective-permute-start.13 = (f32[128,256]{1,0:T(8,128)S(1)}, f32[128,256]{1,0:T(8,128)S(1)}, u32[]{:S(2)}, u32[]{:S(2)}) collective-permute-start(f32[128,256]{1,0:T(8,128)S(1)} %get-tuple-element.52.refs_3_), channel_id=1, source_target_pairs={{0,2},{1,3},{2,0},{3,1},{4,6},{5,7},{6,4},{7,5},{8,10},{9,11},{10,... | collective-permute-start | bytes 393224 | tf_op jit(solution)/shard_map/ppermute | solution.py:355
  64.8 6.6 %collective-permute-start.14 = (f32[128,256]{1,0:T(8,128)S(1)}, f32[128,256]{1,0:T(8,128)S(1)}, u32[]{:S(2)}, u32[]{:S(2)}) collective-permute-start(f32[128,256]{1,0:T(8,128)S(1)} %get-tuple-element.53.refs_4_), channel_id=1, source_target_pairs={{0,3},{1,2},{2,1},{3,0},{4,7},{5,6},{6,5},{7,4},{8,11},{9,10},{10,... | collective-permute-start | bytes 393224 | tf_op jit(solution)/shard_map/ppermute | solution.py:355

commit v10 on v9

--- a/solution.py
+++ b/solution.py
@@ -147,17 +147,17 @@
             second = a * columns[q] - b * columns[p]
             first = jnp.where(subs == p, det - d, jnp.where(subs == q, b, first))
             second = jnp.where(subs == p, b, jnp.where(subs == q, det - a, second))
-            inverse = pltpu.reciprocal(det, approx=True)
+            inverse = 1.0 / det
             for k in range(q + 1, 8):
                 less = first * row_of(columns[k], p) + second * row_of(columns[k], q)
                 columns[k] = columns[k] - less * inverse
             less = first * row_of(fresh, p) + second * row_of(fresh, q)
             fresh = fresh - less * inverse
         delta = stacked_outer(own, fresh)
-        following = (at + 1) % len(bands)
+        following = ((at + 1) % len(bands), (at + 2) % len(bands))
         for other in range(len(bands)):
             value = jnp.where(inside, 0.0, bands[other])
-            if other == following:
+            if other in following:
                 terms = [lane_of(bands[other], base + k) * row_of(fresh, k) for k in range(8)]
                 while len(terms) > 1:
                     terms = [terms[k] + terms[k + 1] for k in range(0, len(terms), 2)]

time: 72.5 us -> 72.6 us (level)
  transfers between devices with their start and end apart: 16 -> 16, of which waited for: 9 -> 9; matrix products, arithmetic and copies ran while one was open for 1% -> 1% of each run, Pallas kernels for 24% -> 25%
where the time goes in v10:
time: 72.6 us; the launch traced here: 72.3 us
  starting transfers between devices  23.7 us (33%)
  Pallas kernels  23.1 us (32%)
  waiting for transfers between devices  20.9 us (29%)
  local copies, waits for them, and re-layouts  3.58 us (5%)
  between operations  0.85 us (1%)
    ppermute x15, starting transfers between devices, swap(): return lax.ppermute(values, axis, [(at, at ^ step) for at in range(size)])  18.6 us
    ppermute x15, waiting for transfers between devices, swap(): return lax.ppermute(values, axis, [(at, at ^ step) for at in range(size)])  13 us
    pallas_call x3, Pallas kernels, next_block(): pl.pallas_call(functools.partial(next_kernel, block), out_shape=jax.Shape...  11.2 us
    all_to_all x1, waiting for transfers between devices, on_device(): lax.all_to_all(copies, 'samp', split_axis=0, concat_axis=0)[:8]  7.82 us
    all_to_all x1, starting transfers between devices, on_device(): lax.all_to_all(copies, 'samp', split_axis=0, concat_axis=0)[:8]  5.08 us
    pallas_call x1, Pallas kernels, first_block(): pl.pallas_call(first_kernel, out_shape=(jax.ShapeDtypeStruct((terms, term...  4.13 us
    pallas_call x2, Pallas kernels, solve(): pl.pallas_call(functools.partial(solve_kernel, samples, steps, rows, fini...  3.31 us
    pallas_call x1, Pallas kernels, design(): pl.pallas_call(functools.partial(design_kernel, 512), out_shape=(jax.Shap...  2.97 us
  transfers between devices with their start and end apart: 16, of which 9 were waited for; matrix products, arithmetic and copies ran while one was open for 1% of the time, Pallas kernels for 25%

profile of v10, /device:TPU:0, one launch (start us, length us, event | category | flops | bytes accessed | tf_op | source)
XLA Modules:
  0.0 72.3 jit_solution(5542480503539033950)
XLA Ops:
  0.7 0.9 %copy-done.1 = f32[24,2048]{1,0:T(8,128)S(1)} copy-done((f32[24,2048]{1,0:T(8,128)S(1)}, f32[24,2048]{1,0:T(8,128)}, u32[]{:S(2)}) %copy-start.1) | copy-done | bytes 196632
  2.3 3.0 %design.1 = (bf16[512,2048]{1,0:T(8,128)(2,1)S(1)}, f32[64,640]{1,0:T(8,128)S(1)}) custom-call(s32[1]{0:T(128)} %bitcast.cell_ref.where_ref, s32[2,512]{1,0:T(2,128)S(1)} %bitcast.38, f32[24,2048]{1,0:T(8,128)S(1)} %copy-done.1), custom_call_target="tpu_custom_call" | custom-call | tf_op jit(solution)/shard_map/design/pallas_call | solution.py:80
  5.3 3.0 %collective-permute-start = (f32[32,640]{1,0:T(8,128)S(1)}, f32[32,640]{1,0:T(8,128)S(1)}, u32[]{:S(2)}, u32[]{:S(2)}) collective-permute-start(f32[32,640]{1,0:T(8,128)S(1)} %dynamic-slice_bitcast_fusion.1), channel_id=1, source_target_pairs={{0,4},{4,0},{8,12},{12,8},{16,20},{20,16},{24,28},{28,24},{1,5},{5... | collective-permute-start | bytes 245768 | tf_op jit(solution)/shard_map/ppermute | solution.py:355
  8.3 1.2 %copy-done = bf16[2048,256]{1,0:T(8,128)(2,1)S(1)} copy-done((bf16[2048,256]{1,0:T(8,128)(2,1)S(1)}, bf16[2048,256]{1,0:T(8,128)(2,1)}, u32[]{:S(2)}) %copy-start) | copy-done | bytes 1048600
  10.8 2.1 %collective-permute-start.1 = (f32[16,640]{1,0:T(8,128)S(1)}, f32[16,640]{1,0:T(8,128)S(1)}, u32[]{:S(2)}, u32[]{:S(2)}) collective-permute-start(f32[16,640]{1,0:T(8,128)S(1)} %dynamic-slice_bitcast_fusion.3), channel_id=1, source_target_pairs={{0,8},{4,12},{8,0},{12,4},{16,24},{20,28},{24,16},{28,20},{1,9},{5... | collective-permute-start | bytes 122888 | tf_op jit(solution)/shard_map/ppermute | solution.py:355
  12.9 1.5 %collective-permute-start.3 = (f32[256,256]{1,0:T(8,128)S(1)}, f32[256,256]{1,0:T(8,128)S(1)}, u32[]{:S(2)}, u32[]{:S(2)}) collective-permute-start(f32[256,256]{1,0:T(8,128)S(1)} %get-tuple-element.35), channel_id=1, source_target_pairs={{0,4},{4,0},{8,12},{12,8},{16,20},{20,16},{24,28},{28,24},{1,5},{5... | collective-permute-start | bytes 786440 | tf_op jit(solution)/shard_map/ppermute | solution.py:355
  14.9 3.1 %collective-permute-start.2 = (f32[8,640]{1,0:T(8,128)S(1)}, f32[8,640]{1,0:T(8,128)S(1)}, u32[]{:S(2)}, u32[]{:S(2)}) collective-permute-start(f32[8,640]{1,0:T(8,128)S(1)} %dynamic-slice_bitcast_fusion.4), channel_id=1, source_target_pairs={{0,16},{4,20},{8,24},{12,28},{16,0},{20,4},{24,8},{28,12},{1,17},{... | collective-permute-start | bytes 61448 | tf_op jit(solution)/shard_map/ppermute | solution.py:355
  18.0 1.8 %collective-permute-done.2 = f32[8,640]{1,0:T(8,128)S(1)} collective-permute-done((f32[8,640]{1,0:T(8,128)S(1)}, f32[8,640]{1,0:T(8,128)S(1)}, u32[]{:S(2)}, u32[]{:S(2)}) %collective-permute-start.2) | collective-permute-done | bytes 20512 | tf_op jit(solution)/shard_map/ppermute | solution.py:355
  19.8 2.0 %collective-permute-start.4 = (f32[128,256]{1,0:T(8,128)S(1)}, f32[128,256]{1,0:T(8,128)S(1)}, u32[]{:S(2)}, u32[]{:S(2)}) collective-permute-start(f32[128,256]{1,0:T(8,128)S(1)} %dynamic-slice_bitcast_fusion), channel_id=1, source_target_pairs={{0,8},{4,12},{8,0},{12,4},{16,24},{20,28},{24,16},{28,20},{1,9},{5... | collective-permute-start | bytes 393224 | tf_op jit(solution)/shard_map/ppermute | solution.py:355
  22.5 5.1 %all-to-all-start = ((f32[8,8,640]{2,1,0:T(8,128)}), f32[8,8,640]{2,1,0:T(8,128)S(1)}, u32[]{:S(2)}, u32[]{:S(2)}) async-start(f32[8,8,640]{2,1,0:T(8,128)} %broadcast_in_dim.2), calls=%async_computation | async-start | bytes 327680 | tf_op jit(solution)/shard_map/all_to_all | solution.py:395
  27.6 7.8 %all-to-all-done = f32[8,8,640]{2,1,0:T(8,128)S(1)} async-done(((f32[8,8,640]{2,1,0:T(8,128)}), f32[8,8,640]{2,1,0:T(8,128)S(1)}, u32[]{:S(2)}, u32[]{:S(2)}) %all-to-all-start) | async-done | bytes 163872 | tf_op jit(solution)/shard_map/all_to_all | solution.py:395
  35.4 1.8 %collective-permute-start.5 = (f32[64,640]{1,0:T(8,128)S(1)}, f32[64,640]{1,0:T(8,128)S(1)}, u32[]{:S(2)}, u32[]{:S(2)}) collective-permute-start(f32[64,640]{1,0:T(8,128)S(1)} %bitcast.33), channel_id=1, source_target_pairs={{0,2},{1,3},{2,0},{3,1},{4,6},{5,7},{6,4},{7,5},{8,10},{9,11},{10,... | collective-permute-start | bytes 491528 | tf_op jit(solution)/shard_map/ppermute | solution.py:355
  38.0 2.8 %collective-permute-done.5.refs_2_ = f32[64,640]{1,0:T(8,128)S(1)} collective-permute-done((f32[64,640]{1,0:T(8,128)S(1)}, f32[64,640]{1,0:T(8,128)S(1)}, u32[]{:S(2)}, u32[]{:S(2)}) %collective-permute-start.5) | collective-permute-done | bytes 163872 | tf_op jit(solution)/shard_map/ppermute | solution.py:355
  40.8 2.1 %collective-permute-done.8 = f32[64,256]{1,0:T(8,128)S(1)} collective-permute-done((f32[64,256]{1,0:T(8,128)S(1)}, f32[64,256]{1,0:T(8,128)S(1)}, u32[]{:S(2)}, u32[]{:S(2)}) %collective-permute-start.8) | collective-permute-done | bytes 65568 | tf_op jit(solution)/shard_map/ppermute | solution.py:355
  43.2 4.1 %block_0.1 = (f32[512,512]{1,0:T(8,128)S(1)}, f32[512,1]{1,0:T(8,128)S(1)}) custom-call(s32[1]{0:T(128)} %bitcast.cell_ref.where_ref, f32[64,640]{1,0:T(8,128)S(1)} %bitcast.35, f32[64,640]{1,0:T(8,128)S(1)} %collective-permute-done.6.refs_1_, f32[64,640]{1,0:T(8,128)S(1)} %collective-permute-done.5.refs_2_, f32[64,640]{1,0:T(8,128)S(1)} %collective-permute-done.7.refs_3_), custom_call_target="tpu_custom_call" | custom-call | flops 1000000000 | bytes 1048576 | tf_op jit(solution)/shard_map/block_0/pallas_call | solution.py:248
  48.2 1.4 %collective-permute-start.10 = (f32[128,256]{1,0:T(8,128)S(1)}, f32[128,256]{1,0:T(8,128)S(1)}, u32[]{:S(2)}, u32[]{:S(2)}) collective-permute-start(f32[128,256]{1,0:T(8,128)S(1)} %pad_maximum_fusion.1), channel_id=1, source_target_pairs={{0,4},{4,0},{8,12},{12,8},{16,20},{20,16},{24,28},{28,24},{1,5},{5... | collective-permute-start | bytes 393224 | tf_op jit(solution)/shard_map/ppermute | solution.py:355
  49.6 3.7 %block_1.1.in_ref = f32[512,512]{1,0:T(8,128)S(1)} custom-call(f32[512,512]{1,0:T(8,128)S(1)} %get-tuple-element.46.in_ref), custom_call_target="tpu_custom_call" | custom-call | flops 1000000000 | bytes 1048576 | tf_op jit(solution)/shard_map/block_1/pallas_call | solution.py:264
  53.9 3.7 %block_2.1.in_ref = f32[512,512]{1,0:T(8,128)S(1)} custom-call(f32[512,512]{1,0:T(8,128)S(1)} %block_1.1.in_ref), custom_call_target="tpu_custom_call" | custom-call | flops 1000000000 | bytes 1048576 | tf_op jit(solution)/shard_map/block_2/pallas_call | solution.py:264
  57.7 3.7 %block_3.1.inverse_ref = f32[512,512]{1,0:T(8,128)S(1)} custom-call(f32[512,512]{1,0:T(8,128)S(1)} %block_2.1.in_ref), custom_call_target="tpu_custom_call" | custom-call | flops 1000000000 | bytes 1048576 | tf_op jit(solution)/shard_map/block_3/pallas_call | solution.py:264
  61.4 1.5 %solve_far.1 = (f32[128,256]{1,0:T(8,128)S(1)}, f32[128,256]{1,0:T(8,128)S(1)}, f32[128,256]{1,0:T(8,128)S(1)}) custom-call(s32[2]{0:T(128)S(1)} %pad_add_fusion.where_ref, s32[8]{0:T(128)S(1)} %copy-done.3, f32[512,512]{1,0:T(8,128)S(1)} %block_3.1.inverse_ref, f32[512,1]{1,0:T(8,128)S(1)} %get-tuple-element.49.scale_ref, ...), custom_call_target="tpu_custom_call" | custom-call | flops 1000000000 | bytes 1048576 | tf_op jit(solution)/shard_map/solve_far/pallas_call | solution.py:322
  63.0 1.9 %collective-permute-start.13 = (f32[128,256]{1,0:T(8,128)S(1)}, f32[128,256]{1,0:T(8,128)S(1)}, u32[]{:S(2)}, u32[]{:S(2)}) collective-permute-start(f32[128,256]{1,0:T(8,128)S(1)} %get-tuple-element.52.refs_3_), channel_id=1, source_target_pairs={{0,2},{1,3},{2,0},{3,1},{4,6},{5,7},{6,4},{7,5},{8,10},{9,11},{10,... | collective-permute-start | bytes 393224 | tf_op jit(solution)/shard_map/ppermute | solution.py:355
  65.0 1.8 %solve_near.1 = (f32[128,256]{1,0:T(8,128)S(1)}, f32[8,256]{1,0:T(8,128)}) custom-call(s32[2]{0:T(128)S(1)} %pad_add_fusion.where_ref, s32[8]{0:T(128)S(1)} %copy-done.3, f32[512,512]{1,0:T(8,128)S(1)} %block_3.1.inverse_ref, f32[512,1]{1,0:T(8,128)S(1)} %get-tuple-element.49.scale_ref, f32[256,256]{1,0:T(8,128)S(1)} %pad_maximum_fusion.refs_0_, ...), custom_call_target="tpu_custom_call" | custom-call | flops 5000000000 | bytes 1048576 | tf_op jit(solution)/shard_map/solve_near/pallas_call | solution.py:322
  66.8 2.6 %collective-permute-done.13.refs_2_ = f32[128,256]{1,0:T(8,128)S(1)} collective-permute-done((f32[128,256]{1,0:T(8,128)S(1)}, f32[128,256]{1,0:T(8,128)S(1)}, u32[]{:S(2)}, u32[]{:S(2)}) %collective-permute-start.13) | collective-permute-done | bytes 131104 | tf_op jit(solution)/shard_map/ppermute | solution.py:355
  69.4 2.1 %collective-permute-done.14.refs_3_ = f32[128,256]{1,0:T(8,128)S(1)} collective-permute-done((f32[128,256]{1,0:T(8,128)S(1)}, f32[128,256]{1,0:T(8,128)S(1)}, u32[]{:S(2)}, u32[]{:S(2)}) %collective-permute-start.14) | collective-permute-done | bytes 131104 | tf_op jit(solution)/shard_map/ppermute | solution.py:355
  (40 shorter events, 6.7 us)
Async XLA Ops:
  0.6 0.9 %copy-start.1 = (f32[24,2048]{1,0:T(8,128)S(1)}, f32[24,2048]{1,0:T(8,128)}, u32[]{:S(2)}) copy-start(f32[24,2048]{1,0:T(8,128)} %points_ref.1) | copy-start | bytes 589828
  1.6 0.7 copy-start.2
  5.3 5.5 %collective-permute-start = (f32[32,640]{1,0:T(8,128)S(1)}, f32[32,640]{1,0:T(8,128)S(1)}, u32[]{:S(2)}, u32[]{:S(2)}) collective-permute-start(f32[32,640]{1,0:T(8,128)S(1)} %dynamic-slice_bitcast_fusion.1), channel_id=1, source_target_pairs={{0,4},{4,0},{8,12},{12,8},{16,20},{20,16},{24,28},{28,24},{1,5},{5... | collective-permute-start | bytes 245768 | tf_op jit(solution)/shard_map/ppermute | solution.py:355
  8.3 1.2 %copy-start = (bf16[2048,256]{1,0:T(8,128)(2,1)S(1)}, bf16[2048,256]{1,0:T(8,128)(2,1)}, u32[]{:S(2)}) copy-start(bf16[2048,256]{1,0:T(8,128)(2,1)} %yields_ref.1) | copy-start | bytes 3145732
  10.8 4.1 %collective-permute-start.1 = (f32[16,640]{1,0:T(8,128)S(1)}, f32[16,640]{1,0:T(8,128)S(1)}, u32[]{:S(2)}, u32[]{:S(2)}) collective-permute-start(f32[16,640]{1,0:T(8,128)S(1)} %dynamic-slice_bitcast_fusion.3), channel_id=1, source_target_pairs={{0,8},{4,12},{8,0},{12,4},{16,24},{20,28},{24,16},{28,20},{1,9},{5... | collective-permute-start | bytes 122888 | tf_op jit(solution)/shard_map/ppermute | solution.py:355
  12.9 6.9 %collective-permute-start.3 = (f32[256,256]{1,0:T(8,128)S(1)}, f32[256,256]{1,0:T(8,128)S(1)}, u32[]{:S(2)}, u32[]{:S(2)}) collective-permute-start(f32[256,256]{1,0:T(8,128)S(1)} %get-tuple-element.35), channel_id=1, source_target_pairs={{0,4},{4,0},{8,12},{12,8},{16,20},{20,16},{24,28},{28,24},{1,5},{5... | collective-permute-start | bytes 786440 | tf_op jit(solution)/shard_map/ppermute | solution.py:355
  14.9 4.9 %collective-permute-start.2 = (f32[8,640]{1,0:T(8,128)S(1)}, f32[8,640]{1,0:T(8,128)S(1)}, u32[]{:S(2)}, u32[]{:S(2)}) collective-permute-start(f32[8,640]{1,0:T(8,128)S(1)} %dynamic-slice_bitcast_fusion.4), channel_id=1, source_target_pairs={{0,16},{4,20},{8,24},{12,28},{16,0},{20,4},{24,8},{28,12},{1,17},{... | collective-permute-start | bytes 61448 | tf_op jit(solution)/shard_map/ppermute | solution.py:355
  19.8 7.7 %collective-permute-start.4 = (f32[128,256]{1,0:T(8,128)S(1)}, f32[128,256]{1,0:T(8,128)S(1)}, u32[]{:S(2)}, u32[]{:S(2)}) collective-permute-start(f32[128,256]{1,0:T(8,128)S(1)} %dynamic-slice_bitcast_fusion), channel_id=1, source_target_pairs={{0,8},{4,12},{8,0},{12,4},{16,24},{20,28},{24,16},{28,20},{1,9},{5... | collective-permute-start | bytes 393224 | tf_op jit(solution)/shard_map/ppermute | solution.py:355
  22.5 12.9 %all-to-all-start = ((f32[8,8,640]{2,1,0:T(8,128)}), f32[8,8,640]{2,1,0:T(8,128)S(1)}, u32[]{:S(2)}, u32[]{:S(2)}) async-start(f32[8,8,640]{2,1,0:T(8,128)} %broadcast_in_dim.2), calls=%async_computation | async-start | bytes 327680 | tf_op jit(solution)/shard_map/all_to_all | solution.py:395
  35.4 5.3 %collective-permute-start.5 = (f32[64,640]{1,0:T(8,128)S(1)}, f32[64,640]{1,0:T(8,128)S(1)}, u32[]{:S(2)}, u32[]{:S(2)}) collective-permute-start(f32[64,640]{1,0:T(8,128)S(1)} %bitcast.33), channel_id=1, source_target_pairs={{0,2},{1,3},{2,0},{3,1},{4,6},{5,7},{6,4},{7,5},{8,10},{9,11},{10,... | collective-permute-start | bytes 491528 | tf_op jit(solution)/shard_map/ppermute | solution.py:355
  37.2 5.6 %collective-permute-start.8 = (f32[64,256]{1,0:T(8,128)S(1)}, f32[64,256]{1,0:T(8,128)S(1)}, u32[]{:S(2)}, u32[]{:S(2)}) collective-permute-start(f32[64,256]{1,0:T(8,128)S(1)} %dynamic-slice_bitcast_fusion.2), channel_id=1, source_target_pairs={{0,16},{4,20},{8,24},{12,28},{16,0},{20,4},{24,8},{28,12},{1,17},{... | collective-permute-start | bytes 196616 | tf_op jit(solution)/shard_map/ppermute | solution.py:355
  38.0 4.9 %collective-permute-start.6 = (f32[64,640]{1,0:T(8,128)S(1)}, f32[64,640]{1,0:T(8,128)S(1)}, u32[]{:S(2)}, u32[]{:S(2)}) collective-permute-start(f32[64,640]{1,0:T(8,128)S(1)} %bitcast.34), channel_id=1, source_target_pairs={{0,1},{1,0},{2,3},{3,2},{4,5},{5,4},{6,7},{7,6},{8,9},{9,8},{10,11... | collective-permute-start | bytes 491528 | tf_op jit(solution)/shard_map/ppermute | solution.py:355
  40.7 2.1 %collective-permute-start.7 = (f32[64,640]{1,0:T(8,128)S(1)}, f32[64,640]{1,0:T(8,128)S(1)}, u32[]{:S(2)}, u32[]{:S(2)}) collective-permute-start(f32[64,640]{1,0:T(8,128)S(1)} %collective-permute-done.5.refs_2_), channel_id=1, source_target_pairs={{0,1},{1,0},{2,3},{3,2},{4,5},{5,4},{6,7},{7,6},{8,9},{9,8},{10,11... | collective-permute-start | bytes 491528 | tf_op jit(solution)/shard_map/ppermute | solution.py:355
  42.9 5.3 %collective-permute-start.9 = (f32[64,256]{1,0:T(8,128)S(1)}, f32[64,256]{1,0:T(8,128)S(1)}, u32[]{:S(2)}, u32[]{:S(2)}) collective-permute-start(f32[64,256]{1,0:T(8,128)S(1)} %bitcast_add_fusion.2), channel_id=1, source_target_pairs={{0,16},{4,20},{8,24},{12,28},{16,0},{20,4},{24,8},{28,12},{1,17},{... | collective-permute-start | bytes 196616 | tf_op jit(solution)/shard_map/ppermute | solution.py:355
  48.2 5.1 %collective-permute-start.10 = (f32[128,256]{1,0:T(8,128)S(1)}, f32[128,256]{1,0:T(8,128)S(1)}, u32[]{:S(2)}, u32[]{:S(2)}) collective-permute-start(f32[128,256]{1,0:T(8,128)S(1)} %pad_maximum_fusion.1), channel_id=1, source_target_pairs={{0,4},{4,0},{8,12},{12,8},{16,20},{20,16},{24,28},{28,24},{1,5},{5... | collective-permute-start | bytes 393224 | tf_op jit(solution)/shard_map/ppermute | solution.py:355
  53.3 8.1 %collective-permute-start.11 = (f32[256,256]{1,0:T(8,128)S(1)}, f32[256,256]{1,0:T(8,128)S(1)}, u32[]{:S(2)}, u32[]{:S(2)}) collective-permute-start(f32[256,256]{1,0:T(8,128)S(1)} %pad_maximum_fusion.refs_0_), channel_id=1, source_target_pairs={{0,8},{4,12},{8,0},{12,4},{16,24},{20,28},{24,16},{28,20},{1,9},{5... | collective-permute-start | bytes 786440 | tf_op jit(solution)/shard_map/ppermute | solution.py:355
  57.7 3.8 %copy-start.3 = (s32[8]{0:T(128)S(1)}, s32[8]{0:T(128)}, u32[]{:S(2)}) copy-start(s32[8]{0:T(128)} %group_ref.3) | copy-start | bytes 100
  63.0 3.9 %collective-permute-start.12 = (f32[128,256]{1,0:T(8,128)S(1)}, f32[128,256]{1,0:T(8,128)S(1)}, u32[]{:S(2)}, u32[]{:S(2)}) collective-permute-start(f32[128,256]{1,0:T(8,128)S(1)} %get-tuple-element.51.refs_2_), channel_id=1, source_target_pairs={{0,1},{1,0},{2,3},{3,2},{4,5},{5,4},{6,7},{7,6},{8,9},{9,8},{10,11... | collective-permute-start | bytes 393224 | tf_op jit(solution)/shard_map/ppermute | solution.py:355
  63.0 6.4 %collective-permute-start.13 = (f32[128,256]{1,0:T(8,128)S(1)}, f32[128,256]{1,0:T(8,128)S(1)}, u32[]{:S(2)}, u32[]{:S(2)}) collective-permute-start(f32[128,256]{1,0:T(8,128)S(1)} %get-tuple-element.52.refs_3_), channel_id=1, source_target_pairs={{0,2},{1,3},{2,0},{3,1},{4,6},{5,7},{6,4},{7,5},{8,10},{9,11},{10,... | collective-permute-start | bytes 393224 | tf_op jit(solution)/shard_map/ppermute | solution.py:355
  64.9 6.5 %collective-permute-start.14 = (f32[128,256]{1,0:T(8,128)S(1)}, f32[128,256]{1,0:T(8,128)S(1)}, u32[]{:S(2)}, u32[]{:S(2)}) collective-permute-start(f32[128,256]{1,0:T(8,128)S(1)} %get-tuple-element.53.refs_4_), channel_id=1, source_target_pairs={{0,3},{1,2},{2,1},{3,0},{4,7},{5,6},{6,5},{7,4},{8,11},{9,10},{10,... | collective-permute-start | bytes 393224 | tf_op jit(solution)/shard_map/ppermute | solution.py:355

commit v11 on v9

--- a/solution.py
+++ b/solution.py
@@ -10,7 +10,6 @@
 BLOCK = 64
 GROUPS = 8
 TILE = 128
-HIGH = lax.Precision.HIGHEST
 VMEM = pl.BlockSpec(memory_space=pltpu.VMEM)
 SMEM = pl.BlockSpec(memory_space=pltpu.SMEM)
 BIG = pltpu.CompilerParams(vmem_limit_bytes=16 * 2**20)
@@ -147,7 +146,7 @@
             second = a * columns[q] - b * columns[p]
             first = jnp.where(subs == p, det - d, jnp.where(subs == q, b, first))
             second = jnp.where(subs == p, b, jnp.where(subs == q, det - a, second))
-            inverse = pltpu.reciprocal(det, approx=True)
+            inverse = 1.0 / det
             for k in range(q + 1, 8):
                 less = first * row_of(columns[k], p) + second * row_of(columns[k], q)
                 columns[k] = columns[k] - less * inverse
@@ -184,14 +183,13 @@
     fresh = -stacked_dot(minus, gram(band, whole))
     parts = [minus if at == block * TILE else fresh[:, at:at + TILE] for at in range(0, terms, TILE)]
     fresh = jnp.concatenate(parts, axis=1)
-    change = stacked_dot(gram(whole, band), fresh)
+    starts = [at for at in range(0, terms, TILE) if at != block * TILE]
+    change = stacked_dot(jnp.concatenate([gram(slice(at, at + TILE), band) for at in starts], axis=0), fresh)
     inside = (lax.broadcasted_iota(jnp.int32, (TILE, terms), 1) // TILE) == block
-    for at in range(0, terms, TILE):
+    out_ref[band, :] = fresh
+    for place, at in enumerate(starts):
         rows = slice(at, at + TILE)
-        if at == block * TILE:
-            out_ref[rows, :] = fresh
-        else:
-            out_ref[rows, :] = jnp.where(inside, 0.0, gram(rows, whole)) - change[rows, :]
+        out_ref[rows, :] = jnp.where(inside, 0.0, gram(rows, whole)) - change[place * TILE:(place + 1) * TILE, :]
 
 
 def sweep(tile):
@@ -287,10 +285,10 @@
     scaled = scale_ref[...] * cross_ref[...]
     size = jnp.sqrt(jnp.float32(samples))
     share = shares[0].shape[0]
-    for step, ref in zip(steps, shares):
-        band = pl.ds(pl.multiple_of((where_ref[1] ^ step) * share, share), share)
-        value = jnp.dot(inverse_ref[band, :], scaled, precision=HIGH, preferred_element_type=jnp.float32)
-        ref[...] = -scale_ref[band, :] * value * size
+    bands = [pl.ds(pl.multiple_of((where_ref[1] ^ step) * share, share), share) for step in steps]
+    values = stacked_dot(jnp.concatenate([inverse_ref[band, :] for band in bands], axis=0), scaled)
+    for at, (band, ref) in enumerate(zip(bands, shares)):
+        ref[...] = -scale_ref[band, :] * values[at * share:(at + 1) * share, :] * size
     if not finish:
         return
     sobol_ref = refs[-2]

time: 72.5 us -> 72.4 us (level)
  transfers between devices with their start and end apart: 16 -> 16, of which waited for: 9 -> 11; matrix products, arithmetic and copies ran while one was open for 1% -> 1% of each run, Pallas kernels for 24% -> 23%
where the time goes in v11:
time: 72.4 us; the launch traced here: 72.1 us
  starting transfers between devices  23.7 us (33%)
  Pallas kernels  22.1 us (31%)
  waiting for transfers between devices  21.7 us (30%)
  local copies, waits for them, and re-layouts  3.58 us (5%)
  between operations  0.82 us (1%)
    ppermute x15, starting transfers between devices, swap(): return lax.ppermute(values, axis, [(at, at ^ step) for at in range(size)])  18.6 us
    ppermute x15, waiting for transfers between devices, swap(): return lax.ppermute(values, axis, [(at, at ^ step) for at in range(size)])  13.9 us
    pallas_call x3, Pallas kernels, next_block(): pl.pallas_call(functools.partial(next_kernel, block), out_shape=jax.Shape...  10.6 us
    all_to_all x1, waiting for transfers between devices, on_device(): lax.all_to_all(copies, 'samp', split_axis=0, concat_axis=0)[:8]  7.82 us
    all_to_all x1, starting transfers between devices, on_device(): lax.all_to_all(copies, 'samp', split_axis=0, concat_axis=0)[:8]  5.08 us
    pallas_call x1, Pallas kernels, first_block(): pl.pallas_call(first_kernel, out_shape=(jax.ShapeDtypeStruct((terms, term...  3.81 us
    pallas_call x2, Pallas kernels, solve(): pl.pallas_call(functools.partial(solve_kernel, samples, steps, rows, fini...  3.17 us
    pallas_call x1, Pallas kernels, design(): pl.pallas_call(functools.partial(design_kernel, 512), out_shape=(jax.Shap...  2.97 us
  transfers between devices with their start and end apart: 16, of which 11 were waited for; matrix products, arithmetic and copies ran while one was open for 1% of the time, Pallas kernels for 23%

profile of v11, /device:TPU:0, one launch (start us, length us, event | category | flops | bytes accessed | tf_op | source)
XLA Modules:
  0.0 72.1 jit_solution(4610981741032015832)
XLA Ops:
  2.3 3.0 %design.1 = (bf16[512,2048]{1,0:T(8,128)(2,1)S(1)}, f32[64,640]{1,0:T(8,128)S(1)}) custom-call(s32[1]{0:T(128)} %bitcast.cell_ref.where_ref, s32[2,512]{1,0:T(2,128)S(1)} %bitcast.38, f32[24,2048]{1,0:T(8,128)S(1)} %copy-done.1), custom_call_target="tpu_custom_call" | custom-call | tf_op jit(solution)/shard_map/design/pallas_call | solution.py:79
  5.3 3.0 %collective-permute-start = (f32[32,640]{1,0:T(8,128)S(1)}, f32[32,640]{1,0:T(8,128)S(1)}, u32[]{:S(2)}, u32[]{:S(2)}) collective-permute-start(f32[32,640]{1,0:T(8,128)S(1)} %dynamic-slice_bitcast_fusion.1), channel_id=1, source_target_pairs={{0,4},{4,0},{8,12},{12,8},{16,20},{20,16},{24,28},{28,24},{1,5},{5... | collective-permute-start | bytes 245768 | tf_op jit(solution)/shard_map/ppermute | solution.py:353
  8.3 1.2 %copy-done = bf16[2048,256]{1,0:T(8,128)(2,1)S(1)} copy-done((bf16[2048,256]{1,0:T(8,128)(2,1)S(1)}, bf16[2048,256]{1,0:T(8,128)(2,1)}, u32[]{:S(2)}) %copy-start) | copy-done | bytes 1048600
  10.8 2.1 %collective-permute-start.1 = (f32[16,640]{1,0:T(8,128)S(1)}, f32[16,640]{1,0:T(8,128)S(1)}, u32[]{:S(2)}, u32[]{:S(2)}) collective-permute-start(f32[16,640]{1,0:T(8,128)S(1)} %dynamic-slice_bitcast_fusion.3), channel_id=1, source_target_pairs={{0,8},{4,12},{8,0},{12,4},{16,24},{20,28},{24,16},{28,20},{1,9},{5... | collective-permute-start | bytes 122888 | tf_op jit(solution)/shard_map/ppermute | solution.py:353
  12.9 1.5 %collective-permute-start.3 = (f32[256,256]{1,0:T(8,128)S(1)}, f32[256,256]{1,0:T(8,128)S(1)}, u32[]{:S(2)}, u32[]{:S(2)}) collective-permute-start(f32[256,256]{1,0:T(8,128)S(1)} %get-tuple-element.35), channel_id=1, source_target_pairs={{0,4},{4,0},{8,12},{12,8},{16,20},{20,16},{24,28},{28,24},{1,5},{5... | collective-permute-start | bytes 786440 | tf_op jit(solution)/shard_map/ppermute | solution.py:353
  14.9 3.1 %collective-permute-start.2 = (f32[8,640]{1,0:T(8,128)S(1)}, f32[8,640]{1,0:T(8,128)S(1)}, u32[]{:S(2)}, u32[]{:S(2)}) collective-permute-start(f32[8,640]{1,0:T(8,128)S(1)} %dynamic-slice_bitcast_fusion.4), channel_id=1, source_target_pairs={{0,16},{4,20},{8,24},{12,28},{16,0},{20,4},{24,8},{28,12},{1,17},{... | collective-permute-start | bytes 61448 | tf_op jit(solution)/shard_map/ppermute | solution.py:353
  18.0 1.8 %collective-permute-done.2 = f32[8,640]{1,0:T(8,128)S(1)} collective-permute-done((f32[8,640]{1,0:T(8,128)S(1)}, f32[8,640]{1,0:T(8,128)S(1)}, u32[]{:S(2)}, u32[]{:S(2)}) %collective-permute-start.2) | collective-permute-done | bytes 20512 | tf_op jit(solution)/shard_map/ppermute | solution.py:353
  19.8 2.0 %collective-permute-start.4 = (f32[128,256]{1,0:T(8,128)S(1)}, f32[128,256]{1,0:T(8,128)S(1)}, u32[]{:S(2)}, u32[]{:S(2)}) collective-permute-start(f32[128,256]{1,0:T(8,128)S(1)} %dynamic-slice_bitcast_fusion), channel_id=1, source_target_pairs={{0,8},{4,12},{8,0},{12,4},{16,24},{20,28},{24,16},{28,20},{1,9},{5... | collective-permute-start | bytes 393224 | tf_op jit(solution)/shard_map/ppermute | solution.py:353
  22.5 5.1 %all-to-all-start = ((f32[8,8,640]{2,1,0:T(8,128)}), f32[8,8,640]{2,1,0:T(8,128)S(1)}, u32[]{:S(2)}, u32[]{:S(2)}) async-start(f32[8,8,640]{2,1,0:T(8,128)} %broadcast_in_dim.2), calls=%async_computation | async-start | bytes 327680 | tf_op jit(solution)/shard_map/all_to_all | solution.py:393
  27.6 7.8 %all-to-all-done = f32[8,8,640]{2,1,0:T(8,128)S(1)} async-done(((f32[8,8,640]{2,1,0:T(8,128)}), f32[8,8,640]{2,1,0:T(8,128)S(1)}, u32[]{:S(2)}, u32[]{:S(2)}) %all-to-all-start) | async-done | bytes 163872 | tf_op jit(solution)/shard_map/all_to_all | solution.py:393
  35.4 1.8 %collective-permute-start.5 = (f32[64,640]{1,0:T(8,128)S(1)}, f32[64,640]{1,0:T(8,128)S(1)}, u32[]{:S(2)}, u32[]{:S(2)}) collective-permute-start(f32[64,640]{1,0:T(8,128)S(1)} %bitcast.33), channel_id=1, source_target_pairs={{0,2},{1,3},{2,0},{3,1},{4,6},{5,7},{6,4},{7,5},{8,10},{9,11},{10,... | collective-permute-start | bytes 491528 | tf_op jit(solution)/shard_map/ppermute | solution.py:353
  38.0 2.8 %collective-permute-done.5.refs_2_ = f32[64,640]{1,0:T(8,128)S(1)} collective-permute-done((f32[64,640]{1,0:T(8,128)S(1)}, f32[64,640]{1,0:T(8,128)S(1)}, u32[]{:S(2)}, u32[]{:S(2)}) %collective-permute-start.5) | collective-permute-done | bytes 163872 | tf_op jit(solution)/shard_map/ppermute | solution.py:353
  40.8 2.1 %collective-permute-done.8 = f32[64,256]{1,0:T(8,128)S(1)} collective-permute-done((f32[64,256]{1,0:T(8,128)S(1)}, f32[64,256]{1,0:T(8,128)S(1)}, u32[]{:S(2)}, u32[]{:S(2)}) %collective-permute-start.8) | collective-permute-done | bytes 65568 | tf_op jit(solution)/shard_map/ppermute | solution.py:353
  43.2 3.8 %block_0.1 = (f32[512,512]{1,0:T(8,128)S(1)}, f32[512,1]{1,0:T(8,128)S(1)}) custom-call(s32[1]{0:T(128)} %bitcast.cell_ref.where_ref, f32[64,640]{1,0:T(8,128)S(1)} %bitcast.35, f32[64,640]{1,0:T(8,128)S(1)} %collective-permute-done.6.refs_1_, f32[64,640]{1,0:T(8,128)S(1)} %collective-permute-done.5.refs_2_, f32[64,640]{1,0:T(8,128)S(1)} %collective-permute-done.7.refs_3_), custom_call_target="tpu_custom_call" | custom-call | flops 1000000000 | bytes 1048576 | tf_op jit(solution)/shard_map/block_0/pallas_call | solution.py:246
  47.1 1.1 %collective-permute-done.9 = f32[64,256]{1,0:T(8,128)S(1)} collective-permute-done((f32[64,256]{1,0:T(8,128)S(1)}, f32[64,256]{1,0:T(8,128)S(1)}, u32[]{:S(2)}, u32[]{:S(2)}) %collective-permute-start.9) | collective-permute-done | bytes 65568 | tf_op jit(solution)/shard_map/ppermute | solution.py:353
  48.2 1.4 %collective-permute-start.10 = (f32[128,256]{1,0:T(8,128)S(1)}, f32[128,256]{1,0:T(8,128)S(1)}, u32[]{:S(2)}, u32[]{:S(2)}) collective-permute-start(f32[128,256]{1,0:T(8,128)S(1)} %pad_maximum_fusion.1), channel_id=1, source_target_pairs={{0,4},{4,0},{8,12},{12,8},{16,20},{20,16},{24,28},{28,24},{1,5},{5... | collective-permute-start | bytes 393224 | tf_op jit(solution)/shard_map/ppermute | solution.py:353
  49.6 3.5 %block_1.1.in_ref = f32[512,512]{1,0:T(8,128)S(1)} custom-call(f32[512,512]{1,0:T(8,128)S(1)} %get-tuple-element.46.in_ref), custom_call_target="tpu_custom_call" | custom-call | flops 1000000000 | bytes 1048576 | tf_op jit(solution)/shard_map/block_1/pallas_call | solution.py:262
  53.4 3.5 %block_2.1.in_ref = f32[512,512]{1,0:T(8,128)S(1)} custom-call(f32[512,512]{1,0:T(8,128)S(1)} %block_1.1.in_ref), custom_call_target="tpu_custom_call" | custom-call | flops 1000000000 | bytes 1048576 | tf_op jit(solution)/shard_map/block_2/pallas_call | solution.py:262
  57.0 3.5 %block_3.1.inverse_ref = f32[512,512]{1,0:T(8,128)S(1)} custom-call(f32[512,512]{1,0:T(8,128)S(1)} %block_2.1.in_ref), custom_call_target="tpu_custom_call" | custom-call | flops 1000000000 | bytes 1048576 | tf_op jit(solution)/shard_map/block_3/pallas_call | solution.py:262
  60.8 1.4 %solve_far.1 = (f32[128,256]{1,0:T(8,128)S(1)}, f32[128,256]{1,0:T(8,128)S(1)}, f32[128,256]{1,0:T(8,128)S(1)}) custom-call(s32[2]{0:T(128)S(1)} %pad_add_fusion.where_ref, s32[8]{0:T(128)S(1)} %copy-done.3, f32[512,512]{1,0:T(8,128)S(1)} %block_3.1.inverse_ref, f32[512,1]{1,0:T(8,128)S(1)} %get-tuple-element.49.scale_ref, ...), custom_call_target="tpu_custom_call" | custom-call | flops 1000000000 | bytes 1048576 | tf_op jit(solution)/shard_map/solve_far/pallas_call | solution.py:320
  62.3 2.3 %collective-permute-start.13 = (f32[128,256]{1,0:T(8,128)S(1)}, f32[128,256]{1,0:T(8,128)S(1)}, u32[]{:S(2)}, u32[]{:S(2)}) collective-permute-start(f32[128,256]{1,0:T(8,128)S(1)} %get-tuple-element.52.refs_3_), channel_id=1, source_target_pairs={{0,2},{1,3},{2,0},{3,1},{4,6},{5,7},{6,4},{7,5},{8,10},{9,11},{10,... | collective-permute-start | bytes 393224 | tf_op jit(solution)/shard_map/ppermute | solution.py:353
  64.7 1.7 %solve_near.1 = (f32[128,256]{1,0:T(8,128)S(1)}, f32[8,256]{1,0:T(8,128)}) custom-call(s32[2]{0:T(128)S(1)} %pad_add_fusion.where_ref, s32[8]{0:T(128)S(1)} %copy-done.3, f32[512,512]{1,0:T(8,128)S(1)} %block_3.1.inverse_ref, f32[512,1]{1,0:T(8,128)S(1)} %get-tuple-element.49.scale_ref, f32[256,256]{1,0:T(8,128)S(1)} %pad_maximum_fusion.refs_0_, ...), custom_call_target="tpu_custom_call" | custom-call | flops 5000000000 | bytes 1048576 | tf_op jit(solution)/shard_map/solve_near/pallas_call | solution.py:320
  66.4 2.5 %collective-permute-done.13.refs_2_ = f32[128,256]{1,0:T(8,128)S(1)} collective-permute-done((f32[128,256]{1,0:T(8,128)S(1)}, f32[128,256]{1,0:T(8,128)S(1)}, u32[]{:S(2)}, u32[]{:S(2)}) %collective-permute-start.13) | collective-permute-done | bytes 131104 | tf_op jit(solution)/shard_map/ppermute | solution.py:353
  69.0 2.3 %collective-permute-done.14.refs_3_ = f32[128,256]{1,0:T(8,128)S(1)} collective-permute-done((f32[128,256]{1,0:T(8,128)S(1)}, f32[128,256]{1,0:T(8,128)S(1)}, u32[]{:S(2)}, u32[]{:S(2)}) %collective-permute-start.14) | collective-permute-done | bytes 131104 | tf_op jit(solution)/shard_map/ppermute | solution.py:353
  (40 shorter events, 6.8 us)
Async XLA Ops:
  0.6 0.9 %copy-start.1 = (f32[24,2048]{1,0:T(8,128)S(1)}, f32[24,2048]{1,0:T(8,128)}, u32[]{:S(2)}) copy-start(f32[24,2048]{1,0:T(8,128)} %points_ref.1) | copy-start | bytes 589828
  1.6 0.7 copy-start.2
  5.3 5.5 %collective-permute-start = (f32[32,640]{1,0:T(8,128)S(1)}, f32[32,640]{1,0:T(8,128)S(1)}, u32[]{:S(2)}, u32[]{:S(2)}) collective-permute-start(f32[32,640]{1,0:T(8,128)S(1)} %dynamic-slice_bitcast_fusion.1), channel_id=1, source_target_pairs={{0,4},{4,0},{8,12},{12,8},{16,20},{20,16},{24,28},{28,24},{1,5},{5... | collective-permute-start | bytes 245768 | tf_op jit(solution)/shard_map/ppermute | solution.py:353
  8.3 1.2 %copy-start = (bf16[2048,256]{1,0:T(8,128)(2,1)S(1)}, bf16[2048,256]{1,0:T(8,128)(2,1)}, u32[]{:S(2)}) copy-start(bf16[2048,256]{1,0:T(8,128)(2,1)} %yields_ref.1) | copy-start | bytes 3145732
  10.8 4.1 %collective-permute-start.1 = (f32[16,640]{1,0:T(8,128)S(1)}, f32[16,640]{1,0:T(8,128)S(1)}, u32[]{:S(2)}, u32[]{:S(2)}) collective-permute-start(f32[16,640]{1,0:T(8,128)S(1)} %dynamic-slice_bitcast_fusion.3), channel_id=1, source_target_pairs={{0,8},{4,12},{8,0},{12,4},{16,24},{20,28},{24,16},{28,20},{1,9},{5... | collective-permute-start | bytes 122888 | tf_op jit(solution)/shard_map/ppermute | solution.py:353
  12.9 6.9 %collective-permute-start.3 = (f32[256,256]{1,0:T(8,128)S(1)}, f32[256,256]{1,0:T(8,128)S(1)}, u32[]{:S(2)}, u32[]{:S(2)}) collective-permute-start(f32[256,256]{1,0:T(8,128)S(1)} %get-tuple-element.35), channel_id=1, source_target_pairs={{0,4},{4,0},{8,12},{12,8},{16,20},{20,16},{24,28},{28,24},{1,5},{5... | collective-permute-start | bytes 786440 | tf_op jit(solution)/shard_map/ppermute | solution.py:353
  14.9 4.9 %collective-permute-start.2 = (f32[8,640]{1,0:T(8,128)S(1)}, f32[8,640]{1,0:T(8,128)S(1)}, u32[]{:S(2)}, u32[]{:S(2)}) collective-permute-start(f32[8,640]{1,0:T(8,128)S(1)} %dynamic-slice_bitcast_fusion.4), channel_id=1, source_target_pairs={{0,16},{4,20},{8,24},{12,28},{16,0},{20,4},{24,8},{28,12},{1,17},{... | collective-permute-start | bytes 61448 | tf_op jit(solution)/shard_map/ppermute | solution.py:353
  19.8 7.7 %collective-permute-start.4 = (f32[128,256]{1,0:T(8,128)S(1)}, f32[128,256]{1,0:T(8,128)S(1)}, u32[]{:S(2)}, u32[]{:S(2)}) collective-permute-start(f32[128,256]{1,0:T(8,128)S(1)} %dynamic-slice_bitcast_fusion), channel_id=1, source_target_pairs={{0,8},{4,12},{8,0},{12,4},{16,24},{20,28},{24,16},{28,20},{1,9},{5... | collective-permute-start | bytes 393224 | tf_op jit(solution)/shard_map/ppermute | solution.py:353
  22.5 12.9 %all-to-all-start = ((f32[8,8,640]{2,1,0:T(8,128)}), f32[8,8,640]{2,1,0:T(8,128)S(1)}, u32[]{:S(2)}, u32[]{:S(2)}) async-start(f32[8,8,640]{2,1,0:T(8,128)} %broadcast_in_dim.2), calls=%async_computation | async-start | bytes 327680 | tf_op jit(solution)/shard_map/all_to_all | solution.py:393
  35.4 5.3 %collective-permute-start.5 = (f32[64,640]{1,0:T(8,128)S(1)}, f32[64,640]{1,0:T(8,128)S(1)}, u32[]{:S(2)}, u32[]{:S(2)}) collective-permute-start(f32[64,640]{1,0:T(8,128)S(1)} %bitcast.33), channel_id=1, source_target_pairs={{0,2},{1,3},{2,0},{3,1},{4,6},{5,7},{6,4},{7,5},{8,10},{9,11},{10,... | collective-permute-start | bytes 491528 | tf_op jit(solution)/shard_map/ppermute | solution.py:353
  37.2 5.6 %collective-permute-start.8 = (f32[64,256]{1,0:T(8,128)S(1)}, f32[64,256]{1,0:T(8,128)S(1)}, u32[]{:S(2)}, u32[]{:S(2)}) collective-permute-start(f32[64,256]{1,0:T(8,128)S(1)} %dynamic-slice_bitcast_fusion.2), channel_id=1, source_target_pairs={{0,16},{4,20},{8,24},{12,28},{16,0},{20,4},{24,8},{28,12},{1,17},{... | collective-permute-start | bytes 196616 | tf_op jit(solution)/shard_map/ppermute | solution.py:353
  38.0 4.9 %collective-permute-start.6 = (f32[64,640]{1,0:T(8,128)S(1)}, f32[64,640]{1,0:T(8,128)S(1)}, u32[]{:S(2)}, u32[]{:S(2)}) collective-permute-start(f32[64,640]{1,0:T(8,128)S(1)} %bitcast.34), channel_id=1, source_target_pairs={{0,1},{1,0},{2,3},{3,2},{4,5},{5,4},{6,7},{7,6},{8,9},{9,8},{10,11... | collective-permute-start | bytes 491528 | tf_op jit(solution)/shard_map/ppermute | solution.py:353
  40.7 2.1 %collective-permute-start.7 = (f32[64,640]{1,0:T(8,128)S(1)}, f32[64,640]{1,0:T(8,128)S(1)}, u32[]{:S(2)}, u32[]{:S(2)}) collective-permute-start(f32[64,640]{1,0:T(8,128)S(1)} %collective-permute-done.5.refs_2_), channel_id=1, source_target_pairs={{0,1},{1,0},{2,3},{3,2},{4,5},{5,4},{6,7},{7,6},{8,9},{9,8},{10,11... | collective-permute-start | bytes 491528 | tf_op jit(solution)/shard_map/ppermute | solution.py:353
  42.9 5.3 %collective-permute-start.9 = (f32[64,256]{1,0:T(8,128)S(1)}, f32[64,256]{1,0:T(8,128)S(1)}, u32[]{:S(2)}, u32[]{:S(2)}) collective-permute-start(f32[64,256]{1,0:T(8,128)S(1)} %bitcast_add_fusion.2), channel_id=1, source_target_pairs={{0,16},{4,20},{8,24},{12,28},{16,0},{20,4},{24,8},{28,12},{1,17},{... | collective-permute-start | bytes 196616 | tf_op jit(solution)/shard_map/ppermute | solution.py:353
  48.2 5.0 %collective-permute-start.10 = (f32[128,256]{1,0:T(8,128)S(1)}, f32[128,256]{1,0:T(8,128)S(1)}, u32[]{:S(2)}, u32[]{:S(2)}) collective-permute-start(f32[128,256]{1,0:T(8,128)S(1)} %pad_maximum_fusion.1), channel_id=1, source_target_pairs={{0,4},{4,0},{8,12},{12,8},{16,20},{20,16},{24,28},{28,24},{1,5},{5... | collective-permute-start | bytes 393224 | tf_op jit(solution)/shard_map/ppermute | solution.py:353
  53.2 7.6 %collective-permute-start.11 = (f32[256,256]{1,0:T(8,128)S(1)}, f32[256,256]{1,0:T(8,128)S(1)}, u32[]{:S(2)}, u32[]{:S(2)}) collective-permute-start(f32[256,256]{1,0:T(8,128)S(1)} %pad_maximum_fusion.refs_0_), channel_id=1, source_target_pairs={{0,8},{4,12},{8,0},{12,4},{16,24},{20,28},{24,16},{28,20},{1,9},{5... | collective-permute-start | bytes 786440 | tf_op jit(solution)/shard_map/ppermute | solution.py:353
  57.0 3.8 %copy-start.3 = (s32[8]{0:T(128)S(1)}, s32[8]{0:T(128)}, u32[]{:S(2)}) copy-start(s32[8]{0:T(128)} %group_ref.3) | copy-start | bytes 100
  62.3 4.2 %collective-permute-start.12 = (f32[128,256]{1,0:T(8,128)S(1)}, f32[128,256]{1,0:T(8,128)S(1)}, u32[]{:S(2)}, u32[]{:S(2)}) collective-permute-start(f32[128,256]{1,0:T(8,128)S(1)} %get-tuple-element.51.refs_2_), channel_id=1, source_target_pairs={{0,1},{1,0},{2,3},{3,2},{4,5},{5,4},{6,7},{7,6},{8,9},{9,8},{10,11... | collective-permute-start | bytes 393224 | tf_op jit(solution)/shard_map/ppermute | solution.py:353
  62.3 6.6 %collective-permute-start.13 = (f32[128,256]{1,0:T(8,128)S(1)}, f32[128,256]{1,0:T(8,128)S(1)}, u32[]{:S(2)}, u32[]{:S(2)}) collective-permute-start(f32[128,256]{1,0:T(8,128)S(1)} %get-tuple-element.52.refs_3_), channel_id=1, source_target_pairs={{0,2},{1,3},{2,0},{3,1},{4,6},{5,7},{6,4},{7,5},{8,10},{9,11},{10,... | collective-permute-start | bytes 393224 | tf_op jit(solution)/shard_map/ppermute | solution.py:353
  64.6 6.6 %collective-permute-start.14 = (f32[128,256]{1,0:T(8,128)S(1)}, f32[128,256]{1,0:T(8,128)S(1)}, u32[]{:S(2)}, u32[]{:S(2)}) collective-permute-start(f32[128,256]{1,0:T(8,128)S(1)} %get-tuple-element.53.refs_4_), channel_id=1, source_target_pairs={{0,3},{1,2},{2,1},{3,0},{4,7},{5,6},{6,5},{7,4},{8,11},{9,10},{10,... | collective-permute-start | bytes 393224 | tf_op jit(solution)/shard_map/ppermute | solution.py:353

commit v12 on v11

--- a/solution.py
+++ b/solution.py
@@ -56,14 +56,19 @@
     blocks = terms // TILE
     part_rows = fold_ref.shape[0] // 2
     cell = cell_ref[0]
+    rows = jnp.concatenate([
+        psi_ref[pl.ds(pl.multiple_of(block * TILE + cell * part_rows, part_rows), part_rows), :]
+        for block in range(blocks)
+    ], axis=0)
+    value = lax.dot_general(
+        psi_ref[...], rows, (((1,), (1,)), ((), ())), preferred_element_type=jnp.float32
+    ).T
     for block in range(blocks):
-        rows = psi_ref[pl.ds(pl.multiple_of(block * TILE + cell * part_rows, part_rows), part_rows), :]
         reach = (block + 1) * TILE
-        value = lax.dot_general(
-            rows, psi_ref[0:reach, :], (((1,), (1,)), ((), ())), preferred_element_type=jnp.float32
+        half, at = fold_place(block, blocks)
+        fold_ref[half * part_rows:(half + 1) * part_rows, at:at + reach] = (
+            value[block * part_rows:(block + 1) * part_rows, 0:reach]
         )
-        half, at = fold_place(block, blocks)
-        fold_ref[half * part_rows:(half + 1) * part_rows, at:at + reach] = value
 
 
 def fold_place(block, blocks):

time: 72.4 us -> 72.7 us (level)
  no operation moved by 1% of the time
where the time goes in v12:
time: 72.7 us; the launch traced here: 72.4 us
  starting transfers between devices  23.6 us (32%)
  Pallas kernels  22.4 us (31%)
  waiting for transfers between devices  21.8 us (30%)
  local copies, waits for them, and re-layouts  3.57 us (5%)
  between operations  0.82 us (1%)
    ppermute x15, starting transfers between devices, swap(): return lax.ppermute(values, axis, [(at, at ^ step) for at in range(size)])  18.6 us
    ppermute x15, waiting for transfers between devices, swap(): return lax.ppermute(values, axis, [(at, at ^ step) for at in range(size)])  13.9 us
    pallas_call x3, Pallas kernels, next_block(): pl.pallas_call(functools.partial(next_kernel, block), out_shape=jax.Shape...  10.6 us
    all_to_all x1, waiting for transfers between devices, on_device(): lax.all_to_all(copies, 'samp', split_axis=0, concat_axis=0)[:8]  7.82 us
    all_to_all x1, starting transfers between devices, on_device(): lax.all_to_all(copies, 'samp', split_axis=0, concat_axis=0)[:8]  5.08 us
    pallas_call x1, Pallas kernels, first_block(): pl.pallas_call(first_kernel, out_shape=(jax.ShapeDtypeStruct((terms, term...  3.81 us
    pallas_call x1, Pallas kernels, design(): pl.pallas_call(functools.partial(design_kernel, 512), out_shape=(jax.Shap...  3.29 us
    pallas_call x2, Pallas kernels, solve(): pl.pallas_call(functools.partial(solve_kernel, samples, steps, rows, fini...  3.17 us
  transfers between devices with their start and end apart: 16, of which 11 were waited for; matrix products, arithmetic and copies ran while one was open for 1% of the time, Pallas kernels for 23%

profile of v12, /device:TPU:0, one launch (start us, length us, event | category | flops | bytes accessed | tf_op | source)
XLA Modules:
  0.0 72.4 jit_solution(4290303539332516677)
XLA Ops:
  2.3 3.3 %design.1 = (bf16[512,2048]{1,0:T(8,128)(2,1)S(1)}, f32[64,640]{1,0:T(8,128)S(1)}) custom-call(s32[1]{0:T(128)} %bitcast.cell_ref.where_ref, s32[2,512]{1,0:T(2,128)S(1)} %bitcast.38, f32[24,2048]{1,0:T(8,128)S(1)} %copy-done.1), custom_call_target="tpu_custom_call" | custom-call | tf_op jit(solution)/shard_map/design/pallas_call | solution.py:84
  5.6 3.0 %collective-permute-start = (f32[32,640]{1,0:T(8,128)S(1)}, f32[32,640]{1,0:T(8,128)S(1)}, u32[]{:S(2)}, u32[]{:S(2)}) collective-permute-start(f32[32,640]{1,0:T(8,128)S(1)} %dynamic-slice_bitcast_fusion.1), channel_id=1, source_target_pairs={{0,4},{4,0},{8,12},{12,8},{16,20},{20,16},{24,28},{28,24},{1,5},{5... | collective-permute-start | bytes 245768 | tf_op jit(solution)/shard_map/ppermute | solution.py:358
  8.6 1.2 %copy-done = bf16[2048,256]{1,0:T(8,128)(2,1)S(1)} copy-done((bf16[2048,256]{1,0:T(8,128)(2,1)S(1)}, bf16[2048,256]{1,0:T(8,128)(2,1)}, u32[]{:S(2)}) %copy-start) | copy-done | bytes 1048600
  11.1 2.1 %collective-permute-start.1 = (f32[16,640]{1,0:T(8,128)S(1)}, f32[16,640]{1,0:T(8,128)S(1)}, u32[]{:S(2)}, u32[]{:S(2)}) collective-permute-start(f32[16,640]{1,0:T(8,128)S(1)} %dynamic-slice_bitcast_fusion.3), channel_id=1, source_target_pairs={{0,8},{4,12},{8,0},{12,4},{16,24},{20,28},{24,16},{28,20},{1,9},{5... | collective-permute-start | bytes 122888 | tf_op jit(solution)/shard_map/ppermute | solution.py:358
  13.2 1.5 %collective-permute-start.3 = (f32[256,256]{1,0:T(8,128)S(1)}, f32[256,256]{1,0:T(8,128)S(1)}, u32[]{:S(2)}, u32[]{:S(2)}) collective-permute-start(f32[256,256]{1,0:T(8,128)S(1)} %get-tuple-element.35), channel_id=1, source_target_pairs={{0,4},{4,0},{8,12},{12,8},{16,20},{20,16},{24,28},{28,24},{1,5},{5... | collective-permute-start | bytes 786440 | tf_op jit(solution)/shard_map/ppermute | solution.py:358
  15.2 3.1 %collective-permute-start.2 = (f32[8,640]{1,0:T(8,128)S(1)}, f32[8,640]{1,0:T(8,128)S(1)}, u32[]{:S(2)}, u32[]{:S(2)}) collective-permute-start(f32[8,640]{1,0:T(8,128)S(1)} %dynamic-slice_bitcast_fusion.4), channel_id=1, source_target_pairs={{0,16},{4,20},{8,24},{12,28},{16,0},{20,4},{24,8},{28,12},{1,17},{... | collective-permute-start | bytes 61448 | tf_op jit(solution)/shard_map/ppermute | solution.py:358
  18.3 1.8 %collective-permute-done.2 = f32[8,640]{1,0:T(8,128)S(1)} collective-permute-done((f32[8,640]{1,0:T(8,128)S(1)}, f32[8,640]{1,0:T(8,128)S(1)}, u32[]{:S(2)}, u32[]{:S(2)}) %collective-permute-start.2) | collective-permute-done | bytes 20512 | tf_op jit(solution)/shard_map/ppermute | solution.py:358
  20.2 2.0 %collective-permute-start.4 = (f32[128,256]{1,0:T(8,128)S(1)}, f32[128,256]{1,0:T(8,128)S(1)}, u32[]{:S(2)}, u32[]{:S(2)}) collective-permute-start(f32[128,256]{1,0:T(8,128)S(1)} %dynamic-slice_bitcast_fusion), channel_id=1, source_target_pairs={{0,8},{4,12},{8,0},{12,4},{16,24},{20,28},{24,16},{28,20},{1,9},{5... | collective-permute-start | bytes 393224 | tf_op jit(solution)/shard_map/ppermute | solution.py:358
  22.8 5.1 %all-to-all-start = ((f32[8,8,640]{2,1,0:T(8,128)}), f32[8,8,640]{2,1,0:T(8,128)S(1)}, u32[]{:S(2)}, u32[]{:S(2)}) async-start(f32[8,8,640]{2,1,0:T(8,128)} %broadcast_in_dim.2), calls=%async_computation | async-start | bytes 327680 | tf_op jit(solution)/shard_map/all_to_all | solution.py:398
  27.9 7.8 %all-to-all-done = f32[8,8,640]{2,1,0:T(8,128)S(1)} async-done(((f32[8,8,640]{2,1,0:T(8,128)}), f32[8,8,640]{2,1,0:T(8,128)S(1)}, u32[]{:S(2)}, u32[]{:S(2)}) %all-to-all-start) | async-done | bytes 163872 | tf_op jit(solution)/shard_map/all_to_all | solution.py:398
  35.7 1.8 %collective-permute-start.5 = (f32[64,640]{1,0:T(8,128)S(1)}, f32[64,640]{1,0:T(8,128)S(1)}, u32[]{:S(2)}, u32[]{:S(2)}) collective-permute-start(f32[64,640]{1,0:T(8,128)S(1)} %bitcast.33), channel_id=1, source_target_pairs={{0,2},{1,3},{2,0},{3,1},{4,6},{5,7},{6,4},{7,5},{8,10},{9,11},{10,... | collective-permute-start | bytes 491528 | tf_op jit(solution)/shard_map/ppermute | solution.py:358
  38.3 2.8 %collective-permute-done.5.refs_2_ = f32[64,640]{1,0:T(8,128)S(1)} collective-permute-done((f32[64,640]{1,0:T(8,128)S(1)}, f32[64,640]{1,0:T(8,128)S(1)}, u32[]{:S(2)}, u32[]{:S(2)}) %collective-permute-start.5) | collective-permute-done | bytes 163872 | tf_op jit(solution)/shard_map/ppermute | solution.py:358
  41.1 2.1 %collective-permute-done.8 = f32[64,256]{1,0:T(8,128)S(1)} collective-permute-done((f32[64,256]{1,0:T(8,128)S(1)}, f32[64,256]{1,0:T(8,128)S(1)}, u32[]{:S(2)}, u32[]{:S(2)}) %collective-permute-start.8) | collective-permute-done | bytes 65568 | tf_op jit(solution)/shard_map/ppermute | solution.py:358
  43.5 3.8 %block_0.1 = (f32[512,512]{1,0:T(8,128)S(1)}, f32[512,1]{1,0:T(8,128)S(1)}) custom-call(s32[1]{0:T(128)} %bitcast.cell_ref.where_ref, f32[64,640]{1,0:T(8,128)S(1)} %bitcast.35, f32[64,640]{1,0:T(8,128)S(1)} %collective-permute-done.6.refs_1_, f32[64,640]{1,0:T(8,128)S(1)} %collective-permute-done.5.refs_2_, f32[64,640]{1,0:T(8,128)S(1)} %collective-permute-done.7.refs_3_), custom_call_target="tpu_custom_call" | custom-call | flops 1000000000 | bytes 1048576 | tf_op jit(solution)/shard_map/block_0/pallas_call | solution.py:251
  47.4 1.1 %collective-permute-done.9 = f32[64,256]{1,0:T(8,128)S(1)} collective-permute-done((f32[64,256]{1,0:T(8,128)S(1)}, f32[64,256]{1,0:T(8,128)S(1)}, u32[]{:S(2)}, u32[]{:S(2)}) %collective-permute-start.9) | collective-permute-done | bytes 65568 | tf_op jit(solution)/shard_map/ppermute | solution.py:358
  48.5 1.4 %collective-permute-start.10 = (f32[128,256]{1,0:T(8,128)S(1)}, f32[128,256]{1,0:T(8,128)S(1)}, u32[]{:S(2)}, u32[]{:S(2)}) collective-permute-start(f32[128,256]{1,0:T(8,128)S(1)} %pad_maximum_fusion.1), channel_id=1, source_target_pairs={{0,4},{4,0},{8,12},{12,8},{16,20},{20,16},{24,28},{28,24},{1,5},{5... | collective-permute-start | bytes 393224 | tf_op jit(solution)/shard_map/ppermute | solution.py:358
  49.9 3.5 %block_1.1.in_ref = f32[512,512]{1,0:T(8,128)S(1)} custom-call(f32[512,512]{1,0:T(8,128)S(1)} %get-tuple-element.46.in_ref), custom_call_target="tpu_custom_call" | custom-call | flops 1000000000 | bytes 1048576 | tf_op jit(solution)/shard_map/block_1/pallas_call | solution.py:267
  53.7 3.5 %block_2.1.in_ref = f32[512,512]{1,0:T(8,128)S(1)} custom-call(f32[512,512]{1,0:T(8,128)S(1)} %block_1.1.in_ref), custom_call_target="tpu_custom_call" | custom-call | flops 1000000000 | bytes 1048576 | tf_op jit(solution)/shard_map/block_2/pallas_call | solution.py:267
  57.3 3.5 %block_3.1.inverse_ref = f32[512,512]{1,0:T(8,128)S(1)} custom-call(f32[512,512]{1,0:T(8,128)S(1)} %block_2.1.in_ref), custom_call_target="tpu_custom_call" | custom-call | flops 1000000000 | bytes 1048576 | tf_op jit(solution)/shard_map/block_3/pallas_call | solution.py:267
  61.1 1.4 %solve_far.1 = (f32[128,256]{1,0:T(8,128)S(1)}, f32[128,256]{1,0:T(8,128)S(1)}, f32[128,256]{1,0:T(8,128)S(1)}) custom-call(s32[2]{0:T(128)S(1)} %pad_add_fusion.where_ref, s32[8]{0:T(128)S(1)} %copy-done.3, f32[512,512]{1,0:T(8,128)S(1)} %block_3.1.inverse_ref, f32[512,1]{1,0:T(8,128)S(1)} %get-tuple-element.49.scale_ref, ...), custom_call_target="tpu_custom_call" | custom-call | flops 1000000000 | bytes 1048576 | tf_op jit(solution)/shard_map/solve_far/pallas_call | solution.py:325
  62.7 2.3 %collective-permute-start.13 = (f32[128,256]{1,0:T(8,128)S(1)}, f32[128,256]{1,0:T(8,128)S(1)}, u32[]{:S(2)}, u32[]{:S(2)}) collective-permute-start(f32[128,256]{1,0:T(8,128)S(1)} %get-tuple-element.52.refs_3_), channel_id=1, source_target_pairs={{0,2},{1,3},{2,0},{3,1},{4,6},{5,7},{6,4},{7,5},{8,10},{9,11},{10,... | collective-permute-start | bytes 393224 | tf_op jit(solution)/shard_map/ppermute | solution.py:358
  65.0 1.7 %solve_near.1 = (f32[128,256]{1,0:T(8,128)S(1)}, f32[8,256]{1,0:T(8,128)}) custom-call(s32[2]{0:T(128)S(1)} %pad_add_fusion.where_ref, s32[8]{0:T(128)S(1)} %copy-done.3, f32[512,512]{1,0:T(8,128)S(1)} %block_3.1.inverse_ref, f32[512,1]{1,0:T(8,128)S(1)} %get-tuple-element.49.scale_ref, f32[256,256]{1,0:T(8,128)S(1)} %pad_maximum_fusion.refs_0_, ...), custom_call_target="tpu_custom_call" | custom-call | flops 5000000000 | bytes 1048576 | tf_op jit(solution)/shard_map/solve_near/pallas_call | solution.py:325
  66.8 2.5 %collective-permute-done.13.refs_2_ = f32[128,256]{1,0:T(8,128)S(1)} collective-permute-done((f32[128,256]{1,0:T(8,128)S(1)}, f32[128,256]{1,0:T(8,128)S(1)}, u32[]{:S(2)}, u32[]{:S(2)}) %collective-permute-start.13) | collective-permute-done | bytes 131104 | tf_op jit(solution)/shard_map/ppermute | solution.py:358
  69.3 2.3 %collective-permute-done.14.refs_3_ = f32[128,256]{1,0:T(8,128)S(1)} collective-permute-done((f32[128,256]{1,0:T(8,128)S(1)}, f32[128,256]{1,0:T(8,128)S(1)}, u32[]{:S(2)}, u32[]{:S(2)}) %collective-permute-start.14) | collective-permute-done | bytes 131104 | tf_op jit(solution)/shard_map/ppermute | solution.py:358
  (40 shorter events, 6.8 us)
Async XLA Ops:
  0.6 0.9 %copy-start.1 = (f32[24,2048]{1,0:T(8,128)S(1)}, f32[24,2048]{1,0:T(8,128)}, u32[]{:S(2)}) copy-start(f32[24,2048]{1,0:T(8,128)} %points_ref.1) | copy-start | bytes 589828
  1.6 0.7 copy-start.2
  5.6 5.5 %collective-permute-start = (f32[32,640]{1,0:T(8,128)S(1)}, f32[32,640]{1,0:T(8,128)S(1)}, u32[]{:S(2)}, u32[]{:S(2)}) collective-permute-start(f32[32,640]{1,0:T(8,128)S(1)} %dynamic-slice_bitcast_fusion.1), channel_id=1, source_target_pairs={{0,4},{4,0},{8,12},{12,8},{16,20},{20,16},{24,28},{28,24},{1,5},{5... | collective-permute-start | bytes 245768 | tf_op jit(solution)/shard_map/ppermute | solution.py:358
  8.6 1.2 %copy-start = (bf16[2048,256]{1,0:T(8,128)(2,1)S(1)}, bf16[2048,256]{1,0:T(8,128)(2,1)}, u32[]{:S(2)}) copy-start(bf16[2048,256]{1,0:T(8,128)(2,1)} %yields_ref.1) | copy-start | bytes 3145732
  11.1 4.1 %collective-permute-start.1 = (f32[16,640]{1,0:T(8,128)S(1)}, f32[16,640]{1,0:T(8,128)S(1)}, u32[]{:S(2)}, u32[]{:S(2)}) collective-permute-start(f32[16,640]{1,0:T(8,128)S(1)} %dynamic-slice_bitcast_fusion.3), channel_id=1, source_target_pairs={{0,8},{4,12},{8,0},{12,4},{16,24},{20,28},{24,16},{28,20},{1,9},{5... | collective-permute-start | bytes 122888 | tf_op jit(solution)/shard_map/ppermute | solution.py:358
  13.2 6.9 %collective-permute-start.3 = (f32[256,256]{1,0:T(8,128)S(1)}, f32[256,256]{1,0:T(8,128)S(1)}, u32[]{:S(2)}, u32[]{:S(2)}) collective-permute-start(f32[256,256]{1,0:T(8,128)S(1)} %get-tuple-element.35), channel_id=1, source_target_pairs={{0,4},{4,0},{8,12},{12,8},{16,20},{20,16},{24,28},{28,24},{1,5},{5... | collective-permute-start | bytes 786440 | tf_op jit(solution)/shard_map/ppermute | solution.py:358
  15.2 4.9 %collective-permute-start.2 = (f32[8,640]{1,0:T(8,128)S(1)}, f32[8,640]{1,0:T(8,128)S(1)}, u32[]{:S(2)}, u32[]{:S(2)}) collective-permute-start(f32[8,640]{1,0:T(8,128)S(1)} %dynamic-slice_bitcast_fusion.4), channel_id=1, source_target_pairs={{0,16},{4,20},{8,24},{12,28},{16,0},{20,4},{24,8},{28,12},{1,17},{... | collective-permute-start | bytes 61448 | tf_op jit(solution)/shard_map/ppermute | solution.py:358
  20.2 7.7 %collective-permute-start.4 = (f32[128,256]{1,0:T(8,128)S(1)}, f32[128,256]{1,0:T(8,128)S(1)}, u32[]{:S(2)}, u32[]{:S(2)}) collective-permute-start(f32[128,256]{1,0:T(8,128)S(1)} %dynamic-slice_bitcast_fusion), channel_id=1, source_target_pairs={{0,8},{4,12},{8,0},{12,4},{16,24},{20,28},{24,16},{28,20},{1,9},{5... | collective-permute-start | bytes 393224 | tf_op jit(solution)/shard_map/ppermute | solution.py:358
  22.8 12.9 %all-to-all-start = ((f32[8,8,640]{2,1,0:T(8,128)}), f32[8,8,640]{2,1,0:T(8,128)S(1)}, u32[]{:S(2)}, u32[]{:S(2)}) async-start(f32[8,8,640]{2,1,0:T(8,128)} %broadcast_in_dim.2), calls=%async_computation | async-start | bytes 327680 | tf_op jit(solution)/shard_map/all_to_all | solution.py:398
  35.7 5.3 %collective-permute-start.5 = (f32[64,640]{1,0:T(8,128)S(1)}, f32[64,640]{1,0:T(8,128)S(1)}, u32[]{:S(2)}, u32[]{:S(2)}) collective-permute-start(f32[64,640]{1,0:T(8,128)S(1)} %bitcast.33), channel_id=1, source_target_pairs={{0,2},{1,3},{2,0},{3,1},{4,6},{5,7},{6,4},{7,5},{8,10},{9,11},{10,... | collective-permute-start | bytes 491528 | tf_op jit(solution)/shard_map/ppermute | solution.py:358
  37.5 5.6 %collective-permute-start.8 = (f32[64,256]{1,0:T(8,128)S(1)}, f32[64,256]{1,0:T(8,128)S(1)}, u32[]{:S(2)}, u32[]{:S(2)}) collective-permute-start(f32[64,256]{1,0:T(8,128)S(1)} %dynamic-slice_bitcast_fusion.2), channel_id=1, source_target_pairs={{0,16},{4,20},{8,24},{12,28},{16,0},{20,4},{24,8},{28,12},{1,17},{... | collective-permute-start | bytes 196616 | tf_op jit(solution)/shard_map/ppermute | solution.py:358
  38.3 4.9 %collective-permute-start.6 = (f32[64,640]{1,0:T(8,128)S(1)}, f32[64,640]{1,0:T(8,128)S(1)}, u32[]{:S(2)}, u32[]{:S(2)}) collective-permute-start(f32[64,640]{1,0:T(8,128)S(1)} %bitcast.34), channel_id=1, source_target_pairs={{0,1},{1,0},{2,3},{3,2},{4,5},{5,4},{6,7},{7,6},{8,9},{9,8},{10,11... | collective-permute-start | bytes 491528 | tf_op jit(solution)/shard_map/ppermute | solution.py:358
  41.1 2.1 %collective-permute-start.7 = (f32[64,640]{1,0:T(8,128)S(1)}, f32[64,640]{1,0:T(8,128)S(1)}, u32[]{:S(2)}, u32[]{:S(2)}) collective-permute-start(f32[64,640]{1,0:T(8,128)S(1)} %collective-permute-done.5.refs_2_), channel_id=1, source_target_pairs={{0,1},{1,0},{2,3},{3,2},{4,5},{5,4},{6,7},{7,6},{8,9},{9,8},{10,11... | collective-permute-start | bytes 491528 | tf_op jit(solution)/shard_map/ppermute | solution.py:358
  43.2 5.3 %collective-permute-start.9 = (f32[64,256]{1,0:T(8,128)S(1)}, f32[64,256]{1,0:T(8,128)S(1)}, u32[]{:S(2)}, u32[]{:S(2)}) collective-permute-start(f32[64,256]{1,0:T(8,128)S(1)} %bitcast_add_fusion.2), channel_id=1, source_target_pairs={{0,16},{4,20},{8,24},{12,28},{16,0},{20,4},{24,8},{28,12},{1,17},{... | collective-permute-start | bytes 196616 | tf_op jit(solution)/shard_map/ppermute | solution.py:358
  48.5 5.0 %collective-permute-start.10 = (f32[128,256]{1,0:T(8,128)S(1)}, f32[128,256]{1,0:T(8,128)S(1)}, u32[]{:S(2)}, u32[]{:S(2)}) collective-permute-start(f32[128,256]{1,0:T(8,128)S(1)} %pad_maximum_fusion.1), channel_id=1, source_target_pairs={{0,4},{4,0},{8,12},{12,8},{16,20},{20,16},{24,28},{28,24},{1,5},{5... | collective-permute-start | bytes 393224 | tf_op jit(solution)/shard_map/ppermute | solution.py:358
  53.5 7.6 %collective-permute-start.11 = (f32[256,256]{1,0:T(8,128)S(1)}, f32[256,256]{1,0:T(8,128)S(1)}, u32[]{:S(2)}, u32[]{:S(2)}) collective-permute-start(f32[256,256]{1,0:T(8,128)S(1)} %pad_maximum_fusion.refs_0_), channel_id=1, source_target_pairs={{0,8},{4,12},{8,0},{12,4},{16,24},{20,28},{24,16},{28,20},{1,9},{5... | collective-permute-start | bytes 786440 | tf_op jit(solution)/shard_map/ppermute | solution.py:358
  57.3 3.9 %copy-start.3 = (s32[8]{0:T(128)S(1)}, s32[8]{0:T(128)}, u32[]{:S(2)}) copy-start(s32[8]{0:T(128)} %group_ref.3) | copy-start | bytes 100
  62.6 4.2 %collective-permute-start.12 = (f32[128,256]{1,0:T(8,128)S(1)}, f32[128,256]{1,0:T(8,128)S(1)}, u32[]{:S(2)}, u32[]{:S(2)}) collective-permute-start(f32[128,256]{1,0:T(8,128)S(1)} %get-tuple-element.51.refs_2_), channel_id=1, source_target_pairs={{0,1},{1,0},{2,3},{3,2},{4,5},{5,4},{6,7},{7,6},{8,9},{9,8},{10,11... | collective-permute-start | bytes 393224 | tf_op jit(solution)/shard_map/ppermute | solution.py:358
  62.7 6.6 %collective-permute-start.13 = (f32[128,256]{1,0:T(8,128)S(1)}, f32[128,256]{1,0:T(8,128)S(1)}, u32[]{:S(2)}, u32[]{:S(2)}) collective-permute-start(f32[128,256]{1,0:T(8,128)S(1)} %get-tuple-element.52.refs_3_), channel_id=1, source_target_pairs={{0,2},{1,3},{2,0},{3,1},{4,6},{5,7},{6,4},{7,5},{8,10},{9,11},{10,... | collective-permute-start | bytes 393224 | tf_op jit(solution)/shard_map/ppermute | solution.py:358
  64.9 6.6 %collective-permute-start.14 = (f32[128,256]{1,0:T(8,128)S(1)}, f32[128,256]{1,0:T(8,128)S(1)}, u32[]{:S(2)}, u32[]{:S(2)}) collective-permute-start(f32[128,256]{1,0:T(8,128)S(1)} %get-tuple-element.53.refs_4_), channel_id=1, source_target_pairs={{0,3},{1,2},{2,1},{3,0},{4,7},{5,6},{6,5},{7,4},{8,11},{9,10},{10,... | collective-permute-start | bytes 393224 | tf_op jit(solution)/shard_map/ppermute | solution.py:358

commit v13 on v12

--- a/solution.py
+++ b/solution.py
@@ -61,8 +61,8 @@
         for block in range(blocks)
     ], axis=0)
     value = lax.dot_general(
-        psi_ref[...], rows, (((1,), (1,)), ((), ())), preferred_element_type=jnp.float32
-    ).T
+        rows, psi_ref[...], (((1,), (1,)), ((), ())), preferred_element_type=jnp.float32
+    )
     for block in range(blocks):
         reach = (block + 1) * TILE
         half, at = fold_place(block, blocks)

time: 72.7 us -> 71.7 us (0.986)
  Pallas kernels: 22.4 us -> 21.3 us
    pallas_call x1, Pallas kernels: 3.29 us -> 2.23 us  [design(): pl.pallas_call(functools.partial(design_kernel, 512), out_shape=(jax.Shap...]
  transfers between devices with their start and end apart: 16 -> 16, of which waited for: 11 -> 11; matrix products, arithmetic and copies ran while one was open for 1% -> 1% of each run, Pallas kernels for 23% -> 24%
where the time goes in v13:
time: 71.7 us; the launch traced here: 71.4 us
  starting transfers between devices  23.6 us (33%)
  waiting for transfers between devices  21.8 us (30%)
  Pallas kernels  21.3 us (30%)
  local copies, waits for them, and re-layouts  3.57 us (5%)
  between operations  0.82 us (1%)
    ppermute x15, starting transfers between devices, swap(): return lax.ppermute(values, axis, [(at, at ^ step) for at in range(size)])  18.5 us
    ppermute x15, waiting for transfers between devices, swap(): return lax.ppermute(values, axis, [(at, at ^ step) for at in range(size)])  14 us
    pallas_call x3, Pallas kernels, next_block(): pl.pallas_call(functools.partial(next_kernel, block), out_shape=jax.Shape...  10.6 us
    all_to_all x1, waiting for transfers between devices, on_device(): lax.all_to_all(copies, 'samp', split_axis=0, concat_axis=0)[:8]  7.82 us
    all_to_all x1, starting transfers between devices, on_device(): lax.all_to_all(copies, 'samp', split_axis=0, concat_axis=0)[:8]  5.08 us
    pallas_call x1, Pallas kernels, first_block(): pl.pallas_call(first_kernel, out_shape=(jax.ShapeDtypeStruct((terms, term...  3.81 us
    pallas_call x2, Pallas kernels, solve(): pl.pallas_call(functools.partial(solve_kernel, samples, steps, rows, fini...  3.18 us
    unnamed x8, local copies, waits for them, and re-layouts  2.84 us
  transfers between devices with their start and end apart: 16, of which 11 were waited for; matrix products, arithmetic and copies ran while one was open for 1% of the time, Pallas kernels for 24%

profile of v13, /device:TPU:0, one launch (start us, length us, event | category | flops | bytes accessed | tf_op | source)
XLA Modules:
  0.0 71.4 jit_solution(2004954201569551795)
XLA Ops:
  2.3 2.2 %design.1 = (bf16[512,2048]{1,0:T(8,128)(2,1)S(1)}, f32[64,640]{1,0:T(8,128)S(1)}) custom-call(s32[1]{0:T(128)} %bitcast.cell_ref.where_ref, s32[2,512]{1,0:T(2,128)S(1)} %bitcast.38, f32[24,2048]{1,0:T(8,128)S(1)} %copy-done.1), custom_call_target="tpu_custom_call" | custom-call | tf_op jit(solution)/shard_map/design/pallas_call | solution.py:84
  4.5 3.0 %collective-permute-start = (f32[32,640]{1,0:T(8,128)S(1)}, f32[32,640]{1,0:T(8,128)S(1)}, u32[]{:S(2)}, u32[]{:S(2)}) collective-permute-start(f32[32,640]{1,0:T(8,128)S(1)} %dynamic-slice_bitcast_fusion.1), channel_id=1, source_target_pairs={{0,4},{4,0},{8,12},{12,8},{16,20},{20,16},{24,28},{28,24},{1,5},{5... | collective-permute-start | bytes 245768 | tf_op jit(solution)/shard_map/ppermute | solution.py:358
  7.5 1.2 %copy-done = bf16[2048,256]{1,0:T(8,128)(2,1)S(1)} copy-done((bf16[2048,256]{1,0:T(8,128)(2,1)S(1)}, bf16[2048,256]{1,0:T(8,128)(2,1)}, u32[]{:S(2)}) %copy-start) | copy-done | bytes 1048600
  10.0 2.1 %collective-permute-start.1 = (f32[16,640]{1,0:T(8,128)S(1)}, f32[16,640]{1,0:T(8,128)S(1)}, u32[]{:S(2)}, u32[]{:S(2)}) collective-permute-start(f32[16,640]{1,0:T(8,128)S(1)} %dynamic-slice_bitcast_fusion.3), channel_id=1, source_target_pairs={{0,8},{4,12},{8,0},{12,4},{16,24},{20,28},{24,16},{28,20},{1,9},{5... | collective-permute-start | bytes 122888 | tf_op jit(solution)/shard_map/ppermute | solution.py:358
  12.1 1.5 %collective-permute-start.3 = (f32[256,256]{1,0:T(8,128)S(1)}, f32[256,256]{1,0:T(8,128)S(1)}, u32[]{:S(2)}, u32[]{:S(2)}) collective-permute-start(f32[256,256]{1,0:T(8,128)S(1)} %get-tuple-element.35), channel_id=1, source_target_pairs={{0,4},{4,0},{8,12},{12,8},{16,20},{20,16},{24,28},{28,24},{1,5},{5... | collective-permute-start | bytes 786440 | tf_op jit(solution)/shard_map/ppermute | solution.py:358
  14.2 3.1 %collective-permute-start.2 = (f32[8,640]{1,0:T(8,128)S(1)}, f32[8,640]{1,0:T(8,128)S(1)}, u32[]{:S(2)}, u32[]{:S(2)}) collective-permute-start(f32[8,640]{1,0:T(8,128)S(1)} %dynamic-slice_bitcast_fusion.4), channel_id=1, source_target_pairs={{0,16},{4,20},{8,24},{12,28},{16,0},{20,4},{24,8},{28,12},{1,17},{... | collective-permute-start | bytes 61448 | tf_op jit(solution)/shard_map/ppermute | solution.py:358
  17.3 1.8 %collective-permute-done.2 = f32[8,640]{1,0:T(8,128)S(1)} collective-permute-done((f32[8,640]{1,0:T(8,128)S(1)}, f32[8,640]{1,0:T(8,128)S(1)}, u32[]{:S(2)}, u32[]{:S(2)}) %collective-permute-start.2) | collective-permute-done | bytes 20512 | tf_op jit(solution)/shard_map/ppermute | solution.py:358
  19.1 2.0 %collective-permute-start.4 = (f32[128,256]{1,0:T(8,128)S(1)}, f32[128,256]{1,0:T(8,128)S(1)}, u32[]{:S(2)}, u32[]{:S(2)}) collective-permute-start(f32[128,256]{1,0:T(8,128)S(1)} %dynamic-slice_bitcast_fusion), channel_id=1, source_target_pairs={{0,8},{4,12},{8,0},{12,4},{16,24},{20,28},{24,16},{28,20},{1,9},{5... | collective-permute-start | bytes 393224 | tf_op jit(solution)/shard_map/ppermute | solution.py:358
  21.7 5.1 %all-to-all-start = ((f32[8,8,640]{2,1,0:T(8,128)}), f32[8,8,640]{2,1,0:T(8,128)S(1)}, u32[]{:S(2)}, u32[]{:S(2)}) async-start(f32[8,8,640]{2,1,0:T(8,128)} %broadcast_in_dim.2), calls=%async_computation | async-start | bytes 327680 | tf_op jit(solution)/shard_map/all_to_all | solution.py:398
  26.9 7.8 %all-to-all-done = f32[8,8,640]{2,1,0:T(8,128)S(1)} async-done(((f32[8,8,640]{2,1,0:T(8,128)}), f32[8,8,640]{2,1,0:T(8,128)S(1)}, u32[]{:S(2)}, u32[]{:S(2)}) %all-to-all-start) | async-done | bytes 163872 | tf_op jit(solution)/shard_map/all_to_all | solution.py:398
  34.7 1.8 %collective-permute-start.5 = (f32[64,640]{1,0:T(8,128)S(1)}, f32[64,640]{1,0:T(8,128)S(1)}, u32[]{:S(2)}, u32[]{:S(2)}) collective-permute-start(f32[64,640]{1,0:T(8,128)S(1)} %bitcast.33), channel_id=1, source_target_pairs={{0,2},{1,3},{2,0},{3,1},{4,6},{5,7},{6,4},{7,5},{8,10},{9,11},{10,... | collective-permute-start | bytes 491528 | tf_op jit(solution)/shard_map/ppermute | solution.py:358
  37.2 2.8 %collective-permute-done.5.refs_2_ = f32[64,640]{1,0:T(8,128)S(1)} collective-permute-done((f32[64,640]{1,0:T(8,128)S(1)}, f32[64,640]{1,0:T(8,128)S(1)}, u32[]{:S(2)}, u32[]{:S(2)}) %collective-permute-start.5) | collective-permute-done | bytes 163872 | tf_op jit(solution)/shard_map/ppermute | solution.py:358
  40.0 2.1 %collective-permute-done.8 = f32[64,256]{1,0:T(8,128)S(1)} collective-permute-done((f32[64,256]{1,0:T(8,128)S(1)}, f32[64,256]{1,0:T(8,128)S(1)}, u32[]{:S(2)}, u32[]{:S(2)}) %collective-permute-start.8) | collective-permute-done | bytes 65568 | tf_op jit(solution)/shard_map/ppermute | solution.py:358
  42.5 3.8 %block_0.1 = (f32[512,512]{1,0:T(8,128)S(1)}, f32[512,1]{1,0:T(8,128)S(1)}) custom-call(s32[1]{0:T(128)} %bitcast.cell_ref.where_ref, f32[64,640]{1,0:T(8,128)S(1)} %bitcast.35, f32[64,640]{1,0:T(8,128)S(1)} %collective-permute-done.6.refs_1_, f32[64,640]{1,0:T(8,128)S(1)} %collective-permute-done.5.refs_2_, f32[64,640]{1,0:T(8,128)S(1)} %collective-permute-done.7.refs_3_), custom_call_target="tpu_custom_call" | custom-call | flops 1000000000 | bytes 1048576 | tf_op jit(solution)/shard_map/block_0/pallas_call | solution.py:251
  46.3 1.1 %collective-permute-done.9 = f32[64,256]{1,0:T(8,128)S(1)} collective-permute-done((f32[64,256]{1,0:T(8,128)S(1)}, f32[64,256]{1,0:T(8,128)S(1)}, u32[]{:S(2)}, u32[]{:S(2)}) %collective-permute-start.9) | collective-permute-done | bytes 65568 | tf_op jit(solution)/shard_map/ppermute | solution.py:358
  47.4 1.4 %collective-permute-start.10 = (f32[128,256]{1,0:T(8,128)S(1)}, f32[128,256]{1,0:T(8,128)S(1)}, u32[]{:S(2)}, u32[]{:S(2)}) collective-permute-start(f32[128,256]{1,0:T(8,128)S(1)} %pad_maximum_fusion.1), channel_id=1, source_target_pairs={{0,4},{4,0},{8,12},{12,8},{16,20},{20,16},{24,28},{28,24},{1,5},{5... | collective-permute-start | bytes 393224 | tf_op jit(solution)/shard_map/ppermute | solution.py:358
  48.8 3.5 %block_1.1.in_ref = f32[512,512]{1,0:T(8,128)S(1)} custom-call(f32[512,512]{1,0:T(8,128)S(1)} %get-tuple-element.46.in_ref), custom_call_target="tpu_custom_call" | custom-call | flops 1000000000 | bytes 1048576 | tf_op jit(solution)/shard_map/block_1/pallas_call | solution.py:267
  52.7 3.5 %block_2.1.in_ref = f32[512,512]{1,0:T(8,128)S(1)} custom-call(f32[512,512]{1,0:T(8,128)S(1)} %block_1.1.in_ref), custom_call_target="tpu_custom_call" | custom-call | flops 1000000000 | bytes 1048576 | tf_op jit(solution)/shard_map/block_2/pallas_call | solution.py:267
  56.2 3.5 %block_3.1.inverse_ref = f32[512,512]{1,0:T(8,128)S(1)} custom-call(f32[512,512]{1,0:T(8,128)S(1)} %block_2.1.in_ref), custom_call_target="tpu_custom_call" | custom-call | flops 1000000000 | bytes 1048576 | tf_op jit(solution)/shard_map/block_3/pallas_call | solution.py:267
  60.1 1.4 %solve_far.1 = (f32[128,256]{1,0:T(8,128)S(1)}, f32[128,256]{1,0:T(8,128)S(1)}, f32[128,256]{1,0:T(8,128)S(1)}) custom-call(s32[2]{0:T(128)S(1)} %pad_add_fusion.where_ref, s32[8]{0:T(128)S(1)} %copy-done.3, f32[512,512]{1,0:T(8,128)S(1)} %block_3.1.inverse_ref, f32[512,1]{1,0:T(8,128)S(1)} %get-tuple-element.49.scale_ref, ...), custom_call_target="tpu_custom_call" | custom-call | flops 1000000000 | bytes 1048576 | tf_op jit(solution)/shard_map/solve_far/pallas_call | solution.py:325
  61.6 2.3 %collective-permute-start.13 = (f32[128,256]{1,0:T(8,128)S(1)}, f32[128,256]{1,0:T(8,128)S(1)}, u32[]{:S(2)}, u32[]{:S(2)}) collective-permute-start(f32[128,256]{1,0:T(8,128)S(1)} %get-tuple-element.52.refs_3_), channel_id=1, source_target_pairs={{0,2},{1,3},{2,0},{3,1},{4,6},{5,7},{6,4},{7,5},{8,10},{9,11},{10,... | collective-permute-start | bytes 393224 | tf_op jit(solution)/shard_map/ppermute | solution.py:358
  64.0 1.7 %solve_near.1 = (f32[128,256]{1,0:T(8,128)S(1)}, f32[8,256]{1,0:T(8,128)}) custom-call(s32[2]{0:T(128)S(1)} %pad_add_fusion.where_ref, s32[8]{0:T(128)S(1)} %copy-done.3, f32[512,512]{1,0:T(8,128)S(1)} %block_3.1.inverse_ref, f32[512,1]{1,0:T(8,128)S(1)} %get-tuple-element.49.scale_ref, f32[256,256]{1,0:T(8,128)S(1)} %pad_maximum_fusion.refs_0_, ...), custom_call_target="tpu_custom_call" | custom-call | flops 5000000000 | bytes 1048576 | tf_op jit(solution)/shard_map/solve_near/pallas_call | solution.py:325
  65.7 2.5 %collective-permute-done.13.refs_2_ = f32[128,256]{1,0:T(8,128)S(1)} collective-permute-done((f32[128,256]{1,0:T(8,128)S(1)}, f32[128,256]{1,0:T(8,128)S(1)}, u32[]{:S(2)}, u32[]{:S(2)}) %collective-permute-start.13) | collective-permute-done | bytes 131104 | tf_op jit(solution)/shard_map/ppermute | solution.py:358
  68.2 2.3 %collective-permute-done.14.refs_3_ = f32[128,256]{1,0:T(8,128)S(1)} collective-permute-done((f32[128,256]{1,0:T(8,128)S(1)}, f32[128,256]{1,0:T(8,128)S(1)}, u32[]{:S(2)}, u32[]{:S(2)}) %collective-permute-start.14) | collective-permute-done | bytes 131104 | tf_op jit(solution)/shard_map/ppermute | solution.py:358
  (40 shorter events, 6.8 us)
Async XLA Ops:
  0.6 0.9 %copy-start.1 = (f32[24,2048]{1,0:T(8,128)S(1)}, f32[24,2048]{1,0:T(8,128)}, u32[]{:S(2)}) copy-start(f32[24,2048]{1,0:T(8,128)} %points_ref.1) | copy-start | bytes 589828
  1.6 0.7 copy-start.2
  4.5 5.5 %collective-permute-start = (f32[32,640]{1,0:T(8,128)S(1)}, f32[32,640]{1,0:T(8,128)S(1)}, u32[]{:S(2)}, u32[]{:S(2)}) collective-permute-start(f32[32,640]{1,0:T(8,128)S(1)} %dynamic-slice_bitcast_fusion.1), channel_id=1, source_target_pairs={{0,4},{4,0},{8,12},{12,8},{16,20},{20,16},{24,28},{28,24},{1,5},{5... | collective-permute-start | bytes 245768 | tf_op jit(solution)/shard_map/ppermute | solution.py:358
  7.5 1.2 %copy-start = (bf16[2048,256]{1,0:T(8,128)(2,1)S(1)}, bf16[2048,256]{1,0:T(8,128)(2,1)}, u32[]{:S(2)}) copy-start(bf16[2048,256]{1,0:T(8,128)(2,1)} %yields_ref.1) | copy-start | bytes 3145732
  10.0 4.1 %collective-permute-start.1 = (f32[16,640]{1,0:T(8,128)S(1)}, f32[16,640]{1,0:T(8,128)S(1)}, u32[]{:S(2)}, u32[]{:S(2)}) collective-permute-start(f32[16,640]{1,0:T(8,128)S(1)} %dynamic-slice_bitcast_fusion.3), channel_id=1, source_target_pairs={{0,8},{4,12},{8,0},{12,4},{16,24},{20,28},{24,16},{28,20},{1,9},{5... | collective-permute-start | bytes 122888 | tf_op jit(solution)/shard_map/ppermute | solution.py:358
  12.1 6.9 %collective-permute-start.3 = (f32[256,256]{1,0:T(8,128)S(1)}, f32[256,256]{1,0:T(8,128)S(1)}, u32[]{:S(2)}, u32[]{:S(2)}) collective-permute-start(f32[256,256]{1,0:T(8,128)S(1)} %get-tuple-element.35), channel_id=1, source_target_pairs={{0,4},{4,0},{8,12},{12,8},{16,20},{20,16},{24,28},{28,24},{1,5},{5... | collective-permute-start | bytes 786440 | tf_op jit(solution)/shard_map/ppermute | solution.py:358
  14.2 4.9 %collective-permute-start.2 = (f32[8,640]{1,0:T(8,128)S(1)}, f32[8,640]{1,0:T(8,128)S(1)}, u32[]{:S(2)}, u32[]{:S(2)}) collective-permute-start(f32[8,640]{1,0:T(8,128)S(1)} %dynamic-slice_bitcast_fusion.4), channel_id=1, source_target_pairs={{0,16},{4,20},{8,24},{12,28},{16,0},{20,4},{24,8},{28,12},{1,17},{... | collective-permute-start | bytes 61448 | tf_op jit(solution)/shard_map/ppermute | solution.py:358
  19.1 7.7 %collective-permute-start.4 = (f32[128,256]{1,0:T(8,128)S(1)}, f32[128,256]{1,0:T(8,128)S(1)}, u32[]{:S(2)}, u32[]{:S(2)}) collective-permute-start(f32[128,256]{1,0:T(8,128)S(1)} %dynamic-slice_bitcast_fusion), channel_id=1, source_target_pairs={{0,8},{4,12},{8,0},{12,4},{16,24},{20,28},{24,16},{28,20},{1,9},{5... | collective-permute-start | bytes 393224 | tf_op jit(solution)/shard_map/ppermute | solution.py:358
  21.7 12.9 %all-to-all-start = ((f32[8,8,640]{2,1,0:T(8,128)}), f32[8,8,640]{2,1,0:T(8,128)S(1)}, u32[]{:S(2)}, u32[]{:S(2)}) async-start(f32[8,8,640]{2,1,0:T(8,128)} %broadcast_in_dim.2), calls=%async_computation | async-start | bytes 327680 | tf_op jit(solution)/shard_map/all_to_all | solution.py:398
  34.7 5.3 %collective-permute-start.5 = (f32[64,640]{1,0:T(8,128)S(1)}, f32[64,640]{1,0:T(8,128)S(1)}, u32[]{:S(2)}, u32[]{:S(2)}) collective-permute-start(f32[64,640]{1,0:T(8,128)S(1)} %bitcast.33), channel_id=1, source_target_pairs={{0,2},{1,3},{2,0},{3,1},{4,6},{5,7},{6,4},{7,5},{8,10},{9,11},{10,... | collective-permute-start | bytes 491528 | tf_op jit(solution)/shard_map/ppermute | solution.py:358
  36.5 5.6 %collective-permute-start.8 = (f32[64,256]{1,0:T(8,128)S(1)}, f32[64,256]{1,0:T(8,128)S(1)}, u32[]{:S(2)}, u32[]{:S(2)}) collective-permute-start(f32[64,256]{1,0:T(8,128)S(1)} %dynamic-slice_bitcast_fusion.2), channel_id=1, source_target_pairs={{0,16},{4,20},{8,24},{12,28},{16,0},{20,4},{24,8},{28,12},{1,17},{... | collective-permute-start | bytes 196616 | tf_op jit(solution)/shard_map/ppermute | solution.py:358
  37.2 4.9 %collective-permute-start.6 = (f32[64,640]{1,0:T(8,128)S(1)}, f32[64,640]{1,0:T(8,128)S(1)}, u32[]{:S(2)}, u32[]{:S(2)}) collective-permute-start(f32[64,640]{1,0:T(8,128)S(1)} %bitcast.34), channel_id=1, source_target_pairs={{0,1},{1,0},{2,3},{3,2},{4,5},{5,4},{6,7},{7,6},{8,9},{9,8},{10,11... | collective-permute-start | bytes 491528 | tf_op jit(solution)/shard_map/ppermute | solution.py:358
  40.0 2.1 %collective-permute-start.7 = (f32[64,640]{1,0:T(8,128)S(1)}, f32[64,640]{1,0:T(8,128)S(1)}, u32[]{:S(2)}, u32[]{:S(2)}) collective-permute-start(f32[64,640]{1,0:T(8,128)S(1)} %collective-permute-done.5.refs_2_), channel_id=1, source_target_pairs={{0,1},{1,0},{2,3},{3,2},{4,5},{5,4},{6,7},{7,6},{8,9},{9,8},{10,11... | collective-permute-start | bytes 491528 | tf_op jit(solution)/shard_map/ppermute | solution.py:358
  42.1 5.3 %collective-permute-start.9 = (f32[64,256]{1,0:T(8,128)S(1)}, f32[64,256]{1,0:T(8,128)S(1)}, u32[]{:S(2)}, u32[]{:S(2)}) collective-permute-start(f32[64,256]{1,0:T(8,128)S(1)} %bitcast_add_fusion.2), channel_id=1, source_target_pairs={{0,16},{4,20},{8,24},{12,28},{16,0},{20,4},{24,8},{28,12},{1,17},{... | collective-permute-start | bytes 196616 | tf_op jit(solution)/shard_map/ppermute | solution.py:358
  47.4 5.0 %collective-permute-start.10 = (f32[128,256]{1,0:T(8,128)S(1)}, f32[128,256]{1,0:T(8,128)S(1)}, u32[]{:S(2)}, u32[]{:S(2)}) collective-permute-start(f32[128,256]{1,0:T(8,128)S(1)} %pad_maximum_fusion.1), channel_id=1, source_target_pairs={{0,4},{4,0},{8,12},{12,8},{16,20},{20,16},{24,28},{28,24},{1,5},{5... | collective-permute-start | bytes 393224 | tf_op jit(solution)/shard_map/ppermute | solution.py:358
  52.5 7.6 %collective-permute-start.11 = (f32[256,256]{1,0:T(8,128)S(1)}, f32[256,256]{1,0:T(8,128)S(1)}, u32[]{:S(2)}, u32[]{:S(2)}) collective-permute-start(f32[256,256]{1,0:T(8,128)S(1)} %pad_maximum_fusion.refs_0_), channel_id=1, source_target_pairs={{0,8},{4,12},{8,0},{12,4},{16,24},{20,28},{24,16},{28,20},{1,9},{5... | collective-permute-start | bytes 786440 | tf_op jit(solution)/shard_map/ppermute | solution.py:358
  56.2 3.9 %copy-start.3 = (s32[8]{0:T(128)S(1)}, s32[8]{0:T(128)}, u32[]{:S(2)}) copy-start(s32[8]{0:T(128)} %group_ref.3) | copy-start | bytes 100
  61.5 4.2 %collective-permute-start.12 = (f32[128,256]{1,0:T(8,128)S(1)}, f32[128,256]{1,0:T(8,128)S(1)}, u32[]{:S(2)}, u32[]{:S(2)}) collective-permute-start(f32[128,256]{1,0:T(8,128)S(1)} %get-tuple-element.51.refs_2_), channel_id=1, source_target_pairs={{0,1},{1,0},{2,3},{3,2},{4,5},{5,4},{6,7},{7,6},{8,9},{9,8},{10,11... | collective-permute-start | bytes 393224 | tf_op jit(solution)/shard_map/ppermute | solution.py:358
  61.6 6.6 %collective-permute-start.13 = (f32[128,256]{1,0:T(8,128)S(1)}, f32[128,256]{1,0:T(8,128)S(1)}, u32[]{:S(2)}, u32[]{:S(2)}) collective-permute-start(f32[128,256]{1,0:T(8,128)S(1)} %get-tuple-element.52.refs_3_), channel_id=1, source_target_pairs={{0,2},{1,3},{2,0},{3,1},{4,6},{5,7},{6,4},{7,5},{8,10},{9,11},{10,... | collective-permute-start | bytes 393224 | tf_op jit(solution)/shard_map/ppermute | solution.py:358
  63.9 6.6 %collective-permute-start.14 = (f32[128,256]{1,0:T(8,128)S(1)}, f32[128,256]{1,0:T(8,128)S(1)}, u32[]{:S(2)}, u32[]{:S(2)}) collective-permute-start(f32[128,256]{1,0:T(8,128)S(1)} %get-tuple-element.53.refs_4_), channel_id=1, source_target_pairs={{0,3},{1,2},{2,1},{3,0},{4,7},{5,6},{6,5},{7,4},{8,11},{9,10},{10,... | collective-permute-start | bytes 393224 | tf_op jit(solution)/shard_map/ppermute | solution.py:358
